TPU v7x, 32 devices: a whole 2x2x4 slice. The times are simulated.
32 devices in a mesh: groups: 2 (over x), ep: 8 (over z, y), sub: 2 (over core).
Axes of the slice: x: 2, y: 2, z: 4, core: 2. Of those that a mesh axis runs over, the one named last changes fastest.
Arguments:
- tokens: bfloat16 [2048, 2048], P(('groups', 'ep', 'sub')), parts along dimension 0, may hold values from -6 to 6
- routes: int32 [2048, 8], P(('groups', 'ep', 'sub')), parts along dimension 0, may hold values from 0 to 15, all different within a row; in each aligned block of 64 rows (0 to 63, 64 to 127, ...) at most 64 rows name the same one
- gates: float32 [2048, 8], P(('groups', 'ep', 'sub')), parts along dimension 0, may hold values from 0.05 to 1
- priority: int32 [2048], P(('groups', 'ep', 'sub')), parts along dimension 0, may hold values from 0 to 15
- capacity: int32 [16], replicated, may hold values from 320 to 640, as said below
- w_gate: bfloat16 [16, 2048, 768], P(('ep', 'sub')), may hold values from -0.125 to 0.125
- w_up: bfloat16 [16, 2048, 768], P(('ep', 'sub')), may hold values from -0.125 to 0.125
- w_down: bfloat16 [16, 768, 2048], P(('ep', 'sub')), may hold values from -0.21875 to 0.21875
Outputs:
- mixed: bfloat16 [2048, 2048], P(('groups', 'ep', 'sub')), parts along dimension 0
There are 2 independent parts, one for each index of `groups`. A program takes and returns all parts, laid end to end along the dimension named above; an argument that names none is the same for every part. Nothing has to cross between parts.
Inputs may be any that keep to these rules, and one draw needn't show every extreme that they name: `capacity`: each expert accepts between 320 and 640 entries; some expert accepts exactly 640.
All inputs are finite; a program needn't handle non-finite values.
Results may differ from a plain program's by a relative error of at most 0.0069.
Values may be sent and summed in bfloat16 or wider, within the bound.
No kernel may reach another device: no remote copies, remote signals or barrier semaphores. Data moves between devices by JAX's collectives and lax.ppermute only.
A program may use at most 64 MiB of HBM per device.

v0:
```python
import jax
import jax.numpy as jnp
from jax import lax
from jax.sharding import PartitionSpec as P

PRIO = 16


block_width = 128


def prefix(array, axis, combine, identity):
    size, place = (lax.axis_size(axis), lax.axis_index(axis))
    everything = lax.all_gather(array, axis)
    start = jnp.broadcast_to(jnp.asarray(identity, array.dtype), array.shape)

    def step(k, before):
        reached = k < place
        new = combine(before, everything[k])
        return jnp.where(reached, new, before)

    return lax.fori_loop(0, size, step, start)


def quantize(activations):
    count = activations.shape[0]
    blocks = activations.astype(jnp.float32).reshape(count, -1, block_width)
    largest = jnp.max(jnp.abs(blocks), axis=-1)
    scales = ((largest + 1e-06) / 448.0).astype(jnp.bfloat16)
    quantized = (blocks / scales.astype(jnp.float32)[..., None]).astype(jnp.bfloat16)
    return (quantized.reshape(count, -1), scales)


def expert_apply(quantized, scales, gate_matrix, up_matrix, down_matrix):
    count = quantized.shape[0]
    restored = (
        quantized.reshape(count, -1, block_width).astype(jnp.float32)
        * scales.astype(jnp.float32)[..., None]
    )
    restored = restored.astype(jnp.bfloat16).reshape(count, -1)
    gated = jnp.dot(restored, gate_matrix, preferred_element_type=jnp.float32)
    upward = jnp.dot(restored, up_matrix, preferred_element_type=jnp.float32)
    hidden = (jax.nn.silu(gated) * upward).astype(jnp.bfloat16)
    return jnp.dot(hidden, down_matrix, preferred_element_type=jnp.float32).astype(jnp.bfloat16)


def combine_add(earlier, later):
    return earlier + later


def on_device(tokens, routes, gates, priority, capacity, w_gate, w_up, w_down):
    devices = lax.axis_size("ep") * lax.axis_size("sub")
    tok_rows, width = tokens.shape
    top_count = routes.shape[1]
    slot_count = 2 * tok_rows * top_count // devices
    entries = tok_rows * top_count
    quantized, scales = quantize(tokens)
    flat_expert = routes.reshape(-1)
    flat_token = jnp.arange(entries, dtype=jnp.int32) // top_count
    flat_prio = jnp.repeat(priority, top_count)
    classes = flat_expert * PRIO + flat_prio
    class_hot = (classes[:, None] == jnp.arange(devices * PRIO, dtype=jnp.int32)[None, :]).astype(
        jnp.float32
    )
    counts = jnp.sum(class_hot, axis=0).reshape(devices, PRIO)
    before = prefix(counts, ("ep", "sub"), combine_add, jnp.zeros_like(counts))
    totals = lax.psum(counts, ("ep", "sub"))
    below = jnp.cumsum(totals, axis=1) - totals
    base = jnp.dot(class_hot, (below + before).reshape(-1), precision=lax.Precision.HIGHEST)
    earlier_token = flat_token[None, :] < flat_token[:, None]
    same_class = (classes[:, None] == classes[None, :]) & earlier_token
    rank = base + jnp.sum(same_class.astype(jnp.float32), axis=1)
    expert_hot = (flat_expert[:, None] == jnp.arange(devices, dtype=jnp.int32)[None, :]).astype(
        jnp.float32
    )
    limit = jnp.dot(expert_hot, capacity.astype(jnp.float32), precision=lax.Precision.HIGHEST)
    kept = rank < limit
    flat_order = jnp.arange(entries, dtype=jnp.int32)
    same_expert = (flat_expert[:, None] == flat_expert[None, :]) & (
        flat_order[None, :] < flat_order[:, None]
    )
    slot_index = jnp.sum(same_expert.astype(jnp.int32), axis=1)
    position = flat_expert * slot_count + slot_index
    source = jnp.full((devices * slot_count,), entries, jnp.int32).at[position].set(flat_order)
    kept_padded = jnp.concatenate([kept, jnp.zeros((1,), bool)])
    live_slot = kept_padded[source]
    source_token = jnp.minimum(source, entries - 1) // top_count
    send_rows = jnp.where(live_slot[:, None], quantized[source_token], jnp.zeros((), jnp.bfloat16))
    send_scales = jnp.where(live_slot[:, None], scales[source_token], jnp.zeros((), jnp.bfloat16))
    send_rows = send_rows.reshape(devices, slot_count, width)
    send_scales = send_scales.reshape(devices, slot_count, -1)
    recv_rows, recv_scales = (
        lax.all_to_all(send_rows, ("ep", "sub"), split_axis=0, concat_axis=0, tiled=True),
        lax.all_to_all(send_scales, ("ep", "sub"), split_axis=0, concat_axis=0, tiled=True),
    )
    received = devices * slot_count
    recv_rows = recv_rows.reshape(received, width)
    recv_scales = recv_scales.reshape(received, -1)
    outputs = expert_apply(recv_rows, recv_scales, w_gate[0], w_up[0], w_down[0])
    returned = lax.all_to_all(
        outputs.reshape(devices, slot_count, width),
        ("ep", "sub"),
        split_axis=0,
        concat_axis=0,
        tiled=True,
    )
    returned = returned.reshape(received, width)
    entry_rows = returned[position]
    weights = jnp.where(kept, gates.reshape(-1), jnp.zeros((), jnp.float32))
    summed = jnp.sum(
        (entry_rows.astype(jnp.float32) * weights[:, None]).reshape(tok_rows, top_count, width),
        axis=1,
    )
    return summed.astype(jnp.bfloat16)


def solution(mesh):
    in_specs = (
        P(("groups", "ep", "sub"), None),
        P(("groups", "ep", "sub"), None),
        P(("groups", "ep", "sub"), None),
        P(("groups", "ep", "sub")),
        P(),
        P(("ep", "sub"), None, None),
        P(("ep", "sub"), None, None),
        P(("ep", "sub"), None, None),
    )
    out_specs = P(("groups", "ep", "sub"), None)
    return jax.shard_map(
        on_device, mesh=mesh, in_specs=in_specs, out_specs=out_specs, check_vma=False
    )
```

profile of v0, /device:TPU:13, one launch (start us, length us, event | category | flops | bytes accessed | tf_op | source)
XLA Modules:
  0.0 326.7 jit_solution(8188873899598888332)
XLA Ops:
  3.1 16.0 %all_gather.3 = f32[16,16,16]{2,1,0:T(8,128)S(1)} all-gather(f32[1,16,16]{2,1,0:T(8,128)S(1)} %all_gather_reshape.3), channel_id=1, replica_groups=mesh['groups'=2,'ep'=8,'sub'=2] {'ep','sub'}, dimensions={0}, use_global_device_ids=true | all-gather | bytes 17408 | tf_op jit(solution)/shard_map/all_gather | solution.py:14
  19.6 23.4 %psum.7 = f32[16,16]{1,0:T(8,128)S(1)} all-reduce(f32[16,16]{1,0:T(8,128)S(1)} %reshape.168), channel_id=1, replica_groups=mesh['groups'=2,'ep'=8,'sub'=2] {'ep','sub'}, use_global_device_ids=true, to_apply=%region_1.2 | all-reduce | flops 256 | bytes 2048 | tf_op jit(solution)/shard_map/psum | solution.py:67
  44.1 1.0 fusion.24
  46.1 2.4 scatter_custom_fusion
  48.6 6.8 %gather_fusion = pred[1024]{0:T(1024)(128)(4,1)S(1)} fusion(pred[513]{0:T(1024)(128)(4,1)S(1)} %pad_add_fusion, s32[1024]{0:T(1024)S(1)} %get-tuple-element.110), kind=kCustom, calls=%fused_computation | custom fusion | bytes 6144 | tf_op jit(solution)/shard_map/gather | solution.py:86
  55.5 1.0 fusion.20
  57.4 1.2 reduce_max.9
  58.7 3.2 gather_fusion.2
  62.8 17.0 %all-to-all-start.1 = ((bf16[16,2,512]{2,1,0:T(2,128)(2,1)}), bf16[16,2,512]{2,1,0:T(2,128)(2,1)S(1)}, u32[]{:S(2)}, u32[]{:S(2)}) async-start(bf16[16,2,512]{2,1,0:T(2,128)(2,1)} %reshape.226), calls=%async_computation.1 | async-start | bytes 65536 | tf_op jit(solution)/shard_map/all_to_all | solution.py:94
  79.9 1.2 fusion.21
  81.1 6.0 %gather_fusion.1 = bf16[1024,2048]{1,0:T(8,128)(2,1)} fusion(bf16[64,2048]{1,0:T(8,128)(2,1)S(1)} %fusion.21, s32[1024]{0:T(1024)S(1)} %get-tuple-element.111), kind=kCustom, calls=%fused_computation.1 | custom fusion | bytes 8392704 | tf_op jit(solution)/shard_map/gather | solution.py:88
  87.1 4.5 %broadcast_select_fusion = bf16[16,64,2048]{2,1,0:T(8,128)(2,1)} fusion(bf16[16,64,2048]{2,1,0:T(8,128)(2,1)} %bitcast.59, pred[16,64]{1,0:T(8,128)(4,1)S(1)} %broadcast_in_dim.66), kind=kLoop, calls=%fused_computation.14 | loop fusion | flops 2097152 | bytes 8389632 | tf_op jit(solution)/shard_map/jit(_where)/select_n | solution.py:88
  91.6 6.1 %all-to-all-start = ((bf16[16,64,2048]{2,1,0:T(8,128)(2,1)}), bf16[16,64,2048]{2,1,0:T(8,128)(2,1)}, u32[]{:S(2)}, u32[]{:S(2)}) async-start(bf16[16,64,2048]{2,1,0:T(8,128)(2,1)} %broadcast_select_fusion), calls=%async_computation | async-start | bytes 8388608 | tf_op jit(solution)/shard_map/all_to_all | solution.py:93
  97.8 1.0 copy.28
  98.8 91.4 %all-to-all-done = bf16[16,64,2048]{2,1,0:T(8,128)(2,1)} async-done(((bf16[16,64,2048]{2,1,0:T(8,128)(2,1)}), bf16[16,64,2048]{2,1,0:T(8,128)(2,1)}, u32[]{:S(2)}, u32[]{:S(2)}) %all-to-all-start) | async-done | bytes 4194336 | tf_op jit(solution)/shard_map/all_to_all | solution.py:93
  190.1 3.6 %copy.32 = f32[128,8,16,128]{3,2,1,0:T(8,128)S(1)} copy(bf16[128,8,16,128]{3,1,2,0:T(8,128)(2,1)} %bitcast.52) | data formatting | bytes 12582912
  193.7 4.0 %fusion = bf16[1024,16,128]{2,1,0:T(8,128)(2,1)S(1)} fusion(f32[128,8,16,128]{3,2,1,0:T(8,128)S(1)} %copy.32, f32[1024,16]{1,0:T(8,128)S(1)} %bitcast.63), kind=kLoop, calls=%fused_computation.7 | loop fusion | flops 4194304 | bytes 12648448 | tf_op jit(solution)/shard_map/convert_element_type | solution.py:40
  197.7 2.0 copy-done.1
  199.7 5.2 %fusion.3 = f32[1024,768]{1,0:T(8,128)} fusion(bf16[128,8,16,128]{3,2,1,0:T(8,128)(2,1)S(1)} %bitcast.60, bf16[1,2048,768]{2,1,0:T(8,128)(2,1)S(1)} %copy-done.3), kind=kOutput, calls=%fused_computation.10 | convolution fusion | flops 3221225472 | bytes 10485760 | tf_op jit(solution)/shard_map/dot_general | solution.py:41
  204.8 12.3 %convolution_convert_fusion = bf16[1024,2048]{1,0:T(8,128)(2,1)} fusion(bf16[1,768,2048]{2,1,0:T(8,128)(2,1)S(1)} %copy-done, f32[1024,768]{1,0:T(8,128)} %fusion.3, bf16[1,2048,768]{2,1,0:T(8,128)(2,1)} %param.16, bf16[128,8,16,128]{3,2,1,0:T(8,128)(2,1)} %bitcast.61), kind=kOutput, calls=%fused_computation.15 | convolution fusion | flops 6449266688 | bytes 17825792 | tf_op jit(solution)/shard_map/dot_general | solution.py:44
  217.2 4.9 %all-to-all-start.2 = ((bf16[16,64,2048]{2,1,0:T(8,128)(2,1)}), bf16[16,64,2048]{2,1,0:T(8,128)(2,1)}, u32[]{:S(2)}, u32[]{:S(2)}) async-start(bf16[16,64,2048]{2,1,0:T(8,128)(2,1)} %bitcast.62), calls=%async_computation.2 | async-start | bytes 8388608 | tf_op jit(solution)/shard_map/all_to_all | solution.py:100
  222.2 92.4 %all-to-all-done.2 = bf16[16,64,2048]{2,1,0:T(8,128)(2,1)} async-done(((bf16[16,64,2048]{2,1,0:T(8,128)(2,1)}), bf16[16,64,2048]{2,1,0:T(8,128)(2,1)}, u32[]{:S(2)}, u32[]{:S(2)}) %all-to-all-start.2) | async-done | bytes 4194336 | tf_op jit(solution)/shard_map/all_to_all | solution.py:100
  314.5 8.0 %gather_fusion.3 = bf16[512,2048]{1,0:T(8,128)(2,1)} fusion(bf16[1024,2048]{1,0:T(8,128)(2,1)} %bitcast.12, s32[1024]{0:T(1024)S(1)} %pad_clamp_fusion), kind=kCustom, calls=%fused_computation.3 | custom fusion | bytes 4196352 | tf_op jit(solution)/shard_map/gather | solution.py:108
  322.6 4.1 %fusion.5 = bf16[64,2048]{1,0:T(8,128)(2,1)} fusion(bf16[512,2048]{1,0:T(8,128)(2,1)} %gather_fusion.3, f32[64,8]{1,0:T(8,128)S(1)} %mul.81), kind=kLoop, calls=%fused_computation.13 | loop fusion | flops 3014656 | bytes 2361344 | tf_op jit(solution)/shard_map/reduce_sum | solution.py:110
  (60 shorter events, 8.2 us)
Async XLA Ops:
  0.0 204.8 %copy-start = (bf16[1,768,2048]{2,1,0:T(8,128)(2,1)S(1)}, bf16[1,768,2048]{2,1,0:T(8,128)(2,1)}, u32[]{:S(2)}) copy-start(bf16[1,768,2048]{2,1,0:T(8,128)(2,1)} %param.17) | copy-start | bytes 9437188
  62.8 28.8 %all-to-all-start.1 = ((bf16[16,2,512]{2,1,0:T(2,128)(2,1)}), bf16[16,2,512]{2,1,0:T(2,128)(2,1)S(1)}, u32[]{:S(2)}, u32[]{:S(2)}) async-start(bf16[16,2,512]{2,1,0:T(2,128)(2,1)} %reshape.226), calls=%async_computation.1 | async-start | bytes 65536 | tf_op jit(solution)/shard_map/all_to_all | solution.py:94
  91.6 98.5 %all-to-all-start = ((bf16[16,64,2048]{2,1,0:T(8,128)(2,1)}), bf16[16,64,2048]{2,1,0:T(8,128)(2,1)}, u32[]{:S(2)}, u32[]{:S(2)}) async-start(bf16[16,64,2048]{2,1,0:T(8,128)(2,1)} %broadcast_select_fusion), calls=%async_computation | async-start | bytes 8388608 | tf_op jit(solution)/shard_map/all_to_all | solution.py:93
  190.1 3.6 %copy-start.2 = (f32[16,64,16]{2,1,0:T(8,128)S(1)}, f32[16,64,16]{2,1,0:T(8,128)}, u32[]{:S(2)}) copy-start(f32[16,64,16]{2,1,0:T(8,128)} %copy.28) | copy-start | bytes 196612
  193.7 6.0 %copy-start.3 = (bf16[1,2048,768]{2,1,0:T(8,128)(2,1)S(1)}, bf16[1,2048,768]{2,1,0:T(8,128)(2,1)}, u32[]{:S(2)}) copy-start(bf16[1,2048,768]{2,1,0:T(8,128)(2,1)} %param.15) | copy-start | bytes 9437188
  197.7 2.0 copy-start.1
  217.2 97.4 %all-to-all-start.2 = ((bf16[16,64,2048]{2,1,0:T(8,128)(2,1)}), bf16[16,64,2048]{2,1,0:T(8,128)(2,1)}, u32[]{:S(2)}, u32[]{:S(2)}) async-start(bf16[16,64,2048]{2,1,0:T(8,128)(2,1)} %bitcast.62), calls=%async_computation.2 | async-start | bytes 8388608 | tf_op jit(solution)/shard_map/all_to_all | solution.py:100
where the time goes:
time: 327 us
  waiting for transfers between devices  184 us (56%)
  blocking collectives  39.4 us (12%)
  local copies, waits for them, and re-layouts  38.3 us (12%)
  starting transfers between devices  27.9 us (9%)
  matrix products  18.8 us (6%)
  other arithmetic  17.9 us (5%)
    all_to_all x1, waiting for transfers between devices, on_device(): lax.all_to_all(outputs.reshape(devices, slot_count, width), ('ep', 'sub')...  92.4 us
    all_to_all x1, waiting for transfers between devices, on_device(): lax.all_to_all(send_rows, ('ep', 'sub'), split_axis=0, concat_axis=0, til...  91.4 us
    psum x1, blocking collectives, on_device(): totals = lax.psum(counts, ('ep', 'sub'))  23.4 us
    all_to_all x1, starting transfers between devices, on_device(): lax.all_to_all(send_scales, ('ep', 'sub'), split_axis=0, concat_axis=0, t...  17 us
    all_gather x1, blocking collectives, prefix(): everything = lax.all_gather(array, axis)  16 us
    dot_general x1, matrix products, expert_apply(): jnp.dot(hidden, down_matrix, preferred_element_type=jnp.float32)  12.3 us
    unnamed x14, local copies, waits for them, and re-layouts  8.95 us
    gather x1, local copies, waits for them, and re-layouts, on_device(): entry_rows = returned[position]  8.02 us
  transfers between devices with their start and end apart: 3, of which 2 were waited for; matrix products, arithmetic and copies ran while one was open for 4% of the time, Pallas kernels for 0%

commit v1 on v0

v1 whole, which is shorter than its diff:
```python
import functools

import jax
import jax.numpy as jnp
from jax import lax
from jax.experimental import pallas as pl
from jax.experimental.pallas import tpu as pltpu
from jax.sharding import PartitionSpec as P

F32 = jnp.float32
BF16 = jnp.bfloat16
LANES = 128
CHUNKS = 2
BIG = 1e9


def iota(shape, dim):
    return lax.broadcasted_iota(jnp.int32, shape, dim)


def prepare_kernel(me_ref, tokens_ref, routes_ref, gates_ref, prio_ref, *out_refs):
    rows, width = tokens_ref.shape
    part = rows // CHUNKS
    for block in range(width // LANES):
        lanes = slice(block * LANES, (block + 1) * LANES)
        x = tokens_ref[:, lanes].astype(F32)
        largest = jnp.max(jnp.abs(x), axis=1, keepdims=True)
        scale = ((largest + 1e-06) / 448.0).astype(BF16).astype(F32)
        quantized = (x / scale).astype(BF16)
        restored = (quantized.astype(F32) * scale).astype(BF16)
        for c in range(CHUNKS):
            out_refs[c][:, lanes] = restored[c * part : (c + 1) * part]
    top = routes_ref.shape[1]
    gates = gates_ref[...]
    high = gates.astype(BF16)
    middle = (gates - high.astype(F32)).astype(BF16)
    low = (gates - high.astype(F32) - middle.astype(F32)).astype(BF16)
    eye = iota((rows, rows), 0) == iota((rows, rows), 1)
    prio = jnp.sum(jnp.where(eye, prio_ref[...].astype(F32), 0.0), axis=1, keepdims=True)
    fields = [routes_ref[...].astype(F32).astype(BF16), high, middle, low]
    facts = jnp.zeros((part, LANES), F32)
    lane = iota((part, LANES), 1)
    for c in range(CHUNKS):
        first = c * (LANES // CHUNKS)
        held = slice(c * part, (c + 1) * part)
        for k, field in enumerate(fields):
            place = iota((top, LANES), 1) == iota((top, LANES), 0) + (first + k * top)
            facts += jnp.dot(field[held], place.astype(F32).astype(BF16), preferred_element_type=F32)
        facts = jnp.where(lane == first + 4 * top, prio[held], facts)
        facts = jnp.where(lane == first + 4 * top + 1, me_ref[0].astype(F32), facts)
    out_refs[0][:, width:] = facts.astype(BF16)


def prepare(me, tokens, routes, gates, priority):
    rows, width = tokens.shape
    part = rows // CHUNKS
    return pl.pallas_call(
        prepare_kernel,
        in_specs=[pl.BlockSpec(memory_space=pltpu.SMEM)] + [pl.BlockSpec(memory_space=pltpu.VMEM)] * 4,
        out_specs=[pl.BlockSpec(memory_space=pltpu.VMEM)] * CHUNKS,
        out_shape=[
            jax.ShapeDtypeStruct((part, width + (LANES if c == 0 else 0)), BF16) for c in range(CHUNKS)
        ],
    )(me, tokens, routes, gates, priority.reshape(1, rows))


def weigh_kernel(top, tok_rows, me_ref, capacity_ref, *refs):
    fact_refs, out_refs, key_ref, row_ref = refs[:4], refs[4 : 4 + CHUNKS], refs[-2], refs[-1]
    part = tok_rows // CHUNKS
    each = fact_refs[0].shape[0]
    total = 4 * each * CHUNKS
    me = me_ref[0]
    eye = iota((LANES, LANES), 0) == iota((LANES, LANES), 1)
    lane = iota((LANES, LANES), 1)
    row = lax.rem(iota((LANES, LANES), 0), part)[:, :1]
    tiles = each // LANES
    for a in range(4):
        def tile_step(i, _, a=a):
            facts = fact_refs[a][pl.ds(pl.multiple_of(i * LANES, LANES), LANES), :].astype(F32)
            values = (
                pltpu.roll(facts, LANES - top, 1)
                + pltpu.roll(facts, LANES - 2 * top, 1)
                + pltpu.roll(facts, LANES - 3 * top, 1)
            )
            for c in range(CHUNKS):
                first = c * (LANES // CHUNKS)
                named = (lane >= first) & (lane < first + top) & (facts == me.astype(F32))
                has = jnp.sum(named.astype(F32), axis=1, keepdims=True)
                gate = jnp.sum(jnp.where(named, values, 0.0), axis=1, keepdims=True)
                prio = jnp.sum(jnp.where(lane == first + 4 * top, facts, 0.0), axis=1, keepdims=True)
                source = jnp.sum(jnp.where(lane == first + 4 * top + 1, facts, 0.0), axis=1, keepdims=True)
                key = prio * float(total) + source * float(tok_rows) + (row + c * part).astype(F32)
                key = jnp.where(has > 0.0, key, BIG)
                at = (c * 4 + a) * tiles + i
                key_ref[at] = jnp.broadcast_to(key, (LANES, LANES))
                row_ref[pl.ds(at, 1), :] = jnp.sum(jnp.where(eye, key, 0.0), axis=0, keepdims=True)
                out_refs[c][pl.ds(pl.multiple_of((a * tiles + i) * LANES, LANES), LANES), :] = (
                    jnp.broadcast_to(gate, (LANES, LANES))
                )
            return 0

        lax.fori_loop(0, tiles, tile_step, 0, unroll=tiles == 1)
    limit = capacity_ref[me].astype(F32)
    count = 4 * tiles * CHUNKS
    per = 4 * tiles

    for c in range(CHUNKS):
        def rank_step(i, _, c=c):
            key = key_ref[c * per + i]

            def add(j, smaller):
                return smaller + (row_ref[pl.ds(j, 1), :] < key).astype(F32)

            smaller = lax.fori_loop(0, count, add, jnp.zeros((LANES, LANES), F32), unroll=min(count, 8))
            rank = jnp.sum(smaller, axis=1, keepdims=True)
            keep = (rank < limit) & (key < BIG)
            at = pl.ds(pl.multiple_of(i * LANES, LANES), LANES)
            out_refs[c][at, :] = jnp.where(keep, out_refs[c][at, :], 0.0)
            return 0

        lax.fori_loop(0, per, rank_step, 0)


def weigh(me, capacity, rows, top, tok_rows):
    each, wide = rows[0].shape
    last = wide // LANES - 1
    count = 4 * each * CHUNKS // LANES
    return pl.pallas_call(
        functools.partial(weigh_kernel, top, tok_rows),
        grid=(1,),
        in_specs=[pl.BlockSpec(memory_space=pltpu.SMEM)] * 2
        + [pl.BlockSpec((each, LANES), lambda i: (0, last))] * 4,
        out_specs=[pl.BlockSpec((4 * each, LANES), lambda i: (0, 0))] * CHUNKS,
        out_shape=[jax.ShapeDtypeStruct((4 * each, LANES), F32)] * CHUNKS,
        scratch_shapes=[pltpu.VMEM((count, LANES, LANES), F32), pltpu.VMEM((count, LANES), F32)],
        compiler_params=pltpu.CompilerParams(vmem_limit_bytes=32 * 1024 * 1024),
    )(me, capacity, *rows)


def expert_kernel(steps, *refs):
    x_refs, weight_ref, gate_ref, up_ref, down_ref = refs[:4], refs[4], refs[5], refs[6], refs[7]
    own_ref, other_ref, x, hidden, sems = refs[8:]
    each, width = x_refs[0].shape[0], x.shape[1]
    tile = gate_ref.shape[1]
    step = pl.program_id(0)

    @pl.when(step == 0)
    def _():
        copies = [
            pltpu.make_async_copy(
                x_refs[a].at[:, pl.ds(0, width)], x.at[pl.ds(a * each, each), :], sems.at[a]
            )
            for a in range(4)
        ]
        for copy in copies:
            copy.start()
        for copy in copies:
            copy.wait()

    @pl.when(step < steps)
    def _():
        gated = jnp.dot(x[...], gate_ref[...], preferred_element_type=F32)
        upward = jnp.dot(x[...], up_ref[...], preferred_element_type=F32)
        result = (gated / (1.0 + jnp.exp(-gated)) * upward).astype(BF16)
        hidden[:, pl.ds(pl.multiple_of(step * tile, tile), tile)] = result

    @pl.when(step >= steps)
    def _():
        for half, ref in enumerate((own_ref, other_ref)):
            rows = slice(half * 2 * each, (half + 1) * 2 * each)
            out = jnp.dot(hidden[rows, :], down_ref[...], preferred_element_type=F32).astype(BF16)
            ref[...] = (out.astype(F32) * weight_ref[rows, :1]).astype(BF16)


def expert(rows, weight, w_gate, w_up, w_down):
    each = rows[0].shape[0]
    unused, width, ff = w_gate.shape
    tile, out_tile = 256, 512
    steps = ff // tile
    grid = steps + width // out_tile

    def out_at(i):
        return (0, jnp.maximum(i - steps, 0))

    return pl.pallas_call(
        functools.partial(expert_kernel, steps),
        grid=(grid,),
        in_specs=[pl.BlockSpec(memory_space=pl.ANY)] * 4
        + [
            pl.BlockSpec((4 * each, LANES), lambda i: (0, 0)),
            pl.BlockSpec((None, width, tile), lambda i: (0, 0, jnp.minimum(i, steps - 1))),
            pl.BlockSpec((None, width, tile), lambda i: (0, 0, jnp.minimum(i, steps - 1))),
            pl.BlockSpec((None, ff, out_tile), lambda i: (0, 0, jnp.maximum(i - steps, 0))),
        ],
        out_specs=[pl.BlockSpec((2 * each, out_tile), out_at)] * 2,
        out_shape=[jax.ShapeDtypeStruct((2 * each, width), BF16)] * 2,
        scratch_shapes=[
            pltpu.VMEM((4 * each, width), BF16),
            pltpu.VMEM((4 * each, ff), BF16),
            pltpu.SemaphoreType.DMA((4,)),
        ],
        compiler_params=pltpu.CompilerParams(vmem_limit_bytes=40 * 1024 * 1024),
        cost_estimate=pl.CostEstimate(
            flops=24 * each * width * ff, bytes_accessed=6 * width * ff, transcendentals=4 * each * ff
        ),
    )(*rows, weight, w_gate, w_up, w_down)


def orders(ep):
    bits = list(range(ep.bit_length() - 1))[::-1]
    return (bits, bits[:-2] + bits[:-3:-1])


def swap(array, ep, step):
    pairs = [
        (2 * place + core, 2 * (place ^ (1 << order[step])) + core)
        for place in range(ep)
        for core, order in enumerate(orders(ep))
    ]
    return lax.ppermute(array, ("ep", "sub"), pairs)


def cross(array):
    return lax.ppermute(array, "sub", [(0, 1), (1, 0)])


def on_device(ep, tokens, routes, gates, priority, capacity, w_gate, w_up, w_down):
    tok_rows, width = tokens.shape
    top = routes.shape[1]
    part = tok_rows // CHUNKS
    steps = ep.bit_length() - 1
    me = (lax.axis_index("ep") * 2 + lax.axis_index("sub")).astype(jnp.int32).reshape(1)
    chunks = prepare(me, tokens, routes, gates, priority)
    gathered = []
    for chunk in chunks:
        held = chunk
        for step in range(steps - 1):
            held = jnp.concatenate([held, swap(held, ep, step)])
        came = swap(held, ep, steps - 1)
        gathered.append([held, came, cross(held), cross(came)])
    weights = weigh(me, capacity, gathered[0], top, tok_rows)
    results = []
    for c in range(CHUNKS):
        own, other = expert(gathered[c], weights[c], w_gate, w_up, w_down)
        terms = [own, cross(other)]
        count = ep * part
        for step in range(steps)[::-1]:
            count //= 2
            send = sum([t[count : 2 * count].astype(F32) for t in terms]).astype(BF16)
            terms.append(swap(send, ep, step))
        results.append(sum([t[:part].astype(F32) for t in terms]).astype(BF16))
    return jnp.concatenate(results)


def solution(mesh):
    in_specs = (
        P(("groups", "ep", "sub"), None),
        P(("groups", "ep", "sub"), None),
        P(("groups", "ep", "sub"), None),
        P(("groups", "ep", "sub")),
        P(),
        P(("ep", "sub"), None, None),
        P(("ep", "sub"), None, None),
        P(("ep", "sub"), None, None),
    )
    out_specs = P(("groups", "ep", "sub"), None)
    return jax.shard_map(
        functools.partial(on_device, mesh.shape["ep"]),
        mesh=mesh,
        in_specs=in_specs,
        out_specs=out_specs,
        check_vma=False,
    )
```

time: 327 us -> 105 us (0.32)
  the two profiles are of different devices: /device:TPU:13 before, /device:TPU:0 now
where the time goes in v1:
time: 105 us; the launch traced here: 104 us
  waiting for transfers between devices  54.5 us (52%)
  Pallas kernels  19.3 us (18%)
  starting transfers between devices  18.5 us (18%)
  local copies, waits for them, and re-layouts  8.58 us (8%)
  other arithmetic  3.33 us (3%)
    ppermute x12, waiting for transfers between devices, swap(): return lax.ppermute(array, ('ep', 'sub'), pairs)  53.6 us
    ppermute x12, starting transfers between devices, swap(): return lax.ppermute(array, ('ep', 'sub'), pairs)  17.3 us
    pallas_call x2, Pallas kernels, expert(): pl.pallas_call(functools.partial(expert_kernel, steps), grid=(grid,), in_...  14.8 us
    unnamed x14, local copies, waits for them, and re-layouts  8.53 us
    pallas_call x1, Pallas kernels, weigh(): pl.pallas_call(functools.partial(weigh_kernel, top, tok_rows), grid=(1,),...  2.51 us
  transfers between devices with their start and end apart: 18, of which 9 were waited for; matrix products, arithmetic and copies ran while one was open for 4% of the time, Pallas kernels for 17%

profile of v1, /device:TPU:0, one launch (start us, length us, event | category | flops | bytes accessed | tf_op | source)
XLA Modules:
  0.0 104.3 jit_solution(11298136184591652980)
XLA Ops:
  0.0 1.5 %copy.10.gates_ref = f32[64,8]{1,0:T(8,128)} copy(f32[64,8]{0,1:T(8,128)} %param.10) | data formatting | bytes 4096 | tf_op args[2]
  1.5 1.4 %copy.9.routes_ref = s32[64,8]{1,0:T(8,128)} copy(s32[64,8]{0,1:T(8,128)} %param.9) | data formatting | bytes 4096 | tf_op args[1]
  2.9 1.9 %shard_map.82 = (bf16[32,2176]{1,0:T(8,128)(2,1)}, bf16[32,2048]{1,0:T(8,128)(2,1)}) custom-call(s32[1]{0:T(128)} %bitcast.me_ref, bf16[64,2048]{1,0:T(8,128)(2,1)} %tokens_ref.1, s32[64,8]{1,0:T(8,128)} %copy.9.routes_ref, f32[64,8]{1,0:T(8,128)} %copy.10.gates_ref, s32[1,64]{1,0:T(1,128)} %bitcast.2), custom_call_target="tpu_custom_call" | custom-call | tf_op jit(solution)/shard_map/pallas_call | solution.py:57
  4.8 4.0 %collective-permute-start = (bf16[32,2176]{1,0:T(8,128)(2,1)}, bf16[32,2176]{1,0:T(8,128)(2,1)S(1)}, u32[]{:S(2)}, u32[]{:S(2)}) collective-permute-start(bf16[32,2176]{1,0:T(8,128)(2,1)} %get-tuple-element.13), channel_id=1, source_target_pairs={{0,8},{1,9},{2,10},{3,11},{4,12},{5,13},{6,14},{7,15},{8,0},{9,1},... | collective-permute-start | bytes 417800 | tf_op jit(solution)/shard_map/ppermute | solution.py:220
  9.8 11.5 %collective-permute-done.9 = bf16[32,2048]{1,0:T(8,128)(2,1)S(1)} collective-permute-done((bf16[32,2048]{1,0:T(8,128)(2,1)}, bf16[32,2048]{1,0:T(8,128)(2,1)S(1)}, u32[]{:S(2)}, u32[]{:S(2)}) %collective-permute-start.9) | collective-permute-done | bytes 131104 | tf_op jit(solution)/shard_map/ppermute | solution.py:220
  21.3 0.9 pad_maximum_fusion.1
  23.2 0.9 pad_maximum_fusion
  24.1 1.3 %collective-permute-start.1 = (bf16[64,2176]{1,0:T(8,128)(2,1)S(1)}, bf16[64,2176]{1,0:T(8,128)(2,1)S(1)}, u32[]{:S(2)}, u32[]{:S(2)}) collective-permute-start(bf16[64,2176]{1,0:T(8,128)(2,1)S(1)} %pad_maximum_fusion), channel_id=1, source_target_pairs={{0,4},{1,3},{2,6},{3,1},{4,0},{5,7},{6,2},{7,5},{8,12},{9,11},{10,... | collective-permute-start | bytes 835592 | tf_op jit(solution)/shard_map/ppermute | solution.py:220
  25.4 6.3 %collective-permute-done.1 = bf16[64,2176]{1,0:T(8,128)(2,1)S(1)} collective-permute-done((bf16[64,2176]{1,0:T(8,128)(2,1)S(1)}, bf16[64,2176]{1,0:T(8,128)(2,1)S(1)}, u32[]{:S(2)}, u32[]{:S(2)}) %collective-permute-start.1) | collective-permute-done | bytes 278560 | tf_op jit(solution)/shard_map/ppermute | solution.py:220
  31.7 1.6 %collective-permute-start.2 = (bf16[128,2176]{1,0:T(8,128)(2,1)S(1)}, bf16[128,2176]{1,0:T(8,128)(2,1)S(1)}, u32[]{:S(2)}, u32[]{:S(2)}) collective-permute-start(bf16[128,2176]{1,0:T(8,128)(2,1)S(1)} %constant_dynamic-update-slice_fusion.refs_0_), channel_id=1, source_target_pairs={{0,2},{1,5},{2,0},{3,7},{4,6},{5,1},{6,4},{7,3},{8,10},{9,13},{10,... | collective-permute-start | bytes 1671176 | tf_op jit(solution)/shard_map/ppermute | solution.py:220
  34.8 6.5 %collective-permute-done.2.refs_1_ = bf16[128,2176]{1,0:T(8,128)(2,1)S(1)} collective-permute-done((bf16[128,2176]{1,0:T(8,128)(2,1)S(1)}, bf16[128,2176]{1,0:T(8,128)(2,1)S(1)}, u32[]{:S(2)}, u32[]{:S(2)}) %collective-permute-start.2) | collective-permute-done | bytes 557088 | tf_op jit(solution)/shard_map/ppermute | solution.py:220
  41.8 5.1 %collective-permute-done.11.refs_1_ = bf16[128,2048]{1,0:T(8,128)(2,1)S(1)} collective-permute-done((bf16[128,2048]{1,0:T(8,128)(2,1)S(1)}, bf16[128,2048]{1,0:T(8,128)(2,1)S(1)}, u32[]{:S(2)}, u32[]{:S(2)}) %collective-permute-start.11) | collective-permute-done | bytes 524320 | tf_op jit(solution)/shard_map/ppermute | solution.py:220
  47.0 2.5 %shard_map.83 = (f32[512,128]{1,0:T(8,128)S(1)}, f32[512,128]{1,0:T(8,128)S(1)}) custom-call(s32[1]{0:T(128)} %bitcast.me_ref, s32[16]{0:T(128)S(1)} %copy-done, bf16[128,2176]{1,0:T(8,128)(2,1)S(1)} %constant_dynamic-update-slice_fusion.refs_0_, bf16[128,2176]{1,0:T(8,128)(2,1)S(1)} %collective-permute-done.2.refs_1_, ...), custom_call_target="tpu_custom_call" | custom-call | tf_op jit(solution)/shard_map/pallas_call | solution.py:128
  49.5 1.9 %copy-done.2 = bf16[1,2048,768]{2,1,0:T(8,128)(2,1)S(1)} copy-done((bf16[1,2048,768]{2,1,0:T(8,128)(2,1)S(1)}, bf16[1,2048,768]{2,1,0:T(8,128)(2,1)}, u32[]{:S(2)}) %copy-start.2) | copy-done | bytes 3145752
  51.4 1.9 %copy-done.3 = bf16[1,768,2048]{2,1,0:T(8,128)(2,1)S(1)} copy-done((bf16[1,768,2048]{2,1,0:T(8,128)(2,1)S(1)}, bf16[1,768,2048]{2,1,0:T(8,128)(2,1)}, u32[]{:S(2)}) %copy-start.3) | copy-done | bytes 3145752
  53.3 7.4 %shard_map.84 = (bf16[256,2048]{1,0:T(8,128)(2,1)S(1)}, bf16[256,2048]{1,0:T(8,128)(2,1)S(1)}) custom-call(bf16[128,2176]{1,0:T(8,128)(2,1)S(1)} %constant_dynamic-update-slice_fusion.refs_0_, bf16[128,2176]{1,0:T(8,128)(2,1)S(1)} %collective-permute-done.2.refs_1_, bf16[128,2176]{1,0:T(8,128)(2,1)S(1)} %collective-permute-done.3.refs_2_, ...), custom_call_target="tpu_custom_call" | custom-call | flops 4831838208 | bytes 9437184 | tf_op jit(solution)/shard_map/pallas_call | solution.py:185
  61.3 7.4 %shard_map.85 = (bf16[256,2048]{1,0:T(8,128)(2,1)S(1)}, bf16[256,2048]{1,0:T(8,128)(2,1)S(1)}) custom-call(bf16[128,2048]{1,0:T(8,128)(2,1)S(1)} %constant_dynamic-update-slice_fusion.3.refs_0_, bf16[128,2048]{1,0:T(8,128)(2,1)S(1)} %collective-permute-done.11.refs_1_, bf16[128,2048]{1,0:T(8,128)(2,1)S(1)} %collective-permute-done.12.refs_2_, ...), custom_call_target="tpu_custom_call" | custom-call | flops 4831838208 | bytes 9437184 | tf_op jit(solution)/shard_map/pallas_call | solution.py:185
  68.9 1.6 %collective-permute-start.6 = (bf16[128,2048]{1,0:T(8,128)(2,1)S(1)}, bf16[128,2048]{1,0:T(8,128)(2,1)S(1)}, u32[]{:S(2)}, u32[]{:S(2)}) collective-permute-start(bf16[128,2048]{1,0:T(8,128)(2,1)S(1)} %add_convert_fusion.1), channel_id=1, source_target_pairs={{0,2},{1,5},{2,0},{3,7},{4,6},{5,1},{6,4},{7,3},{8,10},{9,13},{10,... | collective-permute-start | bytes 1572872 | tf_op jit(solution)/shard_map/ppermute | solution.py:220
  71.5 1.6 %collective-permute-start.15 = (bf16[128,2048]{1,0:T(8,128)(2,1)S(1)}, bf16[128,2048]{1,0:T(8,128)(2,1)S(1)}, u32[]{:S(2)}, u32[]{:S(2)}) collective-permute-start(bf16[128,2048]{1,0:T(8,128)(2,1)S(1)} %add_convert_fusion), channel_id=1, source_target_pairs={{0,2},{1,5},{2,0},{3,7},{4,6},{5,1},{6,4},{7,3},{8,10},{9,13},{10,... | collective-permute-start | bytes 1572872 | tf_op jit(solution)/shard_map/ppermute | solution.py:220
  73.2 5.0 %collective-permute-done.6 = bf16[128,2048]{1,0:T(8,128)(2,1)S(1)} collective-permute-done((bf16[128,2048]{1,0:T(8,128)(2,1)S(1)}, bf16[128,2048]{1,0:T(8,128)(2,1)S(1)}, u32[]{:S(2)}, u32[]{:S(2)}) %collective-permute-start.6) | collective-permute-done | bytes 524320 | tf_op jit(solution)/shard_map/ppermute | solution.py:220
  79.2 7.4 %collective-permute-done.15 = bf16[128,2048]{1,0:T(8,128)(2,1)S(1)} collective-permute-done((bf16[128,2048]{1,0:T(8,128)(2,1)S(1)}, bf16[128,2048]{1,0:T(8,128)(2,1)S(1)}, u32[]{:S(2)}, u32[]{:S(2)}) %collective-permute-start.15) | collective-permute-done | bytes 524320 | tf_op jit(solution)/shard_map/ppermute | solution.py:220
  87.7 3.3 %collective-permute-start.8 = (bf16[32,2048]{1,0:T(8,128)(2,1)S(1)}, bf16[32,2048]{1,0:T(8,128)(2,1)S(1)}, u32[]{:S(2)}, u32[]{:S(2)}) collective-permute-start(bf16[32,2048]{1,0:T(8,128)(2,1)S(1)} %add_convert_fusion.7), channel_id=1, source_target_pairs={{0,8},{1,9},{2,10},{3,11},{4,12},{5,13},{6,14},{7,15},{8,0},{9,1},... | collective-permute-start | bytes 393224 | tf_op jit(solution)/shard_map/ppermute | solution.py:220
  91.0 5.6 %collective-permute-done.16 = bf16[64,2048]{1,0:T(8,128)(2,1)S(1)} collective-permute-done((bf16[64,2048]{1,0:T(8,128)(2,1)S(1)}, bf16[64,2048]{1,0:T(8,128)(2,1)S(1)}, u32[]{:S(2)}, u32[]{:S(2)}) %collective-permute-start.16) | collective-permute-done | bytes 262176 | tf_op jit(solution)/shard_map/ppermute | solution.py:220
  97.3 6.2 %collective-permute-done.17 = bf16[32,2048]{1,0:T(8,128)(2,1)S(1)} collective-permute-done((bf16[32,2048]{1,0:T(8,128)(2,1)S(1)}, bf16[32,2048]{1,0:T(8,128)(2,1)S(1)}, u32[]{:S(2)}, u32[]{:S(2)}) %collective-permute-start.17) | collective-permute-done | bytes 131104 | tf_op jit(solution)/shard_map/ppermute | solution.py:220
  (43 shorter events, 9.2 us)
Async XLA Ops:
  0.0 46.9 %copy-start = (s32[16]{0:T(128)S(1)}, s32[16]{0:T(128)}, u32[]{:S(2)}) copy-start(s32[16]{0:T(128)} %capacity_ref.1) | copy-start | bytes 196
  0.0 49.5 %copy-start.1 = (bf16[1,2048,768]{2,1,0:T(8,128)(2,1)S(1)}, bf16[1,2048,768]{2,1,0:T(8,128)(2,1)}, u32[]{:S(2)}) copy-start(bf16[1,2048,768]{2,1,0:T(8,128)(2,1)} %refs_5_.3) | copy-start | bytes 9437188
  4.8 18.3 %collective-permute-start = (bf16[32,2176]{1,0:T(8,128)(2,1)}, bf16[32,2176]{1,0:T(8,128)(2,1)S(1)}, u32[]{:S(2)}, u32[]{:S(2)}) collective-permute-start(bf16[32,2176]{1,0:T(8,128)(2,1)} %get-tuple-element.13), channel_id=1, source_target_pairs={{0,8},{1,9},{2,10},{3,11},{4,12},{5,13},{6,14},{7,15},{8,0},{9,1},... | collective-permute-start | bytes 417800 | tf_op jit(solution)/shard_map/ppermute | solution.py:220
  8.9 12.5 %collective-permute-start.9 = (bf16[32,2048]{1,0:T(8,128)(2,1)}, bf16[32,2048]{1,0:T(8,128)(2,1)S(1)}, u32[]{:S(2)}, u32[]{:S(2)}) collective-permute-start(bf16[32,2048]{1,0:T(8,128)(2,1)} %get-tuple-element.17), channel_id=1, source_target_pairs={{0,8},{1,9},{2,10},{3,11},{4,12},{5,13},{6,14},{7,15},{8,0},{9,1},... | collective-permute-start | bytes 393224 | tf_op jit(solution)/shard_map/ppermute | solution.py:220
  22.3 12.0 %collective-permute-start.10 = (bf16[64,2048]{1,0:T(8,128)(2,1)S(1)}, bf16[64,2048]{1,0:T(8,128)(2,1)S(1)}, u32[]{:S(2)}, u32[]{:S(2)}) collective-permute-start(bf16[64,2048]{1,0:T(8,128)(2,1)S(1)} %pad_maximum_fusion.1), channel_id=1, source_target_pairs={{0,4},{1,3},{2,6},{3,1},{4,0},{5,7},{6,2},{7,5},{8,12},{9,11},{10,... | collective-permute-start | bytes 786440 | tf_op jit(solution)/shard_map/ppermute | solution.py:220
  24.1 7.6 %collective-permute-start.1 = (bf16[64,2176]{1,0:T(8,128)(2,1)S(1)}, bf16[64,2176]{1,0:T(8,128)(2,1)S(1)}, u32[]{:S(2)}, u32[]{:S(2)}) collective-permute-start(bf16[64,2176]{1,0:T(8,128)(2,1)S(1)} %pad_maximum_fusion), channel_id=1, source_target_pairs={{0,4},{1,3},{2,6},{3,1},{4,0},{5,7},{6,2},{7,5},{8,12},{9,11},{10,... | collective-permute-start | bytes 835592 | tf_op jit(solution)/shard_map/ppermute | solution.py:220
  31.7 9.6 %collective-permute-start.2 = (bf16[128,2176]{1,0:T(8,128)(2,1)S(1)}, bf16[128,2176]{1,0:T(8,128)(2,1)S(1)}, u32[]{:S(2)}, u32[]{:S(2)}) collective-permute-start(bf16[128,2176]{1,0:T(8,128)(2,1)S(1)} %constant_dynamic-update-slice_fusion.refs_0_), channel_id=1, source_target_pairs={{0,2},{1,5},{2,0},{3,7},{4,6},{5,1},{6,4},{7,3},{8,10},{9,13},{10,... | collective-permute-start | bytes 1671176 | tf_op jit(solution)/shard_map/ppermute | solution.py:220
  34.3 12.6 %collective-permute-start.11 = (bf16[128,2048]{1,0:T(8,128)(2,1)S(1)}, bf16[128,2048]{1,0:T(8,128)(2,1)S(1)}, u32[]{:S(2)}, u32[]{:S(2)}) collective-permute-start(bf16[128,2048]{1,0:T(8,128)(2,1)S(1)} %constant_dynamic-update-slice_fusion.3.refs_0_), channel_id=1, source_target_pairs={{0,2},{1,5},{2,0},{3,7},{4,6},{5,1},{6,4},{7,3},{8,10},{9,13},{10,... | collective-permute-start | bytes 1572872 | tf_op jit(solution)/shard_map/ppermute | solution.py:220
  34.8 12.1 %collective-permute-start.3 = (bf16[128,2176]{1,0:T(8,128)(2,1)S(1)}, bf16[128,2176]{1,0:T(8,128)(2,1)S(1)}, u32[]{:S(2)}, u32[]{:S(2)}) collective-permute-start(bf16[128,2176]{1,0:T(8,128)(2,1)S(1)} %constant_dynamic-update-slice_fusion.refs_0_), channel_id=1, source_target_pairs={{0,1},{1,0},{2,3},{3,2},{4,5},{5,4},{6,7},{7,6},{8,9},{9,8},{10,11... | collective-permute-start | bytes 1671176 | tf_op jit(solution)/shard_map/ppermute | solution.py:224
  41.3 5.6 %collective-permute-start.4 = (bf16[128,2176]{1,0:T(8,128)(2,1)S(1)}, bf16[128,2176]{1,0:T(8,128)(2,1)S(1)}, u32[]{:S(2)}, u32[]{:S(2)}) collective-permute-start(bf16[128,2176]{1,0:T(8,128)(2,1)S(1)} %collective-permute-done.2.refs_1_), channel_id=1, source_target_pairs={{0,1},{1,0},{2,3},{3,2},{4,5},{5,4},{6,7},{7,6},{8,9},{9,8},{10,11... | collective-permute-start | bytes 1671176 | tf_op jit(solution)/shard_map/ppermute | solution.py:224
  41.3 19.9 %collective-permute-start.12 = (bf16[128,2048]{1,0:T(8,128)(2,1)S(1)}, bf16[128,2048]{1,0:T(8,128)(2,1)S(1)}, u32[]{:S(2)}, u32[]{:S(2)}) collective-permute-start(bf16[128,2048]{1,0:T(8,128)(2,1)S(1)} %constant_dynamic-update-slice_fusion.3.refs_0_), channel_id=1, source_target_pairs={{0,1},{1,0},{2,3},{3,2},{4,5},{5,4},{6,7},{7,6},{8,9},{9,8},{10,11... | collective-permute-start | bytes 1572872 | tf_op jit(solution)/shard_map/ppermute | solution.py:224
  46.9 14.3 %collective-permute-start.13 = (bf16[128,2048]{1,0:T(8,128)(2,1)S(1)}, bf16[128,2048]{1,0:T(8,128)(2,1)S(1)}, u32[]{:S(2)}, u32[]{:S(2)}) collective-permute-start(bf16[128,2048]{1,0:T(8,128)(2,1)S(1)} %collective-permute-done.11.refs_1_), channel_id=1, source_target_pairs={{0,1},{1,0},{2,3},{3,2},{4,5},{5,4},{6,7},{7,6},{8,9},{9,8},{10,11... | collective-permute-start | bytes 1572872 | tf_op jit(solution)/shard_map/ppermute | solution.py:224
  49.5 1.9 %copy-start.2 = (bf16[1,2048,768]{2,1,0:T(8,128)(2,1)S(1)}, bf16[1,2048,768]{2,1,0:T(8,128)(2,1)}, u32[]{:S(2)}) copy-start(bf16[1,2048,768]{2,1,0:T(8,128)(2,1)} %refs_6_.3) | copy-start | bytes 9437188
  51.4 1.9 %copy-start.3 = (bf16[1,768,2048]{2,1,0:T(8,128)(2,1)S(1)}, bf16[1,768,2048]{2,1,0:T(8,128)(2,1)}, u32[]{:S(2)}) copy-start(bf16[1,768,2048]{2,1,0:T(8,128)(2,1)} %refs_7_.3) | copy-start | bytes 9437188
  60.7 8.1 %collective-permute-start.5 = (bf16[256,2048]{1,0:T(8,128)(2,1)S(1)}, bf16[256,2048]{1,0:T(8,128)(2,1)S(1)}, u32[]{:S(2)}, u32[]{:S(2)}) collective-permute-start(bf16[256,2048]{1,0:T(8,128)(2,1)S(1)} %get-tuple-element.16), channel_id=1, source_target_pairs={{0,1},{1,0},{2,3},{3,2},{4,5},{5,4},{6,7},{7,6},{8,9},{9,8},{10,11... | collective-permute-start | bytes 3145736 | tf_op jit(solution)/shard_map/ppermute | solution.py:224
  68.7 2.7 %collective-permute-start.14 = (bf16[256,2048]{1,0:T(8,128)(2,1)S(1)}, bf16[256,2048]{1,0:T(8,128)(2,1)S(1)}, u32[]{:S(2)}, u32[]{:S(2)}) collective-permute-start(bf16[256,2048]{1,0:T(8,128)(2,1)S(1)} %get-tuple-element.20), channel_id=1, source_target_pairs={{0,1},{1,0},{2,3},{3,2},{4,5},{5,4},{6,7},{7,6},{8,9},{9,8},{10,11... | collective-permute-start | bytes 3145736 | tf_op jit(solution)/shard_map/ppermute | solution.py:224
  68.9 9.2 %collective-permute-start.6 = (bf16[128,2048]{1,0:T(8,128)(2,1)S(1)}, bf16[128,2048]{1,0:T(8,128)(2,1)S(1)}, u32[]{:S(2)}, u32[]{:S(2)}) collective-permute-start(bf16[128,2048]{1,0:T(8,128)(2,1)S(1)} %add_convert_fusion.1), channel_id=1, source_target_pairs={{0,2},{1,5},{2,0},{3,7},{4,6},{5,1},{6,4},{7,3},{8,10},{9,13},{10,... | collective-permute-start | bytes 1572872 | tf_op jit(solution)/shard_map/ppermute | solution.py:220
  71.5 15.1 %collective-permute-start.15 = (bf16[128,2048]{1,0:T(8,128)(2,1)S(1)}, bf16[128,2048]{1,0:T(8,128)(2,1)S(1)}, u32[]{:S(2)}, u32[]{:S(2)}) collective-permute-start(bf16[128,2048]{1,0:T(8,128)(2,1)S(1)} %add_convert_fusion), channel_id=1, source_target_pairs={{0,2},{1,5},{2,0},{3,7},{4,6},{5,1},{6,4},{7,3},{8,10},{9,13},{10,... | collective-permute-start | bytes 1572872 | tf_op jit(solution)/shard_map/ppermute | solution.py:220
  78.3 9.3 %collective-permute-start.7 = (bf16[64,2048]{1,0:T(8,128)(2,1)S(1)}, bf16[64,2048]{1,0:T(8,128)(2,1)S(1)}, u32[]{:S(2)}, u32[]{:S(2)}) collective-permute-start(bf16[64,2048]{1,0:T(8,128)(2,1)S(1)} %add_convert_fusion.3), channel_id=1, source_target_pairs={{0,4},{1,3},{2,6},{3,1},{4,0},{5,7},{6,2},{7,5},{8,12},{9,11},{10,... | collective-permute-start | bytes 786440 | tf_op jit(solution)/shard_map/ppermute | solution.py:220
  86.7 9.9 %collective-permute-start.16 = (bf16[64,2048]{1,0:T(8,128)(2,1)S(1)}, bf16[64,2048]{1,0:T(8,128)(2,1)S(1)}, u32[]{:S(2)}, u32[]{:S(2)}) collective-permute-start(bf16[64,2048]{1,0:T(8,128)(2,1)S(1)} %add_convert_fusion.2), channel_id=1, source_target_pairs={{0,4},{1,3},{2,6},{3,1},{4,0},{5,7},{6,2},{7,5},{8,12},{9,11},{10,... | collective-permute-start | bytes 786440 | tf_op jit(solution)/shard_map/ppermute | solution.py:220
  87.7 9.5 %collective-permute-start.8 = (bf16[32,2048]{1,0:T(8,128)(2,1)S(1)}, bf16[32,2048]{1,0:T(8,128)(2,1)S(1)}, u32[]{:S(2)}, u32[]{:S(2)}) collective-permute-start(bf16[32,2048]{1,0:T(8,128)(2,1)S(1)} %add_convert_fusion.7), channel_id=1, source_target_pairs={{0,8},{1,9},{2,10},{3,11},{4,12},{5,13},{6,14},{7,15},{8,0},{9,1},... | collective-permute-start | bytes 393224 | tf_op jit(solution)/shard_map/ppermute | solution.py:220
  96.7 6.8 %collective-permute-start.17 = (bf16[32,2048]{1,0:T(8,128)(2,1)S(1)}, bf16[32,2048]{1,0:T(8,128)(2,1)S(1)}, u32[]{:S(2)}, u32[]{:S(2)}) collective-permute-start(bf16[32,2048]{1,0:T(8,128)(2,1)S(1)} %add_convert_fusion.5), channel_id=1, source_target_pairs={{0,8},{1,9},{2,10},{3,11},{4,12},{5,13},{6,14},{7,15},{8,0},{9,1},... | collective-permute-start | bytes 393224 | tf_op jit(solution)/shard_map/ppermute | solution.py:220

commit v2 on v1

v2 whole, which is shorter than its diff:
```python
import functools

import jax
import jax.numpy as jnp
from jax import lax
from jax.experimental import pallas as pl
from jax.experimental.pallas import tpu as pltpu
from jax.sharding import PartitionSpec as P

F32 = jnp.float32
BF16 = jnp.bfloat16
LANES = 128
BIG = 1e9
MIB = 1024 * 1024


def iota(shape, dim):
    return lax.broadcasted_iota(jnp.int32, shape, dim)


def prepare_kernel(me_ref, tokens_ref, routes_ref, gates_ref, prio_ref, rows_ref, facts_ref):
    rows, width = tokens_ref.shape
    top = routes_ref.shape[0]
    for block in range(width // LANES):
        lanes = slice(block * LANES, (block + 1) * LANES)
        x = tokens_ref[:, lanes].astype(F32)
        largest = jnp.max(jnp.abs(x), axis=1, keepdims=True)
        scale = ((largest + 1e-06) / 448.0).astype(BF16).astype(F32)
        quantized = (x / scale).astype(BF16)
        rows_ref[:, lanes] = (quantized.astype(F32) * scale).astype(BF16)
    gates = gates_ref[...]
    high = gates.astype(BF16)
    middle = (gates - high.astype(F32)).astype(BF16)
    low = (gates - high.astype(F32) - middle.astype(F32)).astype(BF16)
    place = iota((top, rows), 0)
    other = jnp.where(place == 0, prio_ref[...].astype(F32), jnp.where(place == 1, me_ref[0].astype(F32), 0.0))
    fields = [routes_ref[...].astype(F32).astype(BF16), high, middle, low, other.astype(BF16)]
    half = rows // 2
    facts = jnp.zeros((half, LANES), F32)
    for c in range(2):
        for k, field in enumerate(fields):
            spot = iota((top, LANES), 1) == iota((top, LANES), 0) + (c * (LANES // 2) + k * top)
            laid = lax.dot_general(
                field,
                spot.astype(F32).astype(BF16),
                (((0,), (0,)), ((), ())),
                preferred_element_type=F32,
            )
            facts += laid[c * half : (c + 1) * half]
    facts_ref[...] = facts.astype(BF16)


def prepare(me, tokens, routes, gates, priority):
    rows, width = tokens.shape
    return pl.pallas_call(
        prepare_kernel,
        in_specs=[pl.BlockSpec(memory_space=pltpu.SMEM)] + [pl.BlockSpec(memory_space=pltpu.VMEM)] * 4,
        out_specs=[pl.BlockSpec(memory_space=pltpu.VMEM)] * 2,
        out_shape=[
            jax.ShapeDtypeStruct((rows, width), BF16),
            jax.ShapeDtypeStruct((rows // 2, LANES), BF16),
        ],
    )(me, tokens, routes.T, gates.T, priority.reshape(1, rows))


def weigh_kernel(top, tok_rows, me_ref, capacity_ref, *refs):
    fact_refs, out_refs, key_ref, row_ref, gate_out = refs[:4], refs[4:6], refs[6], refs[7], refs[8]
    half = tok_rows // 2
    each = fact_refs[0].shape[0]
    total = 8 * each
    me = me_ref[0]
    eye = iota((LANES, LANES), 0) == iota((LANES, LANES), 1)
    lane = iota((LANES, LANES), 1)
    row = lax.rem(iota((LANES, LANES), 0), half)[:, :1]
    tiles = each // LANES
    for a in range(4):

        def tile_step(i, _, a=a):
            facts = fact_refs[a][pl.ds(pl.multiple_of(i * LANES, LANES), LANES), :].astype(F32)
            values = (
                pltpu.roll(facts, LANES - top, 1)
                + pltpu.roll(facts, LANES - 2 * top, 1)
                + pltpu.roll(facts, LANES - 3 * top, 1)
            )
            for c in range(2):
                first = c * (LANES // 2)
                named = (lane >= first) & (lane < first + top) & (facts == me.astype(F32))
                has = jnp.sum(named.astype(F32), axis=1, keepdims=True)
                gate = jnp.sum(jnp.where(named, values, 0.0), axis=1, keepdims=True)
                prio = jnp.sum(jnp.where(lane == first + 4 * top, facts, 0.0), axis=1, keepdims=True)
                source = jnp.sum(jnp.where(lane == first + 4 * top + 1, facts, 0.0), axis=1, keepdims=True)
                key = prio * float(total) + source * float(tok_rows) + (row + c * half).astype(F32)
                key = jnp.where(has > 0.0, key, BIG)
                at = (a * tiles + i) * 2 + c
                key_ref[at] = jnp.broadcast_to(key, (LANES, LANES))
                gate_out[at] = jnp.broadcast_to(gate, (LANES, LANES))
                row_ref[pl.ds(at, 1), :] = jnp.sum(jnp.where(eye, key, 0.0), axis=0, keepdims=True)
            return 0

        lax.fori_loop(0, tiles, tile_step, 0, unroll=tiles == 1)
    limit = capacity_ref[me].astype(F32)
    count = 8 * tiles
    owners = LANES // half

    for side in range(2):

        def rank_step(i, _, side=side):
            for c in range(2):
                at = side * (count // 2) + 2 * i + c
                key = key_ref[at]

                def add(j, smaller):
                    return smaller + (row_ref[pl.ds(j, 1), :] < key).astype(F32)

                smaller = lax.fori_loop(0, count, add, jnp.zeros((LANES, LANES), F32), unroll=min(count, 8))
                rank = jnp.sum(smaller, axis=1, keepdims=True)
                weight = jnp.where((rank < limit) & (key < BIG), gate_out[at], 0.0)
                for owner in range(owners):
                    to = pl.multiple_of((i * owners + owner) * tok_rows + c * half, half)
                    out_refs[side][pl.ds(to, half), :] = weight[owner * half : (owner + 1) * half]
            return 0

        lax.fori_loop(0, count // 4, rank_step, 0)


def weigh(me, capacity, facts, top, tok_rows):
    each = facts[0].shape[0]
    count = 8 * each // LANES
    return pl.pallas_call(
        functools.partial(weigh_kernel, top, tok_rows),
        in_specs=[pl.BlockSpec(memory_space=pltpu.SMEM)] * 2 + [pl.BlockSpec(memory_space=pltpu.VMEM)] * 4,
        out_specs=[pl.BlockSpec(memory_space=pltpu.VMEM)] * 2,
        out_shape=[jax.ShapeDtypeStruct((4 * each, LANES), F32)] * 2,
        scratch_shapes=[
            pltpu.VMEM((count, LANES, LANES), F32),
            pltpu.VMEM((count, LANES), F32),
            pltpu.VMEM((count, LANES, LANES), F32),
        ],
        compiler_params=pltpu.CompilerParams(vmem_limit_bytes=24 * MIB),
        cost_estimate=pl.CostEstimate(flops=2000000, bytes_accessed=5000000, transcendentals=0),
    )(me, capacity, *facts)


FF_TILE, OUT_TILE = 256, 512


def expert_kernel(blocks, *refs):
    count = 2 * len(blocks)
    x_refs, weight_refs, gate_ref, up_ref, down_ref = refs[:count], refs[count : count + 2], *refs[count + 2 : count + 5]
    out_refs = refs[count + 5 : count + 7]
    x, gate_w, up_w, down_w, hidden, out, x_sem, w_sem, out_sem = refs[count + 7 :]
    base, width = x_refs[0].shape
    ff = hidden.shape[1]
    rows = count // 2 * base
    ff_tiles, out_tiles = ff // FF_TILE, width // OUT_TILE
    copies = []
    for a, ref in enumerate(x_refs):
        copies.append(pltpu.make_async_copy(ref, x.at[pl.ds(a * base, base), :], x_sem.at[a]))
    first = []
    for k in range(ff_tiles):
        lanes = pl.ds(k * FF_TILE, FF_TILE)
        first.append(pltpu.make_async_copy(gate_ref.at[0, :, lanes], gate_w.at[k], w_sem.at[2 * k]))
        first.append(pltpu.make_async_copy(up_ref.at[0, :, lanes], up_w.at[k], w_sem.at[2 * k + 1]))
    last = []
    for k in range(out_tiles):
        lanes = pl.ds(k * OUT_TILE, OUT_TILE)
        last.append(pltpu.make_async_copy(down_ref.at[0, :, lanes], down_w.at[k], w_sem.at[2 * ff_tiles + k]))
    for copy in copies + first + last:
        copy.start()
    for copy in copies:
        copy.wait()
    for k in range(ff_tiles):
        first[2 * k].wait()
        gated = jnp.dot(x[...], gate_w[k], preferred_element_type=F32)
        first[2 * k + 1].wait()
        upward = jnp.dot(x[...], up_w[k], preferred_element_type=F32)
        result = gated / (1.0 + jnp.exp(-gated)) * upward
        hidden[:, k * FF_TILE : (k + 1) * FF_TILE] = result.astype(BF16)
    sent = []
    for k in range(out_tiles):
        last[k].wait()
        lanes = slice(k * OUT_TILE, (k + 1) * OUT_TILE)
        made = jnp.dot(hidden[...], down_w[k], preferred_element_type=F32).astype(BF16).astype(F32)
        for a in range(count):
            side, block = divmod(a, count // 2)
            held = slice(a * base, (a + 1) * base)
            weight = weight_refs[side][blocks[block] * base : (blocks[block] + 1) * base, :1]
            out[held, lanes] = (made[held] * weight).astype(BF16)
        for side in range(2):
            copy = pltpu.make_async_copy(
                out.at[pl.ds(side * rows, rows), pl.ds(k * OUT_TILE, OUT_TILE)],
                out_refs[side].at[:, pl.ds(k * OUT_TILE, OUT_TILE)],
                out_sem.at[2 * k + side],
            )
            copy.start()
            sent.append(copy)
    for copy in sent:
        copy.wait()


def expert(blocks, own, other, weights, w_gate, w_up, w_down):
    count = 2 * len(blocks)
    base, width = own[blocks[0]].shape
    ff = w_gate.shape[2]
    rows = len(blocks) * base
    ff_tiles, out_tiles = ff // FF_TILE, width // OUT_TILE
    held = 2 * rows * (4 * width + 2 * ff) + 6 * width * ff + 4 * rows * 2 * (2 * FF_TILE + OUT_TILE)
    return pl.pallas_call(
        functools.partial(expert_kernel, blocks),
        in_specs=[pl.BlockSpec(memory_space=pl.ANY)] * count
        + [pl.BlockSpec(memory_space=pltpu.VMEM)] * 2
        + [pl.BlockSpec(memory_space=pltpu.HBM)] * 3,
        out_specs=[pl.BlockSpec(memory_space=pl.ANY)] * 2,
        out_shape=[jax.ShapeDtypeStruct((rows, width), BF16)] * 2,
        scratch_shapes=[
            pltpu.VMEM((2 * rows, width), BF16),
            pltpu.VMEM((ff_tiles, width, FF_TILE), BF16),
            pltpu.VMEM((ff_tiles, width, FF_TILE), BF16),
            pltpu.VMEM((out_tiles, ff, OUT_TILE), BF16),
            pltpu.VMEM((2 * rows, ff), BF16),
            pltpu.VMEM((2 * rows, width), BF16),
            pltpu.SemaphoreType.DMA((count,)),
            pltpu.SemaphoreType.DMA((2 * ff_tiles + out_tiles,)),
            pltpu.SemaphoreType.DMA((2 * out_tiles,)),
        ],
        compiler_params=pltpu.CompilerParams(vmem_limit_bytes=held + 6 * MIB),
        cost_estimate=pl.CostEstimate(
            flops=12 * rows * width * ff, bytes_accessed=6 * width * ff, transcendentals=2 * rows * ff
        ),
    )(*[own[b] for b in blocks], *[other[b] for b in blocks], *weights, w_gate, w_up, w_down)


def orders(ep):
    bits = list(range(ep.bit_length() - 1))[::-1]
    return (bits, bits[:-2] + bits[:-3:-1])


def send(array, ep, flips):
    pairs = []
    for place in range(ep):
        for core, order in enumerate(orders(ep)):
            to = place
            for flip in flips:
                to ^= 1 << order[flip]
            pairs.append((2 * place + core, 2 * to + core))
    return lax.ppermute(array, ("ep", "sub"), pairs)


def cross(array):
    return lax.ppermute(array, "sub", [(0, 1), (1, 0)])


def add(*terms):
    return sum([t.astype(F32) for t in terms]).astype(BF16)


def on_device(ep, tokens, routes, gates, priority, capacity, w_gate, w_up, w_down):
    tok_rows, width = tokens.shape
    top = routes.shape[1]
    steps = ep.bit_length() - 1
    me = (lax.axis_index("ep") * 2 + lax.axis_index("sub")).astype(jnp.int32).reshape(1)
    held, facts = prepare(me, tokens, routes, gates, priority)
    for step in range(steps - 1):
        facts = jnp.concatenate([facts, send(facts, ep, [step])])
    came = send(facts, ep, [steps - 1])
    weights = weigh(me, capacity, [facts, came, cross(facts), cross(came)], top, tok_rows)
    for step in range(steps - 3):
        held = jnp.concatenate([held, send(held, ep, [step])])
    base = held.shape[0]
    own = {0: held}
    own[1] = send(held, ep, [-3])
    own[2] = send(held, ep, [-2])
    own[4] = send(held, ep, [-1])
    own[3] = send(own[1], ep, [-2])
    own[5] = send(own[1], ep, [-1])
    own[7] = send(own[1], ep, [-2, -1])
    own[6] = send(own[2], ep, [-1])
    other = {b: cross(own[b]) for b in own}
    parts = {}
    for blocks in ((0, 1, 2, 4), (3, 5), (7, 6)):
        mine, theirs = expert(blocks, own, other, weights, w_gate, w_up, w_down)
        theirs = cross(theirs)
        for k, b in enumerate(blocks):
            parts[b] = (mine[k * base : (k + 1) * base], theirs[k * base : (k + 1) * base])
    back4 = send(add(*parts[4]), ep, [-1])
    back3 = send(add(*parts[3]), ep, [-2])
    back5 = send(add(*parts[5]), ep, [-1])
    back7 = send(add(*parts[7]), ep, [-2, -1])
    back6 = send(add(*parts[6]), ep, [-1])
    back1 = send(add(*parts[1], back3, back5, back7), ep, [-3])
    back2 = send(add(*parts[2], back6), ep, [-2])
    terms = [*parts[0], back1, back2, back4]
    count = base
    for step in range(steps - 3)[::-1]:
        count //= 2
        terms.append(send(add(*[t[count : 2 * count] for t in terms]), ep, [step]))
    return add(*[t[:tok_rows] for t in terms])


def solution(mesh):
    in_specs = (
        P(("groups", "ep", "sub"), None),
        P(("groups", "ep", "sub"), None),
        P(("groups", "ep", "sub"), None),
        P(("groups", "ep", "sub")),
        P(),
        P(("ep", "sub"), None, None),
        P(("ep", "sub"), None, None),
        P(("ep", "sub"), None, None),
    )
    out_specs = P(("groups", "ep", "sub"), None)
    return jax.shard_map(
        functools.partial(on_device, mesh.shape["ep"]),
        mesh=mesh,
        in_specs=in_specs,
        out_specs=out_specs,
        check_vma=False,
    )
```

time: 105 us -> 111 us (1.057)
  waiting for transfers between devices: 54.5 us -> 37.8 us
  starting transfers between devices: 18.5 us -> 34 us
  Pallas kernels: 19.3 us -> 29.7 us
  local copies, waits for them, and re-layouts: 8.58 us -> 7.09 us
    ppermute x12 -> x17, waiting for transfers between devices: 53.6 us -> 36.8 us  [send(): return lax.ppermute(array, ('ep', 'sub'), pairs)]
    pallas_call x3 -> x4, Pallas kernels: 17.4 us -> 27.7 us  [the longest x3 25.5 us: expert(): pl.pallas_call(functools.partial(expert_kernel, blocks), in_specs=[pl.Blo...]
    ppermute x6 -> x13, starting transfers between devices: 1.19 us -> 9.42 us  [cross(): return lax.ppermute(array, 'sub', [(0, 1), (1, 0)])]
    ppermute x12 -> x17, starting transfers between devices: 17.3 us -> 24.6 us  [send(): return lax.ppermute(array, ('ep', 'sub'), pairs)]
    concatenate x3 -> x1, other arithmetic: 2.57 us -> 0.7 us  [on_device(): facts = jnp.concatenate([facts, send(facts, ep, [step])])]
    unnamed x14 -> x16, local copies, waits for them, and re-layouts: 8.53 us -> 7.08 us
  transfers between devices with their start and end apart: 18 -> 30, of which waited for: 9 -> 9; matrix products, arithmetic and copies ran while one was open for 4% -> 2% of each run, Pallas kernels for 17% -> 25%
where the time goes in v2:
time: 111 us
  waiting for transfers between devices  37.8 us (34%)
  starting transfers between devices  34 us (31%)
  Pallas kernels  29.7 us (27%)
  local copies, waits for them, and re-layouts  7.09 us (6%)
  other arithmetic  2.26 us (2%)
    ppermute x17, waiting for transfers between devices, send(): return lax.ppermute(array, ('ep', 'sub'), pairs)  36.8 us
    pallas_call x3, Pallas kernels, expert(): pl.pallas_call(functools.partial(expert_kernel, blocks), in_specs=[pl.Blo...  25.5 us
    ppermute x17, starting transfers between devices, send(): return lax.ppermute(array, ('ep', 'sub'), pairs)  24.6 us
    ppermute x13, starting transfers between devices, cross(): return lax.ppermute(array, 'sub', [(0, 1), (1, 0)])  9.42 us
    unnamed x16, local copies, waits for them, and re-layouts  7.08 us
  transfers between devices with their start and end apart: 30, of which 9 were waited for; matrix products, arithmetic and copies ran while one was open for 2% of the time, Pallas kernels for 25%

profile of v2, /device:TPU:0, one launch (start us, length us, event | category | flops | bytes accessed | tf_op | source)
XLA Modules:
  0.0 111.0 jit_solution(8752017475820313131)
XLA Ops:
  0.0 2.0 %shard_map.82 = (bf16[64,2048]{1,0:T(8,128)(2,1)}, bf16[32,128]{1,0:T(8,128)(2,1)}) custom-call(s32[1]{0:T(128)} %bitcast.me_ref, bf16[64,2048]{1,0:T(8,128)(2,1)} %tokens_ref.1, s32[8,64]{1,0:T(8,128)} %bitcast.4, f32[8,64]{1,0:T(8,128)} %bitcast.5, s32[1,64]{1,0:T(1,128)} %bitcast.6), custom_call_target="tpu_custom_call" | custom-call | tf_op jit(solution)/shard_map/pallas_call | solution.py:55
  2.0 4.0 %collective-permute-start = (bf16[64,2048]{1,0:T(8,128)(2,1)}, bf16[64,2048]{1,0:T(8,128)(2,1)S(1)}, u32[]{:S(2)}, u32[]{:S(2)}) collective-permute-start(bf16[64,2048]{1,0:T(8,128)(2,1)} %get-tuple-element.15.refs_0_), channel_id=1, source_target_pairs={{0,8},{1,9},{2,10},{3,11},{4,12},{5,13},{6,14},{7,15},{8,0},{9,1},... | collective-permute-start | bytes 786440 | tf_op jit(solution)/shard_map/ppermute | solution.py:246
  6.0 1.6 %collective-permute-start.1 = (bf16[64,2048]{1,0:T(8,128)(2,1)}, bf16[64,2048]{1,0:T(8,128)(2,1)S(1)}, u32[]{:S(2)}, u32[]{:S(2)}) collective-permute-start(bf16[64,2048]{1,0:T(8,128)(2,1)} %get-tuple-element.15.refs_0_), channel_id=1, source_target_pairs={{0,4},{1,3},{2,6},{3,1},{4,0},{5,7},{6,2},{7,5},{8,12},{9,11},{10,... | collective-permute-start | bytes 786440 | tf_op jit(solution)/shard_map/ppermute | solution.py:246
  8.7 9.8 %collective-permute-done.7 = bf16[32,128]{1,0:T(8,128)(2,1)S(1)} collective-permute-done((bf16[32,128]{1,0:T(8,128)(2,1)}, bf16[32,128]{1,0:T(8,128)(2,1)S(1)}, u32[]{:S(2)}, u32[]{:S(2)}) %collective-permute-start.7) | collective-permute-done | bytes 8224 | tf_op jit(solution)/shard_map/ppermute | solution.py:246
  21.2 1.6 %collective-permute-start.14 = (bf16[64,2048]{1,0:T(8,128)(2,1)S(1)}, bf16[64,2048]{1,0:T(8,128)(2,1)S(1)}, u32[]{:S(2)}, u32[]{:S(2)}) collective-permute-start(bf16[64,2048]{1,0:T(8,128)(2,1)S(1)} %collective-permute-done.refs_1_), channel_id=1, source_target_pairs={{0,2},{1,5},{2,0},{3,7},{4,6},{5,1},{6,4},{7,3},{8,10},{9,13},{10,... | collective-permute-start | bytes 786440 | tf_op jit(solution)/shard_map/ppermute | solution.py:246
  23.5 1.6 %collective-permute-start.9 = (bf16[128,128]{1,0:T(8,128)(2,1)S(1)}, bf16[128,128]{1,0:T(8,128)(2,1)S(1)}, u32[]{:S(2)}, u32[]{:S(2)}) collective-permute-start(bf16[128,128]{1,0:T(8,128)(2,1)S(1)} %constant_dynamic-update-slice_fusion.refs_0_), channel_id=1, source_target_pairs={{0,2},{1,5},{2,0},{3,7},{4,6},{5,1},{6,4},{7,3},{8,10},{9,13},{10,... | collective-permute-start | bytes 98312 | tf_op jit(solution)/shard_map/ppermute | solution.py:246
  25.0 3.1 %collective-permute-done.9.refs_1_ = bf16[128,128]{1,0:T(8,128)(2,1)S(1)} collective-permute-done((bf16[128,128]{1,0:T(8,128)(2,1)S(1)}, bf16[128,128]{1,0:T(8,128)(2,1)S(1)}, u32[]{:S(2)}, u32[]{:S(2)}) %collective-permute-start.9) | collective-permute-done | bytes 32800 | tf_op jit(solution)/shard_map/ppermute | solution.py:246
  28.1 5.9 %collective-permute-start.10 = (bf16[128,128]{1,0:T(8,128)(2,1)S(1)}, bf16[128,128]{1,0:T(8,128)(2,1)S(1)}, u32[]{:S(2)}, u32[]{:S(2)}) collective-permute-start(bf16[128,128]{1,0:T(8,128)(2,1)S(1)} %constant_dynamic-update-slice_fusion.refs_0_), channel_id=1, source_target_pairs={{0,1},{1,0},{2,3},{3,2},{4,5},{5,4},{6,7},{7,6},{8,9},{9,8},{10,11... | collective-permute-start | bytes 98312 | tf_op jit(solution)/shard_map/ppermute | solution.py:250
  38.4 2.0 %collective-permute-done.21.refs_1_ = bf16[64,2048]{1,0:T(8,128)(2,1)S(1)} collective-permute-done((bf16[64,2048]{1,0:T(8,128)(2,1)S(1)}, bf16[64,2048]{1,0:T(8,128)(2,1)S(1)}, u32[]{:S(2)}, u32[]{:S(2)}) %collective-permute-start.21) | collective-permute-done | bytes 262176 | tf_op jit(solution)/shard_map/ppermute | solution.py:246
  41.0 2.2 %shard_map.83 = (f32[512,128]{1,0:T(8,128)S(1)}, f32[512,128]{1,0:T(8,128)S(1)}) custom-call(s32[1]{0:T(128)} %bitcast.me_ref, s32[16]{0:T(128)S(1)} %copy-done.5, bf16[128,128]{1,0:T(8,128)(2,1)S(1)} %constant_dynamic-update-slice_fusion.refs_0_, bf16[128,128]{1,0:T(8,128)(2,1)S(1)} %collective-permute-done.9.refs_1_, ...), custom_call_target="tpu_custom_call" | custom-call | flops 2000000 | bytes 5000000 | tf_op jit(solution)/shard_map/pallas_call | solution.py:129
  44.4 1.9 %copy-done = bf16[1,2048,768]{2,1,0:T(8,128)(2,1)S(1)} copy-done((bf16[1,2048,768]{2,1,0:T(8,128)(2,1)S(1)}, bf16[1,2048,768]{2,1,0:T(8,128)(2,1)}, u32[]{:S(2)}) %copy-start) | copy-done | bytes 3145752
  46.3 1.9 %copy-done.2 = bf16[1,2048,768]{2,1,0:T(8,128)(2,1)S(1)} copy-done((bf16[1,2048,768]{2,1,0:T(8,128)(2,1)S(1)}, bf16[1,2048,768]{2,1,0:T(8,128)(2,1)}, u32[]{:S(2)}) %copy-start.2) | copy-done | bytes 3145752
  48.2 1.9 %copy-done.4 = bf16[1,768,2048]{2,1,0:T(8,128)(2,1)S(1)} copy-done((bf16[1,768,2048]{2,1,0:T(8,128)(2,1)S(1)}, bf16[1,768,2048]{2,1,0:T(8,128)(2,1)}, u32[]{:S(2)}) %copy-start.4) | copy-done | bytes 3145752
  50.1 7.0 %shard_map.85 = (bf16[128,2048]{1,0:T(8,128)(2,1)S(1)}, bf16[128,2048]{1,0:T(8,128)(2,1)S(1)}) custom-call(bf16[64,2048]{1,0:T(8,128)(2,1)S(1)} %collective-permute-done.13.refs_0_, bf16[64,2048]{1,0:T(8,128)(2,1)S(1)} %collective-permute-done.14.refs_1_, bf16[64,2048]{1,0:T(8,128)(2,1)S(1)} %collective-permute-done.15.refs_2_, ...), custom_call_target="tpu_custom_call" | custom-call | flops 2415919104 | bytes 9437184 | tf_op jit(solution)/shard_map/pallas_call | solution.py:208
  57.7 7.0 %shard_map.86 = (bf16[128,2048]{1,0:T(8,128)(2,1)S(1)}, bf16[128,2048]{1,0:T(8,128)(2,1)S(1)}) custom-call(bf16[64,2048]{1,0:T(8,128)(2,1)S(1)} %collective-permute-done.20.refs_0_, bf16[64,2048]{1,0:T(8,128)(2,1)S(1)} %collective-permute-done.21.refs_1_, bf16[64,2048]{1,0:T(8,128)(2,1)S(1)} %collective-permute-done.22.refs_2_, ...), custom_call_target="tpu_custom_call" | custom-call | flops 2415919104 | bytes 9437184 | tf_op jit(solution)/shard_map/pallas_call | solution.py:208
  64.9 11.4 %shard_map.84 = (bf16[256,2048]{1,0:T(8,128)(2,1)S(1)}, bf16[256,2048]{1,0:T(8,128)(2,1)S(1)}) custom-call(bf16[64,2048]{1,0:T(8,128)(2,1)S(1)} %copy-done.6, bf16[64,2048]{1,0:T(8,128)(2,1)S(1)} %collective-permute-done.refs_1_, bf16[64,2048]{1,0:T(8,128)(2,1)S(1)} %collective-permute-done.1.refs_2_, bf16[64,2048]{1,0:T(8,128)(2,1)S(1)} %collective-permute-done.2.refs_3_, ...), custom_call_target="tpu_custom_call" | custom-call | flops 4831838208 | bytes 9437184 | tf_op jit(solution)/shard_map/pallas_call | solution.py:208
  77.0 1.4 %collective-permute-start.18 = (bf16[64,2048]{1,0:T(8,128)(2,1)S(1)}, bf16[64,2048]{1,0:T(8,128)(2,1)S(1)}, u32[]{:S(2)}, u32[]{:S(2)}) collective-permute-start(bf16[64,2048]{1,0:T(8,128)(2,1)S(1)} %get-tuple-element.28), channel_id=1, source_target_pairs={{0,4},{1,3},{2,6},{3,1},{4,0},{5,7},{6,2},{7,5},{8,12},{9,11},{10,... | collective-permute-start | bytes 786440 | tf_op jit(solution)/shard_map/ppermute | solution.py:246
  78.3 1.5 %collective-permute-start.19 = (bf16[64,2048]{1,0:T(8,128)(2,1)S(1)}, bf16[64,2048]{1,0:T(8,128)(2,1)S(1)}, u32[]{:S(2)}, u32[]{:S(2)}) collective-permute-start(bf16[64,2048]{1,0:T(8,128)(2,1)S(1)} %get-tuple-element.29), channel_id=1, source_target_pairs={{0,2},{1,5},{2,0},{3,7},{4,6},{5,1},{6,4},{7,3},{8,10},{9,13},{10,... | collective-permute-start | bytes 786440 | tf_op jit(solution)/shard_map/ppermute | solution.py:246
  81.7 4.5 %collective-permute-done.18 = bf16[64,2048]{1,0:T(8,128)(2,1)S(1)} collective-permute-done((bf16[64,2048]{1,0:T(8,128)(2,1)S(1)}, bf16[64,2048]{1,0:T(8,128)(2,1)S(1)}, u32[]{:S(2)}, u32[]{:S(2)}) %collective-permute-start.18) | collective-permute-done | bytes 262176 | tf_op jit(solution)/shard_map/ppermute | solution.py:246
  86.2 6.1 %collective-permute-done.25 = bf16[64,2048]{1,0:T(8,128)(2,1)S(1)} collective-permute-done((bf16[64,2048]{1,0:T(8,128)(2,1)S(1)}, bf16[64,2048]{1,0:T(8,128)(2,1)S(1)}, u32[]{:S(2)}, u32[]{:S(2)}) %collective-permute-start.25) | collective-permute-done | bytes 262176 | tf_op jit(solution)/shard_map/ppermute | solution.py:246
  92.3 1.4 %collective-permute-done.27 = bf16[64,2048]{1,0:T(8,128)(2,1)S(1)} collective-permute-done((bf16[64,2048]{1,0:T(8,128)(2,1)S(1)}, bf16[64,2048]{1,0:T(8,128)(2,1)S(1)}, u32[]{:S(2)}, u32[]{:S(2)}) %collective-permute-start.27) | collective-permute-done | bytes 262176 | tf_op jit(solution)/shard_map/ppermute | solution.py:246
  94.2 2.9 %collective-permute-start.26 = (bf16[64,2048]{1,0:T(8,128)(2,1)S(1)}, bf16[64,2048]{1,0:T(8,128)(2,1)S(1)}, u32[]{:S(2)}, u32[]{:S(2)}) collective-permute-start(bf16[64,2048]{1,0:T(8,128)(2,1)S(1)} %get-tuple-element.25), channel_id=1, source_target_pairs={{0,8},{1,9},{2,10},{3,11},{4,12},{5,13},{6,14},{7,15},{8,0},{9,1},... | collective-permute-start | bytes 786440 | tf_op jit(solution)/shard_map/ppermute | solution.py:246
  97.1 1.9 %collective-permute-start.28 = (bf16[64,2048]{1,0:T(8,128)(2,1)S(1)}, bf16[64,2048]{1,0:T(8,128)(2,1)S(1)}, u32[]{:S(2)}, u32[]{:S(2)}) collective-permute-start(bf16[64,2048]{1,0:T(8,128)(2,1)S(1)} %get-tuple-element.27), channel_id=1, source_target_pairs={{0,4},{1,3},{2,6},{3,1},{4,0},{5,7},{6,2},{7,5},{8,12},{9,11},{10,... | collective-permute-start | bytes 786440 | tf_op jit(solution)/shard_map/ppermute | solution.py:246
  100.3 9.7 %collective-permute-done.26 = bf16[64,2048]{1,0:T(8,128)(2,1)S(1)} collective-permute-done((bf16[64,2048]{1,0:T(8,128)(2,1)S(1)}, bf16[64,2048]{1,0:T(8,128)(2,1)S(1)}, u32[]{:S(2)}, u32[]{:S(2)}) %collective-permute-start.26) | collective-permute-done | bytes 262176 | tf_op jit(solution)/shard_map/ppermute | solution.py:246
  (63 shorter events, 16.6 us)
Async XLA Ops:
  2.0 18.0 %collective-permute-start = (bf16[64,2048]{1,0:T(8,128)(2,1)}, bf16[64,2048]{1,0:T(8,128)(2,1)S(1)}, u32[]{:S(2)}, u32[]{:S(2)}) collective-permute-start(bf16[64,2048]{1,0:T(8,128)(2,1)} %get-tuple-element.15.refs_0_), channel_id=1, source_target_pairs={{0,8},{1,9},{2,10},{3,11},{4,12},{5,13},{6,14},{7,15},{8,0},{9,1},... | collective-permute-start | bytes 786440 | tf_op jit(solution)/shard_map/ppermute | solution.py:246
  6.0 28.0 %collective-permute-start.1 = (bf16[64,2048]{1,0:T(8,128)(2,1)}, bf16[64,2048]{1,0:T(8,128)(2,1)S(1)}, u32[]{:S(2)}, u32[]{:S(2)}) collective-permute-start(bf16[64,2048]{1,0:T(8,128)(2,1)} %get-tuple-element.15.refs_0_), channel_id=1, source_target_pairs={{0,4},{1,3},{2,6},{3,1},{4,0},{5,7},{6,2},{7,5},{8,12},{9,11},{10,... | collective-permute-start | bytes 786440 | tf_op jit(solution)/shard_map/ppermute | solution.py:246
  7.6 10.9 %collective-permute-start.7 = (bf16[32,128]{1,0:T(8,128)(2,1)}, bf16[32,128]{1,0:T(8,128)(2,1)S(1)}, u32[]{:S(2)}, u32[]{:S(2)}) collective-permute-start(bf16[32,128]{1,0:T(8,128)(2,1)} %get-tuple-element.16), channel_id=1, source_target_pairs={{0,8},{1,9},{2,10},{3,11},{4,12},{5,13},{6,14},{7,15},{8,0},{9,1},... | collective-permute-start | bytes 24584 | tf_op jit(solution)/shard_map/ppermute | solution.py:246
  20.0 17.4 %collective-permute-start.13 = (bf16[64,2048]{1,0:T(8,128)(2,1)S(1)}, bf16[64,2048]{1,0:T(8,128)(2,1)S(1)}, u32[]{:S(2)}, u32[]{:S(2)}) collective-permute-start(bf16[64,2048]{1,0:T(8,128)(2,1)S(1)} %collective-permute-done.refs_1_), channel_id=1, source_target_pairs={{0,4},{1,3},{2,6},{3,1},{4,0},{5,7},{6,2},{7,5},{8,12},{9,11},{10,... | collective-permute-start | bytes 786440 | tf_op jit(solution)/shard_map/ppermute | solution.py:246
  21.2 16.6 %collective-permute-start.14 = (bf16[64,2048]{1,0:T(8,128)(2,1)S(1)}, bf16[64,2048]{1,0:T(8,128)(2,1)S(1)}, u32[]{:S(2)}, u32[]{:S(2)}) collective-permute-start(bf16[64,2048]{1,0:T(8,128)(2,1)S(1)} %collective-permute-done.refs_1_), channel_id=1, source_target_pairs={{0,2},{1,5},{2,0},{3,7},{4,6},{5,1},{6,4},{7,3},{8,10},{9,13},{10,... | collective-permute-start | bytes 786440 | tf_op jit(solution)/shard_map/ppermute | solution.py:246
  22.8 15.1 %collective-permute-start.20 = (bf16[64,2048]{1,0:T(8,128)(2,1)S(1)}, bf16[64,2048]{1,0:T(8,128)(2,1)S(1)}, u32[]{:S(2)}, u32[]{:S(2)}) collective-permute-start(bf16[64,2048]{1,0:T(8,128)(2,1)S(1)} %collective-permute-done.refs_1_), channel_id=1, source_target_pairs={{0,6},{1,7},{2,4},{3,5},{4,2},{5,3},{6,0},{7,1},{8,14},{9,15},{10,... | collective-permute-start | bytes 786440 | tf_op jit(solution)/shard_map/ppermute | solution.py:246
  28.1 6.9 %collective-permute-start.10 = (bf16[128,128]{1,0:T(8,128)(2,1)S(1)}, bf16[128,128]{1,0:T(8,128)(2,1)S(1)}, u32[]{:S(2)}, u32[]{:S(2)}) collective-permute-start(bf16[128,128]{1,0:T(8,128)(2,1)S(1)} %constant_dynamic-update-slice_fusion.refs_0_), channel_id=1, source_target_pairs={{0,1},{1,0},{2,3},{3,2},{4,5},{5,4},{6,7},{7,6},{8,9},{9,8},{10,11... | collective-permute-start | bytes 98312 | tf_op jit(solution)/shard_map/ppermute | solution.py:250
  36.2 7.0 %collective-permute-start.2 = (bf16[64,2048]{1,0:T(8,128)(2,1)}, bf16[64,2048]{1,0:T(8,128)(2,1)S(1)}, u32[]{:S(2)}, u32[]{:S(2)}) collective-permute-start(bf16[64,2048]{1,0:T(8,128)(2,1)} %get-tuple-element.15.refs_0_), channel_id=1, source_target_pairs={{0,2},{1,5},{2,0},{3,7},{4,6},{5,1},{6,4},{7,3},{8,10},{9,13},{10,... | collective-permute-start | bytes 786440 | tf_op jit(solution)/shard_map/ppermute | solution.py:246
  37.4 6.5 %collective-permute-start.15 = (bf16[64,2048]{1,0:T(8,128)(2,1)S(1)}, bf16[64,2048]{1,0:T(8,128)(2,1)S(1)}, u32[]{:S(2)}, u32[]{:S(2)}) collective-permute-start(bf16[64,2048]{1,0:T(8,128)(2,1)S(1)} %collective-permute-done.13.refs_0_), channel_id=1, source_target_pairs={{0,1},{1,0},{2,3},{3,2},{4,5},{5,4},{6,7},{7,6},{8,9},{9,8},{10,11... | collective-permute-start | bytes 786440 | tf_op jit(solution)/shard_map/ppermute | solution.py:250
  37.9 6.4 %collective-permute-start.22 = (bf16[64,2048]{1,0:T(8,128)(2,1)S(1)}, bf16[64,2048]{1,0:T(8,128)(2,1)S(1)}, u32[]{:S(2)}, u32[]{:S(2)}) collective-permute-start(bf16[64,2048]{1,0:T(8,128)(2,1)S(1)} %collective-permute-done.20.refs_0_), channel_id=1, source_target_pairs={{0,1},{1,0},{2,3},{3,2},{4,5},{5,4},{6,7},{7,6},{8,9},{9,8},{10,11... | collective-permute-start | bytes 786440 | tf_op jit(solution)/shard_map/ppermute | solution.py:250
  40.4 16.7 %collective-permute-start.23 = (bf16[64,2048]{1,0:T(8,128)(2,1)S(1)}, bf16[64,2048]{1,0:T(8,128)(2,1)S(1)}, u32[]{:S(2)}, u32[]{:S(2)}) collective-permute-start(bf16[64,2048]{1,0:T(8,128)(2,1)S(1)} %collective-permute-done.21.refs_1_), channel_id=1, source_target_pairs={{0,1},{1,0},{2,3},{3,2},{4,5},{5,4},{6,7},{7,6},{8,9},{9,8},{10,11... | collective-permute-start | bytes 786440 | tf_op jit(solution)/shard_map/ppermute | solution.py:250
  43.2 21.4 %collective-permute-start.3 = (bf16[64,2048]{1,0:T(8,128)(2,1)}, bf16[64,2048]{1,0:T(8,128)(2,1)S(1)}, u32[]{:S(2)}, u32[]{:S(2)}) collective-permute-start(bf16[64,2048]{1,0:T(8,128)(2,1)} %get-tuple-element.15.refs_0_), channel_id=1, source_target_pairs={{0,1},{1,0},{2,3},{3,2},{4,5},{5,4},{6,7},{7,6},{8,9},{9,8},{10,11... | collective-permute-start | bytes 786440 | tf_op jit(solution)/shard_map/ppermute | solution.py:250
  43.8 21.0 %collective-permute-start.4 = (bf16[64,2048]{1,0:T(8,128)(2,1)S(1)}, bf16[64,2048]{1,0:T(8,128)(2,1)S(1)}, u32[]{:S(2)}, u32[]{:S(2)}) collective-permute-start(bf16[64,2048]{1,0:T(8,128)(2,1)S(1)} %collective-permute-done.refs_1_), channel_id=1, source_target_pairs={{0,1},{1,0},{2,3},{3,2},{4,5},{5,4},{6,7},{7,6},{8,9},{9,8},{10,11... | collective-permute-start | bytes 786440 | tf_op jit(solution)/shard_map/ppermute | solution.py:250
  43.9 21.0 %collective-permute-start.5 = (bf16[64,2048]{1,0:T(8,128)(2,1)S(1)}, bf16[64,2048]{1,0:T(8,128)(2,1)S(1)}, u32[]{:S(2)}, u32[]{:S(2)}) collective-permute-start(bf16[64,2048]{1,0:T(8,128)(2,1)S(1)} %collective-permute-done.1.refs_2_), channel_id=1, source_target_pairs={{0,1},{1,0},{2,3},{3,2},{4,5},{5,4},{6,7},{7,6},{8,9},{9,8},{10,11... | collective-permute-start | bytes 786440 | tf_op jit(solution)/shard_map/ppermute | solution.py:250
  44.3 20.5 %collective-permute-start.6 = (bf16[64,2048]{1,0:T(8,128)(2,1)S(1)}, bf16[64,2048]{1,0:T(8,128)(2,1)S(1)}, u32[]{:S(2)}, u32[]{:S(2)}) collective-permute-start(bf16[64,2048]{1,0:T(8,128)(2,1)S(1)} %collective-permute-done.2.refs_3_), channel_id=1, source_target_pairs={{0,1},{1,0},{2,3},{3,2},{4,5},{5,4},{6,7},{7,6},{8,9},{9,8},{10,11... | collective-permute-start | bytes 786440 | tf_op jit(solution)/shard_map/ppermute | solution.py:250
  57.2 19.7 %collective-permute-start.17 = (bf16[128,2048]{1,0:T(8,128)(2,1)S(1)}, bf16[128,2048]{1,0:T(8,128)(2,1)S(1)}, u32[]{:S(2)}, u32[]{:S(2)}) collective-permute-start(bf16[128,2048]{1,0:T(8,128)(2,1)S(1)} %get-tuple-element.22), channel_id=1, source_target_pairs={{0,1},{1,0},{2,3},{3,2},{4,5},{5,4},{6,7},{7,6},{8,9},{9,8},{10,11... | collective-permute-start | bytes 1572872 | tf_op jit(solution)/shard_map/ppermute | solution.py:250
  64.7 15.1 %collective-permute-start.24 = (bf16[128,2048]{1,0:T(8,128)(2,1)S(1)}, bf16[128,2048]{1,0:T(8,128)(2,1)S(1)}, u32[]{:S(2)}, u32[]{:S(2)}) collective-permute-start(bf16[128,2048]{1,0:T(8,128)(2,1)S(1)} %get-tuple-element.24), channel_id=1, source_target_pairs={{0,1},{1,0},{2,3},{3,2},{4,5},{5,4},{6,7},{7,6},{8,9},{9,8},{10,11... | collective-permute-start | bytes 1572872 | tf_op jit(solution)/shard_map/ppermute | solution.py:250
  77.0 9.2 %collective-permute-start.18 = (bf16[64,2048]{1,0:T(8,128)(2,1)S(1)}, bf16[64,2048]{1,0:T(8,128)(2,1)S(1)}, u32[]{:S(2)}, u32[]{:S(2)}) collective-permute-start(bf16[64,2048]{1,0:T(8,128)(2,1)S(1)} %get-tuple-element.28), channel_id=1, source_target_pairs={{0,4},{1,3},{2,6},{3,1},{4,0},{5,7},{6,2},{7,5},{8,12},{9,11},{10,... | collective-permute-start | bytes 786440 | tf_op jit(solution)/shard_map/ppermute | solution.py:246
  78.3 7.9 %collective-permute-start.19 = (bf16[64,2048]{1,0:T(8,128)(2,1)S(1)}, bf16[64,2048]{1,0:T(8,128)(2,1)S(1)}, u32[]{:S(2)}, u32[]{:S(2)}) collective-permute-start(bf16[64,2048]{1,0:T(8,128)(2,1)S(1)} %get-tuple-element.29), channel_id=1, source_target_pairs={{0,2},{1,5},{2,0},{3,7},{4,6},{5,1},{6,4},{7,3},{8,10},{9,13},{10,... | collective-permute-start | bytes 786440 | tf_op jit(solution)/shard_map/ppermute | solution.py:246
  79.9 12.4 %collective-permute-start.25 = (bf16[64,2048]{1,0:T(8,128)(2,1)S(1)}, bf16[64,2048]{1,0:T(8,128)(2,1)S(1)}, u32[]{:S(2)}, u32[]{:S(2)}) collective-permute-start(bf16[64,2048]{1,0:T(8,128)(2,1)S(1)} %get-tuple-element.30), channel_id=1, source_target_pairs={{0,6},{1,7},{2,4},{3,5},{4,2},{5,3},{6,0},{7,1},{8,14},{9,15},{10,... | collective-permute-start | bytes 786440 | tf_op jit(solution)/shard_map/ppermute | solution.py:246
  80.7 13.0 %collective-permute-start.27 = (bf16[64,2048]{1,0:T(8,128)(2,1)S(1)}, bf16[64,2048]{1,0:T(8,128)(2,1)S(1)}, u32[]{:S(2)}, u32[]{:S(2)}) collective-permute-start(bf16[64,2048]{1,0:T(8,128)(2,1)S(1)} %get-tuple-element.31), channel_id=1, source_target_pairs={{0,2},{1,5},{2,0},{3,7},{4,6},{5,1},{6,4},{7,3},{8,10},{9,13},{10,... | collective-permute-start | bytes 786440 | tf_op jit(solution)/shard_map/ppermute | solution.py:246
  94.2 15.7 %collective-permute-start.26 = (bf16[64,2048]{1,0:T(8,128)(2,1)S(1)}, bf16[64,2048]{1,0:T(8,128)(2,1)S(1)}, u32[]{:S(2)}, u32[]{:S(2)}) collective-permute-start(bf16[64,2048]{1,0:T(8,128)(2,1)S(1)} %get-tuple-element.25), channel_id=1, source_target_pairs={{0,8},{1,9},{2,10},{3,11},{4,12},{5,13},{6,14},{7,15},{8,0},{9,1},... | collective-permute-start | bytes 786440 | tf_op jit(solution)/shard_map/ppermute | solution.py:246
  97.1 13.0 %collective-permute-start.28 = (bf16[64,2048]{1,0:T(8,128)(2,1)S(1)}, bf16[64,2048]{1,0:T(8,128)(2,1)S(1)}, u32[]{:S(2)}, u32[]{:S(2)}) collective-permute-start(bf16[64,2048]{1,0:T(8,128)(2,1)S(1)} %get-tuple-element.27), channel_id=1, source_target_pairs={{0,4},{1,3},{2,6},{3,1},{4,0},{5,7},{6,2},{7,5},{8,12},{9,11},{10,... | collective-permute-start | bytes 786440 | tf_op jit(solution)/shard_map/ppermute | solution.py:246
  99.0 11.1 %collective-permute-start.29 = (bf16[64,2048]{1,0:T(8,128)(2,1)S(1)}, bf16[64,2048]{1,0:T(8,128)(2,1)S(1)}, u32[]{:S(2)}, u32[]{:S(2)}) collective-permute-start(bf16[64,2048]{1,0:T(8,128)(2,1)S(1)} %get-tuple-element.26), channel_id=1, source_target_pairs={{0,2},{1,5},{2,0},{3,7},{4,6},{5,1},{6,4},{7,3},{8,10},{9,13},{10,... | collective-permute-start | bytes 786440 | tf_op jit(solution)/shard_map/ppermute | solution.py:246
  (13 other events, 57.2 us)

commit v3 on v2

v3 whole, which is shorter than its diff:
```python
import functools

import jax
import jax.numpy as jnp
from jax import lax
from jax.experimental import pallas as pl
from jax.experimental.pallas import tpu as pltpu
from jax.sharding import PartitionSpec as P

F32 = jnp.float32
BF16 = jnp.bfloat16
LANES = 128
BIG = 1e9
MIB = 1024 * 1024


def iota(shape, dim):
    return lax.broadcasted_iota(jnp.int32, shape, dim)


def prepare_kernel(me_ref, tokens_ref, routes_ref, gates_ref, prio_ref, rows_ref):
    rows, width = tokens_ref.shape
    top = routes_ref.shape[0]
    for block in range(width // LANES):
        lanes = slice(block * LANES, (block + 1) * LANES)
        x = tokens_ref[:, lanes].astype(F32)
        largest = jnp.max(jnp.abs(x), axis=1, keepdims=True)
        scale = ((largest + 1e-06) / 448.0).astype(BF16).astype(F32)
        quantized = (x / scale).astype(BF16)
        rows_ref[:, lanes] = (quantized.astype(F32) * scale).astype(BF16)
    gates = gates_ref[...]
    high = gates.astype(BF16)
    middle = (gates - high.astype(F32)).astype(BF16)
    low = (gates - high.astype(F32) - middle.astype(F32)).astype(BF16)
    place, token = iota((top, rows), 0), iota((top, rows), 1)
    other = jnp.where(place == 0, prio_ref[...], jnp.where(place == 1, me_ref[0], token))
    fields = [routes_ref[...].astype(F32), high.astype(F32), middle.astype(F32), low.astype(F32), other.astype(F32)]
    facts = jnp.zeros((rows, LANES), F32)
    for k, field in enumerate(fields):
        spot = iota((top, LANES), 1) == iota((top, LANES), 0) + k * top
        facts += lax.dot_general(
            field.astype(BF16),
            spot.astype(F32).astype(BF16),
            (((0,), (0,)), ((), ())),
            preferred_element_type=F32,
        )
    rows_ref[:, width:] = facts.astype(BF16)


def prepare(me, tokens, routes, gates, priority):
    rows, width = tokens.shape
    return pl.pallas_call(
        prepare_kernel,
        in_specs=[pl.BlockSpec(memory_space=pltpu.SMEM)] + [pl.BlockSpec(memory_space=pltpu.VMEM)] * 4,
        out_specs=pl.BlockSpec(memory_space=pltpu.VMEM),
        out_shape=jax.ShapeDtypeStruct((rows, width + LANES), BF16),
    )(me, tokens, routes.T, gates.T, priority.reshape(1, rows))


def weigh_kernel(top, tok_rows, me_ref, capacity_ref, *refs):
    fact_refs, out_ref, (all_ref, key_ref, row_ref) = refs[:5], refs[5], refs[6:]
    total = out_ref.shape[0]
    at = 0
    for ref in fact_refs:
        rows, wide = ref.shape
        all_ref[at : at + rows, :] = ref[:, wide - LANES :]
        at += rows
    me = me_ref[0].astype(F32)
    limit = capacity_ref[me_ref[0]].astype(F32)
    eye = iota((LANES, LANES), 0) == iota((LANES, LANES), 1)
    lane = iota((LANES, LANES), 1)
    tiles = total // LANES
    worth = jnp.where(lane == 4 * top, float(total), 0.0)
    worth = jnp.where(lane == 4 * top + 1, float(tok_rows), jnp.where(lane == 4 * top + 2, 1.0, worth))

    def read(i, _):
        held = pl.ds(pl.multiple_of(i * LANES, LANES), LANES)
        facts = all_ref[held, :].astype(F32)
        values = (
            pltpu.roll(facts, LANES - top, 1)
            + pltpu.roll(facts, LANES - 2 * top, 1)
            + pltpu.roll(facts, LANES - 3 * top, 1)
        )
        named = (lane < top) & (facts == me)
        gate = jnp.sum(jnp.where(named, values, 0.0), axis=1, keepdims=True)
        key = jnp.sum(facts * worth, axis=1, keepdims=True)
        key = jnp.where(gate > 0.0, key, BIG)
        key_ref[i] = jnp.broadcast_to(key, (LANES, LANES))
        out_ref[held, :] = jnp.broadcast_to(gate, (LANES, LANES))
        row_ref[pl.ds(i, 1), :] = jnp.sum(jnp.where(eye, key, 0.0), axis=0, keepdims=True)
        return 0

    lax.fori_loop(0, tiles, read, 0, unroll=2)

    def judge(i, _):
        held = pl.ds(pl.multiple_of(i * LANES, LANES), LANES)
        key = key_ref[i]

        def count(j, smaller):
            return smaller + (row_ref[pl.ds(j, 1), :] < key).astype(F32)

        smaller = lax.fori_loop(0, tiles, count, jnp.zeros((LANES, LANES), F32), unroll=min(tiles, 8))
        rank = jnp.sum(smaller, axis=1, keepdims=True)
        out_ref[held, :] = jnp.where(rank < limit, out_ref[held, :], 0.0)
        return 0

    lax.fori_loop(0, tiles, judge, 0)


def weigh(me, capacity, facts, top, tok_rows):
    total = sum(f.shape[0] for f in facts)
    return pl.pallas_call(
        functools.partial(weigh_kernel, top, tok_rows),
        in_specs=[pl.BlockSpec(memory_space=pltpu.SMEM)] * 2 + [pl.BlockSpec(memory_space=pltpu.VMEM)] * 5,
        out_specs=pl.BlockSpec(memory_space=pltpu.VMEM),
        out_shape=jax.ShapeDtypeStruct((total, LANES), F32),
        scratch_shapes=[
            pltpu.VMEM((total, LANES), BF16),
            pltpu.VMEM((total // LANES, LANES, LANES), F32),
            pltpu.VMEM((total // LANES, LANES), F32),
        ],
        compiler_params=pltpu.CompilerParams(vmem_limit_bytes=24 * MIB),
        cost_estimate=pl.CostEstimate(flops=1, bytes_accessed=1, transcendentals=0),
    )(me, capacity, *facts)


def pack_kernel(*refs):
    ins, packed, facts, first, second = refs[:4], *refs[4:]
    rows, width = first.shape
    for k, ref in enumerate(ins):
        facts[k * rows : (k + 1) * rows, :] = ref[:, width:]
        if k > 0:
            packed[(k - 1) * rows : k * rows, :] = ref[...]
    first[...] = ins[1][:, :width]
    second[...] = ins[2][:, :width]


def pack(blocks):
    rows, wide = blocks[0].shape
    return pl.pallas_call(
        pack_kernel,
        in_specs=[pl.BlockSpec(memory_space=pltpu.VMEM)] * 4,
        out_specs=[pl.BlockSpec(memory_space=pltpu.VMEM)] * 4,
        out_shape=[
            jax.ShapeDtypeStruct((3 * rows, wide), BF16),
            jax.ShapeDtypeStruct((4 * rows, LANES), BF16),
            jax.ShapeDtypeStruct((rows, wide - LANES), BF16),
            jax.ShapeDtypeStruct((rows, wide - LANES), BF16),
        ],
        compiler_params=pltpu.CompilerParams(vmem_limit_bytes=24 * MIB),
        cost_estimate=pl.CostEstimate(flops=1, bytes_accessed=1, transcendentals=0),
    )(*blocks)


def load_kernel(*refs):
    count = len(refs) // 2
    sems = refs[-1]
    copies = [pltpu.make_async_copy(refs[k], refs[count + k], sems.at[k]) for k in range(count)]
    for copy in copies:
        copy.start()
    for copy in copies:
        copy.wait()


def load(*arrays):
    size = sum(a.size * 2 for a in arrays)
    return pl.pallas_call(
        load_kernel,
        in_specs=[pl.BlockSpec(memory_space=pl.ANY)] * len(arrays),
        out_specs=[pl.BlockSpec(memory_space=pltpu.VMEM)] * len(arrays),
        out_shape=[jax.ShapeDtypeStruct(a.shape, a.dtype) for a in arrays],
        scratch_shapes=[pltpu.SemaphoreType.DMA((len(arrays),))],
        compiler_params=pltpu.CompilerParams(vmem_limit_bytes=size + 4 * MIB),
    )(*arrays)


FF_TILE, OUT_TILE = 256, 512


def expert_kernel(places, base, split, *refs):
    count = len(refs) - 8
    x_refs, (weight_ref, gate_ref, up_ref, down_ref) = refs[:count], refs[count : count + 4]
    out_refs, (x, hidden) = refs[count + 4 : count + 6], refs[count + 6 :]
    width, ff = x.shape[1], hidden.shape[1]
    at = 0
    for ref in x_refs:
        x[at : at + ref.shape[0], :] = ref[:, :width]
        at += ref.shape[0]
    for k in range(ff // FF_TILE):
        lanes = slice(k * FF_TILE, (k + 1) * FF_TILE)
        gated = jnp.dot(x[...], gate_ref[0, :, lanes], preferred_element_type=F32)
        upward = jnp.dot(x[...], up_ref[0, :, lanes], preferred_element_type=F32)
        hidden[:, lanes] = (gated / (1.0 + jnp.exp(-gated)) * upward).astype(BF16)
    for k in range(width // OUT_TILE):
        lanes = slice(k * OUT_TILE, (k + 1) * OUT_TILE)
        made = jnp.dot(hidden[...], down_ref[0, :, lanes], preferred_element_type=F32).astype(BF16).astype(F32)
        for side in range(2):
            for k, place in enumerate(places[side]):
                first = side * split + k * base
                weight = weight_ref[place * base : (place + 1) * base, :1]
                out_refs[side][k * base : (k + 1) * base, lanes] = (made[first : first + base] * weight).astype(BF16)


def expert(own, other, places, weights, matrices):
    ff, width = matrices[2].shape[1:]
    rows = sum(a.shape[0] for a in own)
    held = 2 * rows * 2 * (width + ff) + 4 * 2 * rows * (2 * FF_TILE + OUT_TILE)
    return pl.pallas_call(
        functools.partial(expert_kernel, places, rows // len(places[0]), rows),
        in_specs=[pl.BlockSpec(memory_space=pltpu.VMEM)] * (len(own) + len(other) + 4),
        out_specs=[pl.BlockSpec(memory_space=pltpu.VMEM)] * 2,
        out_shape=[jax.ShapeDtypeStruct((rows, width), BF16)] * 2,
        scratch_shapes=[pltpu.VMEM((2 * rows, width), BF16), pltpu.VMEM((2 * rows, ff), BF16)],
        compiler_params=pltpu.CompilerParams(vmem_limit_bytes=held + 20 * MIB),
        cost_estimate=pl.CostEstimate(flops=1, bytes_accessed=1, transcendentals=0),
    )(*own, *other, weights, *matrices)


def orders(ep):
    bits = list(range(ep.bit_length() - 1))[::-1]
    return (bits, bits[:-2] + bits[:-3:-1])


def send(array, ep, flips):
    pairs = []
    for place in range(ep):
        for core, order in enumerate(orders(ep)):
            to = place
            for flip in flips:
                to ^= 1 << order[flip]
            pairs.append((2 * place + core, 2 * to + core))
    return lax.ppermute(array, ("ep", "sub"), pairs)


def cross(array):
    return lax.ppermute(array, "sub", [(0, 1), (1, 0)])


def add(*terms):
    return sum([t.astype(F32) for t in terms]).astype(BF16)


def on_device(ep, tokens, routes, gates, priority, capacity, w_gate, w_up, w_down):
    tok_rows, width = tokens.shape
    top = routes.shape[1]
    steps = ep.bit_length() - 1
    me = (lax.axis_index("ep") * 2 + lax.axis_index("sub")).astype(jnp.int32).reshape(1)
    held = prepare(me, tokens, routes, gates, priority)
    for step in range(steps - 3):
        held = jnp.concatenate([held, send(held, ep, [step])])
    base = held.shape[0]
    own1, own2, own4 = send(held, ep, [-3]), send(held, ep, [-2]), send(held, ep, [-1])
    first = cross(held)
    matrices = load(w_gate, w_up, w_down)
    own1, own2, own4, first, matrices = lax.optimization_barrier((own1, own2, own4, first, matrices))
    packed, facts, rows1, rows2 = pack([held, own1, own2, own4])
    own3 = send(rows1, ep, [-2])
    own5 = send(rows1, ep, [-1])
    own7 = send(rows1, ep, [-2, -1])
    own6 = send(rows2, ep, [-1])
    crossed = cross(packed)
    far_facts = send(facts, ep, [-3, -2, -1])
    weights = weigh(me, capacity, [facts, first, crossed, far_facts, cross(far_facts)], top, tok_rows)
    parts = {}

    def work(blocks, mine, others, places):
        places = (places, tuple(p + 4 for p in places))
        made, theirs = expert(mine, others, places, weights, matrices)
        back = cross(theirs)
        for k, b in enumerate(blocks):
            parts[b] = (made[k * base : (k + 1) * base], back[k * base : (k + 1) * base])
        return made

    made = work((0, 1, 2, 4), [held, own1, own2, own4], [first, crossed], (0, 1, 2, 3))
    own3, own5, own7, own6, unused = lax.optimization_barrier((own3, own5, own7, own6, made))
    work((3, 5), [own3, own5], [cross(own3), cross(own5)], (11, 10))
    work((7, 6), [own7, own6], [cross(own7), cross(own6)], (8, 9))
    back4 = send(add(*parts[4]), ep, [-1])
    back3 = send(add(*parts[3]), ep, [-2])
    back5 = send(add(*parts[5]), ep, [-1])
    back7 = send(add(*parts[7]), ep, [-2, -1])
    back6 = send(add(*parts[6]), ep, [-1])
    back1 = send(add(*parts[1], back3, back5, back7), ep, [-3])
    back2 = send(add(*parts[2], back6), ep, [-2])
    terms = [*parts[0], back1, back2, back4]
    count = base
    for step in range(steps - 3)[::-1]:
        count //= 2
        terms.append(send(add(*[t[count : 2 * count] for t in terms]), ep, [step]))
    return add(*[t[:tok_rows] for t in terms])


def solution(mesh):
    in_specs = (
        P(("groups", "ep", "sub"), None),
        P(("groups", "ep", "sub"), None),
        P(("groups", "ep", "sub"), None),
        P(("groups", "ep", "sub")),
        P(),
        P(("ep", "sub"), None, None),
        P(("ep", "sub"), None, None),
        P(("ep", "sub"), None, None),
    )
    out_specs = P(("groups", "ep", "sub"), None)
    return jax.shard_map(
        functools.partial(on_device, mesh.shape["ep"]),
        mesh=mesh,
        in_specs=in_specs,
        out_specs=out_specs,
        check_vma=False,
    )
```

time: 111 us -> 90.4 us (0.81)
  Pallas kernels: 29.7 us -> 15.9 us
  starting transfers between devices: 34 us -> 24 us
  waiting for transfers between devices: 37.8 us -> 42.9 us
  local copies, waits for them, and re-layouts: 7.09 us -> 5.67 us
    pallas_call x3 -> x5, Pallas kernels: 25.5 us -> 11.1 us  [the longest x3 10.3 us: expert(): pl.pallas_call(functools.partial(expert_kernel, places, rows // len(place...]
    ppermute x13 -> x10, starting transfers between devices: 9.42 us -> 1.87 us  [cross(): return lax.ppermute(array, 'sub', [(0, 1), (1, 0)])]
    ppermute x17 -> x15, waiting for transfers between devices: 36.8 us -> 39.5 us  [send(): return lax.ppermute(array, ('ep', 'sub'), pairs)]
    ppermute x17 -> x15, starting transfers between devices: 24.6 us -> 22.1 us  [send(): return lax.ppermute(array, ('ep', 'sub'), pairs)]
    ppermute x13 -> x10, waiting for transfers between devices: 1.03 us -> 3.43 us  [cross(): return lax.ppermute(array, 'sub', [(0, 1), (1, 0)])]
    unnamed x16 -> x10, local copies, waits for them, and re-layouts: 7.08 us -> 5.67 us
  transfers between devices with their start and end apart: 30 -> 25, of which waited for: 9 -> 14; matrix products, arithmetic and copies ran while one was open for 2% -> 0% of each run, Pallas kernels for 25% -> 12%
where the time goes in v3:
time: 90.4 us; the launch traced here: 90.2 us
  waiting for transfers between devices  42.9 us (47%)
  starting transfers between devices  24 us (27%)
  Pallas kernels  15.9 us (18%)
  local copies, waits for them, and re-layouts  5.67 us (6%)
  other arithmetic  1.56 us (2%)
    ppermute x15, waiting for transfers between devices, send(): return lax.ppermute(array, ('ep', 'sub'), pairs)  39.5 us
    ppermute x15, starting transfers between devices, send(): return lax.ppermute(array, ('ep', 'sub'), pairs)  22.1 us
    pallas_call x3, Pallas kernels, expert(): pl.pallas_call(functools.partial(expert_kernel, places, rows // len(place...  10.3 us
    unnamed x10, local copies, waits for them, and re-layouts  5.67 us
    ppermute x10, waiting for transfers between devices, cross(): return lax.ppermute(array, 'sub', [(0, 1), (1, 0)])  3.43 us
    pallas_call x1, Pallas kernels, weigh(): pl.pallas_call(functools.partial(weigh_kernel, top, tok_rows), in_specs=[...  2.86 us
    pallas_call x1, Pallas kernels, prepare(): pl.pallas_call(prepare_kernel, in_specs=[pl.BlockSpec(memory_space=pltpu....  1.99 us
    ppermute x10, starting transfers between devices, cross(): return lax.ppermute(array, 'sub', [(0, 1), (1, 0)])  1.87 us
  transfers between devices with their start and end apart: 25, of which 14 were waited for; matrix products, arithmetic and copies ran while one was open for 0% of the time, Pallas kernels for 12%

profile of v3, /device:TPU:0, one launch (start us, length us, event | category | flops | bytes accessed | tf_op | source)
XLA Modules:
  0.0 90.2 jit_solution(4910908289087195981)
XLA Ops:
  0.0 2.0 %shard_map.82.refs_0_ = bf16[64,2176]{1,0:T(8,128)(2,1)} custom-call(s32[1]{0:T(128)} %bitcast.me_ref, bf16[64,2048]{1,0:T(8,128)(2,1)} %tokens_ref.1, s32[8,64]{1,0:T(8,128)} %bitcast.4, f32[8,64]{1,0:T(8,128)} %bitcast.5, s32[1,64]{1,0:T(1,128)} %bitcast.6), custom_call_target="tpu_custom_call" | custom-call | tf_op jit(solution)/shard_map/pallas_call | solution.py:52
  2.0 4.0 %collective-permute-start = (bf16[64,2176]{1,0:T(8,128)(2,1)}, bf16[64,2176]{1,0:T(8,128)(2,1)S(1)}, u32[]{:S(2)}, u32[]{:S(2)}) collective-permute-start(bf16[64,2176]{1,0:T(8,128)(2,1)} %shard_map.82.refs_0_), channel_id=1, source_target_pairs={{0,8},{1,9},{2,10},{3,11},{4,12},{5,13},{6,14},{7,15},{8,0},{9,1},... | collective-permute-start | bytes 835592 | tf_op jit(solution)/shard_map/ppermute | solution.py:232
  6.0 1.6 %collective-permute-start.1 = (bf16[64,2176]{1,0:T(8,128)(2,1)}, bf16[64,2176]{1,0:T(8,128)(2,1)S(1)}, u32[]{:S(2)}, u32[]{:S(2)}) collective-permute-start(bf16[64,2176]{1,0:T(8,128)(2,1)} %shard_map.82.refs_0_), channel_id=1, source_target_pairs={{0,4},{1,3},{2,6},{3,1},{4,0},{5,7},{6,2},{7,5},{8,12},{9,11},{10,... | collective-permute-start | bytes 835592 | tf_op jit(solution)/shard_map/ppermute | solution.py:232
  7.6 1.5 %collective-permute-start.2 = (bf16[64,2176]{1,0:T(8,128)(2,1)}, bf16[64,2176]{1,0:T(8,128)(2,1)S(1)}, u32[]{:S(2)}, u32[]{:S(2)}) collective-permute-start(bf16[64,2176]{1,0:T(8,128)(2,1)} %shard_map.82.refs_0_), channel_id=1, source_target_pairs={{0,2},{1,5},{2,0},{3,7},{4,6},{5,1},{6,4},{7,3},{8,10},{9,13},{10,... | collective-permute-start | bytes 835592 | tf_op jit(solution)/shard_map/ppermute | solution.py:232
  9.1 1.9 %copy-done = bf16[1,2048,768]{2,1,0:T(8,128)(2,1)S(1)} copy-done((bf16[1,2048,768]{2,1,0:T(8,128)(2,1)S(1)}, bf16[1,2048,768]{2,1,0:T(8,128)(2,1)}, u32[]{:S(2)}) %copy-start) | copy-done | bytes 3145752
  11.0 1.9 %copy-done.1 = bf16[1,2048,768]{2,1,0:T(8,128)(2,1)S(1)} copy-done((bf16[1,2048,768]{2,1,0:T(8,128)(2,1)S(1)}, bf16[1,2048,768]{2,1,0:T(8,128)(2,1)}, u32[]{:S(2)}) %copy-start.1) | copy-done | bytes 3145752
  12.9 1.9 %copy-done.2 = bf16[1,768,2048]{2,1,0:T(8,128)(2,1)S(1)} copy-done((bf16[1,768,2048]{2,1,0:T(8,128)(2,1)S(1)}, bf16[1,768,2048]{2,1,0:T(8,128)(2,1)}, u32[]{:S(2)}) %copy-start.2) | copy-done | bytes 3145752
  15.5 3.5 %collective-permute-done.refs_1_ = bf16[64,2176]{1,0:T(8,128)(2,1)S(1)} collective-permute-done((bf16[64,2176]{1,0:T(8,128)(2,1)}, bf16[64,2176]{1,0:T(8,128)(2,1)S(1)}, u32[]{:S(2)}, u32[]{:S(2)}) %collective-permute-start) | collective-permute-done | bytes 278560 | tf_op jit(solution)/shard_map/ppermute | solution.py:232
  20.6 3.0 %collective-permute-start.5 = (bf16[256,128]{1,0:T(8,128)(2,1)S(1)}, bf16[256,128]{1,0:T(8,128)(2,1)S(1)}, u32[]{:S(2)}, u32[]{:S(2)}) collective-permute-start(bf16[256,128]{1,0:T(8,128)(2,1)S(1)} %get-tuple-element.37.refs_0_), channel_id=1, source_target_pairs={{0,14},{1,15},{2,12},{3,13},{4,10},{5,11},{6,8},{7,9},{8,6},{9,7},... | collective-permute-start | bytes 196616 | tf_op jit(solution)/shard_map/ppermute | solution.py:232
  23.6 4.2 %collective-permute-done.5.refs_3_ = bf16[256,128]{1,0:T(8,128)(2,1)S(1)} collective-permute-done((bf16[256,128]{1,0:T(8,128)(2,1)S(1)}, bf16[256,128]{1,0:T(8,128)(2,1)S(1)}, u32[]{:S(2)}, u32[]{:S(2)}) %collective-permute-start.5) | collective-permute-done | bytes 65568 | tf_op jit(solution)/shard_map/ppermute | solution.py:232
  32.0 2.9 %shard_map.85.refs_6_.refs_4_ = f32[1024,128]{1,0:T(8,128)S(1)} custom-call(s32[1]{0:T(128)} %bitcast.me_ref, s32[16]{0:T(128)S(1)} %copy-done.4, bf16[256,128]{1,0:T(8,128)(2,1)S(1)} %get-tuple-element.37.refs_0_, bf16[64,2176]{1,0:T(8,128)(2,1)S(1)} %collective-permute-done.3.refs_1_.refs_4_, bf16[192,2176]{1,0:T(8,128)(2,1)S(1)} %collective-permute-done.4.refs_2_.refs_5_, ...), custom_call_target="tpu_custom_call" | custom-call | flops 1 | bytes 1 | tf_op jit(solution)/shard_map/pallas_call | solution.py:112
  34.8 5.1 %shard_map.86 = (bf16[256,2048]{1,0:T(8,128)(2,1)S(1)}, bf16[256,2048]{1,0:T(8,128)(2,1)S(1)}) custom-call(bf16[64,2176]{1,0:T(8,128)(2,1)S(1)} %copy-done.3, bf16[64,2176]{1,0:T(8,128)(2,1)S(1)} %collective-permute-done.refs_1_, bf16[64,2176]{1,0:T(8,128)(2,1)S(1)} %collective-permute-done.1.refs_2_, bf16[64,2176]{1,0:T(8,128)(2,1)S(1)} %collective-permute-done.2.refs_3_, ...), custom_call_target="tpu_custom_call" | custom-call | flops 1 | bytes 1 | tf_op jit(solution)/shard_map/pallas_call | solution.py:208
  39.9 2.8 %collective-permute-done.11.refs_1_ = bf16[64,2048]{1,0:T(8,128)(2,1)S(1)} collective-permute-done((bf16[64,2048]{1,0:T(8,128)(2,1)S(1)}, bf16[64,2048]{1,0:T(8,128)(2,1)S(1)}, u32[]{:S(2)}, u32[]{:S(2)}) %collective-permute-start.11) | collective-permute-done | bytes 262176 | tf_op jit(solution)/shard_map/ppermute | solution.py:232
  42.7 2.8 %collective-permute-done.9.refs_1_ = bf16[64,2048]{1,0:T(8,128)(2,1)S(1)} collective-permute-done((bf16[64,2048]{1,0:T(8,128)(2,1)S(1)}, bf16[64,2048]{1,0:T(8,128)(2,1)S(1)}, u32[]{:S(2)}, u32[]{:S(2)}) %collective-permute-start.9) | collective-permute-done | bytes 262176 | tf_op jit(solution)/shard_map/ppermute | solution.py:232
  47.4 2.6 %shard_map.87 = (bf16[128,2048]{1,0:T(8,128)(2,1)S(1)}, bf16[128,2048]{1,0:T(8,128)(2,1)S(1)}) custom-call(bf16[64,2048]{1,0:T(8,128)(2,1)S(1)} %collective-permute-done.8.refs_0_, bf16[64,2048]{1,0:T(8,128)(2,1)S(1)} %collective-permute-done.9.refs_1_, bf16[64,2048]{1,0:T(8,128)(2,1)S(1)} %collective-permute-done.12.refs_2_, ...), custom_call_target="tpu_custom_call" | custom-call | flops 1 | bytes 1 | tf_op jit(solution)/shard_map/pallas_call | solution.py:208
  50.7 1.6 %collective-permute-done.17.refs_2_ = bf16[64,2048]{1,0:T(8,128)(2,1)S(1)} collective-permute-done((bf16[64,2048]{1,0:T(8,128)(2,1)S(1)}, bf16[64,2048]{1,0:T(8,128)(2,1)S(1)}, u32[]{:S(2)}, u32[]{:S(2)}) %collective-permute-start.17) | collective-permute-done | bytes 262176 | tf_op jit(solution)/shard_map/ppermute | solution.py:236
  52.8 2.6 %shard_map.88 = (bf16[128,2048]{1,0:T(8,128)(2,1)S(1)}, bf16[128,2048]{1,0:T(8,128)(2,1)S(1)}) custom-call(bf16[64,2048]{1,0:T(8,128)(2,1)S(1)} %collective-permute-done.10.refs_0_, bf16[64,2048]{1,0:T(8,128)(2,1)S(1)} %collective-permute-done.11.refs_1_, bf16[64,2048]{1,0:T(8,128)(2,1)S(1)} %collective-permute-done.17.refs_2_, ...), custom_call_target="tpu_custom_call" | custom-call | flops 1 | bytes 1 | tf_op jit(solution)/shard_map/pallas_call | solution.py:208
  56.2 1.7 %collective-permute-start.16 = (bf16[64,2048]{1,0:T(8,128)(2,1)S(1)}, bf16[64,2048]{1,0:T(8,128)(2,1)S(1)}, u32[]{:S(2)}, u32[]{:S(2)}) collective-permute-start(bf16[64,2048]{1,0:T(8,128)(2,1)S(1)} %get-tuple-element.57), channel_id=1, source_target_pairs={{0,2},{1,5},{2,0},{3,7},{4,6},{5,1},{6,4},{7,3},{8,10},{9,13},{10,... | collective-permute-start | bytes 786440 | tf_op jit(solution)/shard_map/ppermute | solution.py:232
  58.0 1.8 %collective-permute-start.20 = (bf16[64,2048]{1,0:T(8,128)(2,1)S(1)}, bf16[64,2048]{1,0:T(8,128)(2,1)S(1)}, u32[]{:S(2)}, u32[]{:S(2)}) collective-permute-start(bf16[64,2048]{1,0:T(8,128)(2,1)S(1)} %get-tuple-element.58), channel_id=1, source_target_pairs={{0,6},{1,7},{2,4},{3,5},{4,2},{5,3},{6,0},{7,1},{8,14},{9,15},{10,... | collective-permute-start | bytes 786440 | tf_op jit(solution)/shard_map/ppermute | solution.py:232
  60.3 5.0 %collective-permute-done.15 = bf16[64,2048]{1,0:T(8,128)(2,1)S(1)} collective-permute-done((bf16[64,2048]{1,0:T(8,128)(2,1)S(1)}, bf16[64,2048]{1,0:T(8,128)(2,1)S(1)}, u32[]{:S(2)}, u32[]{:S(2)}) %collective-permute-start.15) | collective-permute-done | bytes 262176 | tf_op jit(solution)/shard_map/ppermute | solution.py:232
  65.3 5.2 %collective-permute-done.20 = bf16[64,2048]{1,0:T(8,128)(2,1)S(1)} collective-permute-done((bf16[64,2048]{1,0:T(8,128)(2,1)S(1)}, bf16[64,2048]{1,0:T(8,128)(2,1)S(1)}, u32[]{:S(2)}, u32[]{:S(2)}) %collective-permute-start.20) | collective-permute-done | bytes 262176 | tf_op jit(solution)/shard_map/ppermute | solution.py:232
  70.5 2.4 %collective-permute-done.22 = bf16[64,2048]{1,0:T(8,128)(2,1)S(1)} collective-permute-done((bf16[64,2048]{1,0:T(8,128)(2,1)S(1)}, bf16[64,2048]{1,0:T(8,128)(2,1)S(1)}, u32[]{:S(2)}, u32[]{:S(2)}) %collective-permute-start.22) | collective-permute-done | bytes 262176 | tf_op jit(solution)/shard_map/ppermute | solution.py:232
  74.7 1.5 %collective-permute-start.23 = (bf16[64,2048]{1,0:T(8,128)(2,1)S(1)}, bf16[64,2048]{1,0:T(8,128)(2,1)S(1)}, u32[]{:S(2)}, u32[]{:S(2)}) collective-permute-start(bf16[64,2048]{1,0:T(8,128)(2,1)S(1)} %get-tuple-element.55), channel_id=1, source_target_pairs={{0,4},{1,3},{2,6},{3,1},{4,0},{5,7},{6,2},{7,5},{8,12},{9,11},{10,... | collective-permute-start | bytes 786440 | tf_op jit(solution)/shard_map/ppermute | solution.py:232
  77.1 11.3 %collective-permute-done.21 = bf16[64,2048]{1,0:T(8,128)(2,1)S(1)} collective-permute-done((bf16[64,2048]{1,0:T(8,128)(2,1)S(1)}, bf16[64,2048]{1,0:T(8,128)(2,1)S(1)}, u32[]{:S(2)}, u32[]{:S(2)}) %collective-permute-start.21) | collective-permute-done | bytes 262176 | tf_op jit(solution)/shard_map/ppermute | solution.py:232
  (47 shorter events, 15.3 us)
Async XLA Ops:
  2.0 17.0 %collective-permute-start = (bf16[64,2176]{1,0:T(8,128)(2,1)}, bf16[64,2176]{1,0:T(8,128)(2,1)S(1)}, u32[]{:S(2)}, u32[]{:S(2)}) collective-permute-start(bf16[64,2176]{1,0:T(8,128)(2,1)} %shard_map.82.refs_0_), channel_id=1, source_target_pairs={{0,8},{1,9},{2,10},{3,11},{4,12},{5,13},{6,14},{7,15},{8,0},{9,1},... | collective-permute-start | bytes 835592 | tf_op jit(solution)/shard_map/ppermute | solution.py:232
  6.0 14.4 %collective-permute-start.1 = (bf16[64,2176]{1,0:T(8,128)(2,1)}, bf16[64,2176]{1,0:T(8,128)(2,1)S(1)}, u32[]{:S(2)}, u32[]{:S(2)}) collective-permute-start(bf16[64,2176]{1,0:T(8,128)(2,1)} %shard_map.82.refs_0_), channel_id=1, source_target_pairs={{0,4},{1,3},{2,6},{3,1},{4,0},{5,7},{6,2},{7,5},{8,12},{9,11},{10,... | collective-permute-start | bytes 835592 | tf_op jit(solution)/shard_map/ppermute | solution.py:232
  7.6 12.8 %collective-permute-start.2 = (bf16[64,2176]{1,0:T(8,128)(2,1)}, bf16[64,2176]{1,0:T(8,128)(2,1)S(1)}, u32[]{:S(2)}, u32[]{:S(2)}) collective-permute-start(bf16[64,2176]{1,0:T(8,128)(2,1)} %shard_map.82.refs_0_), channel_id=1, source_target_pairs={{0,2},{1,5},{2,0},{3,7},{4,6},{5,1},{6,4},{7,3},{8,10},{9,13},{10,... | collective-permute-start | bytes 835592 | tf_op jit(solution)/shard_map/ppermute | solution.py:232
  9.1 11.3 %collective-permute-start.3 = (bf16[64,2176]{1,0:T(8,128)(2,1)}, bf16[64,2176]{1,0:T(8,128)(2,1)S(1)}, u32[]{:S(2)}, u32[]{:S(2)}) collective-permute-start(bf16[64,2176]{1,0:T(8,128)(2,1)} %shard_map.82.refs_0_), channel_id=1, source_target_pairs={{0,1},{1,0},{2,3},{3,2},{4,5},{5,4},{6,7},{7,6},{8,9},{9,8},{10,11... | collective-permute-start | bytes 835592 | tf_op jit(solution)/shard_map/ppermute | solution.py:236
  20.5 11.5 %collective-permute-start.4 = (bf16[192,2176]{1,0:T(8,128)(2,1)S(1)}, bf16[192,2176]{1,0:T(8,128)(2,1)S(1)}, u32[]{:S(2)}, u32[]{:S(2)}) collective-permute-start(bf16[192,2176]{1,0:T(8,128)(2,1)S(1)} %get-tuple-element.36), channel_id=1, source_target_pairs={{0,1},{1,0},{2,3},{3,2},{4,5},{5,4},{6,7},{7,6},{8,9},{9,8},{10,11... | collective-permute-start | bytes 2506760 | tf_op jit(solution)/shard_map/ppermute | solution.py:236
  20.6 7.2 %collective-permute-start.5 = (bf16[256,128]{1,0:T(8,128)(2,1)S(1)}, bf16[256,128]{1,0:T(8,128)(2,1)S(1)}, u32[]{:S(2)}, u32[]{:S(2)}) collective-permute-start(bf16[256,128]{1,0:T(8,128)(2,1)S(1)} %get-tuple-element.37.refs_0_), channel_id=1, source_target_pairs={{0,14},{1,15},{2,12},{3,13},{4,10},{5,11},{6,8},{7,9},{8,6},{9,7},... | collective-permute-start | bytes 196616 | tf_op jit(solution)/shard_map/ppermute | solution.py:232
  27.8 3.5 %collective-permute-start.6 = (bf16[256,128]{1,0:T(8,128)(2,1)S(1)}, bf16[256,128]{1,0:T(8,128)(2,1)S(1)}, u32[]{:S(2)}, u32[]{:S(2)}) collective-permute-start(bf16[256,128]{1,0:T(8,128)(2,1)S(1)} %collective-permute-done.5.refs_3_), channel_id=1, source_target_pairs={{0,1},{1,0},{2,3},{3,2},{4,5},{5,4},{6,7},{7,6},{8,9},{9,8},{10,11... | collective-permute-start | bytes 196616 | tf_op jit(solution)/shard_map/ppermute | solution.py:236
  27.8 12.1 %collective-permute-start.10 = (bf16[64,2048]{1,0:T(8,128)(2,1)S(1)}, bf16[64,2048]{1,0:T(8,128)(2,1)S(1)}, u32[]{:S(2)}, u32[]{:S(2)}) collective-permute-start(bf16[64,2048]{1,0:T(8,128)(2,1)S(1)} %get-tuple-element.43), channel_id=1, source_target_pairs={{0,6},{1,7},{2,4},{3,5},{4,2},{5,3},{6,0},{7,1},{8,14},{9,15},{10,... | collective-permute-start | bytes 786440 | tf_op jit(solution)/shard_map/ppermute | solution.py:232
  28.6 14.1 %collective-permute-start.8 = (bf16[64,2048]{1,0:T(8,128)(2,1)S(1)}, bf16[64,2048]{1,0:T(8,128)(2,1)S(1)}, u32[]{:S(2)}, u32[]{:S(2)}) collective-permute-start(bf16[64,2048]{1,0:T(8,128)(2,1)S(1)} %get-tuple-element.43), channel_id=1, source_target_pairs={{0,4},{1,3},{2,6},{3,1},{4,0},{5,7},{6,2},{7,5},{8,12},{9,11},{10,... | collective-permute-start | bytes 786440 | tf_op jit(solution)/shard_map/ppermute | solution.py:232
  29.9 12.7 %collective-permute-start.11 = (bf16[64,2048]{1,0:T(8,128)(2,1)S(1)}, bf16[64,2048]{1,0:T(8,128)(2,1)S(1)}, u32[]{:S(2)}, u32[]{:S(2)}) collective-permute-start(bf16[64,2048]{1,0:T(8,128)(2,1)S(1)} %get-tuple-element.44), channel_id=1, source_target_pairs={{0,2},{1,5},{2,0},{3,7},{4,6},{5,1},{6,4},{7,3},{8,10},{9,13},{10,... | collective-permute-start | bytes 786440 | tf_op jit(solution)/shard_map/ppermute | solution.py:232
  31.3 14.2 %collective-permute-start.9 = (bf16[64,2048]{1,0:T(8,128)(2,1)S(1)}, bf16[64,2048]{1,0:T(8,128)(2,1)S(1)}, u32[]{:S(2)}, u32[]{:S(2)}) collective-permute-start(bf16[64,2048]{1,0:T(8,128)(2,1)S(1)} %get-tuple-element.43), channel_id=1, source_target_pairs={{0,2},{1,5},{2,0},{3,7},{4,6},{5,1},{6,4},{7,3},{8,10},{9,13},{10,... | collective-permute-start | bytes 786440 | tf_op jit(solution)/shard_map/ppermute | solution.py:232
  45.5 1.9 %collective-permute-start.13 = (bf16[64,2048]{1,0:T(8,128)(2,1)S(1)}, bf16[64,2048]{1,0:T(8,128)(2,1)S(1)}, u32[]{:S(2)}, u32[]{:S(2)}) collective-permute-start(bf16[64,2048]{1,0:T(8,128)(2,1)S(1)} %collective-permute-done.9.refs_1_), channel_id=1, source_target_pairs={{0,1},{1,0},{2,3},{3,2},{4,5},{5,4},{6,7},{7,6},{8,9},{9,8},{10,11... | collective-permute-start | bytes 786440 | tf_op jit(solution)/shard_map/ppermute | solution.py:236
  50.0 5.9 %collective-permute-start.14 = (bf16[128,2048]{1,0:T(8,128)(2,1)S(1)}, bf16[128,2048]{1,0:T(8,128)(2,1)S(1)}, u32[]{:S(2)}, u32[]{:S(2)}) collective-permute-start(bf16[128,2048]{1,0:T(8,128)(2,1)S(1)} %get-tuple-element.48), channel_id=1, source_target_pairs={{0,1},{1,0},{2,3},{3,2},{4,5},{5,4},{6,7},{7,6},{8,9},{9,8},{10,11... | collective-permute-start | bytes 1572872 | tf_op jit(solution)/shard_map/ppermute | solution.py:236
  50.2 2.1 %collective-permute-start.17 = (bf16[64,2048]{1,0:T(8,128)(2,1)S(1)}, bf16[64,2048]{1,0:T(8,128)(2,1)S(1)}, u32[]{:S(2)}, u32[]{:S(2)}) collective-permute-start(bf16[64,2048]{1,0:T(8,128)(2,1)S(1)} %collective-permute-done.10.refs_0_), channel_id=1, source_target_pairs={{0,1},{1,0},{2,3},{3,2},{4,5},{5,4},{6,7},{7,6},{8,9},{9,8},{10,11... | collective-permute-start | bytes 786440 | tf_op jit(solution)/shard_map/ppermute | solution.py:236
  50.6 2.1 %collective-permute-start.18 = (bf16[64,2048]{1,0:T(8,128)(2,1)S(1)}, bf16[64,2048]{1,0:T(8,128)(2,1)S(1)}, u32[]{:S(2)}, u32[]{:S(2)}) collective-permute-start(bf16[64,2048]{1,0:T(8,128)(2,1)S(1)} %collective-permute-done.11.refs_1_), channel_id=1, source_target_pairs={{0,1},{1,0},{2,3},{3,2},{4,5},{5,4},{6,7},{7,6},{8,9},{9,8},{10,11... | collective-permute-start | bytes 786440 | tf_op jit(solution)/shard_map/ppermute | solution.py:236
  55.4 2.5 %collective-permute-start.19 = (bf16[128,2048]{1,0:T(8,128)(2,1)S(1)}, bf16[128,2048]{1,0:T(8,128)(2,1)S(1)}, u32[]{:S(2)}, u32[]{:S(2)}) collective-permute-start(bf16[128,2048]{1,0:T(8,128)(2,1)S(1)} %get-tuple-element.52), channel_id=1, source_target_pairs={{0,1},{1,0},{2,3},{3,2},{4,5},{5,4},{6,7},{7,6},{8,9},{9,8},{10,11... | collective-permute-start | bytes 1572872 | tf_op jit(solution)/shard_map/ppermute | solution.py:236
  55.6 17.4 %collective-permute-start.7 = (bf16[256,2048]{1,0:T(8,128)(2,1)S(1)}, bf16[256,2048]{1,0:T(8,128)(2,1)S(1)}, u32[]{:S(2)}, u32[]{:S(2)}) collective-permute-start(bf16[256,2048]{1,0:T(8,128)(2,1)S(1)} %get-tuple-element.42), channel_id=1, source_target_pairs={{0,1},{1,0},{2,3},{3,2},{4,5},{5,4},{6,7},{7,6},{8,9},{9,8},{10,11... | collective-permute-start | bytes 3145736 | tf_op jit(solution)/shard_map/ppermute | solution.py:236
  56.1 9.2 %collective-permute-start.15 = (bf16[64,2048]{1,0:T(8,128)(2,1)S(1)}, bf16[64,2048]{1,0:T(8,128)(2,1)S(1)}, u32[]{:S(2)}, u32[]{:S(2)}) collective-permute-start(bf16[64,2048]{1,0:T(8,128)(2,1)S(1)} %get-tuple-element.56), channel_id=1, source_target_pairs={{0,4},{1,3},{2,6},{3,1},{4,0},{5,7},{6,2},{7,5},{8,12},{9,11},{10,... | collective-permute-start | bytes 786440 | tf_op jit(solution)/shard_map/ppermute | solution.py:232
  56.2 9.1 %collective-permute-start.16 = (bf16[64,2048]{1,0:T(8,128)(2,1)S(1)}, bf16[64,2048]{1,0:T(8,128)(2,1)S(1)}, u32[]{:S(2)}, u32[]{:S(2)}) collective-permute-start(bf16[64,2048]{1,0:T(8,128)(2,1)S(1)} %get-tuple-element.57), channel_id=1, source_target_pairs={{0,2},{1,5},{2,0},{3,7},{4,6},{5,1},{6,4},{7,3},{8,10},{9,13},{10,... | collective-permute-start | bytes 786440 | tf_op jit(solution)/shard_map/ppermute | solution.py:232
  58.0 12.5 %collective-permute-start.20 = (bf16[64,2048]{1,0:T(8,128)(2,1)S(1)}, bf16[64,2048]{1,0:T(8,128)(2,1)S(1)}, u32[]{:S(2)}, u32[]{:S(2)}) collective-permute-start(bf16[64,2048]{1,0:T(8,128)(2,1)S(1)} %get-tuple-element.58), channel_id=1, source_target_pairs={{0,6},{1,7},{2,4},{3,5},{4,2},{5,3},{6,0},{7,1},{8,14},{9,15},{10,... | collective-permute-start | bytes 786440 | tf_op jit(solution)/shard_map/ppermute | solution.py:232
  59.9 13.1 %collective-permute-start.22 = (bf16[64,2048]{1,0:T(8,128)(2,1)S(1)}, bf16[64,2048]{1,0:T(8,128)(2,1)S(1)}, u32[]{:S(2)}, u32[]{:S(2)}) collective-permute-start(bf16[64,2048]{1,0:T(8,128)(2,1)S(1)} %get-tuple-element.59), channel_id=1, source_target_pairs={{0,2},{1,5},{2,0},{3,7},{4,6},{5,1},{6,4},{7,3},{8,10},{9,13},{10,... | collective-permute-start | bytes 786440 | tf_op jit(solution)/shard_map/ppermute | solution.py:232
  73.4 15.0 %collective-permute-start.21 = (bf16[64,2048]{1,0:T(8,128)(2,1)S(1)}, bf16[64,2048]{1,0:T(8,128)(2,1)S(1)}, u32[]{:S(2)}, u32[]{:S(2)}) collective-permute-start(bf16[64,2048]{1,0:T(8,128)(2,1)S(1)} %get-tuple-element.53), channel_id=1, source_target_pairs={{0,8},{1,9},{2,10},{3,11},{4,12},{5,13},{6,14},{7,15},{8,0},{9,1},... | collective-permute-start | bytes 786440 | tf_op jit(solution)/shard_map/ppermute | solution.py:232
  74.7 14.6 %collective-permute-start.23 = (bf16[64,2048]{1,0:T(8,128)(2,1)S(1)}, bf16[64,2048]{1,0:T(8,128)(2,1)S(1)}, u32[]{:S(2)}, u32[]{:S(2)}) collective-permute-start(bf16[64,2048]{1,0:T(8,128)(2,1)S(1)} %get-tuple-element.55), channel_id=1, source_target_pairs={{0,4},{1,3},{2,6},{3,1},{4,0},{5,7},{6,2},{7,5},{8,12},{9,11},{10,... | collective-permute-start | bytes 786440 | tf_op jit(solution)/shard_map/ppermute | solution.py:232
  76.2 13.1 %collective-permute-start.24 = (bf16[64,2048]{1,0:T(8,128)(2,1)S(1)}, bf16[64,2048]{1,0:T(8,128)(2,1)S(1)}, u32[]{:S(2)}, u32[]{:S(2)}) collective-permute-start(bf16[64,2048]{1,0:T(8,128)(2,1)S(1)} %get-tuple-element.54), channel_id=1, source_target_pairs={{0,2},{1,5},{2,0},{3,7},{4,6},{5,1},{6,4},{7,3},{8,10},{9,13},{10,... | collective-permute-start | bytes 786440 | tf_op jit(solution)/shard_map/ppermute | solution.py:232
  (6 other events, 44.8 us)

commit v4 on v3

--- a/solution.py
+++ b/solution.py
@@ -90,7 +90,7 @@
         row_ref[pl.ds(i, 1), :] = jnp.sum(jnp.where(eye, key, 0.0), axis=0, keepdims=True)
         return 0
 
-    lax.fori_loop(0, tiles, read, 0, unroll=2)
+    lax.fori_loop(0, tiles, read, 0, unroll=min(tiles, 8))
 
     def judge(i, _):
         held = pl.ds(pl.multiple_of(i * LANES, LANES), LANES)
@@ -104,7 +104,7 @@
         out_ref[held, :] = jnp.where(rank < limit, out_ref[held, :], 0.0)
         return 0
 
-    lax.fori_loop(0, tiles, judge, 0)
+    lax.fori_loop(0, tiles, judge, 0, unroll=min(tiles, 8))
 
 
 def weigh(me, capacity, facts, top, tok_rows):
@@ -177,10 +177,10 @@
 FF_TILE, OUT_TILE = 256, 512
 
 
-def expert_kernel(places, base, split, *refs):
-    count = len(refs) - 8
+def expert_kernel(places, base, splits, *refs):
+    count = len(refs) - 6 - len(splits)
     x_refs, (weight_ref, gate_ref, up_ref, down_ref) = refs[:count], refs[count : count + 4]
-    out_refs, (x, hidden) = refs[count + 4 : count + 6], refs[count + 6 :]
+    out_refs, (x, hidden) = refs[count + 4 : -2], refs[-2:]
     width, ff = x.shape[1], hidden.shape[1]
     at = 0
     for ref in x_refs:
@@ -194,26 +194,31 @@
     for k in range(width // OUT_TILE):
         lanes = slice(k * OUT_TILE, (k + 1) * OUT_TILE)
         made = jnp.dot(hidden[...], down_ref[0, :, lanes], preferred_element_type=F32).astype(BF16).astype(F32)
-        for side in range(2):
-            for k, place in enumerate(places[side]):
-                first = side * split + k * base
+        block = 0
+        for out_ref, blocks in zip(out_refs, splits):
+            for to in range(blocks):
+                place = places[block]
                 weight = weight_ref[place * base : (place + 1) * base, :1]
-                out_refs[side][k * base : (k + 1) * base, lanes] = (made[first : first + base] * weight).astype(BF16)
-
-
-def expert(own, other, places, weights, matrices):
+                out_ref[to * base : (to + 1) * base, lanes] = (
+                    made[block * base : (block + 1) * base] * weight
+                ).astype(BF16)
+                block += 1
+
+
+def expert(arrays, places, splits, weights, matrices):
     ff, width = matrices[2].shape[1:]
-    rows = sum(a.shape[0] for a in own)
-    held = 2 * rows * 2 * (width + ff) + 4 * 2 * rows * (2 * FF_TILE + OUT_TILE)
-    return pl.pallas_call(
-        functools.partial(expert_kernel, places, rows // len(places[0]), rows),
-        in_specs=[pl.BlockSpec(memory_space=pltpu.VMEM)] * (len(own) + len(other) + 4),
-        out_specs=[pl.BlockSpec(memory_space=pltpu.VMEM)] * 2,
-        out_shape=[jax.ShapeDtypeStruct((rows, width), BF16)] * 2,
-        scratch_shapes=[pltpu.VMEM((2 * rows, width), BF16), pltpu.VMEM((2 * rows, ff), BF16)],
+    rows = sum(a.shape[0] for a in arrays)
+    base = rows // len(places)
+    held = rows * 2 * (width + ff) + 4 * rows * (2 * FF_TILE + OUT_TILE)
+    return pl.pallas_call(
+        functools.partial(expert_kernel, places, base, splits),
+        in_specs=[pl.BlockSpec(memory_space=pltpu.VMEM)] * (len(arrays) + 4),
+        out_specs=[pl.BlockSpec(memory_space=pltpu.VMEM)] * len(splits),
+        out_shape=[jax.ShapeDtypeStruct((blocks * base, width), BF16) for blocks in splits],
+        scratch_shapes=[pltpu.VMEM((rows, width), BF16), pltpu.VMEM((rows, ff), BF16)],
         compiler_params=pltpu.CompilerParams(vmem_limit_bytes=held + 20 * MIB),
         cost_estimate=pl.CostEstimate(flops=1, bytes_accessed=1, transcendentals=0),
-    )(*own, *other, weights, *matrices)
+    )(*arrays, weights, *matrices)
 
 
 def orders(ep):
@@ -256,32 +261,41 @@
     packed, facts, rows1, rows2 = pack([held, own1, own2, own4])
     own3 = send(rows1, ep, [-2])
     own5 = send(rows1, ep, [-1])
+    far_facts = send(facts, ep, [-3, -2, -1])
+    crossed = cross(packed)
+    rows1, rows2, far_facts = lax.optimization_barrier((rows1, rows2, far_facts))
     own7 = send(rows1, ep, [-2, -1])
     own6 = send(rows2, ep, [-1])
-    crossed = cross(packed)
-    far_facts = send(facts, ep, [-3, -2, -1])
-    weights = weigh(me, capacity, [facts, first, crossed, far_facts, cross(far_facts)], top, tok_rows)
+    far_crossed = cross(far_facts)
+    own3, own5, far_crossed = lax.optimization_barrier((own3, own5, far_crossed))
+    weights = weigh(me, capacity, [facts, first, crossed, far_facts, far_crossed], top, tok_rows)
     parts = {}
 
-    def work(blocks, mine, others, places):
-        places = (places, tuple(p + 4 for p in places))
-        made, theirs = expert(mine, others, places, weights, matrices)
+    def pair(blocks, arrays, places):
+        made, theirs = expert(
+            arrays + [cross(a) for a in arrays], places + [p + 4 for p in places], (2, 2), weights, matrices
+        )
         back = cross(theirs)
         for k, b in enumerate(blocks):
             parts[b] = (made[k * base : (k + 1) * base], back[k * base : (k + 1) * base])
         return made
 
-    made = work((0, 1, 2, 4), [held, own1, own2, own4], [first, crossed], (0, 1, 2, 3))
-    own3, own5, own7, own6, unused = lax.optimization_barrier((own3, own5, own7, own6, made))
-    work((3, 5), [own3, own5], [cross(own3), cross(own5)], (11, 10))
-    work((7, 6), [own7, own6], [cross(own7), cross(own6)], (8, 9))
-    back4 = send(add(*parts[4]), ep, [-1])
+    made = pair((3, 5), [own3, own5], [11, 10])
+    first, made = lax.optimization_barrier((first, made))
+    (theirs,) = expert([first, crossed], [4, 5, 6, 7], (4,), weights, matrices)
+    own7, own6, theirs = lax.optimization_barrier((own7, own6, theirs))
     back3 = send(add(*parts[3]), ep, [-2])
     back5 = send(add(*parts[5]), ep, [-1])
+    pair((7, 6), [own7, own6], [8, 9])
     back7 = send(add(*parts[7]), ep, [-2, -1])
     back6 = send(add(*parts[6]), ep, [-1])
+    (made,) = expert([held, own1, own2, own4], [0, 1, 2, 3], (4,), weights, matrices)
+    back = cross(theirs)
+    for k, b in enumerate((0, 1, 2, 4)):
+        parts[b] = (made[k * base : (k + 1) * base], back[k * base : (k + 1) * base])
     back1 = send(add(*parts[1], back3, back5, back7), ep, [-3])
     back2 = send(add(*parts[2], back6), ep, [-2])
+    back4 = send(add(*parts[4]), ep, [-1])
     terms = [*parts[0], back1, back2, back4]
     count = base
     for step in range(steps - 3)[::-1]:

time: 90.4 us -> 84.5 us (0.935)
  waiting for transfers between devices: 42.9 us -> 39.1 us
  starting transfers between devices: 24 us -> 22.5 us
    ppermute x15, waiting for transfers between devices: 39.5 us -> 36.3 us  [send(): return lax.ppermute(array, ('ep', 'sub'), pairs)]
    ppermute x15, starting transfers between devices: 22.1 us -> 19.5 us  [send(): return lax.ppermute(array, ('ep', 'sub'), pairs)]
    ppermute x10, starting transfers between devices: 1.87 us -> 3.07 us  [cross(): return lax.ppermute(array, 'sub', [(0, 1), (1, 0)])]
    pallas_call x1, Pallas kernels: 2.86 us -> 1.88 us  [weigh(): pl.pallas_call(functools.partial(weigh_kernel, top, tok_rows), in_specs=[...]
    pallas_call x3 -> x4, Pallas kernels: 10.3 us -> 10.7 us  [expert(): pl.pallas_call(functools.partial(expert_kernel, places, base, splits), in...]
  transfers between devices with their start and end apart: 25 -> 25, of which waited for: 14 -> 13; matrix products, arithmetic and copies ran while one was open for 0% -> 0% of each run, Pallas kernels for 12% -> 16%
where the time goes in v4:
time: 84.5 us; the launch traced here: 84.3 us
  waiting for transfers between devices  39.1 us (46%)
  starting transfers between devices  22.5 us (27%)
  Pallas kernels  15.3 us (18%)
  local copies, waits for them, and re-layouts  5.67 us (7%)
  other arithmetic  1.55 us (2%)
    ppermute x15, waiting for transfers between devices, send(): return lax.ppermute(array, ('ep', 'sub'), pairs)  36.3 us
    ppermute x15, starting transfers between devices, send(): return lax.ppermute(array, ('ep', 'sub'), pairs)  19.5 us
    pallas_call x4, Pallas kernels, expert(): pl.pallas_call(functools.partial(expert_kernel, places, base, splits), in...  10.7 us
    unnamed x10, local copies, waits for them, and re-layouts  5.67 us
    ppermute x10, starting transfers between devices, cross(): return lax.ppermute(array, 'sub', [(0, 1), (1, 0)])  3.07 us
    ppermute x10, waiting for transfers between devices, cross(): return lax.ppermute(array, 'sub', [(0, 1), (1, 0)])  2.77 us
    pallas_call x1, Pallas kernels, prepare(): pl.pallas_call(prepare_kernel, in_specs=[pl.BlockSpec(memory_space=pltpu....  1.99 us
    pallas_call x1, Pallas kernels, weigh(): pl.pallas_call(functools.partial(weigh_kernel, top, tok_rows), in_specs=[...  1.88 us
  transfers between devices with their start and end apart: 25, of which 13 were waited for; matrix products, arithmetic and copies ran while one was open for 0% of the time, Pallas kernels for 16%

profile of v4, /device:TPU:0, one launch (start us, length us, event | category | flops | bytes accessed | tf_op | source)
XLA Modules:
  0.0 84.3 jit_solution(17781416350069531942)
XLA Ops:
  0.0 2.0 %shard_map.82.refs_0_ = bf16[64,2176]{1,0:T(8,128)(2,1)} custom-call(s32[1]{0:T(128)} %bitcast.me_ref, bf16[64,2048]{1,0:T(8,128)(2,1)} %tokens_ref.1, s32[8,64]{1,0:T(8,128)} %bitcast.4, f32[8,64]{1,0:T(8,128)} %bitcast.5, s32[1,64]{1,0:T(1,128)} %bitcast.6), custom_call_target="tpu_custom_call" | custom-call | tf_op jit(solution)/shard_map/pallas_call | solution.py:52
  2.0 4.0 %collective-permute-start = (bf16[64,2176]{1,0:T(8,128)(2,1)}, bf16[64,2176]{1,0:T(8,128)(2,1)S(1)}, u32[]{:S(2)}, u32[]{:S(2)}) collective-permute-start(bf16[64,2176]{1,0:T(8,128)(2,1)} %shard_map.82.refs_0_), channel_id=1, source_target_pairs={{0,8},{1,9},{2,10},{3,11},{4,12},{5,13},{6,14},{7,15},{8,0},{9,1},... | collective-permute-start | bytes 835592 | tf_op jit(solution)/shard_map/ppermute | solution.py:237
  6.0 1.6 %collective-permute-start.1 = (bf16[64,2176]{1,0:T(8,128)(2,1)}, bf16[64,2176]{1,0:T(8,128)(2,1)S(1)}, u32[]{:S(2)}, u32[]{:S(2)}) collective-permute-start(bf16[64,2176]{1,0:T(8,128)(2,1)} %shard_map.82.refs_0_), channel_id=1, source_target_pairs={{0,4},{1,3},{2,6},{3,1},{4,0},{5,7},{6,2},{7,5},{8,12},{9,11},{10,... | collective-permute-start | bytes 835592 | tf_op jit(solution)/shard_map/ppermute | solution.py:237
  7.6 1.5 %collective-permute-start.2 = (bf16[64,2176]{1,0:T(8,128)(2,1)}, bf16[64,2176]{1,0:T(8,128)(2,1)S(1)}, u32[]{:S(2)}, u32[]{:S(2)}) collective-permute-start(bf16[64,2176]{1,0:T(8,128)(2,1)} %shard_map.82.refs_0_), channel_id=1, source_target_pairs={{0,2},{1,5},{2,0},{3,7},{4,6},{5,1},{6,4},{7,3},{8,10},{9,13},{10,... | collective-permute-start | bytes 835592 | tf_op jit(solution)/shard_map/ppermute | solution.py:237
  9.1 1.9 %copy-done = bf16[1,2048,768]{2,1,0:T(8,128)(2,1)S(1)} copy-done((bf16[1,2048,768]{2,1,0:T(8,128)(2,1)S(1)}, bf16[1,2048,768]{2,1,0:T(8,128)(2,1)}, u32[]{:S(2)}) %copy-start) | copy-done | bytes 3145752
  11.0 1.9 %copy-done.1 = bf16[1,2048,768]{2,1,0:T(8,128)(2,1)S(1)} copy-done((bf16[1,2048,768]{2,1,0:T(8,128)(2,1)S(1)}, bf16[1,2048,768]{2,1,0:T(8,128)(2,1)}, u32[]{:S(2)}) %copy-start.1) | copy-done | bytes 3145752
  12.9 1.9 %copy-done.2 = bf16[1,768,2048]{2,1,0:T(8,128)(2,1)S(1)} copy-done((bf16[1,768,2048]{2,1,0:T(8,128)(2,1)S(1)}, bf16[1,768,2048]{2,1,0:T(8,128)(2,1)}, u32[]{:S(2)}) %copy-start.2) | copy-done | bytes 3145752
  15.5 3.5 %collective-permute-done.refs_1_ = bf16[64,2176]{1,0:T(8,128)(2,1)S(1)} collective-permute-done((bf16[64,2176]{1,0:T(8,128)(2,1)}, bf16[64,2176]{1,0:T(8,128)(2,1)S(1)}, u32[]{:S(2)}, u32[]{:S(2)}) %collective-permute-start) | collective-permute-done | bytes 278560 | tf_op jit(solution)/shard_map/ppermute | solution.py:237
  19.0 1.4 %collective-permute-done.1.refs_2_ = bf16[64,2176]{1,0:T(8,128)(2,1)S(1)} collective-permute-done((bf16[64,2176]{1,0:T(8,128)(2,1)}, bf16[64,2176]{1,0:T(8,128)(2,1)S(1)}, u32[]{:S(2)}, u32[]{:S(2)}) %collective-permute-start.1) | collective-permute-done | bytes 278560 | tf_op jit(solution)/shard_map/ppermute | solution.py:237
  20.9 1.5 %collective-permute-start.7 = (bf16[64,2048]{1,0:T(8,128)(2,1)S(1)}, bf16[64,2048]{1,0:T(8,128)(2,1)S(1)}, u32[]{:S(2)}, u32[]{:S(2)}) collective-permute-start(bf16[64,2048]{1,0:T(8,128)(2,1)S(1)} %get-tuple-element.49), channel_id=1, source_target_pairs={{0,2},{1,5},{2,0},{3,7},{4,6},{5,1},{6,4},{7,3},{8,10},{9,13},{10,... | collective-permute-start | bytes 786440 | tf_op jit(solution)/shard_map/ppermute | solution.py:237
  22.4 2.2 %collective-permute-start.5 = (bf16[256,128]{1,0:T(8,128)(2,1)S(1)}, bf16[256,128]{1,0:T(8,128)(2,1)S(1)}, u32[]{:S(2)}, u32[]{:S(2)}) collective-permute-start(bf16[256,128]{1,0:T(8,128)(2,1)S(1)} %get-tuple-element.39.refs_0_), channel_id=1, source_target_pairs={{0,14},{1,15},{2,12},{3,13},{4,10},{5,11},{6,8},{7,9},{8,6},{9,7},... | collective-permute-start | bytes 196616 | tf_op jit(solution)/shard_map/ppermute | solution.py:237
  24.7 7.2 %collective-permute-done.5.refs_3_ = bf16[256,128]{1,0:T(8,128)(2,1)S(1)} collective-permute-done((bf16[256,128]{1,0:T(8,128)(2,1)S(1)}, bf16[256,128]{1,0:T(8,128)(2,1)S(1)}, u32[]{:S(2)}, u32[]{:S(2)}) %collective-permute-start.5) | collective-permute-done | bytes 65568 | tf_op jit(solution)/shard_map/ppermute | solution.py:237
  34.5 1.9 %shard_map.85.refs_4_.refs_2_ = f32[1024,128]{1,0:T(8,128)S(1)} custom-call(s32[1]{0:T(128)} %bitcast.me_ref, s32[16]{0:T(128)S(1)} %copy-done.4, bf16[256,128]{1,0:T(8,128)(2,1)S(1)} %get-tuple-element.39.refs_0_, bf16[64,2176]{1,0:T(8,128)(2,1)S(1)} %collective-permute-done.3.refs_1_.refs_0_, bf16[192,2176]{1,0:T(8,128)(2,1)S(1)} %collective-permute-done.4.refs_2_.refs_1_, ...), custom_call_target="tpu_custom_call" | custom-call | flops 1 | bytes 1 | tf_op jit(solution)/shard_map/pallas_call | solution.py:112
  36.4 2.6 %shard_map.87 = (bf16[128,2048]{1,0:T(8,128)(2,1)S(1)}, bf16[128,2048]{1,0:T(8,128)(2,1)S(1)}) custom-call(bf16[64,2048]{1,0:T(8,128)(2,1)S(1)} %collective-permute-done.6.refs_0_, bf16[64,2048]{1,0:T(8,128)(2,1)S(1)} %collective-permute-done.7.refs_1_, bf16[64,2048]{1,0:T(8,128)(2,1)S(1)} %collective-permute-done.11.refs_2_, ...), custom_call_target="tpu_custom_call" | custom-call | flops 1 | bytes 1 | tf_op jit(solution)/shard_map/pallas_call | solution.py:213
  40.3 2.7 %shard_map.88 = bf16[256,2048]{1,0:T(8,128)(2,1)S(1)} custom-call(bf16[64,2176]{1,0:T(8,128)(2,1)S(1)} %collective-permute-done.3.refs_1_.refs_0_, bf16[192,2176]{1,0:T(8,128)(2,1)S(1)} %collective-permute-done.4.refs_2_.refs_1_, f32[1024,128]{1,0:T(8,128)S(1)} %shard_map.85.refs_4_.refs_2_, bf16[1,2048,768]{2,1,0:T(8,128)(2,1)S(1)} %get-tuple-element.46.refs_5_.refs_3_, ...), custom_call_target="tpu_custom_call" | custom-call | flops 1 | bytes 1 | tf_op jit(solution)/shard_map/pallas_call | solution.py:213
  43.0 2.6 %collective-permute-done.10.refs_1_ = bf16[64,2048]{1,0:T(8,128)(2,1)S(1)} collective-permute-done((bf16[64,2048]{1,0:T(8,128)(2,1)S(1)}, bf16[64,2048]{1,0:T(8,128)(2,1)S(1)}, u32[]{:S(2)}, u32[]{:S(2)}) %collective-permute-start.10) | collective-permute-done | bytes 262176 | tf_op jit(solution)/shard_map/ppermute | solution.py:237
  47.5 2.7 %shard_map.89 = (bf16[128,2048]{1,0:T(8,128)(2,1)S(1)}, bf16[128,2048]{1,0:T(8,128)(2,1)S(1)}) custom-call(bf16[64,2048]{1,0:T(8,128)(2,1)S(1)} %collective-permute-done.9.refs_0_, bf16[64,2048]{1,0:T(8,128)(2,1)S(1)} %collective-permute-done.10.refs_1_, bf16[64,2048]{1,0:T(8,128)(2,1)S(1)} %collective-permute-done.17.refs_2_, ...), custom_call_target="tpu_custom_call" | custom-call | flops 1 | bytes 1 | tf_op jit(solution)/shard_map/pallas_call | solution.py:213
  52.3 2.4 %collective-permute-start.20 = (bf16[64,2048]{1,0:T(8,128)(2,1)S(1)}, bf16[64,2048]{1,0:T(8,128)(2,1)S(1)}, u32[]{:S(2)}, u32[]{:S(2)}) collective-permute-start(bf16[64,2048]{1,0:T(8,128)(2,1)S(1)} %get-tuple-element.66), channel_id=1, source_target_pairs={{0,6},{1,7},{2,4},{3,5},{4,2},{5,3},{6,0},{7,1},{8,14},{9,15},{10,... | collective-permute-start | bytes 786440 | tf_op jit(solution)/shard_map/ppermute | solution.py:237
  55.5 2.7 %shard_map.86 = bf16[256,2048]{1,0:T(8,128)(2,1)S(1)} custom-call(bf16[64,2176]{1,0:T(8,128)(2,1)S(1)} %copy-done.3, bf16[64,2176]{1,0:T(8,128)(2,1)S(1)} %collective-permute-done.refs_1_, bf16[64,2176]{1,0:T(8,128)(2,1)S(1)} %collective-permute-done.1.refs_2_, bf16[64,2176]{1,0:T(8,128)(2,1)S(1)} %collective-permute-done.2.refs_3_, ...), custom_call_target="tpu_custom_call" | custom-call | flops 1 | bytes 1 | tf_op jit(solution)/shard_map/pallas_call | solution.py:213
  58.2 1.9 %collective-permute-done.15 = bf16[64,2048]{1,0:T(8,128)(2,1)S(1)} collective-permute-done((bf16[64,2048]{1,0:T(8,128)(2,1)S(1)}, bf16[64,2048]{1,0:T(8,128)(2,1)S(1)}, u32[]{:S(2)}, u32[]{:S(2)}) %collective-permute-start.15) | collective-permute-done | bytes 262176 | tf_op jit(solution)/shard_map/ppermute | solution.py:237
  60.2 6.0 %collective-permute-done.20 = bf16[64,2048]{1,0:T(8,128)(2,1)S(1)} collective-permute-done((bf16[64,2048]{1,0:T(8,128)(2,1)S(1)}, bf16[64,2048]{1,0:T(8,128)(2,1)S(1)}, u32[]{:S(2)}, u32[]{:S(2)}) %collective-permute-start.20) | collective-permute-done | bytes 262176 | tf_op jit(solution)/shard_map/ppermute | solution.py:237
  66.1 1.6 %collective-permute-done.22 = bf16[64,2048]{1,0:T(8,128)(2,1)S(1)} collective-permute-done((bf16[64,2048]{1,0:T(8,128)(2,1)S(1)}, bf16[64,2048]{1,0:T(8,128)(2,1)S(1)}, u32[]{:S(2)}, u32[]{:S(2)}) %collective-permute-start.22) | collective-permute-done | bytes 262176 | tf_op jit(solution)/shard_map/ppermute | solution.py:237
  69.1 2.0 %collective-permute-start.23 = (bf16[64,2048]{1,0:T(8,128)(2,1)S(1)}, bf16[64,2048]{1,0:T(8,128)(2,1)S(1)}, u32[]{:S(2)}, u32[]{:S(2)}) collective-permute-start(bf16[64,2048]{1,0:T(8,128)(2,1)S(1)} %get-tuple-element.63), channel_id=1, source_target_pairs={{0,4},{1,3},{2,6},{3,1},{4,0},{5,7},{6,2},{7,5},{8,12},{9,11},{10,... | collective-permute-start | bytes 786440 | tf_op jit(solution)/shard_map/ppermute | solution.py:237
  71.4 11.9 %collective-permute-done.21 = bf16[64,2048]{1,0:T(8,128)(2,1)S(1)} collective-permute-done((bf16[64,2048]{1,0:T(8,128)(2,1)S(1)}, bf16[64,2048]{1,0:T(8,128)(2,1)S(1)}, u32[]{:S(2)}, u32[]{:S(2)}) %collective-permute-start.21) | collective-permute-done | bytes 262176 | tf_op jit(solution)/shard_map/ppermute | solution.py:237
  (48 shorter events, 12.6 us)
Async XLA Ops:
  2.0 17.0 %collective-permute-start = (bf16[64,2176]{1,0:T(8,128)(2,1)}, bf16[64,2176]{1,0:T(8,128)(2,1)S(1)}, u32[]{:S(2)}, u32[]{:S(2)}) collective-permute-start(bf16[64,2176]{1,0:T(8,128)(2,1)} %shard_map.82.refs_0_), channel_id=1, source_target_pairs={{0,8},{1,9},{2,10},{3,11},{4,12},{5,13},{6,14},{7,15},{8,0},{9,1},... | collective-permute-start | bytes 835592 | tf_op jit(solution)/shard_map/ppermute | solution.py:237
  6.0 14.4 %collective-permute-start.1 = (bf16[64,2176]{1,0:T(8,128)(2,1)}, bf16[64,2176]{1,0:T(8,128)(2,1)S(1)}, u32[]{:S(2)}, u32[]{:S(2)}) collective-permute-start(bf16[64,2176]{1,0:T(8,128)(2,1)} %shard_map.82.refs_0_), channel_id=1, source_target_pairs={{0,4},{1,3},{2,6},{3,1},{4,0},{5,7},{6,2},{7,5},{8,12},{9,11},{10,... | collective-permute-start | bytes 835592 | tf_op jit(solution)/shard_map/ppermute | solution.py:237
  7.6 12.8 %collective-permute-start.2 = (bf16[64,2176]{1,0:T(8,128)(2,1)}, bf16[64,2176]{1,0:T(8,128)(2,1)S(1)}, u32[]{:S(2)}, u32[]{:S(2)}) collective-permute-start(bf16[64,2176]{1,0:T(8,128)(2,1)} %shard_map.82.refs_0_), channel_id=1, source_target_pairs={{0,2},{1,5},{2,0},{3,7},{4,6},{5,1},{6,4},{7,3},{8,10},{9,13},{10,... | collective-permute-start | bytes 835592 | tf_op jit(solution)/shard_map/ppermute | solution.py:237
  9.1 11.3 %collective-permute-start.3 = (bf16[64,2176]{1,0:T(8,128)(2,1)}, bf16[64,2176]{1,0:T(8,128)(2,1)S(1)}, u32[]{:S(2)}, u32[]{:S(2)}) collective-permute-start(bf16[64,2176]{1,0:T(8,128)(2,1)} %shard_map.82.refs_0_), channel_id=1, source_target_pairs={{0,1},{1,0},{2,3},{3,2},{4,5},{5,4},{6,7},{7,6},{8,9},{9,8},{10,11... | collective-permute-start | bytes 835592 | tf_op jit(solution)/shard_map/ppermute | solution.py:241
  20.5 14.0 %collective-permute-start.4 = (bf16[192,2176]{1,0:T(8,128)(2,1)S(1)}, bf16[192,2176]{1,0:T(8,128)(2,1)S(1)}, u32[]{:S(2)}, u32[]{:S(2)}) collective-permute-start(bf16[192,2176]{1,0:T(8,128)(2,1)S(1)} %get-tuple-element.41), channel_id=1, source_target_pairs={{0,1},{1,0},{2,3},{3,2},{4,5},{5,4},{6,7},{7,6},{8,9},{9,8},{10,11... | collective-permute-start | bytes 2506760 | tf_op jit(solution)/shard_map/ppermute | solution.py:241
  20.6 12.5 %collective-permute-start.6 = (bf16[64,2048]{1,0:T(8,128)(2,1)S(1)}, bf16[64,2048]{1,0:T(8,128)(2,1)S(1)}, u32[]{:S(2)}, u32[]{:S(2)}) collective-permute-start(bf16[64,2048]{1,0:T(8,128)(2,1)S(1)} %get-tuple-element.49), channel_id=1, source_target_pairs={{0,4},{1,3},{2,6},{3,1},{4,0},{5,7},{6,2},{7,5},{8,12},{9,11},{10,... | collective-permute-start | bytes 786440 | tf_op jit(solution)/shard_map/ppermute | solution.py:237
  20.9 12.2 %collective-permute-start.7 = (bf16[64,2048]{1,0:T(8,128)(2,1)S(1)}, bf16[64,2048]{1,0:T(8,128)(2,1)S(1)}, u32[]{:S(2)}, u32[]{:S(2)}) collective-permute-start(bf16[64,2048]{1,0:T(8,128)(2,1)S(1)} %get-tuple-element.49), channel_id=1, source_target_pairs={{0,2},{1,5},{2,0},{3,7},{4,6},{5,1},{6,4},{7,3},{8,10},{9,13},{10,... | collective-permute-start | bytes 786440 | tf_op jit(solution)/shard_map/ppermute | solution.py:237
  22.4 9.4 %collective-permute-start.5 = (bf16[256,128]{1,0:T(8,128)(2,1)S(1)}, bf16[256,128]{1,0:T(8,128)(2,1)S(1)}, u32[]{:S(2)}, u32[]{:S(2)}) collective-permute-start(bf16[256,128]{1,0:T(8,128)(2,1)S(1)} %get-tuple-element.39.refs_0_), channel_id=1, source_target_pairs={{0,14},{1,15},{2,12},{3,13},{4,10},{5,11},{6,8},{7,9},{8,6},{9,7},... | collective-permute-start | bytes 196616 | tf_op jit(solution)/shard_map/ppermute | solution.py:237
  33.1 3.3 %collective-permute-start.11 = (bf16[64,2048]{1,0:T(8,128)(2,1)S(1)}, bf16[64,2048]{1,0:T(8,128)(2,1)S(1)}, u32[]{:S(2)}, u32[]{:S(2)}) collective-permute-start(bf16[64,2048]{1,0:T(8,128)(2,1)S(1)} %collective-permute-done.6.refs_0_), channel_id=1, source_target_pairs={{0,1},{1,0},{2,3},{3,2},{4,5},{5,4},{6,7},{7,6},{8,9},{9,8},{10,11... | collective-permute-start | bytes 786440 | tf_op jit(solution)/shard_map/ppermute | solution.py:241
  33.3 3.1 %collective-permute-start.12 = (bf16[64,2048]{1,0:T(8,128)(2,1)S(1)}, bf16[64,2048]{1,0:T(8,128)(2,1)S(1)}, u32[]{:S(2)}, u32[]{:S(2)}) collective-permute-start(bf16[64,2048]{1,0:T(8,128)(2,1)S(1)} %collective-permute-done.7.refs_1_), channel_id=1, source_target_pairs={{0,1},{1,0},{2,3},{3,2},{4,5},{5,4},{6,7},{7,6},{8,9},{9,8},{10,11... | collective-permute-start | bytes 786440 | tf_op jit(solution)/shard_map/ppermute | solution.py:241
  33.6 12.0 %collective-permute-start.10 = (bf16[64,2048]{1,0:T(8,128)(2,1)S(1)}, bf16[64,2048]{1,0:T(8,128)(2,1)S(1)}, u32[]{:S(2)}, u32[]{:S(2)}) collective-permute-start(bf16[64,2048]{1,0:T(8,128)(2,1)S(1)} %get-tuple-element.50), channel_id=1, source_target_pairs={{0,2},{1,5},{2,0},{3,7},{4,6},{5,1},{6,4},{7,3},{8,10},{9,13},{10,... | collective-permute-start | bytes 786440 | tf_op jit(solution)/shard_map/ppermute | solution.py:237
  34.5 11.1 %collective-permute-start.9 = (bf16[64,2048]{1,0:T(8,128)(2,1)S(1)}, bf16[64,2048]{1,0:T(8,128)(2,1)S(1)}, u32[]{:S(2)}, u32[]{:S(2)}) collective-permute-start(bf16[64,2048]{1,0:T(8,128)(2,1)S(1)} %get-tuple-element.49), channel_id=1, source_target_pairs={{0,6},{1,7},{2,4},{3,5},{4,2},{5,3},{6,0},{7,1},{8,14},{9,15},{10,... | collective-permute-start | bytes 786440 | tf_op jit(solution)/shard_map/ppermute | solution.py:237
  39.1 11.7 %collective-permute-start.14 = (bf16[128,2048]{1,0:T(8,128)(2,1)S(1)}, bf16[128,2048]{1,0:T(8,128)(2,1)S(1)}, u32[]{:S(2)}, u32[]{:S(2)}) collective-permute-start(bf16[128,2048]{1,0:T(8,128)(2,1)S(1)} %get-tuple-element.56), channel_id=1, source_target_pairs={{0,1},{1,0},{2,3},{3,2},{4,5},{5,4},{6,7},{7,6},{8,9},{9,8},{10,11... | collective-permute-start | bytes 1572872 | tf_op jit(solution)/shard_map/ppermute | solution.py:241
  45.6 1.5 %collective-permute-start.17 = (bf16[64,2048]{1,0:T(8,128)(2,1)S(1)}, bf16[64,2048]{1,0:T(8,128)(2,1)S(1)}, u32[]{:S(2)}, u32[]{:S(2)}) collective-permute-start(bf16[64,2048]{1,0:T(8,128)(2,1)S(1)} %collective-permute-done.9.refs_0_), channel_id=1, source_target_pairs={{0,1},{1,0},{2,3},{3,2},{4,5},{5,4},{6,7},{7,6},{8,9},{9,8},{10,11... | collective-permute-start | bytes 786440 | tf_op jit(solution)/shard_map/ppermute | solution.py:241
  45.6 1.9 %collective-permute-start.18 = (bf16[64,2048]{1,0:T(8,128)(2,1)S(1)}, bf16[64,2048]{1,0:T(8,128)(2,1)S(1)}, u32[]{:S(2)}, u32[]{:S(2)}) collective-permute-start(bf16[64,2048]{1,0:T(8,128)(2,1)S(1)} %collective-permute-done.10.refs_1_), channel_id=1, source_target_pairs={{0,1},{1,0},{2,3},{3,2},{4,5},{5,4},{6,7},{7,6},{8,9},{9,8},{10,11... | collective-permute-start | bytes 786440 | tf_op jit(solution)/shard_map/ppermute | solution.py:241
  50.2 2.0 %collective-permute-start.19 = (bf16[128,2048]{1,0:T(8,128)(2,1)S(1)}, bf16[128,2048]{1,0:T(8,128)(2,1)S(1)}, u32[]{:S(2)}, u32[]{:S(2)}) collective-permute-start(bf16[128,2048]{1,0:T(8,128)(2,1)S(1)} %get-tuple-element.60), channel_id=1, source_target_pairs={{0,1},{1,0},{2,3},{3,2},{4,5},{5,4},{6,7},{7,6},{8,9},{9,8},{10,11... | collective-permute-start | bytes 1572872 | tf_op jit(solution)/shard_map/ppermute | solution.py:241
  50.4 17.4 %collective-permute-start.13 = (bf16[256,2048]{1,0:T(8,128)(2,1)S(1)}, bf16[256,2048]{1,0:T(8,128)(2,1)S(1)}, u32[]{:S(2)}, u32[]{:S(2)}) collective-permute-start(bf16[256,2048]{1,0:T(8,128)(2,1)S(1)} %shard_map.88), channel_id=1, source_target_pairs={{0,1},{1,0},{2,3},{3,2},{4,5},{5,4},{6,7},{7,6},{8,9},{9,8},{10,11... | collective-permute-start | bytes 3145736 | tf_op jit(solution)/shard_map/ppermute | solution.py:241
  50.9 9.2 %collective-permute-start.15 = (bf16[64,2048]{1,0:T(8,128)(2,1)S(1)}, bf16[64,2048]{1,0:T(8,128)(2,1)S(1)}, u32[]{:S(2)}, u32[]{:S(2)}) collective-permute-start(bf16[64,2048]{1,0:T(8,128)(2,1)S(1)} %get-tuple-element.64), channel_id=1, source_target_pairs={{0,4},{1,3},{2,6},{3,1},{4,0},{5,7},{6,2},{7,5},{8,12},{9,11},{10,... | collective-permute-start | bytes 786440 | tf_op jit(solution)/shard_map/ppermute | solution.py:237
  51.0 9.2 %collective-permute-start.16 = (bf16[64,2048]{1,0:T(8,128)(2,1)S(1)}, bf16[64,2048]{1,0:T(8,128)(2,1)S(1)}, u32[]{:S(2)}, u32[]{:S(2)}) collective-permute-start(bf16[64,2048]{1,0:T(8,128)(2,1)S(1)} %get-tuple-element.65), channel_id=1, source_target_pairs={{0,2},{1,5},{2,0},{3,7},{4,6},{5,1},{6,4},{7,3},{8,10},{9,13},{10,... | collective-permute-start | bytes 786440 | tf_op jit(solution)/shard_map/ppermute | solution.py:237
  52.3 13.8 %collective-permute-start.20 = (bf16[64,2048]{1,0:T(8,128)(2,1)S(1)}, bf16[64,2048]{1,0:T(8,128)(2,1)S(1)}, u32[]{:S(2)}, u32[]{:S(2)}) collective-permute-start(bf16[64,2048]{1,0:T(8,128)(2,1)S(1)} %get-tuple-element.66), channel_id=1, source_target_pairs={{0,6},{1,7},{2,4},{3,5},{4,2},{5,3},{6,0},{7,1},{8,14},{9,15},{10,... | collective-permute-start | bytes 786440 | tf_op jit(solution)/shard_map/ppermute | solution.py:237
  54.7 13.1 %collective-permute-start.22 = (bf16[64,2048]{1,0:T(8,128)(2,1)S(1)}, bf16[64,2048]{1,0:T(8,128)(2,1)S(1)}, u32[]{:S(2)}, u32[]{:S(2)}) collective-permute-start(bf16[64,2048]{1,0:T(8,128)(2,1)S(1)} %get-tuple-element.67), channel_id=1, source_target_pairs={{0,2},{1,5},{2,0},{3,7},{4,6},{5,1},{6,4},{7,3},{8,10},{9,13},{10,... | collective-permute-start | bytes 786440 | tf_op jit(solution)/shard_map/ppermute | solution.py:237
  68.2 15.0 %collective-permute-start.21 = (bf16[64,2048]{1,0:T(8,128)(2,1)S(1)}, bf16[64,2048]{1,0:T(8,128)(2,1)S(1)}, u32[]{:S(2)}, u32[]{:S(2)}) collective-permute-start(bf16[64,2048]{1,0:T(8,128)(2,1)S(1)} %get-tuple-element.61), channel_id=1, source_target_pairs={{0,8},{1,9},{2,10},{3,11},{4,12},{5,13},{6,14},{7,15},{8,0},{9,1},... | collective-permute-start | bytes 786440 | tf_op jit(solution)/shard_map/ppermute | solution.py:237
  69.1 14.4 %collective-permute-start.23 = (bf16[64,2048]{1,0:T(8,128)(2,1)S(1)}, bf16[64,2048]{1,0:T(8,128)(2,1)S(1)}, u32[]{:S(2)}, u32[]{:S(2)}) collective-permute-start(bf16[64,2048]{1,0:T(8,128)(2,1)S(1)} %get-tuple-element.63), channel_id=1, source_target_pairs={{0,4},{1,3},{2,6},{3,1},{4,0},{5,7},{6,2},{7,5},{8,12},{9,11},{10,... | collective-permute-start | bytes 786440 | tf_op jit(solution)/shard_map/ppermute | solution.py:237
  71.0 12.4 %collective-permute-start.24 = (bf16[64,2048]{1,0:T(8,128)(2,1)S(1)}, bf16[64,2048]{1,0:T(8,128)(2,1)S(1)}, u32[]{:S(2)}, u32[]{:S(2)}) collective-permute-start(bf16[64,2048]{1,0:T(8,128)(2,1)S(1)} %get-tuple-element.62), channel_id=1, source_target_pairs={{0,2},{1,5},{2,0},{3,7},{4,6},{5,1},{6,4},{7,3},{8,10},{9,13},{10,... | collective-permute-start | bytes 786440 | tf_op jit(solution)/shard_map/ppermute | solution.py:237
  (6 other events, 47.0 us)

commit v5 on v3

v5 whole, which is shorter than its diff:
```python
import functools

import jax
import jax.numpy as jnp
from jax import lax
from jax.experimental import pallas as pl
from jax.experimental.pallas import tpu as pltpu
from jax.sharding import PartitionSpec as P

F32 = jnp.float32
BF16 = jnp.bfloat16
LANES = 128
BIG = 1e9
MIB = 1024 * 1024


def iota(shape, dim):
    return lax.broadcasted_iota(jnp.int32, shape, dim)


def prepare_kernel(me_ref, tokens_ref, routes_ref, gates_ref, prio_ref, rows_ref):
    rows, width = tokens_ref.shape
    top = routes_ref.shape[0]
    for block in range(width // LANES):
        lanes = slice(block * LANES, (block + 1) * LANES)
        x = tokens_ref[:, lanes].astype(F32)
        largest = jnp.max(jnp.abs(x), axis=1, keepdims=True)
        scale = ((largest + 1e-06) / 448.0).astype(BF16).astype(F32)
        quantized = (x / scale).astype(BF16)
        rows_ref[:, lanes] = (quantized.astype(F32) * scale).astype(BF16)
    gates = gates_ref[...]
    high = gates.astype(BF16)
    middle = (gates - high.astype(F32)).astype(BF16)
    low = (gates - high.astype(F32) - middle.astype(F32)).astype(BF16)
    place, token = iota((top, rows), 0), iota((top, rows), 1)
    other = jnp.where(place == 0, prio_ref[...], jnp.where(place == 1, me_ref[0], token))
    fields = [routes_ref[...].astype(F32), high.astype(F32), middle.astype(F32), low.astype(F32), other.astype(F32)]
    facts = jnp.zeros((rows, LANES), F32)
    for k, field in enumerate(fields):
        spot = iota((top, LANES), 1) == iota((top, LANES), 0) + k * top
        facts += lax.dot_general(
            field.astype(BF16),
            spot.astype(F32).astype(BF16),
            (((0,), (0,)), ((), ())),
            preferred_element_type=F32,
        )
    rows_ref[:, width:] = facts.astype(BF16)


def prepare(me, tokens, routes, gates, priority):
    rows, width = tokens.shape
    return pl.pallas_call(
        prepare_kernel,
        in_specs=[pl.BlockSpec(memory_space=pltpu.SMEM)] + [pl.BlockSpec(memory_space=pltpu.VMEM)] * 4,
        out_specs=pl.BlockSpec(memory_space=pltpu.VMEM),
        out_shape=jax.ShapeDtypeStruct((rows, width + LANES), BF16),
    )(me, tokens, routes.T, gates.T, priority.reshape(1, rows))


def weigh_kernel(top, tok_rows, me_ref, capacity_ref, *refs):
    fact_refs, out_ref, (all_ref, key_ref, row_ref) = refs[:-4], refs[-4], refs[-3:]
    total = all_ref.shape[0]
    at = 0
    for ref in fact_refs:
        rows, wide = ref.shape
        all_ref[at : at + rows, :] = ref[:, wide - LANES :]
        at += rows
    eye = iota((LANES, LANES), 0) == iota((LANES, LANES), 1)
    lane = iota((LANES, LANES), 1)
    tiles = total // LANES
    mine = tiles // 2
    experts = (me_ref[0], me_ref[0] + 1 - 2 * lax.rem(me_ref[0], 2))
    worth = jnp.where(lane == 4 * top, float(total), 0.0)
    worth = jnp.where(lane == 4 * top + 1, float(tok_rows), jnp.where(lane == 4 * top + 2, 1.0, worth))

    def read(i, _, own):
        facts = all_ref[pl.ds(pl.multiple_of(i * LANES, LANES), LANES), :].astype(F32)
        values = (
            pltpu.roll(facts, LANES - top, 1)
            + pltpu.roll(facts, LANES - 2 * top, 1)
            + pltpu.roll(facts, LANES - 3 * top, 1)
        )
        order = jnp.sum(facts * worth, axis=1, keepdims=True)
        for e, expert in enumerate(experts):
            named = (lane < top) & (facts == expert.astype(F32))
            gate = jnp.sum(jnp.where(named, values, 0.0), axis=1, keepdims=True)
            key = jnp.where(gate > 0.0, order, BIG)
            row_ref[e, pl.ds(i, 1), :] = jnp.sum(jnp.where(eye, key, 0.0), axis=0, keepdims=True)
            if own:
                key_ref[e, i] = jnp.broadcast_to(key, (LANES, LANES))
                held = pl.ds(pl.multiple_of((e * mine + i) * LANES, LANES), LANES)
                out_ref[held, :] = jnp.broadcast_to(gate, (LANES, LANES))
        return 0

    lax.fori_loop(0, mine, functools.partial(read, own=True), 0, unroll=min(mine, 4))
    lax.fori_loop(mine, tiles, functools.partial(read, own=False), 0, unroll=min(mine, 4))
    for e, expert in enumerate(experts):
        limit = capacity_ref[expert].astype(F32)

        def judge(i, _, e=e, limit=limit):
            held = pl.ds(pl.multiple_of((e * mine + i) * LANES, LANES), LANES)
            key = key_ref[e, i]

            def count(j, smaller):
                return smaller + (row_ref[e, pl.ds(j, 1), :] < key).astype(F32)

            smaller = lax.fori_loop(0, tiles, count, jnp.zeros((LANES, LANES), F32), unroll=min(tiles, 8))
            rank = jnp.sum(smaller, axis=1, keepdims=True)
            out_ref[held, :] = jnp.where(rank < limit, out_ref[held, :], 0.0)
            return 0

        lax.fori_loop(0, mine, judge, 0, unroll=min(mine, 4))


def weigh(me, capacity, facts, top, tok_rows):
    total = sum(f.shape[0] for f in facts)
    tiles = total // LANES
    return pl.pallas_call(
        functools.partial(weigh_kernel, top, tok_rows),
        in_specs=[pl.BlockSpec(memory_space=pltpu.SMEM)] * 2
        + [pl.BlockSpec(memory_space=pltpu.VMEM)] * len(facts),
        out_specs=pl.BlockSpec(memory_space=pltpu.VMEM),
        out_shape=jax.ShapeDtypeStruct((total, LANES), F32),
        scratch_shapes=[
            pltpu.VMEM((total, LANES), BF16),
            pltpu.VMEM((2, tiles // 2, LANES, LANES), F32),
            pltpu.VMEM((2, tiles, LANES), F32),
        ],
        compiler_params=pltpu.CompilerParams(vmem_limit_bytes=24 * MIB),
        cost_estimate=pl.CostEstimate(flops=1, bytes_accessed=1, transcendentals=0),
    )(me, capacity, *facts)


def pack_kernel(*refs):
    rows = refs[0].shape[0]
    for k, ref in enumerate(refs[:-1]):
        refs[-1][k * rows : (k + 1) * rows, :] = ref[...]


def pack(blocks):
    rows, wide = blocks[0].shape
    return pl.pallas_call(
        pack_kernel,
        in_specs=[pl.BlockSpec(memory_space=pltpu.VMEM)] * len(blocks),
        out_specs=pl.BlockSpec(memory_space=pltpu.VMEM),
        out_shape=jax.ShapeDtypeStruct((len(blocks) * rows, wide), BF16),
        compiler_params=pltpu.CompilerParams(vmem_limit_bytes=24 * MIB),
        cost_estimate=pl.CostEstimate(flops=1, bytes_accessed=1, transcendentals=0),
    )(*blocks)


def combine_kernel(rows, sums, weighted, *refs):
    ins, outs = refs[: -len(sums)], refs[-len(sums) :]
    width = outs[0].shape[1]
    for lanes in range(0, width, 256):
        for terms, out in zip(sums, outs):
            total = None
            for which, first, place in terms:
                value = ins[which][first : first + rows, lanes : lanes + 256].astype(F32)
                if place is not None:
                    value = value * ins[weighted][place : place + rows, :1]
                total = value if total is None else total + value
            out[:, lanes : lanes + 256] = total.astype(BF16)


def combine(arrays, weights, sums):
    rows = weights.shape[0] // 16
    width = arrays[0].shape[1]
    sums = [[(a, b * rows, None if p is None else p * rows) for a, b, p in terms] for terms in sums]
    return pl.pallas_call(
        functools.partial(combine_kernel, rows, sums, len(arrays)),
        in_specs=[pl.BlockSpec(memory_space=pltpu.VMEM)] * (len(arrays) + 1),
        out_specs=[pl.BlockSpec(memory_space=pltpu.VMEM)] * len(sums),
        out_shape=[jax.ShapeDtypeStruct((rows, width), BF16)] * len(sums),
        compiler_params=pltpu.CompilerParams(vmem_limit_bytes=24 * MIB),
        cost_estimate=pl.CostEstimate(flops=1, bytes_accessed=1, transcendentals=0),
    )(*arrays, weights)


def load_kernel(*refs):
    count = len(refs) // 2
    sems = refs[-1]
    copies = [pltpu.make_async_copy(refs[k], refs[count + k], sems.at[k]) for k in range(count)]
    for copy in copies:
        copy.start()
    for copy in copies:
        copy.wait()


def load(*arrays):
    size = sum(a.size * 2 for a in arrays)
    return pl.pallas_call(
        load_kernel,
        in_specs=[pl.BlockSpec(memory_space=pl.ANY)] * len(arrays),
        out_specs=[pl.BlockSpec(memory_space=pltpu.VMEM)] * len(arrays),
        out_shape=[jax.ShapeDtypeStruct(a.shape, a.dtype) for a in arrays],
        scratch_shapes=[pltpu.SemaphoreType.DMA((len(arrays),))],
        compiler_params=pltpu.CompilerParams(vmem_limit_bytes=size + 4 * MIB),
    )(*arrays)


FF_TILE, OUT_TILE = 256, 512


def expert_kernel(*refs):
    x_refs, (gate_ref, up_ref, down_ref, out_ref, x, hidden) = refs[:-6], refs[-6:]
    width, ff = x.shape[1], hidden.shape[1]
    at = 0
    for ref in x_refs:
        x[at : at + ref.shape[0], :] = ref[:, :width]
        at += ref.shape[0]
    for k in range(ff // FF_TILE):
        lanes = slice(k * FF_TILE, (k + 1) * FF_TILE)
        gated = jnp.dot(x[...], gate_ref[0, :, lanes], preferred_element_type=F32)
        upward = jnp.dot(x[...], up_ref[0, :, lanes], preferred_element_type=F32)
        hidden[:, lanes] = (gated / (1.0 + jnp.exp(-gated)) * upward).astype(BF16)
    for k in range(width // OUT_TILE):
        lanes = slice(k * OUT_TILE, (k + 1) * OUT_TILE)
        out_ref[:, lanes] = jnp.dot(hidden[...], down_ref[0, :, lanes], preferred_element_type=F32).astype(BF16)


def expert(arrays, matrices):
    ff, width = matrices[2].shape[1:]
    rows = sum(a.shape[0] for a in arrays)
    held = rows * 2 * (width + ff) + 4 * rows * (2 * FF_TILE + OUT_TILE)
    return pl.pallas_call(
        expert_kernel,
        in_specs=[pl.BlockSpec(memory_space=pltpu.VMEM)] * (len(arrays) + 3),
        out_specs=pl.BlockSpec(memory_space=pltpu.VMEM),
        out_shape=jax.ShapeDtypeStruct((rows, width), BF16),
        scratch_shapes=[pltpu.VMEM((rows, width), BF16), pltpu.VMEM((rows, ff), BF16)],
        compiler_params=pltpu.CompilerParams(vmem_limit_bytes=held + 20 * MIB),
        cost_estimate=pl.CostEstimate(flops=1, bytes_accessed=1, transcendentals=0),
    )(*arrays, *matrices)


def orders(ep):
    bits = list(range(ep.bit_length() - 1))[::-1]
    return (bits, bits[:-2] + bits[:-3:-1])


def send(array, ep, flips):
    pairs = []
    for place in range(ep):
        for core, order in enumerate(orders(ep)):
            to = place
            for flip in flips:
                to ^= 1 << order[flip]
            pairs.append((2 * place + core, 2 * to + core))
    return lax.ppermute(array, ("ep", "sub"), pairs)


def cross(array):
    return lax.ppermute(array, "sub", [(0, 1), (1, 0)])


def add(*terms):
    return sum([t.astype(F32) for t in terms]).astype(BF16)


def on_device(ep, tokens, routes, gates, priority, capacity, w_gate, w_up, w_down):
    tok_rows, width = tokens.shape
    top = routes.shape[1]
    steps = ep.bit_length() - 1
    me = (lax.axis_index("ep") * 2 + lax.axis_index("sub")).astype(jnp.int32).reshape(1)
    held = prepare(me, tokens, routes, gates, priority)
    for step in range(steps - 3):
        held = jnp.concatenate([held, send(held, ep, [step])])
    base = held.shape[0]
    own1, own2, own4 = send(held, ep, [-3]), send(held, ep, [-2]), send(held, ep, [-1])
    first = cross(held)
    matrices = load(w_gate, w_up, w_down)
    own1, own2, own4, first, matrices = lax.optimization_barrier((own1, own2, own4, first, matrices))
    crossed = cross(pack([own1, own2, own4]))
    own3 = send(own1, ep, [-2])
    own5 = send(own1, ep, [-1])
    own6 = send(own2, ep, [-1])
    own7 = send(own3, ep, [-1])
    theirs = expert([first, crossed], matrices)
    own3, own5, own6, own7, theirs = lax.optimization_barrier((own3, own5, own6, own7, theirs))
    far = [own3, own5, own6, own7]
    far_crossed = cross(pack(far))
    far_made = expert(far, matrices)
    far_crossed, far_made = lax.optimization_barrier((far_crossed, far_made))
    far_back = cross(expert([far_crossed], matrices))
    near = [held, own1, own2, own4]
    weights = weigh(me, capacity, near + far + [first, crossed, far_crossed], top, tok_rows)

    def part(mine, back, block, place):
        return [(mine, block, place), (back, block, 8 + place)]

    send5, send6, send7 = combine(
        [far_made, far_back], weights, [part(0, 1, 1, 5), part(0, 1, 2, 6), part(0, 1, 3, 7)]
    )
    back7 = send(send7, ep, [-1])
    back5 = send(send5, ep, [-1])
    back6 = send(send6, ep, [-1])
    (send3,) = combine([far_made, far_back, back7], weights, [part(0, 1, 0, 4) + [(2, 0, None)]])
    back3 = send(send3, ep, [-2])
    near_made = expert(near, matrices)
    near_back = cross(theirs)
    send1, send2, send4 = combine(
        [near_made, near_back, back3, back5, back6],
        weights,
        [
            part(0, 1, 1, 1) + [(2, 0, None), (3, 0, None)],
            part(0, 1, 2, 2) + [(4, 0, None)],
            part(0, 1, 3, 3),
        ],
    )
    back1 = send(send1, ep, [-3])
    back2 = send(send2, ep, [-2])
    back4 = send(send4, ep, [-1])
    (total,) = combine(
        [near_made, near_back, back1, back2, back4],
        weights,
        [part(0, 1, 0, 0) + [(2, 0, None), (3, 0, None), (4, 0, None)]],
    )
    for step in range(steps - 3)[::-1]:
        half = total.shape[0] // 2
        total = add(total[:half], send(total[half:], ep, [step]))
    return total


def solution(mesh):
    in_specs = (
        P(("groups", "ep", "sub"), None),
        P(("groups", "ep", "sub"), None),
        P(("groups", "ep", "sub"), None),
        P(("groups", "ep", "sub")),
        P(),
        P(("ep", "sub"), None, None),
        P(("ep", "sub"), None, None),
        P(("ep", "sub"), None, None),
    )
    out_specs = P(("groups", "ep", "sub"), None)
    return jax.shard_map(
        functools.partial(on_device, mesh.shape["ep"]),
        mesh=mesh,
        in_specs=in_specs,
        out_specs=out_specs,
        check_vma=False,
    )
```

time: 90.4 us -> 77.3 us (0.86)
  starting transfers between devices: 24 us -> 16.4 us
  waiting for transfers between devices: 42.9 us -> 37.4 us
  other arithmetic: 1.56 us -> 0 us
  Pallas kernels: 15.9 us -> 17.3 us
    ppermute x15 -> x14, starting transfers between devices: 22.1 us -> 15.7 us  [send(): return lax.ppermute(array, ('ep', 'sub'), pairs)]
    ppermute x10 -> x5, waiting for transfers between devices: 3.43 us -> 0.39 us  [cross(): return lax.ppermute(array, 'sub', [(0, 1), (1, 0)])]
    ppermute x15 -> x14, waiting for transfers between devices: 39.5 us -> 37 us  [send(): return lax.ppermute(array, ('ep', 'sub'), pairs)]
    pallas_call x3 -> x8, Pallas kernels: 10.3 us -> 12.7 us  [the longest x4 10.5 us: expert(): pl.pallas_call(expert_kernel, in_specs=[pl.BlockSpec(memory_space=pltpu.V...]
    convert_element_type x4 -> x0, other arithmetic: 1.56 us -> none  [add(): return sum([t.astype(F32) for t in terms]).astype(BF16)]
    ppermute x10 -> x5, starting transfers between devices: 1.87 us -> 0.72 us  [cross(): return lax.ppermute(array, 'sub', [(0, 1), (1, 0)])]
    pallas_call x1, Pallas kernels: 2.86 us -> 1.89 us  [weigh(): pl.pallas_call(functools.partial(weigh_kernel, top, tok_rows), in_specs=[...]
  transfers between devices with their start and end apart: 25 -> 19, of which waited for: 14 -> 11; matrix products, arithmetic and copies ran while one was open for 0% -> 0% of each run, Pallas kernels for 12% -> 14%
where the time goes in v5:
time: 77.3 us; the launch traced here: 77 us
  waiting for transfers between devices  37.4 us (48%)
  Pallas kernels  17.3 us (22%)
  starting transfers between devices  16.4 us (21%)
  local copies, waits for them, and re-layouts  5.68 us (7%)
    ppermute x14, waiting for transfers between devices, send(): return lax.ppermute(array, ('ep', 'sub'), pairs)  37 us
    ppermute x14, starting transfers between devices, send(): return lax.ppermute(array, ('ep', 'sub'), pairs)  15.7 us
    pallas_call x4, Pallas kernels, expert(): pl.pallas_call(expert_kernel, in_specs=[pl.BlockSpec(memory_space=pltpu.V...  10.5 us
    unnamed x10, local copies, waits for them, and re-layouts  5.68 us
    pallas_call x4, Pallas kernels, combine(): pl.pallas_call(functools.partial(combine_kernel, rows, sums, len(arrays))...  2.17 us
    pallas_call x1, Pallas kernels, prepare(): pl.pallas_call(prepare_kernel, in_specs=[pl.BlockSpec(memory_space=pltpu....  1.97 us
    pallas_call x1, Pallas kernels, weigh(): pl.pallas_call(functools.partial(weigh_kernel, top, tok_rows), in_specs=[...  1.89 us
  transfers between devices with their start and end apart: 19, of which 11 were waited for; matrix products, arithmetic and copies ran while one was open for 0% of the time, Pallas kernels for 14%

profile of v5, /device:TPU:0, one launch (start us, length us, event | category | flops | bytes accessed | tf_op | source)
XLA Modules:
  0.0 77.0 jit_solution(18245776401301575371)
XLA Ops:
  0.0 2.0 %shard_map.82.refs_0_ = bf16[64,2176]{1,0:T(8,128)(2,1)} custom-call(s32[1]{0:T(128)} %bitcast.me_ref, bf16[64,2048]{1,0:T(8,128)(2,1)} %tokens_ref.1, s32[8,64]{1,0:T(8,128)} %bitcast.4, f32[8,64]{1,0:T(8,128)} %bitcast.5, s32[1,64]{1,0:T(1,128)} %bitcast.6), custom_call_target="tpu_custom_call" | custom-call | tf_op jit(solution)/shard_map/pallas_call | solution.py:52
  2.0 4.0 %collective-permute-start = (bf16[64,2176]{1,0:T(8,128)(2,1)}, bf16[64,2176]{1,0:T(8,128)(2,1)S(1)}, u32[]{:S(2)}, u32[]{:S(2)}) collective-permute-start(bf16[64,2176]{1,0:T(8,128)(2,1)} %shard_map.82.refs_0_), channel_id=1, source_target_pairs={{0,8},{1,9},{2,10},{3,11},{4,12},{5,13},{6,14},{7,15},{8,0},{9,1},... | collective-permute-start | bytes 835592 | tf_op jit(solution)/shard_map/ppermute | solution.py:250
  6.0 1.6 %collective-permute-start.1 = (bf16[64,2176]{1,0:T(8,128)(2,1)}, bf16[64,2176]{1,0:T(8,128)(2,1)S(1)}, u32[]{:S(2)}, u32[]{:S(2)}) collective-permute-start(bf16[64,2176]{1,0:T(8,128)(2,1)} %shard_map.82.refs_0_), channel_id=1, source_target_pairs={{0,4},{1,3},{2,6},{3,1},{4,0},{5,7},{6,2},{7,5},{8,12},{9,11},{10,... | collective-permute-start | bytes 835592 | tf_op jit(solution)/shard_map/ppermute | solution.py:250
  7.6 1.5 %collective-permute-start.2 = (bf16[64,2176]{1,0:T(8,128)(2,1)}, bf16[64,2176]{1,0:T(8,128)(2,1)S(1)}, u32[]{:S(2)}, u32[]{:S(2)}) collective-permute-start(bf16[64,2176]{1,0:T(8,128)(2,1)} %shard_map.82.refs_0_), channel_id=1, source_target_pairs={{0,2},{1,5},{2,0},{3,7},{4,6},{5,1},{6,4},{7,3},{8,10},{9,13},{10,... | collective-permute-start | bytes 835592 | tf_op jit(solution)/shard_map/ppermute | solution.py:250
  9.1 1.9 %copy-done = bf16[1,2048,768]{2,1,0:T(8,128)(2,1)S(1)} copy-done((bf16[1,2048,768]{2,1,0:T(8,128)(2,1)S(1)}, bf16[1,2048,768]{2,1,0:T(8,128)(2,1)}, u32[]{:S(2)}) %copy-start) | copy-done | bytes 3145752
  11.0 1.9 %copy-done.1 = bf16[1,2048,768]{2,1,0:T(8,128)(2,1)S(1)} copy-done((bf16[1,2048,768]{2,1,0:T(8,128)(2,1)S(1)}, bf16[1,2048,768]{2,1,0:T(8,128)(2,1)}, u32[]{:S(2)}) %copy-start.1) | copy-done | bytes 3145752
  12.9 1.9 %copy-done.2 = bf16[1,768,2048]{2,1,0:T(8,128)(2,1)S(1)} copy-done((bf16[1,768,2048]{2,1,0:T(8,128)(2,1)S(1)}, bf16[1,768,2048]{2,1,0:T(8,128)(2,1)}, u32[]{:S(2)}) %copy-start.2) | copy-done | bytes 3145752
  15.4 3.5 %collective-permute-done.refs_1_.refs_0_ = bf16[64,2176]{1,0:T(8,128)(2,1)S(1)} collective-permute-done((bf16[64,2176]{1,0:T(8,128)(2,1)}, bf16[64,2176]{1,0:T(8,128)(2,1)S(1)}, u32[]{:S(2)}, u32[]{:S(2)}) %collective-permute-start) | collective-permute-done | bytes 278560 | tf_op jit(solution)/shard_map/ppermute | solution.py:250
  19.0 1.4 %collective-permute-done.1.refs_2_.refs_1_ = bf16[64,2176]{1,0:T(8,128)(2,1)S(1)} collective-permute-done((bf16[64,2176]{1,0:T(8,128)(2,1)}, bf16[64,2176]{1,0:T(8,128)(2,1)S(1)}, u32[]{:S(2)}, u32[]{:S(2)}) %collective-permute-start.1) | collective-permute-done | bytes 278560 | tf_op jit(solution)/shard_map/ppermute | solution.py:250
  20.8 1.5 %collective-permute-start.5 = (bf16[64,2176]{1,0:T(8,128)(2,1)S(1)}, bf16[64,2176]{1,0:T(8,128)(2,1)S(1)}, u32[]{:S(2)}, u32[]{:S(2)}) collective-permute-start(bf16[64,2176]{1,0:T(8,128)(2,1)S(1)} %collective-permute-done.refs_1_.refs_0_), channel_id=1, source_target_pairs={{0,2},{1,5},{2,0},{3,7},{4,6},{5,1},{6,4},{7,3},{8,10},{9,13},{10,... | collective-permute-start | bytes 835592 | tf_op jit(solution)/shard_map/ppermute | solution.py:250
  22.9 7.2 %collective-permute-done.4.refs_0_.refs_4_ = bf16[64,2176]{1,0:T(8,128)(2,1)S(1)} collective-permute-done((bf16[64,2176]{1,0:T(8,128)(2,1)S(1)}, bf16[64,2176]{1,0:T(8,128)(2,1)S(1)}, u32[]{:S(2)}, u32[]{:S(2)}) %collective-permute-start.4) | collective-permute-done | bytes 278560 | tf_op jit(solution)/shard_map/ppermute | solution.py:250
  30.1 2.6 %shard_map.86 = bf16[256,2048]{1,0:T(8,128)(2,1)S(1)} custom-call(bf16[64,2176]{1,0:T(8,128)(2,1)S(1)} %collective-permute-done.3.refs_0_.refs_8_, bf16[192,2176]{1,0:T(8,128)(2,1)S(1)} %collective-permute-done.8.refs_1_.refs_9_, bf16[1,2048,768]{2,1,0:T(8,128)(2,1)S(1)} %get-tuple-element.34.refs_4_.refs_2_.refs_1_, ...), custom_call_target="tpu_custom_call" | custom-call | flops 1 | bytes 1 | tf_op jit(solution)/shard_map/pallas_call | solution.py:226
  32.8 3.9 %collective-permute-done.7.refs_3_.refs_7_ = bf16[64,2176]{1,0:T(8,128)(2,1)S(1)} collective-permute-done((bf16[64,2176]{1,0:T(8,128)(2,1)S(1)}, bf16[64,2176]{1,0:T(8,128)(2,1)S(1)}, u32[]{:S(2)}, u32[]{:S(2)}) %collective-permute-start.7) | collective-permute-done | bytes 278560 | tf_op jit(solution)/shard_map/ppermute | solution.py:250
  36.8 2.6 %shard_map.88.refs_0_ = bf16[256,2048]{1,0:T(8,128)(2,1)S(1)} custom-call(bf16[64,2176]{1,0:T(8,128)(2,1)S(1)} %collective-permute-done.4.refs_0_.refs_4_, bf16[64,2176]{1,0:T(8,128)(2,1)S(1)} %collective-permute-done.5.refs_1_.refs_5_, bf16[64,2176]{1,0:T(8,128)(2,1)S(1)} %collective-permute-done.6.refs_2_.refs_6_, ...), custom_call_target="tpu_custom_call" | custom-call | flops 1 | bytes 1 | tf_op jit(solution)/shard_map/pallas_call | solution.py:226
  39.6 2.6 %shard_map.89 = bf16[256,2048]{1,0:T(8,128)(2,1)S(1)} custom-call(bf16[256,2176]{1,0:T(8,128)(2,1)S(1)} %collective-permute-done.10.refs_0_.refs_10_, bf16[1,2048,768]{2,1,0:T(8,128)(2,1)S(1)} %get-tuple-element.34.refs_4_.refs_2_.refs_1_, bf16[1,2048,768]{2,1,0:T(8,128)(2,1)S(1)} %get-tuple-element.35.refs_5_.refs_3_.refs_2_, ...), custom_call_target="tpu_custom_call" | custom-call | flops 1 | bytes 1 | tf_op jit(solution)/shard_map/pallas_call | solution.py:226
  42.8 1.9 %shard_map.90.refs_2_.refs_3_.refs_5_ = f32[1024,128]{1,0:T(8,128)S(1)} custom-call(s32[1]{0:T(128)} %bitcast.me_ref, s32[16]{0:T(128)S(1)} %copy-done.4, bf16[64,2176]{1,0:T(8,128)(2,1)S(1)} %copy-done.3, bf16[64,2176]{1,0:T(8,128)(2,1)S(1)} %collective-permute-done.refs_1_.refs_0_, bf16[64,2176]{1,0:T(8,128)(2,1)S(1)} %collective-permute-done.1.refs_2_.refs_1_, ...), custom_call_target="tpu_custom_call" | custom-call | flops 1 | bytes 1 | tf_op jit(solution)/shard_map/pallas_call | solution.py:118
  45.5 2.0 %collective-permute-start.14 = (bf16[64,2048]{1,0:T(8,128)(2,1)S(1)}, bf16[64,2048]{1,0:T(8,128)(2,1)S(1)}, u32[]{:S(2)}, u32[]{:S(2)}) collective-permute-start(bf16[64,2048]{1,0:T(8,128)(2,1)S(1)} %get-tuple-element.46), channel_id=1, source_target_pairs={{0,2},{1,5},{2,0},{3,7},{4,6},{5,1},{6,4},{7,3},{8,10},{9,13},{10,... | collective-permute-start | bytes 786440 | tf_op jit(solution)/shard_map/ppermute | solution.py:250
  47.6 4.3 %collective-permute-done.12.refs_2_ = bf16[64,2048]{1,0:T(8,128)(2,1)S(1)} collective-permute-done((bf16[64,2048]{1,0:T(8,128)(2,1)S(1)}, bf16[64,2048]{1,0:T(8,128)(2,1)S(1)}, u32[]{:S(2)}, u32[]{:S(2)}) %collective-permute-start.12) | collective-permute-done | bytes 262176 | tf_op jit(solution)/shard_map/ppermute | solution.py:250
  52.2 2.6 %shard_map.84.refs_0_ = bf16[256,2048]{1,0:T(8,128)(2,1)S(1)} custom-call(bf16[64,2176]{1,0:T(8,128)(2,1)S(1)} %copy-done.3, bf16[64,2176]{1,0:T(8,128)(2,1)S(1)} %collective-permute-done.refs_1_.refs_0_, bf16[64,2176]{1,0:T(8,128)(2,1)S(1)} %collective-permute-done.1.refs_2_.refs_1_, bf16[64,2176]{1,0:T(8,128)(2,1)S(1)} %collective-permute-done.2.refs_3_.refs_2_, ...), custom_call_target="tpu_custom_call" | custom-call | flops 1 | bytes 1 | tf_op jit(solution)/shard_map/pallas_call | solution.py:226
  55.0 5.3 %collective-permute-done.15.refs_4_ = bf16[64,2048]{1,0:T(8,128)(2,1)S(1)} collective-permute-done((bf16[64,2048]{1,0:T(8,128)(2,1)S(1)}, bf16[64,2048]{1,0:T(8,128)(2,1)S(1)}, u32[]{:S(2)}, u32[]{:S(2)}) %collective-permute-start.15) | collective-permute-done | bytes 262176 | tf_op jit(solution)/shard_map/ppermute | solution.py:250
  61.4 2.3 %collective-permute-start.17 = (bf16[64,2048]{1,0:T(8,128)(2,1)S(1)}, bf16[64,2048]{1,0:T(8,128)(2,1)S(1)}, u32[]{:S(2)}, u32[]{:S(2)}) collective-permute-start(bf16[64,2048]{1,0:T(8,128)(2,1)S(1)} %get-tuple-element.49), channel_id=1, source_target_pairs={{0,4},{1,3},{2,6},{3,1},{4,0},{5,7},{6,2},{7,5},{8,12},{9,11},{10,... | collective-permute-start | bytes 786440 | tf_op jit(solution)/shard_map/ppermute | solution.py:250
  63.7 1.1 %collective-permute-start.18 = (bf16[64,2048]{1,0:T(8,128)(2,1)S(1)}, bf16[64,2048]{1,0:T(8,128)(2,1)S(1)}, u32[]{:S(2)}, u32[]{:S(2)}) collective-permute-start(bf16[64,2048]{1,0:T(8,128)(2,1)S(1)} %get-tuple-element.50), channel_id=1, source_target_pairs={{0,2},{1,5},{2,0},{3,7},{4,6},{5,1},{6,4},{7,3},{8,10},{9,13},{10,... | collective-permute-start | bytes 786440 | tf_op jit(solution)/shard_map/ppermute | solution.py:250
  64.8 10.2 %collective-permute-done.16.refs_2_ = bf16[64,2048]{1,0:T(8,128)(2,1)S(1)} collective-permute-done((bf16[64,2048]{1,0:T(8,128)(2,1)S(1)}, bf16[64,2048]{1,0:T(8,128)(2,1)S(1)}, u32[]{:S(2)}, u32[]{:S(2)}) %collective-permute-start.16) | collective-permute-done | bytes 262176 | tf_op jit(solution)/shard_map/ppermute | solution.py:250
  76.1 1.0 %shard_map.94 = bf16[64,2048]{1,0:T(8,128)(2,1)} custom-call(bf16[256,2048]{1,0:T(8,128)(2,1)S(1)} %shard_map.84.refs_0_, bf16[256,2048]{1,0:T(8,128)(2,1)S(1)} %collective-permute-done.9.refs_1_, bf16[64,2048]{1,0:T(8,128)(2,1)S(1)} %collective-permute-done.16.refs_2_, bf16[64,2048]{1,0:T(8,128)(2,1)S(1)} %collective-permute-done.17.refs_3_, ...), custom_call_target="tpu_custom_call" | custom-call | flops 1 | bytes 1 | tf_op jit(solution)/shard_map/pallas_call | solution.py:170
  (37 shorter events, 5.9 us)
Async XLA Ops:
  2.0 17.0 %collective-permute-start = (bf16[64,2176]{1,0:T(8,128)(2,1)}, bf16[64,2176]{1,0:T(8,128)(2,1)S(1)}, u32[]{:S(2)}, u32[]{:S(2)}) collective-permute-start(bf16[64,2176]{1,0:T(8,128)(2,1)} %shard_map.82.refs_0_), channel_id=1, source_target_pairs={{0,8},{1,9},{2,10},{3,11},{4,12},{5,13},{6,14},{7,15},{8,0},{9,1},... | collective-permute-start | bytes 835592 | tf_op jit(solution)/shard_map/ppermute | solution.py:250
  6.0 14.4 %collective-permute-start.1 = (bf16[64,2176]{1,0:T(8,128)(2,1)}, bf16[64,2176]{1,0:T(8,128)(2,1)S(1)}, u32[]{:S(2)}, u32[]{:S(2)}) collective-permute-start(bf16[64,2176]{1,0:T(8,128)(2,1)} %shard_map.82.refs_0_), channel_id=1, source_target_pairs={{0,4},{1,3},{2,6},{3,1},{4,0},{5,7},{6,2},{7,5},{8,12},{9,11},{10,... | collective-permute-start | bytes 835592 | tf_op jit(solution)/shard_map/ppermute | solution.py:250
  7.6 12.8 %collective-permute-start.2 = (bf16[64,2176]{1,0:T(8,128)(2,1)}, bf16[64,2176]{1,0:T(8,128)(2,1)S(1)}, u32[]{:S(2)}, u32[]{:S(2)}) collective-permute-start(bf16[64,2176]{1,0:T(8,128)(2,1)} %shard_map.82.refs_0_), channel_id=1, source_target_pairs={{0,2},{1,5},{2,0},{3,7},{4,6},{5,1},{6,4},{7,3},{8,10},{9,13},{10,... | collective-permute-start | bytes 835592 | tf_op jit(solution)/shard_map/ppermute | solution.py:250
  9.1 11.3 %collective-permute-start.3 = (bf16[64,2176]{1,0:T(8,128)(2,1)}, bf16[64,2176]{1,0:T(8,128)(2,1)S(1)}, u32[]{:S(2)}, u32[]{:S(2)}) collective-permute-start(bf16[64,2176]{1,0:T(8,128)(2,1)} %shard_map.82.refs_0_), channel_id=1, source_target_pairs={{0,1},{1,0},{2,3},{3,2},{4,5},{5,4},{6,7},{7,6},{8,9},{9,8},{10,11... | collective-permute-start | bytes 835592 | tf_op jit(solution)/shard_map/ppermute | solution.py:254
  9.1 1.9 %copy-start = (bf16[1,2048,768]{2,1,0:T(8,128)(2,1)S(1)}, bf16[1,2048,768]{2,1,0:T(8,128)(2,1)}, u32[]{:S(2)}) copy-start(bf16[1,2048,768]{2,1,0:T(8,128)(2,1)} %refs_0_.1) | copy-start | bytes 9437188
  11.0 1.9 %copy-start.1 = (bf16[1,2048,768]{2,1,0:T(8,128)(2,1)S(1)}, bf16[1,2048,768]{2,1,0:T(8,128)(2,1)}, u32[]{:S(2)}) copy-start(bf16[1,2048,768]{2,1,0:T(8,128)(2,1)} %refs_1_.1) | copy-start | bytes 9437188
  12.9 1.9 %copy-start.2 = (bf16[1,768,2048]{2,1,0:T(8,128)(2,1)S(1)}, bf16[1,768,2048]{2,1,0:T(8,128)(2,1)}, u32[]{:S(2)}) copy-start(bf16[1,768,2048]{2,1,0:T(8,128)(2,1)} %refs_2_.1) | copy-start | bytes 9437188
  20.4 9.7 %collective-permute-start.8 = (bf16[192,2176]{1,0:T(8,128)(2,1)S(1)}, bf16[192,2176]{1,0:T(8,128)(2,1)S(1)}, u32[]{:S(2)}, u32[]{:S(2)}) collective-permute-start(bf16[192,2176]{1,0:T(8,128)(2,1)S(1)} %shard_map.85), channel_id=1, source_target_pairs={{0,1},{1,0},{2,3},{3,2},{4,5},{5,4},{6,7},{7,6},{8,9},{9,8},{10,11... | collective-permute-start | bytes 2506760 | tf_op jit(solution)/shard_map/ppermute | solution.py:254
  20.5 9.6 %collective-permute-start.4 = (bf16[64,2176]{1,0:T(8,128)(2,1)S(1)}, bf16[64,2176]{1,0:T(8,128)(2,1)S(1)}, u32[]{:S(2)}, u32[]{:S(2)}) collective-permute-start(bf16[64,2176]{1,0:T(8,128)(2,1)S(1)} %collective-permute-done.refs_1_.refs_0_), channel_id=1, source_target_pairs={{0,4},{1,3},{2,6},{3,1},{4,0},{5,7},{6,2},{7,5},{8,12},{9,11},{10,... | collective-permute-start | bytes 835592 | tf_op jit(solution)/shard_map/ppermute | solution.py:250
  20.8 11.9 %collective-permute-start.5 = (bf16[64,2176]{1,0:T(8,128)(2,1)S(1)}, bf16[64,2176]{1,0:T(8,128)(2,1)S(1)}, u32[]{:S(2)}, u32[]{:S(2)}) collective-permute-start(bf16[64,2176]{1,0:T(8,128)(2,1)S(1)} %collective-permute-done.refs_1_.refs_0_), channel_id=1, source_target_pairs={{0,2},{1,5},{2,0},{3,7},{4,6},{5,1},{6,4},{7,3},{8,10},{9,13},{10,... | collective-permute-start | bytes 835592 | tf_op jit(solution)/shard_map/ppermute | solution.py:250
  22.4 10.4 %collective-permute-start.6 = (bf16[64,2176]{1,0:T(8,128)(2,1)S(1)}, bf16[64,2176]{1,0:T(8,128)(2,1)S(1)}, u32[]{:S(2)}, u32[]{:S(2)}) collective-permute-start(bf16[64,2176]{1,0:T(8,128)(2,1)S(1)} %collective-permute-done.1.refs_2_.refs_1_), channel_id=1, source_target_pairs={{0,2},{1,5},{2,0},{3,7},{4,6},{5,1},{6,4},{7,3},{8,10},{9,13},{10,... | collective-permute-start | bytes 835592 | tf_op jit(solution)/shard_map/ppermute | solution.py:250
  30.1 6.5 %collective-permute-start.7 = (bf16[64,2176]{1,0:T(8,128)(2,1)S(1)}, bf16[64,2176]{1,0:T(8,128)(2,1)S(1)}, u32[]{:S(2)}, u32[]{:S(2)}) collective-permute-start(bf16[64,2176]{1,0:T(8,128)(2,1)S(1)} %collective-permute-done.4.refs_0_.refs_4_), channel_id=1, source_target_pairs={{0,2},{1,5},{2,0},{3,7},{4,6},{5,1},{6,4},{7,3},{8,10},{9,13},{10,... | collective-permute-start | bytes 835592 | tf_op jit(solution)/shard_map/ppermute | solution.py:250
  36.8 2.8 %collective-permute-start.10 = (bf16[256,2176]{1,0:T(8,128)(2,1)S(1)}, bf16[256,2176]{1,0:T(8,128)(2,1)S(1)}, u32[]{:S(2)}, u32[]{:S(2)}) collective-permute-start(bf16[256,2176]{1,0:T(8,128)(2,1)S(1)} %shard_map.87), channel_id=1, source_target_pairs={{0,1},{1,0},{2,3},{3,2},{4,5},{5,4},{6,7},{7,6},{8,9},{9,8},{10,11... | collective-permute-start | bytes 3342344 | tf_op jit(solution)/shard_map/ppermute | solution.py:254
  39.5 3.3 %copy-start.3 = (bf16[64,2176]{1,0:T(8,128)(2,1)S(1)}, bf16[64,2176]{1,0:T(8,128)(2,1)}, u32[]{:S(2)}) copy-start(bf16[64,2176]{1,0:T(8,128)(2,1)} %shard_map.82.refs_0_) | copy-start | bytes 835588
  39.5 3.3 %copy-start.4 = (s32[16]{0:T(128)S(1)}, s32[16]{0:T(128)}, u32[]{:S(2)}) copy-start(s32[16]{0:T(128)} %capacity_ref.1) | copy-start | bytes 196
  42.2 2.8 %collective-permute-start.11 = (bf16[256,2048]{1,0:T(8,128)(2,1)S(1)}, bf16[256,2048]{1,0:T(8,128)(2,1)S(1)}, u32[]{:S(2)}, u32[]{:S(2)}) collective-permute-start(bf16[256,2048]{1,0:T(8,128)(2,1)S(1)} %shard_map.89), channel_id=1, source_target_pairs={{0,1},{1,0},{2,3},{3,2},{4,5},{5,4},{6,7},{7,6},{8,9},{9,8},{10,11... | collective-permute-start | bytes 3145736 | tf_op jit(solution)/shard_map/ppermute | solution.py:254
  42.7 12.1 %collective-permute-start.9 = (bf16[256,2048]{1,0:T(8,128)(2,1)S(1)}, bf16[256,2048]{1,0:T(8,128)(2,1)S(1)}, u32[]{:S(2)}, u32[]{:S(2)}) collective-permute-start(bf16[256,2048]{1,0:T(8,128)(2,1)S(1)} %shard_map.86), channel_id=1, source_target_pairs={{0,1},{1,0},{2,3},{3,2},{4,5},{5,4},{6,7},{7,6},{8,9},{9,8},{10,11... | collective-permute-start | bytes 3145736 | tf_op jit(solution)/shard_map/ppermute | solution.py:254
  45.4 6.4 %collective-permute-start.12 = (bf16[64,2048]{1,0:T(8,128)(2,1)S(1)}, bf16[64,2048]{1,0:T(8,128)(2,1)S(1)}, u32[]{:S(2)}, u32[]{:S(2)}) collective-permute-start(bf16[64,2048]{1,0:T(8,128)(2,1)S(1)} %get-tuple-element.45), channel_id=1, source_target_pairs={{0,2},{1,5},{2,0},{3,7},{4,6},{5,1},{6,4},{7,3},{8,10},{9,13},{10,... | collective-permute-start | bytes 786440 | tf_op jit(solution)/shard_map/ppermute | solution.py:250
  45.5 9.5 %collective-permute-start.14 = (bf16[64,2048]{1,0:T(8,128)(2,1)S(1)}, bf16[64,2048]{1,0:T(8,128)(2,1)S(1)}, u32[]{:S(2)}, u32[]{:S(2)}) collective-permute-start(bf16[64,2048]{1,0:T(8,128)(2,1)S(1)} %get-tuple-element.46), channel_id=1, source_target_pairs={{0,2},{1,5},{2,0},{3,7},{4,6},{5,1},{6,4},{7,3},{8,10},{9,13},{10,... | collective-permute-start | bytes 786440 | tf_op jit(solution)/shard_map/ppermute | solution.py:250
  47.5 12.8 %collective-permute-start.15 = (bf16[64,2048]{1,0:T(8,128)(2,1)S(1)}, bf16[64,2048]{1,0:T(8,128)(2,1)S(1)}, u32[]{:S(2)}, u32[]{:S(2)}) collective-permute-start(bf16[64,2048]{1,0:T(8,128)(2,1)S(1)} %get-tuple-element.47), channel_id=1, source_target_pairs={{0,2},{1,5},{2,0},{3,7},{4,6},{5,1},{6,4},{7,3},{8,10},{9,13},{10,... | collective-permute-start | bytes 786440 | tf_op jit(solution)/shard_map/ppermute | solution.py:250
  52.1 8.2 %collective-permute-start.13 = (bf16[64,2048]{1,0:T(8,128)(2,1)S(1)}, bf16[64,2048]{1,0:T(8,128)(2,1)S(1)}, u32[]{:S(2)}, u32[]{:S(2)}) collective-permute-start(bf16[64,2048]{1,0:T(8,128)(2,1)S(1)} %shard_map.92), channel_id=1, source_target_pairs={{0,4},{1,3},{2,6},{3,1},{4,0},{5,7},{6,2},{7,5},{8,12},{9,11},{10,... | collective-permute-start | bytes 786440 | tf_op jit(solution)/shard_map/ppermute | solution.py:250
  60.8 14.3 %collective-permute-start.16 = (bf16[64,2048]{1,0:T(8,128)(2,1)S(1)}, bf16[64,2048]{1,0:T(8,128)(2,1)S(1)}, u32[]{:S(2)}, u32[]{:S(2)}) collective-permute-start(bf16[64,2048]{1,0:T(8,128)(2,1)S(1)} %get-tuple-element.48), channel_id=1, source_target_pairs={{0,8},{1,9},{2,10},{3,11},{4,12},{5,13},{6,14},{7,15},{8,0},{9,1},... | collective-permute-start | bytes 786440 | tf_op jit(solution)/shard_map/ppermute | solution.py:250
  61.4 14.7 %collective-permute-start.17 = (bf16[64,2048]{1,0:T(8,128)(2,1)S(1)}, bf16[64,2048]{1,0:T(8,128)(2,1)S(1)}, u32[]{:S(2)}, u32[]{:S(2)}) collective-permute-start(bf16[64,2048]{1,0:T(8,128)(2,1)S(1)} %get-tuple-element.49), channel_id=1, source_target_pairs={{0,4},{1,3},{2,6},{3,1},{4,0},{5,7},{6,2},{7,5},{8,12},{9,11},{10,... | collective-permute-start | bytes 786440 | tf_op jit(solution)/shard_map/ppermute | solution.py:250
  63.7 12.4 %collective-permute-start.18 = (bf16[64,2048]{1,0:T(8,128)(2,1)S(1)}, bf16[64,2048]{1,0:T(8,128)(2,1)S(1)}, u32[]{:S(2)}, u32[]{:S(2)}) collective-permute-start(bf16[64,2048]{1,0:T(8,128)(2,1)S(1)} %get-tuple-element.50), channel_id=1, source_target_pairs={{0,2},{1,5},{2,0},{3,7},{4,6},{5,1},{6,4},{7,3},{8,10},{9,13},{10,... | collective-permute-start | bytes 786440 | tf_op jit(solution)/shard_map/ppermute | solution.py:250

commit v6 on v5

--- a/solution.py
+++ b/solution.py
@@ -160,10 +160,10 @@
                 if place is not None:
                     value = value * ins[weighted][place : place + rows, :1]
                 total = value if total is None else total + value
-            out[:, lanes : lanes + 256] = total.astype(BF16)
-
-
-def combine(arrays, weights, sums):
+            out[:, lanes : lanes + 256] = total.astype(out.dtype)
+
+
+def combine(arrays, weights, sums, kind=BF16):
     rows = weights.shape[0] // 16
     width = arrays[0].shape[1]
     sums = [[(a, b * rows, None if p is None else p * rows) for a, b, p in terms] for terms in sums]
@@ -171,7 +171,7 @@
         functools.partial(combine_kernel, rows, sums, len(arrays)),
         in_specs=[pl.BlockSpec(memory_space=pltpu.VMEM)] * (len(arrays) + 1),
         out_specs=[pl.BlockSpec(memory_space=pltpu.VMEM)] * len(sums),
-        out_shape=[jax.ShapeDtypeStruct((rows, width), BF16)] * len(sums),
+        out_shape=[jax.ShapeDtypeStruct((rows, width), kind)] * len(sums),
         compiler_params=pltpu.CompilerParams(vmem_limit_bytes=24 * MIB),
         cost_estimate=pl.CostEstimate(flops=1, bytes_accessed=1, transcendentals=0),
     )(*arrays, weights)
@@ -270,7 +270,7 @@
     own1, own2, own4 = send(held, ep, [-3]), send(held, ep, [-2]), send(held, ep, [-1])
     first = cross(held)
     matrices = load(w_gate, w_up, w_down)
-    own1, own2, own4, first, matrices = lax.optimization_barrier((own1, own2, own4, first, matrices))
+    own1, first, matrices = lax.optimization_barrier((own1, first, matrices))
     crossed = cross(pack([own1, own2, own4]))
     own3 = send(own1, ep, [-2])
     own5 = send(own1, ep, [-1])
@@ -289,33 +289,28 @@
     def part(mine, back, block, place):
         return [(mine, block, place), (back, block, 8 + place)]
 
-    send5, send6, send7 = combine(
-        [far_made, far_back], weights, [part(0, 1, 1, 5), part(0, 1, 2, 6), part(0, 1, 3, 7)]
-    )
+    send7, send5 = combine([far_made, far_back], weights, [part(0, 1, 3, 7), part(0, 1, 1, 5)])
     back7 = send(send7, ep, [-1])
     back5 = send(send5, ep, [-1])
+    send3, send6 = combine(
+        [far_made, far_back, back7], weights, [part(0, 1, 0, 4) + [(2, 0, None)], part(0, 1, 2, 6)]
+    )
+    back3 = send(send3, ep, [-2])
     back6 = send(send6, ep, [-1])
-    (send3,) = combine([far_made, far_back, back7], weights, [part(0, 1, 0, 4) + [(2, 0, None)]])
-    back3 = send(send3, ep, [-2])
     near_made = expert(near, matrices)
     near_back = cross(theirs)
-    send1, send2, send4 = combine(
-        [near_made, near_back, back3, back5, back6],
-        weights,
-        [
-            part(0, 1, 1, 1) + [(2, 0, None), (3, 0, None)],
-            part(0, 1, 2, 2) + [(4, 0, None)],
-            part(0, 1, 3, 3),
-        ],
+    near_made, back3, back5 = lax.optimization_barrier((near_made, back3, back5))
+    (send1,) = combine([near_made, near_back, back3, back5], weights, [part(0, 1, 1, 1) + [(2, 0, None), (3, 0, None)]])
+    back1 = send(send1, ep, [-3])
+    back6, send1 = lax.optimization_barrier((back6, send1))
+    send2, send4 = combine(
+        [near_made, near_back, back6], weights, [part(0, 1, 2, 2) + [(2, 0, None)], part(0, 1, 3, 3)]
     )
-    back1 = send(send1, ep, [-3])
     back2 = send(send2, ep, [-2])
     back4 = send(send4, ep, [-1])
-    (total,) = combine(
-        [near_made, near_back, back1, back2, back4],
-        weights,
-        [part(0, 1, 0, 0) + [(2, 0, None), (3, 0, None), (4, 0, None)]],
-    )
+    (total,) = combine([near_made, near_back, back1], weights, [part(0, 1, 0, 0) + [(2, 0, None)]], F32)
+    back2, back4, total = lax.optimization_barrier((back2, back4, total))
+    (total,) = combine([total, back2, back4], weights, [[(0, 0, None), (1, 0, None), (2, 0, None)]])
     for step in range(steps - 3)[::-1]:
         half = total.shape[0] // 2
         total = add(total[:half], send(total[half:], ep, [step]))

time: 77.3 us -> 76.5 us (0.990)
  waiting for transfers between devices: 37.4 us -> 31.4 us
  starting transfers between devices: 16.4 us -> 21.7 us
    ppermute x14, waiting for transfers between devices: 37 us -> 31 us  [send(): return lax.ppermute(array, ('ep', 'sub'), pairs)]
    ppermute x14, starting transfers between devices: 15.7 us -> 20.4 us  [send(): return lax.ppermute(array, ('ep', 'sub'), pairs)]
    pallas_call x4 -> x6, Pallas kernels: 2.17 us -> 2.26 us  [combine(): pl.pallas_call(functools.partial(combine_kernel, rows, sums, len(arrays))...]
  transfers between devices with their start and end apart: 19 -> 19, of which waited for: 11 -> 10; matrix products, arithmetic and copies ran while one was open for 0% -> 0% of each run, Pallas kernels for 14% -> 16%
where the time goes in v6:
time: 76.5 us; the launch traced here: 76.3 us
  waiting for transfers between devices  31.4 us (41%)
  starting transfers between devices  21.7 us (28%)
  Pallas kernels  17.4 us (23%)
  local copies, waits for them, and re-layouts  5.68 us (7%)
    ppermute x14, waiting for transfers between devices, send(): return lax.ppermute(array, ('ep', 'sub'), pairs)  31 us
    ppermute x14, starting transfers between devices, send(): return lax.ppermute(array, ('ep', 'sub'), pairs)  20.4 us
    pallas_call x4, Pallas kernels, expert(): pl.pallas_call(expert_kernel, in_specs=[pl.BlockSpec(memory_space=pltpu.V...  10.5 us
    unnamed x10, local copies, waits for them, and re-layouts  5.68 us
    pallas_call x6, Pallas kernels, combine(): pl.pallas_call(functools.partial(combine_kernel, rows, sums, len(arrays))...  2.26 us
    pallas_call x1, Pallas kernels, prepare(): pl.pallas_call(prepare_kernel, in_specs=[pl.BlockSpec(memory_space=pltpu....  1.98 us
    pallas_call x1, Pallas kernels, weigh(): pl.pallas_call(functools.partial(weigh_kernel, top, tok_rows), in_specs=[...  1.89 us
  transfers between devices with their start and end apart: 19, of which 10 were waited for; matrix products, arithmetic and copies ran while one was open for 0% of the time, Pallas kernels for 16%

profile of v6, /device:TPU:0, one launch (start us, length us, event | category | flops | bytes accessed | tf_op | source)
XLA Modules:
  0.0 76.3 jit_solution(1311342267250124950)
XLA Ops:
  0.0 2.0 %shard_map.82.refs_0_ = bf16[64,2176]{1,0:T(8,128)(2,1)} custom-call(s32[1]{0:T(128)} %bitcast.me_ref, bf16[64,2048]{1,0:T(8,128)(2,1)} %tokens_ref.1, s32[8,64]{1,0:T(8,128)} %bitcast.4, f32[8,64]{1,0:T(8,128)} %bitcast.5, s32[1,64]{1,0:T(1,128)} %bitcast.6), custom_call_target="tpu_custom_call" | custom-call | tf_op jit(solution)/shard_map/pallas_call | solution.py:52
  2.0 4.0 %collective-permute-start = (bf16[64,2176]{1,0:T(8,128)(2,1)}, bf16[64,2176]{1,0:T(8,128)(2,1)S(1)}, u32[]{:S(2)}, u32[]{:S(2)}) collective-permute-start(bf16[64,2176]{1,0:T(8,128)(2,1)} %shard_map.82.refs_0_), channel_id=1, source_target_pairs={{0,8},{1,9},{2,10},{3,11},{4,12},{5,13},{6,14},{7,15},{8,0},{9,1},... | collective-permute-start | bytes 835592 | tf_op jit(solution)/shard_map/ppermute | solution.py:250
  6.0 1.6 %collective-permute-start.2 = (bf16[64,2176]{1,0:T(8,128)(2,1)}, bf16[64,2176]{1,0:T(8,128)(2,1)S(1)}, u32[]{:S(2)}, u32[]{:S(2)}) collective-permute-start(bf16[64,2176]{1,0:T(8,128)(2,1)} %shard_map.82.refs_0_), channel_id=1, source_target_pairs={{0,4},{1,3},{2,6},{3,1},{4,0},{5,7},{6,2},{7,5},{8,12},{9,11},{10,... | collective-permute-start | bytes 835592 | tf_op jit(solution)/shard_map/ppermute | solution.py:250
  7.6 1.5 %collective-permute-start.3 = (bf16[64,2176]{1,0:T(8,128)(2,1)}, bf16[64,2176]{1,0:T(8,128)(2,1)S(1)}, u32[]{:S(2)}, u32[]{:S(2)}) collective-permute-start(bf16[64,2176]{1,0:T(8,128)(2,1)} %shard_map.82.refs_0_), channel_id=1, source_target_pairs={{0,2},{1,5},{2,0},{3,7},{4,6},{5,1},{6,4},{7,3},{8,10},{9,13},{10,... | collective-permute-start | bytes 835592 | tf_op jit(solution)/shard_map/ppermute | solution.py:250
  9.1 1.9 %copy-done = bf16[1,2048,768]{2,1,0:T(8,128)(2,1)S(1)} copy-done((bf16[1,2048,768]{2,1,0:T(8,128)(2,1)S(1)}, bf16[1,2048,768]{2,1,0:T(8,128)(2,1)}, u32[]{:S(2)}) %copy-start) | copy-done | bytes 3145752
  11.0 1.9 %copy-done.1 = bf16[1,2048,768]{2,1,0:T(8,128)(2,1)S(1)} copy-done((bf16[1,2048,768]{2,1,0:T(8,128)(2,1)S(1)}, bf16[1,2048,768]{2,1,0:T(8,128)(2,1)}, u32[]{:S(2)}) %copy-start.1) | copy-done | bytes 3145752
  12.9 1.9 %copy-done.2 = bf16[1,768,2048]{2,1,0:T(8,128)(2,1)S(1)} copy-done((bf16[1,768,2048]{2,1,0:T(8,128)(2,1)S(1)}, bf16[1,768,2048]{2,1,0:T(8,128)(2,1)}, u32[]{:S(2)}) %copy-start.2) | copy-done | bytes 3145752
  15.5 3.5 %collective-permute-done.refs_1_.refs_0_ = bf16[64,2176]{1,0:T(8,128)(2,1)S(1)} collective-permute-done((bf16[64,2176]{1,0:T(8,128)(2,1)}, bf16[64,2176]{1,0:T(8,128)(2,1)S(1)}, u32[]{:S(2)}, u32[]{:S(2)}) %collective-permute-start) | collective-permute-done | bytes 278560 | tf_op jit(solution)/shard_map/ppermute | solution.py:250
  20.8 1.5 %collective-permute-start.5 = (bf16[64,2176]{1,0:T(8,128)(2,1)S(1)}, bf16[64,2176]{1,0:T(8,128)(2,1)S(1)}, u32[]{:S(2)}, u32[]{:S(2)}) collective-permute-start(bf16[64,2176]{1,0:T(8,128)(2,1)S(1)} %collective-permute-done.refs_1_.refs_0_), channel_id=1, source_target_pairs={{0,2},{1,5},{2,0},{3,7},{4,6},{5,1},{6,4},{7,3},{8,10},{9,13},{10,... | collective-permute-start | bytes 835592 | tf_op jit(solution)/shard_map/ppermute | solution.py:250
  22.9 6.4 %collective-permute-done.4.refs_0_.refs_4_ = bf16[64,2176]{1,0:T(8,128)(2,1)S(1)} collective-permute-done((bf16[64,2176]{1,0:T(8,128)(2,1)S(1)}, bf16[64,2176]{1,0:T(8,128)(2,1)S(1)}, u32[]{:S(2)}, u32[]{:S(2)}) %collective-permute-start.4) | collective-permute-done | bytes 278560 | tf_op jit(solution)/shard_map/ppermute | solution.py:250
  29.3 2.3 %collective-permute-start.7 = (bf16[64,2176]{1,0:T(8,128)(2,1)S(1)}, bf16[64,2176]{1,0:T(8,128)(2,1)S(1)}, u32[]{:S(2)}, u32[]{:S(2)}) collective-permute-start(bf16[64,2176]{1,0:T(8,128)(2,1)S(1)} %collective-permute-done.4.refs_0_.refs_4_), channel_id=1, source_target_pairs={{0,2},{1,5},{2,0},{3,7},{4,6},{5,1},{6,4},{7,3},{8,10},{9,13},{10,... | collective-permute-start | bytes 835592 | tf_op jit(solution)/shard_map/ppermute | solution.py:250
  31.6 2.6 %shard_map.86 = bf16[256,2048]{1,0:T(8,128)(2,1)S(1)} custom-call(bf16[64,2176]{1,0:T(8,128)(2,1)S(1)} %collective-permute-done.1.refs_0_.refs_8_, bf16[192,2176]{1,0:T(8,128)(2,1)S(1)} %collective-permute-done.8.refs_1_.refs_9_, bf16[1,2048,768]{2,1,0:T(8,128)(2,1)S(1)} %get-tuple-element.37.refs_4_.refs_2_.refs_1_, ...), custom_call_target="tpu_custom_call" | custom-call | flops 1 | bytes 1 | tf_op jit(solution)/shard_map/pallas_call | solution.py:226
  34.3 1.8 %collective-permute-done.7.refs_3_.refs_7_ = bf16[64,2176]{1,0:T(8,128)(2,1)S(1)} collective-permute-done((bf16[64,2176]{1,0:T(8,128)(2,1)S(1)}, bf16[64,2176]{1,0:T(8,128)(2,1)S(1)}, u32[]{:S(2)}, u32[]{:S(2)}) %collective-permute-start.7) | collective-permute-done | bytes 278560 | tf_op jit(solution)/shard_map/ppermute | solution.py:250
  36.3 2.6 %shard_map.88.refs_0_ = bf16[256,2048]{1,0:T(8,128)(2,1)S(1)} custom-call(bf16[64,2176]{1,0:T(8,128)(2,1)S(1)} %collective-permute-done.4.refs_0_.refs_4_, bf16[64,2176]{1,0:T(8,128)(2,1)S(1)} %collective-permute-done.5.refs_1_.refs_5_, bf16[64,2176]{1,0:T(8,128)(2,1)S(1)} %collective-permute-done.6.refs_2_.refs_6_, ...), custom_call_target="tpu_custom_call" | custom-call | flops 1 | bytes 1 | tf_op jit(solution)/shard_map/pallas_call | solution.py:226
  39.0 2.6 %shard_map.89 = bf16[256,2048]{1,0:T(8,128)(2,1)S(1)} custom-call(bf16[256,2176]{1,0:T(8,128)(2,1)S(1)} %collective-permute-done.9.refs_0_.refs_10_, bf16[1,2048,768]{2,1,0:T(8,128)(2,1)S(1)} %get-tuple-element.37.refs_4_.refs_2_.refs_1_, bf16[1,2048,768]{2,1,0:T(8,128)(2,1)S(1)} %get-tuple-element.38.refs_5_.refs_3_.refs_2_, ...), custom_call_target="tpu_custom_call" | custom-call | flops 1 | bytes 1 | tf_op jit(solution)/shard_map/pallas_call | solution.py:226
  42.2 1.9 %shard_map.90.refs_2_.refs_3_.refs_4_ = f32[1024,128]{1,0:T(8,128)S(1)} custom-call(s32[1]{0:T(128)} %bitcast.me_ref, s32[16]{0:T(128)S(1)} %copy-done.4, bf16[64,2176]{1,0:T(8,128)(2,1)S(1)} %copy-done.3, bf16[64,2176]{1,0:T(8,128)(2,1)S(1)} %collective-permute-done.refs_1_.refs_0_, bf16[64,2176]{1,0:T(8,128)(2,1)S(1)} %collective-permute-done.2.refs_2_.refs_1_, ...), custom_call_target="tpu_custom_call" | custom-call | flops 1 | bytes 1 | tf_op jit(solution)/shard_map/pallas_call | solution.py:118
  44.7 2.1 %collective-permute-start.11 = (bf16[64,2048]{1,0:T(8,128)(2,1)S(1)}, bf16[64,2048]{1,0:T(8,128)(2,1)S(1)}, u32[]{:S(2)}, u32[]{:S(2)}) collective-permute-start(bf16[64,2048]{1,0:T(8,128)(2,1)S(1)} %get-tuple-element.47), channel_id=1, source_target_pairs={{0,2},{1,5},{2,0},{3,7},{4,6},{5,1},{6,4},{7,3},{8,10},{9,13},{10,... | collective-permute-start | bytes 786440 | tf_op jit(solution)/shard_map/ppermute | solution.py:250
  46.9 4.3 %collective-permute-done.11.refs_2_ = bf16[64,2048]{1,0:T(8,128)(2,1)S(1)} collective-permute-done((bf16[64,2048]{1,0:T(8,128)(2,1)S(1)}, bf16[64,2048]{1,0:T(8,128)(2,1)S(1)}, u32[]{:S(2)}, u32[]{:S(2)}) %collective-permute-start.11) | collective-permute-done | bytes 262176 | tf_op jit(solution)/shard_map/ppermute | solution.py:250
  51.9 2.0 %collective-permute-start.15 = (bf16[64,2048]{1,0:T(8,128)(2,1)S(1)}, bf16[64,2048]{1,0:T(8,128)(2,1)S(1)}, u32[]{:S(2)}, u32[]{:S(2)}) collective-permute-start(bf16[64,2048]{1,0:T(8,128)(2,1)S(1)} %get-tuple-element.52), channel_id=1, source_target_pairs={{0,2},{1,5},{2,0},{3,7},{4,6},{5,1},{6,4},{7,3},{8,10},{9,13},{10,... | collective-permute-start | bytes 786440 | tf_op jit(solution)/shard_map/ppermute | solution.py:250
  53.9 2.6 %shard_map.84.refs_0_ = bf16[256,2048]{1,0:T(8,128)(2,1)S(1)} custom-call(bf16[64,2176]{1,0:T(8,128)(2,1)S(1)} %copy-done.3, bf16[64,2176]{1,0:T(8,128)(2,1)S(1)} %collective-permute-done.refs_1_.refs_0_, bf16[64,2176]{1,0:T(8,128)(2,1)S(1)} %collective-permute-done.2.refs_2_.refs_1_, bf16[64,2176]{1,0:T(8,128)(2,1)S(1)} %collective-permute-done.3.refs_3_.refs_2_, ...), custom_call_target="tpu_custom_call" | custom-call | flops 1 | bytes 1 | tf_op jit(solution)/shard_map/pallas_call | solution.py:226
  56.6 3.9 %collective-permute-done.12.refs_2_ = bf16[64,2048]{1,0:T(8,128)(2,1)S(1)} collective-permute-done((bf16[64,2048]{1,0:T(8,128)(2,1)S(1)}, bf16[64,2048]{1,0:T(8,128)(2,1)S(1)}, u32[]{:S(2)}, u32[]{:S(2)}) %collective-permute-start.12) | collective-permute-done | bytes 262176 | tf_op jit(solution)/shard_map/ppermute | solution.py:250
  62.0 2.2 %collective-permute-start.16 = (bf16[64,2048]{1,0:T(8,128)(2,1)S(1)}, bf16[64,2048]{1,0:T(8,128)(2,1)S(1)}, u32[]{:S(2)}, u32[]{:S(2)}) collective-permute-start(bf16[64,2048]{1,0:T(8,128)(2,1)S(1)} %get-tuple-element.56), channel_id=1, source_target_pairs={{0,4},{1,3},{2,6},{3,1},{4,0},{5,7},{6,2},{7,5},{8,12},{9,11},{10,... | collective-permute-start | bytes 786440 | tf_op jit(solution)/shard_map/ppermute | solution.py:250
  65.1 8.1 %collective-permute-done.18.refs_2_ = bf16[64,2048]{1,0:T(8,128)(2,1)S(1)} collective-permute-done((bf16[64,2048]{1,0:T(8,128)(2,1)S(1)}, bf16[64,2048]{1,0:T(8,128)(2,1)S(1)}, u32[]{:S(2)}, u32[]{:S(2)}) %collective-permute-start.18) | collective-permute-done | bytes 262176 | tf_op jit(solution)/shard_map/ppermute | solution.py:250
  73.5 2.0 %collective-permute-done.16.refs_1_ = bf16[64,2048]{1,0:T(8,128)(2,1)S(1)} collective-permute-done((bf16[64,2048]{1,0:T(8,128)(2,1)S(1)}, bf16[64,2048]{1,0:T(8,128)(2,1)S(1)}, u32[]{:S(2)}, u32[]{:S(2)}) %collective-permute-start.16) | collective-permute-done | bytes 262176 | tf_op jit(solution)/shard_map/ppermute | solution.py:250
  (39 shorter events, 8.8 us)
Async XLA Ops:
  2.0 17.0 %collective-permute-start = (bf16[64,2176]{1,0:T(8,128)(2,1)}, bf16[64,2176]{1,0:T(8,128)(2,1)S(1)}, u32[]{:S(2)}, u32[]{:S(2)}) collective-permute-start(bf16[64,2176]{1,0:T(8,128)(2,1)} %shard_map.82.refs_0_), channel_id=1, source_target_pairs={{0,8},{1,9},{2,10},{3,11},{4,12},{5,13},{6,14},{7,15},{8,0},{9,1},... | collective-permute-start | bytes 835592 | tf_op jit(solution)/shard_map/ppermute | solution.py:250
  6.0 12.9 %collective-permute-start.1 = (bf16[64,2176]{1,0:T(8,128)(2,1)}, bf16[64,2176]{1,0:T(8,128)(2,1)S(1)}, u32[]{:S(2)}, u32[]{:S(2)}) collective-permute-start(bf16[64,2176]{1,0:T(8,128)(2,1)} %shard_map.82.refs_0_), channel_id=1, source_target_pairs={{0,1},{1,0},{2,3},{3,2},{4,5},{5,4},{6,7},{7,6},{8,9},{9,8},{10,11... | collective-permute-start | bytes 835592 | tf_op jit(solution)/shard_map/ppermute | solution.py:254
  6.0 13.8 %collective-permute-start.2 = (bf16[64,2176]{1,0:T(8,128)(2,1)}, bf16[64,2176]{1,0:T(8,128)(2,1)S(1)}, u32[]{:S(2)}, u32[]{:S(2)}) collective-permute-start(bf16[64,2176]{1,0:T(8,128)(2,1)} %shard_map.82.refs_0_), channel_id=1, source_target_pairs={{0,4},{1,3},{2,6},{3,1},{4,0},{5,7},{6,2},{7,5},{8,12},{9,11},{10,... | collective-permute-start | bytes 835592 | tf_op jit(solution)/shard_map/ppermute | solution.py:250
  7.6 12.2 %collective-permute-start.3 = (bf16[64,2176]{1,0:T(8,128)(2,1)}, bf16[64,2176]{1,0:T(8,128)(2,1)S(1)}, u32[]{:S(2)}, u32[]{:S(2)}) collective-permute-start(bf16[64,2176]{1,0:T(8,128)(2,1)} %shard_map.82.refs_0_), channel_id=1, source_target_pairs={{0,2},{1,5},{2,0},{3,7},{4,6},{5,1},{6,4},{7,3},{8,10},{9,13},{10,... | collective-permute-start | bytes 835592 | tf_op jit(solution)/shard_map/ppermute | solution.py:250
  9.1 1.9 %copy-start = (bf16[1,2048,768]{2,1,0:T(8,128)(2,1)S(1)}, bf16[1,2048,768]{2,1,0:T(8,128)(2,1)}, u32[]{:S(2)}) copy-start(bf16[1,2048,768]{2,1,0:T(8,128)(2,1)} %refs_0_.1) | copy-start | bytes 9437188
  11.0 1.9 %copy-start.1 = (bf16[1,2048,768]{2,1,0:T(8,128)(2,1)S(1)}, bf16[1,2048,768]{2,1,0:T(8,128)(2,1)}, u32[]{:S(2)}) copy-start(bf16[1,2048,768]{2,1,0:T(8,128)(2,1)} %refs_1_.1) | copy-start | bytes 9437188
  12.9 1.9 %copy-start.2 = (bf16[1,768,2048]{2,1,0:T(8,128)(2,1)S(1)}, bf16[1,768,2048]{2,1,0:T(8,128)(2,1)}, u32[]{:S(2)}) copy-start(bf16[1,768,2048]{2,1,0:T(8,128)(2,1)} %refs_2_.1) | copy-start | bytes 9437188
  19.9 11.7 %collective-permute-start.8 = (bf16[192,2176]{1,0:T(8,128)(2,1)S(1)}, bf16[192,2176]{1,0:T(8,128)(2,1)S(1)}, u32[]{:S(2)}, u32[]{:S(2)}) collective-permute-start(bf16[192,2176]{1,0:T(8,128)(2,1)S(1)} %shard_map.85), channel_id=1, source_target_pairs={{0,1},{1,0},{2,3},{3,2},{4,5},{5,4},{6,7},{7,6},{8,9},{9,8},{10,11... | collective-permute-start | bytes 2506760 | tf_op jit(solution)/shard_map/ppermute | solution.py:254
  20.5 8.8 %collective-permute-start.4 = (bf16[64,2176]{1,0:T(8,128)(2,1)S(1)}, bf16[64,2176]{1,0:T(8,128)(2,1)S(1)}, u32[]{:S(2)}, u32[]{:S(2)}) collective-permute-start(bf16[64,2176]{1,0:T(8,128)(2,1)S(1)} %collective-permute-done.refs_1_.refs_0_), channel_id=1, source_target_pairs={{0,4},{1,3},{2,6},{3,1},{4,0},{5,7},{6,2},{7,5},{8,12},{9,11},{10,... | collective-permute-start | bytes 835592 | tf_op jit(solution)/shard_map/ppermute | solution.py:250
  20.8 13.4 %collective-permute-start.5 = (bf16[64,2176]{1,0:T(8,128)(2,1)S(1)}, bf16[64,2176]{1,0:T(8,128)(2,1)S(1)}, u32[]{:S(2)}, u32[]{:S(2)}) collective-permute-start(bf16[64,2176]{1,0:T(8,128)(2,1)S(1)} %collective-permute-done.refs_1_.refs_0_), channel_id=1, source_target_pairs={{0,2},{1,5},{2,0},{3,7},{4,6},{5,1},{6,4},{7,3},{8,10},{9,13},{10,... | collective-permute-start | bytes 835592 | tf_op jit(solution)/shard_map/ppermute | solution.py:250
  22.4 11.9 %collective-permute-start.6 = (bf16[64,2176]{1,0:T(8,128)(2,1)S(1)}, bf16[64,2176]{1,0:T(8,128)(2,1)S(1)}, u32[]{:S(2)}, u32[]{:S(2)}) collective-permute-start(bf16[64,2176]{1,0:T(8,128)(2,1)S(1)} %collective-permute-done.2.refs_2_.refs_1_), channel_id=1, source_target_pairs={{0,2},{1,5},{2,0},{3,7},{4,6},{5,1},{6,4},{7,3},{8,10},{9,13},{10,... | collective-permute-start | bytes 835592 | tf_op jit(solution)/shard_map/ppermute | solution.py:250
  29.3 6.8 %collective-permute-start.7 = (bf16[64,2176]{1,0:T(8,128)(2,1)S(1)}, bf16[64,2176]{1,0:T(8,128)(2,1)S(1)}, u32[]{:S(2)}, u32[]{:S(2)}) collective-permute-start(bf16[64,2176]{1,0:T(8,128)(2,1)S(1)} %collective-permute-done.4.refs_0_.refs_4_), channel_id=1, source_target_pairs={{0,2},{1,5},{2,0},{3,7},{4,6},{5,1},{6,4},{7,3},{8,10},{9,13},{10,... | collective-permute-start | bytes 835592 | tf_op jit(solution)/shard_map/ppermute | solution.py:250
  36.2 2.8 %collective-permute-start.9 = (bf16[256,2176]{1,0:T(8,128)(2,1)S(1)}, bf16[256,2176]{1,0:T(8,128)(2,1)S(1)}, u32[]{:S(2)}, u32[]{:S(2)}) collective-permute-start(bf16[256,2176]{1,0:T(8,128)(2,1)S(1)} %shard_map.87), channel_id=1, source_target_pairs={{0,1},{1,0},{2,3},{3,2},{4,5},{5,4},{6,7},{7,6},{8,9},{9,8},{10,11... | collective-permute-start | bytes 3342344 | tf_op jit(solution)/shard_map/ppermute | solution.py:254
  38.9 3.3 %copy-start.3 = (bf16[64,2176]{1,0:T(8,128)(2,1)S(1)}, bf16[64,2176]{1,0:T(8,128)(2,1)}, u32[]{:S(2)}) copy-start(bf16[64,2176]{1,0:T(8,128)(2,1)} %shard_map.82.refs_0_) | copy-start | bytes 835588
  38.9 3.3 %copy-start.4 = (s32[16]{0:T(128)S(1)}, s32[16]{0:T(128)}, u32[]{:S(2)}) copy-start(s32[16]{0:T(128)} %capacity_ref.1) | copy-start | bytes 196
  41.6 2.8 %collective-permute-start.10 = (bf16[256,2048]{1,0:T(8,128)(2,1)S(1)}, bf16[256,2048]{1,0:T(8,128)(2,1)S(1)}, u32[]{:S(2)}, u32[]{:S(2)}) collective-permute-start(bf16[256,2048]{1,0:T(8,128)(2,1)S(1)} %shard_map.89), channel_id=1, source_target_pairs={{0,1},{1,0},{2,3},{3,2},{4,5},{5,4},{6,7},{7,6},{8,9},{9,8},{10,11... | collective-permute-start | bytes 3145736 | tf_op jit(solution)/shard_map/ppermute | solution.py:254
  42.1 18.4 %collective-permute-start.14 = (bf16[256,2048]{1,0:T(8,128)(2,1)S(1)}, bf16[256,2048]{1,0:T(8,128)(2,1)S(1)}, u32[]{:S(2)}, u32[]{:S(2)}) collective-permute-start(bf16[256,2048]{1,0:T(8,128)(2,1)S(1)} %shard_map.86), channel_id=1, source_target_pairs={{0,1},{1,0},{2,3},{3,2},{4,5},{5,4},{6,7},{7,6},{8,9},{9,8},{10,11... | collective-permute-start | bytes 3145736 | tf_op jit(solution)/shard_map/ppermute | solution.py:254
  44.7 6.4 %collective-permute-start.11 = (bf16[64,2048]{1,0:T(8,128)(2,1)S(1)}, bf16[64,2048]{1,0:T(8,128)(2,1)S(1)}, u32[]{:S(2)}, u32[]{:S(2)}) collective-permute-start(bf16[64,2048]{1,0:T(8,128)(2,1)S(1)} %get-tuple-element.47), channel_id=1, source_target_pairs={{0,2},{1,5},{2,0},{3,7},{4,6},{5,1},{6,4},{7,3},{8,10},{9,13},{10,... | collective-permute-start | bytes 786440 | tf_op jit(solution)/shard_map/ppermute | solution.py:250
  46.8 9.7 %collective-permute-start.13 = (bf16[64,2048]{1,0:T(8,128)(2,1)S(1)}, bf16[64,2048]{1,0:T(8,128)(2,1)S(1)}, u32[]{:S(2)}, u32[]{:S(2)}) collective-permute-start(bf16[64,2048]{1,0:T(8,128)(2,1)S(1)} %get-tuple-element.49), channel_id=1, source_target_pairs={{0,2},{1,5},{2,0},{3,7},{4,6},{5,1},{6,4},{7,3},{8,10},{9,13},{10,... | collective-permute-start | bytes 786440 | tf_op jit(solution)/shard_map/ppermute | solution.py:250
  51.5 9.0 %collective-permute-start.12 = (bf16[64,2048]{1,0:T(8,128)(2,1)S(1)}, bf16[64,2048]{1,0:T(8,128)(2,1)S(1)}, u32[]{:S(2)}, u32[]{:S(2)}) collective-permute-start(bf16[64,2048]{1,0:T(8,128)(2,1)S(1)} %get-tuple-element.48), channel_id=1, source_target_pairs={{0,4},{1,3},{2,6},{3,1},{4,0},{5,7},{6,2},{7,5},{8,12},{9,11},{10,... | collective-permute-start | bytes 786440 | tf_op jit(solution)/shard_map/ppermute | solution.py:250
  51.9 9.8 %collective-permute-start.15 = (bf16[64,2048]{1,0:T(8,128)(2,1)S(1)}, bf16[64,2048]{1,0:T(8,128)(2,1)S(1)}, u32[]{:S(2)}, u32[]{:S(2)}) collective-permute-start(bf16[64,2048]{1,0:T(8,128)(2,1)S(1)} %get-tuple-element.52), channel_id=1, source_target_pairs={{0,2},{1,5},{2,0},{3,7},{4,6},{5,1},{6,4},{7,3},{8,10},{9,13},{10,... | collective-permute-start | bytes 786440 | tf_op jit(solution)/shard_map/ppermute | solution.py:250
  60.7 12.5 %collective-permute-start.18 = (bf16[64,2048]{1,0:T(8,128)(2,1)S(1)}, bf16[64,2048]{1,0:T(8,128)(2,1)S(1)}, u32[]{:S(2)}, u32[]{:S(2)}) collective-permute-start(bf16[64,2048]{1,0:T(8,128)(2,1)S(1)} %shard_map.93), channel_id=1, source_target_pairs={{0,8},{1,9},{2,10},{3,11},{4,12},{5,13},{6,14},{7,15},{8,0},{9,1},... | collective-permute-start | bytes 786440 | tf_op jit(solution)/shard_map/ppermute | solution.py:250
  62.0 13.5 %collective-permute-start.16 = (bf16[64,2048]{1,0:T(8,128)(2,1)S(1)}, bf16[64,2048]{1,0:T(8,128)(2,1)S(1)}, u32[]{:S(2)}, u32[]{:S(2)}) collective-permute-start(bf16[64,2048]{1,0:T(8,128)(2,1)S(1)} %get-tuple-element.56), channel_id=1, source_target_pairs={{0,4},{1,3},{2,6},{3,1},{4,0},{5,7},{6,2},{7,5},{8,12},{9,11},{10,... | collective-permute-start | bytes 786440 | tf_op jit(solution)/shard_map/ppermute | solution.py:250
  64.2 11.3 %collective-permute-start.17 = (bf16[64,2048]{1,0:T(8,128)(2,1)S(1)}, bf16[64,2048]{1,0:T(8,128)(2,1)S(1)}, u32[]{:S(2)}, u32[]{:S(2)}) collective-permute-start(bf16[64,2048]{1,0:T(8,128)(2,1)S(1)} %get-tuple-element.57), channel_id=1, source_target_pairs={{0,2},{1,5},{2,0},{3,7},{4,6},{5,1},{6,4},{7,3},{8,10},{9,13},{10,... | collective-permute-start | bytes 786440 | tf_op jit(solution)/shard_map/ppermute | solution.py:250

commit v7 on v6

--- a/solution.py
+++ b/solution.py
@@ -275,8 +275,9 @@
     own3 = send(own1, ep, [-2])
     own5 = send(own1, ep, [-1])
     own6 = send(own2, ep, [-1])
+    theirs = expert([first, crossed], matrices)
+    own3, theirs = lax.optimization_barrier((own3, theirs))
     own7 = send(own3, ep, [-1])
-    theirs = expert([first, crossed], matrices)
     own3, own5, own6, own7, theirs = lax.optimization_barrier((own3, own5, own6, own7, theirs))
     far = [own3, own5, own6, own7]
     far_crossed = cross(pack(far))
@@ -296,8 +297,9 @@
         [far_made, far_back, back7], weights, [part(0, 1, 0, 4) + [(2, 0, None)], part(0, 1, 2, 6)]
     )
     back3 = send(send3, ep, [-2])
+    near_made = expert(near, matrices)
+    near_made, send6 = lax.optimization_barrier((near_made, send6))
     back6 = send(send6, ep, [-1])
-    near_made = expert(near, matrices)
     near_back = cross(theirs)
     near_made, back3, back5 = lax.optimization_barrier((near_made, back3, back5))
     (send1,) = combine([near_made, near_back, back3, back5], weights, [part(0, 1, 1, 1) + [(2, 0, None), (3, 0, None)]])

time: 76.5 us -> 75.6 us (0.988)
  waiting for transfers between devices: 31.4 us -> 29.1 us
  starting transfers between devices: 21.7 us -> 23 us
    ppermute x14, waiting for transfers between devices: 31 us -> 28.7 us  [send(): return lax.ppermute(array, ('ep', 'sub'), pairs)]
    ppermute x14, starting transfers between devices: 20.4 us -> 21.7 us  [send(): return lax.ppermute(array, ('ep', 'sub'), pairs)]
  transfers between devices with their start and end apart: 19 -> 19, of which waited for: 10 -> 12; matrix products, arithmetic and copies ran while one was open for 0% -> 0% of each run, Pallas kernels for 16% -> 16%
where the time goes in v7:
time: 75.6 us; the launch traced here: 75.3 us
  waiting for transfers between devices  29.1 us (38%)
  starting transfers between devices  23 us (30%)
  Pallas kernels  17.4 us (23%)
  local copies, waits for them, and re-layouts  5.68 us (8%)
    ppermute x14, waiting for transfers between devices, send(): return lax.ppermute(array, ('ep', 'sub'), pairs)  28.7 us
    ppermute x14, starting transfers between devices, send(): return lax.ppermute(array, ('ep', 'sub'), pairs)  21.7 us
    pallas_call x4, Pallas kernels, expert(): pl.pallas_call(expert_kernel, in_specs=[pl.BlockSpec(memory_space=pltpu.V...  10.5 us
    unnamed x10, local copies, waits for them, and re-layouts  5.68 us
    pallas_call x6, Pallas kernels, combine(): pl.pallas_call(functools.partial(combine_kernel, rows, sums, len(arrays))...  2.26 us
    pallas_call x1, Pallas kernels, prepare(): pl.pallas_call(prepare_kernel, in_specs=[pl.BlockSpec(memory_space=pltpu....  1.98 us
    pallas_call x1, Pallas kernels, weigh(): pl.pallas_call(functools.partial(weigh_kernel, top, tok_rows), in_specs=[...  1.89 us
  transfers between devices with their start and end apart: 19, of which 12 were waited for; matrix products, arithmetic and copies ran while one was open for 0% of the time, Pallas kernels for 16%

profile of v7, /device:TPU:0, one launch (start us, length us, event | category | flops | bytes accessed | tf_op | source)
XLA Modules:
  0.0 75.3 jit_solution(5976034526950102901)
XLA Ops:
  0.0 2.0 %shard_map.82.refs_0_ = bf16[64,2176]{1,0:T(8,128)(2,1)} custom-call(s32[1]{0:T(128)} %bitcast.me_ref, bf16[64,2048]{1,0:T(8,128)(2,1)} %tokens_ref.1, s32[8,64]{1,0:T(8,128)} %bitcast.4, f32[8,64]{1,0:T(8,128)} %bitcast.5, s32[1,64]{1,0:T(1,128)} %bitcast.6), custom_call_target="tpu_custom_call" | custom-call | tf_op jit(solution)/shard_map/pallas_call | solution.py:52
  2.0 4.0 %collective-permute-start = (bf16[64,2176]{1,0:T(8,128)(2,1)}, bf16[64,2176]{1,0:T(8,128)(2,1)S(1)}, u32[]{:S(2)}, u32[]{:S(2)}) collective-permute-start(bf16[64,2176]{1,0:T(8,128)(2,1)} %shard_map.82.refs_0_), channel_id=1, source_target_pairs={{0,8},{1,9},{2,10},{3,11},{4,12},{5,13},{6,14},{7,15},{8,0},{9,1},... | collective-permute-start | bytes 835592 | tf_op jit(solution)/shard_map/ppermute | solution.py:250
  6.0 1.6 %collective-permute-start.2 = (bf16[64,2176]{1,0:T(8,128)(2,1)}, bf16[64,2176]{1,0:T(8,128)(2,1)S(1)}, u32[]{:S(2)}, u32[]{:S(2)}) collective-permute-start(bf16[64,2176]{1,0:T(8,128)(2,1)} %shard_map.82.refs_0_), channel_id=1, source_target_pairs={{0,4},{1,3},{2,6},{3,1},{4,0},{5,7},{6,2},{7,5},{8,12},{9,11},{10,... | collective-permute-start | bytes 835592 | tf_op jit(solution)/shard_map/ppermute | solution.py:250
  7.6 1.5 %collective-permute-start.3 = (bf16[64,2176]{1,0:T(8,128)(2,1)}, bf16[64,2176]{1,0:T(8,128)(2,1)S(1)}, u32[]{:S(2)}, u32[]{:S(2)}) collective-permute-start(bf16[64,2176]{1,0:T(8,128)(2,1)} %shard_map.82.refs_0_), channel_id=1, source_target_pairs={{0,2},{1,5},{2,0},{3,7},{4,6},{5,1},{6,4},{7,3},{8,10},{9,13},{10,... | collective-permute-start | bytes 835592 | tf_op jit(solution)/shard_map/ppermute | solution.py:250
  9.1 1.9 %copy-done = bf16[1,2048,768]{2,1,0:T(8,128)(2,1)S(1)} copy-done((bf16[1,2048,768]{2,1,0:T(8,128)(2,1)S(1)}, bf16[1,2048,768]{2,1,0:T(8,128)(2,1)}, u32[]{:S(2)}) %copy-start) | copy-done | bytes 3145752
  11.0 1.9 %copy-done.1 = bf16[1,2048,768]{2,1,0:T(8,128)(2,1)S(1)} copy-done((bf16[1,2048,768]{2,1,0:T(8,128)(2,1)S(1)}, bf16[1,2048,768]{2,1,0:T(8,128)(2,1)}, u32[]{:S(2)}) %copy-start.1) | copy-done | bytes 3145752
  12.9 1.9 %copy-done.2 = bf16[1,768,2048]{2,1,0:T(8,128)(2,1)S(1)} copy-done((bf16[1,768,2048]{2,1,0:T(8,128)(2,1)S(1)}, bf16[1,768,2048]{2,1,0:T(8,128)(2,1)}, u32[]{:S(2)}) %copy-start.2) | copy-done | bytes 3145752
  15.5 3.5 %collective-permute-done.refs_1_.refs_0_ = bf16[64,2176]{1,0:T(8,128)(2,1)S(1)} collective-permute-done((bf16[64,2176]{1,0:T(8,128)(2,1)}, bf16[64,2176]{1,0:T(8,128)(2,1)S(1)}, u32[]{:S(2)}, u32[]{:S(2)}) %collective-permute-start) | collective-permute-done | bytes 278560 | tf_op jit(solution)/shard_map/ppermute | solution.py:250
  20.8 1.5 %collective-permute-start.6 = (bf16[64,2176]{1,0:T(8,128)(2,1)S(1)}, bf16[64,2176]{1,0:T(8,128)(2,1)S(1)}, u32[]{:S(2)}, u32[]{:S(2)}) collective-permute-start(bf16[64,2176]{1,0:T(8,128)(2,1)S(1)} %collective-permute-done.refs_1_.refs_0_), channel_id=1, source_target_pairs={{0,2},{1,5},{2,0},{3,7},{4,6},{5,1},{6,4},{7,3},{8,10},{9,13},{10,... | collective-permute-start | bytes 835592 | tf_op jit(solution)/shard_map/ppermute | solution.py:250
  22.9 2.6 %shard_map.86 = bf16[256,2048]{1,0:T(8,128)(2,1)S(1)} custom-call(bf16[64,2176]{1,0:T(8,128)(2,1)S(1)} %collective-permute-done.1.refs_0_.refs_8_, bf16[192,2176]{1,0:T(8,128)(2,1)S(1)} %collective-permute-done.5.refs_1_.refs_9_, bf16[1,2048,768]{2,1,0:T(8,128)(2,1)S(1)} %get-tuple-element.41.refs_4_.refs_2_.refs_1_, ...), custom_call_target="tpu_custom_call" | custom-call | flops 1 | bytes 1 | tf_op jit(solution)/shard_map/pallas_call | solution.py:226
  25.5 3.8 %collective-permute-done.4.refs_0_.refs_4_ = bf16[64,2176]{1,0:T(8,128)(2,1)S(1)} collective-permute-done((bf16[64,2176]{1,0:T(8,128)(2,1)S(1)}, bf16[64,2176]{1,0:T(8,128)(2,1)S(1)}, u32[]{:S(2)}, u32[]{:S(2)}) %collective-permute-start.4) | collective-permute-done | bytes 278560 | tf_op jit(solution)/shard_map/ppermute | solution.py:250
  29.3 2.3 %collective-permute-start.8 = (bf16[64,2176]{1,0:T(8,128)(2,1)S(1)}, bf16[64,2176]{1,0:T(8,128)(2,1)S(1)}, u32[]{:S(2)}, u32[]{:S(2)}) collective-permute-start(bf16[64,2176]{1,0:T(8,128)(2,1)S(1)} %collective-permute-done.4.refs_0_.refs_4_), channel_id=1, source_target_pairs={{0,2},{1,5},{2,0},{3,7},{4,6},{5,1},{6,4},{7,3},{8,10},{9,13},{10,... | collective-permute-start | bytes 835592 | tf_op jit(solution)/shard_map/ppermute | solution.py:250
  32.3 3.8 %collective-permute-done.8.refs_3_.refs_7_ = bf16[64,2176]{1,0:T(8,128)(2,1)S(1)} collective-permute-done((bf16[64,2176]{1,0:T(8,128)(2,1)S(1)}, bf16[64,2176]{1,0:T(8,128)(2,1)S(1)}, u32[]{:S(2)}, u32[]{:S(2)}) %collective-permute-start.8) | collective-permute-done | bytes 278560 | tf_op jit(solution)/shard_map/ppermute | solution.py:250
  36.3 2.6 %shard_map.88.refs_0_ = bf16[256,2048]{1,0:T(8,128)(2,1)S(1)} custom-call(bf16[64,2176]{1,0:T(8,128)(2,1)S(1)} %collective-permute-done.4.refs_0_.refs_4_, bf16[64,2176]{1,0:T(8,128)(2,1)S(1)} %collective-permute-done.6.refs_1_.refs_5_, bf16[64,2176]{1,0:T(8,128)(2,1)S(1)} %collective-permute-done.7.refs_2_.refs_6_, ...), custom_call_target="tpu_custom_call" | custom-call | flops 1 | bytes 1 | tf_op jit(solution)/shard_map/pallas_call | solution.py:226
  39.0 2.6 %shard_map.89 = bf16[256,2048]{1,0:T(8,128)(2,1)S(1)} custom-call(bf16[256,2176]{1,0:T(8,128)(2,1)S(1)} %collective-permute-done.9.refs_0_.refs_10_, bf16[1,2048,768]{2,1,0:T(8,128)(2,1)S(1)} %get-tuple-element.41.refs_4_.refs_2_.refs_1_, bf16[1,2048,768]{2,1,0:T(8,128)(2,1)S(1)} %get-tuple-element.42.refs_5_.refs_3_.refs_2_, ...), custom_call_target="tpu_custom_call" | custom-call | flops 1 | bytes 1 | tf_op jit(solution)/shard_map/pallas_call | solution.py:226
  42.2 1.9 %shard_map.90.refs_2_.refs_3_.refs_4_ = f32[1024,128]{1,0:T(8,128)S(1)} custom-call(s32[1]{0:T(128)} %bitcast.me_ref, s32[16]{0:T(128)S(1)} %copy-done.4, bf16[64,2176]{1,0:T(8,128)(2,1)S(1)} %copy-done.3, bf16[64,2176]{1,0:T(8,128)(2,1)S(1)} %collective-permute-done.refs_1_.refs_0_, bf16[64,2176]{1,0:T(8,128)(2,1)S(1)} %collective-permute-done.2.refs_2_.refs_1_, ...), custom_call_target="tpu_custom_call" | custom-call | flops 1 | bytes 1 | tf_op jit(solution)/shard_map/pallas_call | solution.py:118
  44.7 2.1 %collective-permute-start.11 = (bf16[64,2048]{1,0:T(8,128)(2,1)S(1)}, bf16[64,2048]{1,0:T(8,128)(2,1)S(1)}, u32[]{:S(2)}, u32[]{:S(2)}) collective-permute-start(bf16[64,2048]{1,0:T(8,128)(2,1)S(1)} %get-tuple-element.53), channel_id=1, source_target_pairs={{0,2},{1,5},{2,0},{3,7},{4,6},{5,1},{6,4},{7,3},{8,10},{9,13},{10,... | collective-permute-start | bytes 786440 | tf_op jit(solution)/shard_map/ppermute | solution.py:250
  46.9 4.3 %collective-permute-done.11.refs_2_ = bf16[64,2048]{1,0:T(8,128)(2,1)S(1)} collective-permute-done((bf16[64,2048]{1,0:T(8,128)(2,1)S(1)}, bf16[64,2048]{1,0:T(8,128)(2,1)S(1)}, u32[]{:S(2)}, u32[]{:S(2)}) %collective-permute-start.11) | collective-permute-done | bytes 262176 | tf_op jit(solution)/shard_map/ppermute | solution.py:250
  51.9 2.6 %shard_map.84.refs_0_ = bf16[256,2048]{1,0:T(8,128)(2,1)S(1)} custom-call(bf16[64,2176]{1,0:T(8,128)(2,1)S(1)} %copy-done.3, bf16[64,2176]{1,0:T(8,128)(2,1)S(1)} %collective-permute-done.refs_1_.refs_0_, bf16[64,2176]{1,0:T(8,128)(2,1)S(1)} %collective-permute-done.2.refs_2_.refs_1_, bf16[64,2176]{1,0:T(8,128)(2,1)S(1)} %collective-permute-done.3.refs_3_.refs_2_, ...), custom_call_target="tpu_custom_call" | custom-call | flops 1 | bytes 1 | tf_op jit(solution)/shard_map/pallas_call | solution.py:226
  54.5 2.1 %collective-permute-start.15 = (bf16[64,2048]{1,0:T(8,128)(2,1)S(1)}, bf16[64,2048]{1,0:T(8,128)(2,1)S(1)}, u32[]{:S(2)}, u32[]{:S(2)}) collective-permute-start(bf16[64,2048]{1,0:T(8,128)(2,1)S(1)} %get-tuple-element.60), channel_id=1, source_target_pairs={{0,2},{1,5},{2,0},{3,7},{4,6},{5,1},{6,4},{7,3},{8,10},{9,13},{10,... | collective-permute-start | bytes 786440 | tf_op jit(solution)/shard_map/ppermute | solution.py:250
  61.3 1.8 %collective-permute-start.16 = (bf16[64,2048]{1,0:T(8,128)(2,1)S(1)}, bf16[64,2048]{1,0:T(8,128)(2,1)S(1)}, u32[]{:S(2)}, u32[]{:S(2)}) collective-permute-start(bf16[64,2048]{1,0:T(8,128)(2,1)S(1)} %get-tuple-element.64), channel_id=1, source_target_pairs={{0,4},{1,3},{2,6},{3,1},{4,0},{5,7},{6,2},{7,5},{8,12},{9,11},{10,... | collective-permute-start | bytes 786440 | tf_op jit(solution)/shard_map/ppermute | solution.py:250
  63.1 2.1 %collective-permute-start.17 = (bf16[64,2048]{1,0:T(8,128)(2,1)S(1)}, bf16[64,2048]{1,0:T(8,128)(2,1)S(1)}, u32[]{:S(2)}, u32[]{:S(2)}) collective-permute-start(bf16[64,2048]{1,0:T(8,128)(2,1)S(1)} %get-tuple-element.65), channel_id=1, source_target_pairs={{0,2},{1,5},{2,0},{3,7},{4,6},{5,1},{6,4},{7,3},{8,10},{9,13},{10,... | collective-permute-start | bytes 786440 | tf_op jit(solution)/shard_map/ppermute | solution.py:250
  65.2 6.8 %collective-permute-done.18.refs_2_ = bf16[64,2048]{1,0:T(8,128)(2,1)S(1)} collective-permute-done((bf16[64,2048]{1,0:T(8,128)(2,1)S(1)}, bf16[64,2048]{1,0:T(8,128)(2,1)S(1)}, u32[]{:S(2)}, u32[]{:S(2)}) %collective-permute-start.18) | collective-permute-done | bytes 262176 | tf_op jit(solution)/shard_map/ppermute | solution.py:250
  72.3 2.2 %collective-permute-done.16.refs_1_ = bf16[64,2048]{1,0:T(8,128)(2,1)S(1)} collective-permute-done((bf16[64,2048]{1,0:T(8,128)(2,1)S(1)}, bf16[64,2048]{1,0:T(8,128)(2,1)S(1)}, u32[]{:S(2)}, u32[]{:S(2)}) %collective-permute-start.16) | collective-permute-done | bytes 262176 | tf_op jit(solution)/shard_map/ppermute | solution.py:250
  (39 shorter events, 11.8 us)
Async XLA Ops:
  2.0 17.0 %collective-permute-start = (bf16[64,2176]{1,0:T(8,128)(2,1)}, bf16[64,2176]{1,0:T(8,128)(2,1)S(1)}, u32[]{:S(2)}, u32[]{:S(2)}) collective-permute-start(bf16[64,2176]{1,0:T(8,128)(2,1)} %shard_map.82.refs_0_), channel_id=1, source_target_pairs={{0,8},{1,9},{2,10},{3,11},{4,12},{5,13},{6,14},{7,15},{8,0},{9,1},... | collective-permute-start | bytes 835592 | tf_op jit(solution)/shard_map/ppermute | solution.py:250
  6.0 12.9 %collective-permute-start.1 = (bf16[64,2176]{1,0:T(8,128)(2,1)}, bf16[64,2176]{1,0:T(8,128)(2,1)S(1)}, u32[]{:S(2)}, u32[]{:S(2)}) collective-permute-start(bf16[64,2176]{1,0:T(8,128)(2,1)} %shard_map.82.refs_0_), channel_id=1, source_target_pairs={{0,1},{1,0},{2,3},{3,2},{4,5},{5,4},{6,7},{7,6},{8,9},{9,8},{10,11... | collective-permute-start | bytes 835592 | tf_op jit(solution)/shard_map/ppermute | solution.py:254
  6.0 13.8 %collective-permute-start.2 = (bf16[64,2176]{1,0:T(8,128)(2,1)}, bf16[64,2176]{1,0:T(8,128)(2,1)S(1)}, u32[]{:S(2)}, u32[]{:S(2)}) collective-permute-start(bf16[64,2176]{1,0:T(8,128)(2,1)} %shard_map.82.refs_0_), channel_id=1, source_target_pairs={{0,4},{1,3},{2,6},{3,1},{4,0},{5,7},{6,2},{7,5},{8,12},{9,11},{10,... | collective-permute-start | bytes 835592 | tf_op jit(solution)/shard_map/ppermute | solution.py:250
  7.6 12.2 %collective-permute-start.3 = (bf16[64,2176]{1,0:T(8,128)(2,1)}, bf16[64,2176]{1,0:T(8,128)(2,1)S(1)}, u32[]{:S(2)}, u32[]{:S(2)}) collective-permute-start(bf16[64,2176]{1,0:T(8,128)(2,1)} %shard_map.82.refs_0_), channel_id=1, source_target_pairs={{0,2},{1,5},{2,0},{3,7},{4,6},{5,1},{6,4},{7,3},{8,10},{9,13},{10,... | collective-permute-start | bytes 835592 | tf_op jit(solution)/shard_map/ppermute | solution.py:250
  9.1 1.9 %copy-start = (bf16[1,2048,768]{2,1,0:T(8,128)(2,1)S(1)}, bf16[1,2048,768]{2,1,0:T(8,128)(2,1)}, u32[]{:S(2)}) copy-start(bf16[1,2048,768]{2,1,0:T(8,128)(2,1)} %refs_0_.1) | copy-start | bytes 9437188
  11.0 1.9 %copy-start.1 = (bf16[1,2048,768]{2,1,0:T(8,128)(2,1)S(1)}, bf16[1,2048,768]{2,1,0:T(8,128)(2,1)}, u32[]{:S(2)}) copy-start(bf16[1,2048,768]{2,1,0:T(8,128)(2,1)} %refs_1_.1) | copy-start | bytes 9437188
  12.9 1.9 %copy-start.2 = (bf16[1,768,2048]{2,1,0:T(8,128)(2,1)S(1)}, bf16[1,768,2048]{2,1,0:T(8,128)(2,1)}, u32[]{:S(2)}) copy-start(bf16[1,768,2048]{2,1,0:T(8,128)(2,1)} %refs_2_.1) | copy-start | bytes 9437188
  19.9 3.0 %collective-permute-start.5 = (bf16[192,2176]{1,0:T(8,128)(2,1)S(1)}, bf16[192,2176]{1,0:T(8,128)(2,1)S(1)}, u32[]{:S(2)}, u32[]{:S(2)}) collective-permute-start(bf16[192,2176]{1,0:T(8,128)(2,1)S(1)} %shard_map.85), channel_id=1, source_target_pairs={{0,1},{1,0},{2,3},{3,2},{4,5},{5,4},{6,7},{7,6},{8,9},{9,8},{10,11... | collective-permute-start | bytes 2506760 | tf_op jit(solution)/shard_map/ppermute | solution.py:254
  20.5 8.8 %collective-permute-start.4 = (bf16[64,2176]{1,0:T(8,128)(2,1)S(1)}, bf16[64,2176]{1,0:T(8,128)(2,1)S(1)}, u32[]{:S(2)}, u32[]{:S(2)}) collective-permute-start(bf16[64,2176]{1,0:T(8,128)(2,1)S(1)} %collective-permute-done.refs_1_.refs_0_), channel_id=1, source_target_pairs={{0,4},{1,3},{2,6},{3,1},{4,0},{5,7},{6,2},{7,5},{8,12},{9,11},{10,... | collective-permute-start | bytes 835592 | tf_op jit(solution)/shard_map/ppermute | solution.py:250
  20.8 10.7 %collective-permute-start.6 = (bf16[64,2176]{1,0:T(8,128)(2,1)S(1)}, bf16[64,2176]{1,0:T(8,128)(2,1)S(1)}, u32[]{:S(2)}, u32[]{:S(2)}) collective-permute-start(bf16[64,2176]{1,0:T(8,128)(2,1)S(1)} %collective-permute-done.refs_1_.refs_0_), channel_id=1, source_target_pairs={{0,2},{1,5},{2,0},{3,7},{4,6},{5,1},{6,4},{7,3},{8,10},{9,13},{10,... | collective-permute-start | bytes 835592 | tf_op jit(solution)/shard_map/ppermute | solution.py:250
  22.4 10.0 %collective-permute-start.7 = (bf16[64,2176]{1,0:T(8,128)(2,1)S(1)}, bf16[64,2176]{1,0:T(8,128)(2,1)S(1)}, u32[]{:S(2)}, u32[]{:S(2)}) collective-permute-start(bf16[64,2176]{1,0:T(8,128)(2,1)S(1)} %collective-permute-done.2.refs_2_.refs_1_), channel_id=1, source_target_pairs={{0,2},{1,5},{2,0},{3,7},{4,6},{5,1},{6,4},{7,3},{8,10},{9,13},{10,... | collective-permute-start | bytes 835592 | tf_op jit(solution)/shard_map/ppermute | solution.py:250
  29.3 6.8 %collective-permute-start.8 = (bf16[64,2176]{1,0:T(8,128)(2,1)S(1)}, bf16[64,2176]{1,0:T(8,128)(2,1)S(1)}, u32[]{:S(2)}, u32[]{:S(2)}) collective-permute-start(bf16[64,2176]{1,0:T(8,128)(2,1)S(1)} %collective-permute-done.4.refs_0_.refs_4_), channel_id=1, source_target_pairs={{0,2},{1,5},{2,0},{3,7},{4,6},{5,1},{6,4},{7,3},{8,10},{9,13},{10,... | collective-permute-start | bytes 835592 | tf_op jit(solution)/shard_map/ppermute | solution.py:250
  36.2 2.8 %collective-permute-start.9 = (bf16[256,2176]{1,0:T(8,128)(2,1)S(1)}, bf16[256,2176]{1,0:T(8,128)(2,1)S(1)}, u32[]{:S(2)}, u32[]{:S(2)}) collective-permute-start(bf16[256,2176]{1,0:T(8,128)(2,1)S(1)} %shard_map.87), channel_id=1, source_target_pairs={{0,1},{1,0},{2,3},{3,2},{4,5},{5,4},{6,7},{7,6},{8,9},{9,8},{10,11... | collective-permute-start | bytes 3342344 | tf_op jit(solution)/shard_map/ppermute | solution.py:254
  38.9 3.3 %copy-start.3 = (bf16[64,2176]{1,0:T(8,128)(2,1)S(1)}, bf16[64,2176]{1,0:T(8,128)(2,1)}, u32[]{:S(2)}) copy-start(bf16[64,2176]{1,0:T(8,128)(2,1)} %shard_map.82.refs_0_) | copy-start | bytes 835588
  38.9 3.3 %copy-start.4 = (s32[16]{0:T(128)S(1)}, s32[16]{0:T(128)}, u32[]{:S(2)}) copy-start(s32[16]{0:T(128)} %capacity_ref.1) | copy-start | bytes 196
  41.6 2.8 %collective-permute-start.10 = (bf16[256,2048]{1,0:T(8,128)(2,1)S(1)}, bf16[256,2048]{1,0:T(8,128)(2,1)S(1)}, u32[]{:S(2)}, u32[]{:S(2)}) collective-permute-start(bf16[256,2048]{1,0:T(8,128)(2,1)S(1)} %shard_map.89), channel_id=1, source_target_pairs={{0,1},{1,0},{2,3},{3,2},{4,5},{5,4},{6,7},{7,6},{8,9},{9,8},{10,11... | collective-permute-start | bytes 3145736 | tf_op jit(solution)/shard_map/ppermute | solution.py:254
  42.1 15.9 %collective-permute-start.14 = (bf16[256,2048]{1,0:T(8,128)(2,1)S(1)}, bf16[256,2048]{1,0:T(8,128)(2,1)S(1)}, u32[]{:S(2)}, u32[]{:S(2)}) collective-permute-start(bf16[256,2048]{1,0:T(8,128)(2,1)S(1)} %shard_map.86), channel_id=1, source_target_pairs={{0,1},{1,0},{2,3},{3,2},{4,5},{5,4},{6,7},{7,6},{8,9},{9,8},{10,11... | collective-permute-start | bytes 3145736 | tf_op jit(solution)/shard_map/ppermute | solution.py:254
  44.7 6.4 %collective-permute-start.11 = (bf16[64,2048]{1,0:T(8,128)(2,1)S(1)}, bf16[64,2048]{1,0:T(8,128)(2,1)S(1)}, u32[]{:S(2)}, u32[]{:S(2)}) collective-permute-start(bf16[64,2048]{1,0:T(8,128)(2,1)S(1)} %get-tuple-element.53), channel_id=1, source_target_pairs={{0,2},{1,5},{2,0},{3,7},{4,6},{5,1},{6,4},{7,3},{8,10},{9,13},{10,... | collective-permute-start | bytes 786440 | tf_op jit(solution)/shard_map/ppermute | solution.py:250
  46.8 9.8 %collective-permute-start.13 = (bf16[64,2048]{1,0:T(8,128)(2,1)S(1)}, bf16[64,2048]{1,0:T(8,128)(2,1)S(1)}, u32[]{:S(2)}, u32[]{:S(2)}) collective-permute-start(bf16[64,2048]{1,0:T(8,128)(2,1)S(1)} %get-tuple-element.57), channel_id=1, source_target_pairs={{0,2},{1,5},{2,0},{3,7},{4,6},{5,1},{6,4},{7,3},{8,10},{9,13},{10,... | collective-permute-start | bytes 786440 | tf_op jit(solution)/shard_map/ppermute | solution.py:250
  51.5 6.4 %collective-permute-start.12 = (bf16[64,2048]{1,0:T(8,128)(2,1)S(1)}, bf16[64,2048]{1,0:T(8,128)(2,1)S(1)}, u32[]{:S(2)}, u32[]{:S(2)}) collective-permute-start(bf16[64,2048]{1,0:T(8,128)(2,1)S(1)} %get-tuple-element.56), channel_id=1, source_target_pairs={{0,4},{1,3},{2,6},{3,1},{4,0},{5,7},{6,2},{7,5},{8,12},{9,11},{10,... | collective-permute-start | bytes 786440 | tf_op jit(solution)/shard_map/ppermute | solution.py:250
  54.5 6.4 %collective-permute-start.15 = (bf16[64,2048]{1,0:T(8,128)(2,1)S(1)}, bf16[64,2048]{1,0:T(8,128)(2,1)S(1)}, u32[]{:S(2)}, u32[]{:S(2)}) collective-permute-start(bf16[64,2048]{1,0:T(8,128)(2,1)S(1)} %get-tuple-element.60), channel_id=1, source_target_pairs={{0,2},{1,5},{2,0},{3,7},{4,6},{5,1},{6,4},{7,3},{8,10},{9,13},{10,... | collective-permute-start | bytes 786440 | tf_op jit(solution)/shard_map/ppermute | solution.py:250
  58.2 13.8 %collective-permute-start.18 = (bf16[64,2048]{1,0:T(8,128)(2,1)S(1)}, bf16[64,2048]{1,0:T(8,128)(2,1)S(1)}, u32[]{:S(2)}, u32[]{:S(2)}) collective-permute-start(bf16[64,2048]{1,0:T(8,128)(2,1)S(1)} %shard_map.93), channel_id=1, source_target_pairs={{0,8},{1,9},{2,10},{3,11},{4,12},{5,13},{6,14},{7,15},{8,0},{9,1},... | collective-permute-start | bytes 786440 | tf_op jit(solution)/shard_map/ppermute | solution.py:250
  61.3 13.2 %collective-permute-start.16 = (bf16[64,2048]{1,0:T(8,128)(2,1)S(1)}, bf16[64,2048]{1,0:T(8,128)(2,1)S(1)}, u32[]{:S(2)}, u32[]{:S(2)}) collective-permute-start(bf16[64,2048]{1,0:T(8,128)(2,1)S(1)} %get-tuple-element.64), channel_id=1, source_target_pairs={{0,4},{1,3},{2,6},{3,1},{4,0},{5,7},{6,2},{7,5},{8,12},{9,11},{10,... | collective-permute-start | bytes 786440 | tf_op jit(solution)/shard_map/ppermute | solution.py:250
  63.1 11.4 %collective-permute-start.17 = (bf16[64,2048]{1,0:T(8,128)(2,1)S(1)}, bf16[64,2048]{1,0:T(8,128)(2,1)S(1)}, u32[]{:S(2)}, u32[]{:S(2)}) collective-permute-start(bf16[64,2048]{1,0:T(8,128)(2,1)S(1)} %get-tuple-element.65), channel_id=1, source_target_pairs={{0,2},{1,5},{2,0},{3,7},{4,6},{5,1},{6,4},{7,3},{8,10},{9,13},{10,... | collective-permute-start | bytes 786440 | tf_op jit(solution)/shard_map/ppermute | solution.py:250

commit v8 on v7

--- a/solution.py
+++ b/solution.py
@@ -301,18 +301,19 @@
     near_made, send6 = lax.optimization_barrier((near_made, send6))
     back6 = send(send6, ep, [-1])
     near_back = cross(theirs)
-    near_made, back3, back5 = lax.optimization_barrier((near_made, back3, back5))
+    (send4,) = combine([near_made, near_back], weights, [part(0, 1, 3, 3)])
+    back4 = send(send4, ep, [-1])
+    back3, back5, send4 = lax.optimization_barrier((back3, back5, send4))
     (send1,) = combine([near_made, near_back, back3, back5], weights, [part(0, 1, 1, 1) + [(2, 0, None), (3, 0, None)]])
     back1 = send(send1, ep, [-3])
     back6, send1 = lax.optimization_barrier((back6, send1))
-    send2, send4 = combine(
-        [near_made, near_back, back6], weights, [part(0, 1, 2, 2) + [(2, 0, None)], part(0, 1, 3, 3)]
-    )
+    (send2,) = combine([near_made, near_back, back6], weights, [part(0, 1, 2, 2) + [(2, 0, None)]])
     back2 = send(send2, ep, [-2])
-    back4 = send(send4, ep, [-1])
-    (total,) = combine([near_made, near_back, back1], weights, [part(0, 1, 0, 0) + [(2, 0, None)]], F32)
-    back2, back4, total = lax.optimization_barrier((back2, back4, total))
-    (total,) = combine([total, back2, back4], weights, [[(0, 0, None), (1, 0, None), (2, 0, None)]])
+    (total,) = combine([near_made, near_back, back4], weights, [part(0, 1, 0, 0) + [(2, 0, None)]], F32)
+    back1, total = lax.optimization_barrier((back1, total))
+    (total,) = combine([total, back1], weights, [[(0, 0, None), (1, 0, None)]], F32)
+    back2, total = lax.optimization_barrier((back2, total))
+    (total,) = combine([total, back2], weights, [[(0, 0, None), (1, 0, None)]])
     for step in range(steps - 3)[::-1]:
         half = total.shape[0] // 2
         total = add(total[:half], send(total[half:], ep, [step]))

time: 75.6 us -> 73.4 us (0.971)
  starting transfers between devices: 23 us -> 21.3 us
    ppermute x14, starting transfers between devices: 21.7 us -> 20 us  [send(): return lax.ppermute(array, ('ep', 'sub'), pairs)]
    pallas_call x6 -> x8, Pallas kernels: 2.26 us -> 2.34 us  [combine(): pl.pallas_call(functools.partial(combine_kernel, rows, sums, len(arrays))...]
where the time goes in v8:
time: 73.4 us; the launch traced here: 73.2 us
  waiting for transfers between devices  28.6 us (39%)
  starting transfers between devices  21.3 us (29%)
  Pallas kernels  17.5 us (24%)
  local copies, waits for them, and re-layouts  5.68 us (8%)
    ppermute x14, waiting for transfers between devices, send(): return lax.ppermute(array, ('ep', 'sub'), pairs)  28.2 us
    ppermute x14, starting transfers between devices, send(): return lax.ppermute(array, ('ep', 'sub'), pairs)  20 us
    pallas_call x4, Pallas kernels, expert(): pl.pallas_call(expert_kernel, in_specs=[pl.BlockSpec(memory_space=pltpu.V...  10.5 us
    unnamed x10, local copies, waits for them, and re-layouts  5.68 us
    pallas_call x8, Pallas kernels, combine(): pl.pallas_call(functools.partial(combine_kernel, rows, sums, len(arrays))...  2.34 us
    pallas_call x1, Pallas kernels, prepare(): pl.pallas_call(prepare_kernel, in_specs=[pl.BlockSpec(memory_space=pltpu....  1.97 us
    pallas_call x1, Pallas kernels, weigh(): pl.pallas_call(functools.partial(weigh_kernel, top, tok_rows), in_specs=[...  1.89 us
  transfers between devices with their start and end apart: 19, of which 12 were waited for; matrix products, arithmetic and copies ran while one was open for 0% of the time, Pallas kernels for 16%

profile of v8, /device:TPU:0, one launch (start us, length us, event | category | flops | bytes accessed | tf_op | source)
XLA Modules:
  0.0 73.2 jit_solution(14654967575714002745)
XLA Ops:
  0.0 2.0 %shard_map.82.refs_0_ = bf16[64,2176]{1,0:T(8,128)(2,1)} custom-call(s32[1]{0:T(128)} %bitcast.me_ref, bf16[64,2048]{1,0:T(8,128)(2,1)} %tokens_ref.1, s32[8,64]{1,0:T(8,128)} %bitcast.4, f32[8,64]{1,0:T(8,128)} %bitcast.5, s32[1,64]{1,0:T(1,128)} %bitcast.6), custom_call_target="tpu_custom_call" | custom-call | tf_op jit(solution)/shard_map/pallas_call | solution.py:52
  2.0 4.0 %collective-permute-start = (bf16[64,2176]{1,0:T(8,128)(2,1)}, bf16[64,2176]{1,0:T(8,128)(2,1)S(1)}, u32[]{:S(2)}, u32[]{:S(2)}) collective-permute-start(bf16[64,2176]{1,0:T(8,128)(2,1)} %shard_map.82.refs_0_), channel_id=1, source_target_pairs={{0,8},{1,9},{2,10},{3,11},{4,12},{5,13},{6,14},{7,15},{8,0},{9,1},... | collective-permute-start | bytes 835592 | tf_op jit(solution)/shard_map/ppermute | solution.py:250
  6.0 1.6 %collective-permute-start.2 = (bf16[64,2176]{1,0:T(8,128)(2,1)}, bf16[64,2176]{1,0:T(8,128)(2,1)S(1)}, u32[]{:S(2)}, u32[]{:S(2)}) collective-permute-start(bf16[64,2176]{1,0:T(8,128)(2,1)} %shard_map.82.refs_0_), channel_id=1, source_target_pairs={{0,4},{1,3},{2,6},{3,1},{4,0},{5,7},{6,2},{7,5},{8,12},{9,11},{10,... | collective-permute-start | bytes 835592 | tf_op jit(solution)/shard_map/ppermute | solution.py:250
  7.6 1.5 %collective-permute-start.3 = (bf16[64,2176]{1,0:T(8,128)(2,1)}, bf16[64,2176]{1,0:T(8,128)(2,1)S(1)}, u32[]{:S(2)}, u32[]{:S(2)}) collective-permute-start(bf16[64,2176]{1,0:T(8,128)(2,1)} %shard_map.82.refs_0_), channel_id=1, source_target_pairs={{0,2},{1,5},{2,0},{3,7},{4,6},{5,1},{6,4},{7,3},{8,10},{9,13},{10,... | collective-permute-start | bytes 835592 | tf_op jit(solution)/shard_map/ppermute | solution.py:250
  9.1 1.9 %copy-done = bf16[1,2048,768]{2,1,0:T(8,128)(2,1)S(1)} copy-done((bf16[1,2048,768]{2,1,0:T(8,128)(2,1)S(1)}, bf16[1,2048,768]{2,1,0:T(8,128)(2,1)}, u32[]{:S(2)}) %copy-start) | copy-done | bytes 3145752
  11.0 1.9 %copy-done.1 = bf16[1,2048,768]{2,1,0:T(8,128)(2,1)S(1)} copy-done((bf16[1,2048,768]{2,1,0:T(8,128)(2,1)S(1)}, bf16[1,2048,768]{2,1,0:T(8,128)(2,1)}, u32[]{:S(2)}) %copy-start.1) | copy-done | bytes 3145752
  12.9 1.9 %copy-done.2 = bf16[1,768,2048]{2,1,0:T(8,128)(2,1)S(1)} copy-done((bf16[1,768,2048]{2,1,0:T(8,128)(2,1)S(1)}, bf16[1,768,2048]{2,1,0:T(8,128)(2,1)}, u32[]{:S(2)}) %copy-start.2) | copy-done | bytes 3145752
  15.4 3.5 %collective-permute-done.refs_1_.refs_0_ = bf16[64,2176]{1,0:T(8,128)(2,1)S(1)} collective-permute-done((bf16[64,2176]{1,0:T(8,128)(2,1)}, bf16[64,2176]{1,0:T(8,128)(2,1)S(1)}, u32[]{:S(2)}, u32[]{:S(2)}) %collective-permute-start) | collective-permute-done | bytes 278560 | tf_op jit(solution)/shard_map/ppermute | solution.py:250
  20.8 1.5 %collective-permute-start.6 = (bf16[64,2176]{1,0:T(8,128)(2,1)S(1)}, bf16[64,2176]{1,0:T(8,128)(2,1)S(1)}, u32[]{:S(2)}, u32[]{:S(2)}) collective-permute-start(bf16[64,2176]{1,0:T(8,128)(2,1)S(1)} %collective-permute-done.refs_1_.refs_0_), channel_id=1, source_target_pairs={{0,2},{1,5},{2,0},{3,7},{4,6},{5,1},{6,4},{7,3},{8,10},{9,13},{10,... | collective-permute-start | bytes 835592 | tf_op jit(solution)/shard_map/ppermute | solution.py:250
  22.9 2.6 %shard_map.86 = bf16[256,2048]{1,0:T(8,128)(2,1)S(1)} custom-call(bf16[64,2176]{1,0:T(8,128)(2,1)S(1)} %collective-permute-done.1.refs_0_.refs_8_, bf16[192,2176]{1,0:T(8,128)(2,1)S(1)} %collective-permute-done.5.refs_1_.refs_9_, bf16[1,2048,768]{2,1,0:T(8,128)(2,1)S(1)} %get-tuple-element.39.refs_4_.refs_2_.refs_1_, ...), custom_call_target="tpu_custom_call" | custom-call | flops 1 | bytes 1 | tf_op jit(solution)/shard_map/pallas_call | solution.py:226
  25.5 3.8 %collective-permute-done.4.refs_0_.refs_4_ = bf16[64,2176]{1,0:T(8,128)(2,1)S(1)} collective-permute-done((bf16[64,2176]{1,0:T(8,128)(2,1)S(1)}, bf16[64,2176]{1,0:T(8,128)(2,1)S(1)}, u32[]{:S(2)}, u32[]{:S(2)}) %collective-permute-start.4) | collective-permute-done | bytes 278560 | tf_op jit(solution)/shard_map/ppermute | solution.py:250
  29.3 2.3 %collective-permute-start.8 = (bf16[64,2176]{1,0:T(8,128)(2,1)S(1)}, bf16[64,2176]{1,0:T(8,128)(2,1)S(1)}, u32[]{:S(2)}, u32[]{:S(2)}) collective-permute-start(bf16[64,2176]{1,0:T(8,128)(2,1)S(1)} %collective-permute-done.4.refs_0_.refs_4_), channel_id=1, source_target_pairs={{0,2},{1,5},{2,0},{3,7},{4,6},{5,1},{6,4},{7,3},{8,10},{9,13},{10,... | collective-permute-start | bytes 835592 | tf_op jit(solution)/shard_map/ppermute | solution.py:250
  32.3 3.8 %collective-permute-done.8.refs_3_.refs_7_ = bf16[64,2176]{1,0:T(8,128)(2,1)S(1)} collective-permute-done((bf16[64,2176]{1,0:T(8,128)(2,1)S(1)}, bf16[64,2176]{1,0:T(8,128)(2,1)S(1)}, u32[]{:S(2)}, u32[]{:S(2)}) %collective-permute-start.8) | collective-permute-done | bytes 278560 | tf_op jit(solution)/shard_map/ppermute | solution.py:250
  36.3 2.6 %shard_map.88.refs_0_ = bf16[256,2048]{1,0:T(8,128)(2,1)S(1)} custom-call(bf16[64,2176]{1,0:T(8,128)(2,1)S(1)} %collective-permute-done.4.refs_0_.refs_4_, bf16[64,2176]{1,0:T(8,128)(2,1)S(1)} %collective-permute-done.6.refs_1_.refs_5_, bf16[64,2176]{1,0:T(8,128)(2,1)S(1)} %collective-permute-done.7.refs_2_.refs_6_, ...), custom_call_target="tpu_custom_call" | custom-call | flops 1 | bytes 1 | tf_op jit(solution)/shard_map/pallas_call | solution.py:226
  39.0 2.6 %shard_map.89 = bf16[256,2048]{1,0:T(8,128)(2,1)S(1)} custom-call(bf16[256,2176]{1,0:T(8,128)(2,1)S(1)} %collective-permute-done.9.refs_0_.refs_10_, bf16[1,2048,768]{2,1,0:T(8,128)(2,1)S(1)} %get-tuple-element.39.refs_4_.refs_2_.refs_1_, bf16[1,2048,768]{2,1,0:T(8,128)(2,1)S(1)} %get-tuple-element.40.refs_5_.refs_3_.refs_2_, ...), custom_call_target="tpu_custom_call" | custom-call | flops 1 | bytes 1 | tf_op jit(solution)/shard_map/pallas_call | solution.py:226
  42.2 1.9 %shard_map.90.refs_2_.refs_3_.refs_4_ = f32[1024,128]{1,0:T(8,128)S(1)} custom-call(s32[1]{0:T(128)} %bitcast.me_ref, s32[16]{0:T(128)S(1)} %copy-done.4, bf16[64,2176]{1,0:T(8,128)(2,1)S(1)} %copy-done.3, bf16[64,2176]{1,0:T(8,128)(2,1)S(1)} %collective-permute-done.refs_1_.refs_0_, bf16[64,2176]{1,0:T(8,128)(2,1)S(1)} %collective-permute-done.2.refs_2_.refs_1_, ...), custom_call_target="tpu_custom_call" | custom-call | flops 1 | bytes 1 | tf_op jit(solution)/shard_map/pallas_call | solution.py:118
  44.7 2.1 %collective-permute-start.11 = (bf16[64,2048]{1,0:T(8,128)(2,1)S(1)}, bf16[64,2048]{1,0:T(8,128)(2,1)S(1)}, u32[]{:S(2)}, u32[]{:S(2)}) collective-permute-start(bf16[64,2048]{1,0:T(8,128)(2,1)S(1)} %get-tuple-element.51), channel_id=1, source_target_pairs={{0,2},{1,5},{2,0},{3,7},{4,6},{5,1},{6,4},{7,3},{8,10},{9,13},{10,... | collective-permute-start | bytes 786440 | tf_op jit(solution)/shard_map/ppermute | solution.py:250
  46.9 4.3 %collective-permute-done.11.refs_2_ = bf16[64,2048]{1,0:T(8,128)(2,1)S(1)} collective-permute-done((bf16[64,2048]{1,0:T(8,128)(2,1)S(1)}, bf16[64,2048]{1,0:T(8,128)(2,1)S(1)}, u32[]{:S(2)}, u32[]{:S(2)}) %collective-permute-start.11) | collective-permute-done | bytes 262176 | tf_op jit(solution)/shard_map/ppermute | solution.py:250
  51.9 2.6 %shard_map.84.refs_0_ = bf16[256,2048]{1,0:T(8,128)(2,1)S(1)} custom-call(bf16[64,2176]{1,0:T(8,128)(2,1)S(1)} %copy-done.3, bf16[64,2176]{1,0:T(8,128)(2,1)S(1)} %collective-permute-done.refs_1_.refs_0_, bf16[64,2176]{1,0:T(8,128)(2,1)S(1)} %collective-permute-done.2.refs_2_.refs_1_, bf16[64,2176]{1,0:T(8,128)(2,1)S(1)} %collective-permute-done.3.refs_3_.refs_2_, ...), custom_call_target="tpu_custom_call" | custom-call | flops 1 | bytes 1 | tf_op jit(solution)/shard_map/pallas_call | solution.py:226
  54.5 2.1 %collective-permute-start.13 = (bf16[64,2048]{1,0:T(8,128)(2,1)S(1)}, bf16[64,2048]{1,0:T(8,128)(2,1)S(1)}, u32[]{:S(2)}, u32[]{:S(2)}) collective-permute-start(bf16[64,2048]{1,0:T(8,128)(2,1)S(1)} %get-tuple-element.55), channel_id=1, source_target_pairs={{0,2},{1,5},{2,0},{3,7},{4,6},{5,1},{6,4},{7,3},{8,10},{9,13},{10,... | collective-permute-start | bytes 786440 | tf_op jit(solution)/shard_map/ppermute | solution.py:250
  56.9 1.0 %collective-permute-done.14.refs_2_ = bf16[64,2048]{1,0:T(8,128)(2,1)S(1)} collective-permute-done((bf16[64,2048]{1,0:T(8,128)(2,1)S(1)}, bf16[64,2048]{1,0:T(8,128)(2,1)S(1)}, u32[]{:S(2)}, u32[]{:S(2)}) %collective-permute-start.14) | collective-permute-done | bytes 262176 | tf_op jit(solution)/shard_map/ppermute | solution.py:250
  58.2 1.7 %collective-permute-start.17 = (bf16[64,2048]{1,0:T(8,128)(2,1)S(1)}, bf16[64,2048]{1,0:T(8,128)(2,1)S(1)}, u32[]{:S(2)}, u32[]{:S(2)}) collective-permute-start(bf16[64,2048]{1,0:T(8,128)(2,1)S(1)} %shard_map.94), channel_id=1, source_target_pairs={{0,8},{1,9},{2,10},{3,11},{4,12},{5,13},{6,14},{7,15},{8,0},{9,1},... | collective-permute-start | bytes 786440 | tf_op jit(solution)/shard_map/ppermute | solution.py:250
  61.2 1.8 %collective-permute-start.16 = (bf16[64,2048]{1,0:T(8,128)(2,1)S(1)}, bf16[64,2048]{1,0:T(8,128)(2,1)S(1)}, u32[]{:S(2)}, u32[]{:S(2)}) collective-permute-start(bf16[64,2048]{1,0:T(8,128)(2,1)S(1)} %shard_map.95), channel_id=1, source_target_pairs={{0,4},{1,3},{2,6},{3,1},{4,0},{5,7},{6,2},{7,5},{8,12},{9,11},{10,... | collective-permute-start | bytes 786440 | tf_op jit(solution)/shard_map/ppermute | solution.py:250
  64.0 8.4 %collective-permute-done.17.refs_1_ = bf16[64,2048]{1,0:T(8,128)(2,1)S(1)} collective-permute-done((bf16[64,2048]{1,0:T(8,128)(2,1)S(1)}, bf16[64,2048]{1,0:T(8,128)(2,1)S(1)}, u32[]{:S(2)}, u32[]{:S(2)}) %collective-permute-start.17) | collective-permute-done | bytes 262176 | tf_op jit(solution)/shard_map/ppermute | solution.py:250
  (41 shorter events, 9.7 us)
Async XLA Ops:
  2.0 17.0 %collective-permute-start = (bf16[64,2176]{1,0:T(8,128)(2,1)}, bf16[64,2176]{1,0:T(8,128)(2,1)S(1)}, u32[]{:S(2)}, u32[]{:S(2)}) collective-permute-start(bf16[64,2176]{1,0:T(8,128)(2,1)} %shard_map.82.refs_0_), channel_id=1, source_target_pairs={{0,8},{1,9},{2,10},{3,11},{4,12},{5,13},{6,14},{7,15},{8,0},{9,1},... | collective-permute-start | bytes 835592 | tf_op jit(solution)/shard_map/ppermute | solution.py:250
  6.0 12.9 %collective-permute-start.1 = (bf16[64,2176]{1,0:T(8,128)(2,1)}, bf16[64,2176]{1,0:T(8,128)(2,1)S(1)}, u32[]{:S(2)}, u32[]{:S(2)}) collective-permute-start(bf16[64,2176]{1,0:T(8,128)(2,1)} %shard_map.82.refs_0_), channel_id=1, source_target_pairs={{0,1},{1,0},{2,3},{3,2},{4,5},{5,4},{6,7},{7,6},{8,9},{9,8},{10,11... | collective-permute-start | bytes 835592 | tf_op jit(solution)/shard_map/ppermute | solution.py:254
  6.0 13.8 %collective-permute-start.2 = (bf16[64,2176]{1,0:T(8,128)(2,1)}, bf16[64,2176]{1,0:T(8,128)(2,1)S(1)}, u32[]{:S(2)}, u32[]{:S(2)}) collective-permute-start(bf16[64,2176]{1,0:T(8,128)(2,1)} %shard_map.82.refs_0_), channel_id=1, source_target_pairs={{0,4},{1,3},{2,6},{3,1},{4,0},{5,7},{6,2},{7,5},{8,12},{9,11},{10,... | collective-permute-start | bytes 835592 | tf_op jit(solution)/shard_map/ppermute | solution.py:250
  7.6 12.2 %collective-permute-start.3 = (bf16[64,2176]{1,0:T(8,128)(2,1)}, bf16[64,2176]{1,0:T(8,128)(2,1)S(1)}, u32[]{:S(2)}, u32[]{:S(2)}) collective-permute-start(bf16[64,2176]{1,0:T(8,128)(2,1)} %shard_map.82.refs_0_), channel_id=1, source_target_pairs={{0,2},{1,5},{2,0},{3,7},{4,6},{5,1},{6,4},{7,3},{8,10},{9,13},{10,... | collective-permute-start | bytes 835592 | tf_op jit(solution)/shard_map/ppermute | solution.py:250
  9.1 1.9 %copy-start = (bf16[1,2048,768]{2,1,0:T(8,128)(2,1)S(1)}, bf16[1,2048,768]{2,1,0:T(8,128)(2,1)}, u32[]{:S(2)}) copy-start(bf16[1,2048,768]{2,1,0:T(8,128)(2,1)} %refs_0_.1) | copy-start | bytes 9437188
  11.0 1.9 %copy-start.1 = (bf16[1,2048,768]{2,1,0:T(8,128)(2,1)S(1)}, bf16[1,2048,768]{2,1,0:T(8,128)(2,1)}, u32[]{:S(2)}) copy-start(bf16[1,2048,768]{2,1,0:T(8,128)(2,1)} %refs_1_.1) | copy-start | bytes 9437188
  12.9 1.9 %copy-start.2 = (bf16[1,768,2048]{2,1,0:T(8,128)(2,1)S(1)}, bf16[1,768,2048]{2,1,0:T(8,128)(2,1)}, u32[]{:S(2)}) copy-start(bf16[1,768,2048]{2,1,0:T(8,128)(2,1)} %refs_2_.1) | copy-start | bytes 9437188
  19.9 3.0 %collective-permute-start.5 = (bf16[192,2176]{1,0:T(8,128)(2,1)S(1)}, bf16[192,2176]{1,0:T(8,128)(2,1)S(1)}, u32[]{:S(2)}, u32[]{:S(2)}) collective-permute-start(bf16[192,2176]{1,0:T(8,128)(2,1)S(1)} %shard_map.85), channel_id=1, source_target_pairs={{0,1},{1,0},{2,3},{3,2},{4,5},{5,4},{6,7},{7,6},{8,9},{9,8},{10,11... | collective-permute-start | bytes 2506760 | tf_op jit(solution)/shard_map/ppermute | solution.py:254
  20.5 8.8 %collective-permute-start.4 = (bf16[64,2176]{1,0:T(8,128)(2,1)S(1)}, bf16[64,2176]{1,0:T(8,128)(2,1)S(1)}, u32[]{:S(2)}, u32[]{:S(2)}) collective-permute-start(bf16[64,2176]{1,0:T(8,128)(2,1)S(1)} %collective-permute-done.refs_1_.refs_0_), channel_id=1, source_target_pairs={{0,4},{1,3},{2,6},{3,1},{4,0},{5,7},{6,2},{7,5},{8,12},{9,11},{10,... | collective-permute-start | bytes 835592 | tf_op jit(solution)/shard_map/ppermute | solution.py:250
  20.8 10.7 %collective-permute-start.6 = (bf16[64,2176]{1,0:T(8,128)(2,1)S(1)}, bf16[64,2176]{1,0:T(8,128)(2,1)S(1)}, u32[]{:S(2)}, u32[]{:S(2)}) collective-permute-start(bf16[64,2176]{1,0:T(8,128)(2,1)S(1)} %collective-permute-done.refs_1_.refs_0_), channel_id=1, source_target_pairs={{0,2},{1,5},{2,0},{3,7},{4,6},{5,1},{6,4},{7,3},{8,10},{9,13},{10,... | collective-permute-start | bytes 835592 | tf_op jit(solution)/shard_map/ppermute | solution.py:250
  22.4 10.0 %collective-permute-start.7 = (bf16[64,2176]{1,0:T(8,128)(2,1)S(1)}, bf16[64,2176]{1,0:T(8,128)(2,1)S(1)}, u32[]{:S(2)}, u32[]{:S(2)}) collective-permute-start(bf16[64,2176]{1,0:T(8,128)(2,1)S(1)} %collective-permute-done.2.refs_2_.refs_1_), channel_id=1, source_target_pairs={{0,2},{1,5},{2,0},{3,7},{4,6},{5,1},{6,4},{7,3},{8,10},{9,13},{10,... | collective-permute-start | bytes 835592 | tf_op jit(solution)/shard_map/ppermute | solution.py:250
  29.3 6.8 %collective-permute-start.8 = (bf16[64,2176]{1,0:T(8,128)(2,1)S(1)}, bf16[64,2176]{1,0:T(8,128)(2,1)S(1)}, u32[]{:S(2)}, u32[]{:S(2)}) collective-permute-start(bf16[64,2176]{1,0:T(8,128)(2,1)S(1)} %collective-permute-done.4.refs_0_.refs_4_), channel_id=1, source_target_pairs={{0,2},{1,5},{2,0},{3,7},{4,6},{5,1},{6,4},{7,3},{8,10},{9,13},{10,... | collective-permute-start | bytes 835592 | tf_op jit(solution)/shard_map/ppermute | solution.py:250
  36.2 2.8 %collective-permute-start.9 = (bf16[256,2176]{1,0:T(8,128)(2,1)S(1)}, bf16[256,2176]{1,0:T(8,128)(2,1)S(1)}, u32[]{:S(2)}, u32[]{:S(2)}) collective-permute-start(bf16[256,2176]{1,0:T(8,128)(2,1)S(1)} %shard_map.87), channel_id=1, source_target_pairs={{0,1},{1,0},{2,3},{3,2},{4,5},{5,4},{6,7},{7,6},{8,9},{9,8},{10,11... | collective-permute-start | bytes 3342344 | tf_op jit(solution)/shard_map/ppermute | solution.py:254
  38.9 3.3 %copy-start.3 = (bf16[64,2176]{1,0:T(8,128)(2,1)S(1)}, bf16[64,2176]{1,0:T(8,128)(2,1)}, u32[]{:S(2)}) copy-start(bf16[64,2176]{1,0:T(8,128)(2,1)} %shard_map.82.refs_0_) | copy-start | bytes 835588
  38.9 3.3 %copy-start.4 = (s32[16]{0:T(128)S(1)}, s32[16]{0:T(128)}, u32[]{:S(2)}) copy-start(s32[16]{0:T(128)} %capacity_ref.1) | copy-start | bytes 196
  41.6 2.8 %collective-permute-start.10 = (bf16[256,2048]{1,0:T(8,128)(2,1)S(1)}, bf16[256,2048]{1,0:T(8,128)(2,1)S(1)}, u32[]{:S(2)}, u32[]{:S(2)}) collective-permute-start(bf16[256,2048]{1,0:T(8,128)(2,1)S(1)} %shard_map.89), channel_id=1, source_target_pairs={{0,1},{1,0},{2,3},{3,2},{4,5},{5,4},{6,7},{7,6},{8,9},{9,8},{10,11... | collective-permute-start | bytes 3145736 | tf_op jit(solution)/shard_map/ppermute | solution.py:254
  42.1 14.5 %collective-permute-start.12 = (bf16[256,2048]{1,0:T(8,128)(2,1)S(1)}, bf16[256,2048]{1,0:T(8,128)(2,1)S(1)}, u32[]{:S(2)}, u32[]{:S(2)}) collective-permute-start(bf16[256,2048]{1,0:T(8,128)(2,1)S(1)} %shard_map.86), channel_id=1, source_target_pairs={{0,1},{1,0},{2,3},{3,2},{4,5},{5,4},{6,7},{7,6},{8,9},{9,8},{10,11... | collective-permute-start | bytes 3145736 | tf_op jit(solution)/shard_map/ppermute | solution.py:254
  44.7 6.4 %collective-permute-start.11 = (bf16[64,2048]{1,0:T(8,128)(2,1)S(1)}, bf16[64,2048]{1,0:T(8,128)(2,1)S(1)}, u32[]{:S(2)}, u32[]{:S(2)}) collective-permute-start(bf16[64,2048]{1,0:T(8,128)(2,1)S(1)} %get-tuple-element.51), channel_id=1, source_target_pairs={{0,2},{1,5},{2,0},{3,7},{4,6},{5,1},{6,4},{7,3},{8,10},{9,13},{10,... | collective-permute-start | bytes 786440 | tf_op jit(solution)/shard_map/ppermute | solution.py:250
  46.8 10.1 %collective-permute-start.15 = (bf16[64,2048]{1,0:T(8,128)(2,1)S(1)}, bf16[64,2048]{1,0:T(8,128)(2,1)S(1)}, u32[]{:S(2)}, u32[]{:S(2)}) collective-permute-start(bf16[64,2048]{1,0:T(8,128)(2,1)S(1)} %get-tuple-element.57), channel_id=1, source_target_pairs={{0,2},{1,5},{2,0},{3,7},{4,6},{5,1},{6,4},{7,3},{8,10},{9,13},{10,... | collective-permute-start | bytes 786440 | tf_op jit(solution)/shard_map/ppermute | solution.py:250
  51.5 6.4 %collective-permute-start.14 = (bf16[64,2048]{1,0:T(8,128)(2,1)S(1)}, bf16[64,2048]{1,0:T(8,128)(2,1)S(1)}, u32[]{:S(2)}, u32[]{:S(2)}) collective-permute-start(bf16[64,2048]{1,0:T(8,128)(2,1)S(1)} %get-tuple-element.56), channel_id=1, source_target_pairs={{0,4},{1,3},{2,6},{3,1},{4,0},{5,7},{6,2},{7,5},{8,12},{9,11},{10,... | collective-permute-start | bytes 786440 | tf_op jit(solution)/shard_map/ppermute | solution.py:250
  54.5 6.4 %collective-permute-start.13 = (bf16[64,2048]{1,0:T(8,128)(2,1)S(1)}, bf16[64,2048]{1,0:T(8,128)(2,1)S(1)}, u32[]{:S(2)}, u32[]{:S(2)}) collective-permute-start(bf16[64,2048]{1,0:T(8,128)(2,1)S(1)} %get-tuple-element.55), channel_id=1, source_target_pairs={{0,2},{1,5},{2,0},{3,7},{4,6},{5,1},{6,4},{7,3},{8,10},{9,13},{10,... | collective-permute-start | bytes 786440 | tf_op jit(solution)/shard_map/ppermute | solution.py:250
  56.8 6.9 %collective-permute-start.18 = (bf16[64,2048]{1,0:T(8,128)(2,1)S(1)}, bf16[64,2048]{1,0:T(8,128)(2,1)S(1)}, u32[]{:S(2)}, u32[]{:S(2)}) collective-permute-start(bf16[64,2048]{1,0:T(8,128)(2,1)S(1)} %shard_map.93), channel_id=1, source_target_pairs={{0,2},{1,5},{2,0},{3,7},{4,6},{5,1},{6,4},{7,3},{8,10},{9,13},{10,... | collective-permute-start | bytes 786440 | tf_op jit(solution)/shard_map/ppermute | solution.py:250
  58.2 14.2 %collective-permute-start.17 = (bf16[64,2048]{1,0:T(8,128)(2,1)S(1)}, bf16[64,2048]{1,0:T(8,128)(2,1)S(1)}, u32[]{:S(2)}, u32[]{:S(2)}) collective-permute-start(bf16[64,2048]{1,0:T(8,128)(2,1)S(1)} %shard_map.94), channel_id=1, source_target_pairs={{0,8},{1,9},{2,10},{3,11},{4,12},{5,13},{6,14},{7,15},{8,0},{9,1},... | collective-permute-start | bytes 786440 | tf_op jit(solution)/shard_map/ppermute | solution.py:250
  61.2 11.3 %collective-permute-start.16 = (bf16[64,2048]{1,0:T(8,128)(2,1)S(1)}, bf16[64,2048]{1,0:T(8,128)(2,1)S(1)}, u32[]{:S(2)}, u32[]{:S(2)}) collective-permute-start(bf16[64,2048]{1,0:T(8,128)(2,1)S(1)} %shard_map.95), channel_id=1, source_target_pairs={{0,4},{1,3},{2,6},{3,1},{4,0},{5,7},{6,2},{7,5},{8,12},{9,11},{10,... | collective-permute-start | bytes 786440 | tf_op jit(solution)/shard_map/ppermute | solution.py:250

commit v9 on v8

--- a/solution.py
+++ b/solution.py
@@ -66,30 +66,37 @@
         all_ref[at : at + rows, :] = ref[:, wide - LANES :]
         at += rows
     eye = iota((LANES, LANES), 0) == iota((LANES, LANES), 1)
-    lane = iota((LANES, LANES), 1)
+    lane, line = iota((LANES, LANES), 1), iota((LANES, LANES), 0)
     tiles = total // LANES
     mine = tiles // 2
     experts = (me_ref[0], me_ref[0] + 1 - 2 * lax.rem(me_ref[0], 2))
-    worth = jnp.where(lane == 4 * top, float(total), 0.0)
-    worth = jnp.where(lane == 4 * top + 1, float(tok_rows), jnp.where(lane == 4 * top + 2, 1.0, worth))
+
+    def table(values):
+        return values.astype(F32).astype(BF16)
+
+    def times(left, right):
+        return jnp.dot(left, right, preferred_element_type=F32)
+
+    ones = jnp.ones((LANES, LANES), BF16)
+    worth = jnp.where(line == 4 * top, float(total), 0.0)
+    worth = jnp.where(line == 4 * top + 1, float(tok_rows), jnp.where(line == 4 * top + 2, 1.0, worth))
+    worth = table(worth)
+    shift = lane - line
+    spread = table((line < top) & ((shift == top) | (shift == 2 * top) | (shift == 3 * top)))
 
     def read(i, _, own):
-        facts = all_ref[pl.ds(pl.multiple_of(i * LANES, LANES), LANES), :].astype(F32)
-        values = (
-            pltpu.roll(facts, LANES - top, 1)
-            + pltpu.roll(facts, LANES - 2 * top, 1)
-            + pltpu.roll(facts, LANES - 3 * top, 1)
-        )
-        order = jnp.sum(facts * worth, axis=1, keepdims=True)
+        facts = all_ref[pl.ds(pl.multiple_of(i * LANES, LANES), LANES), :]
+        order = times(facts, worth)
         for e, expert in enumerate(experts):
-            named = (lane < top) & (facts == expert.astype(F32))
-            gate = jnp.sum(jnp.where(named, values, 0.0), axis=1, keepdims=True)
+            named = table((lane < top) & (facts.astype(F32) == expert.astype(F32)))
+            parts = (times(named, spread) * facts.astype(F32)).astype(BF16)
+            gate = times(parts, ones)
             key = jnp.where(gate > 0.0, order, BIG)
             row_ref[e, pl.ds(i, 1), :] = jnp.sum(jnp.where(eye, key, 0.0), axis=0, keepdims=True)
             if own:
-                key_ref[e, i] = jnp.broadcast_to(key, (LANES, LANES))
+                key_ref[e, i] = key
                 held = pl.ds(pl.multiple_of((e * mine + i) * LANES, LANES), LANES)
-                out_ref[held, :] = jnp.broadcast_to(gate, (LANES, LANES))
+                out_ref[held, :] = gate
         return 0
 
     lax.fori_loop(0, mine, functools.partial(read, own=True), 0, unroll=min(mine, 4))
@@ -105,7 +112,7 @@
                 return smaller + (row_ref[e, pl.ds(j, 1), :] < key).astype(F32)
 
             smaller = lax.fori_loop(0, tiles, count, jnp.zeros((LANES, LANES), F32), unroll=min(tiles, 8))
-            rank = jnp.sum(smaller, axis=1, keepdims=True)
+            rank = times(smaller.astype(BF16), ones)
             out_ref[held, :] = jnp.where(rank < limit, out_ref[held, :], 0.0)
             return 0
 
@@ -202,8 +209,9 @@
 FF_TILE, OUT_TILE = 256, 512
 
 
-def expert_kernel(*refs):
-    x_refs, (gate_ref, up_ref, down_ref, out_ref, x, hidden) = refs[:-6], refs[-6:]
+def expert_kernel(pieces, *refs):
+    x_refs, (gate_ref, up_ref, down_ref) = refs[: -5 - pieces], refs[-5 - pieces : -2 - pieces]
+    out_refs, (x, hidden) = refs[-2 - pieces : -2], refs[-2:]
     width, ff = x.shape[1], hidden.shape[1]
     at = 0
     for ref in x_refs:
@@ -216,22 +224,26 @@
         hidden[:, lanes] = (gated / (1.0 + jnp.exp(-gated)) * upward).astype(BF16)
     for k in range(width // OUT_TILE):
         lanes = slice(k * OUT_TILE, (k + 1) * OUT_TILE)
-        out_ref[:, lanes] = jnp.dot(hidden[...], down_ref[0, :, lanes], preferred_element_type=F32).astype(BF16)
-
-
-def expert(arrays, matrices):
+        made = jnp.dot(hidden[...], down_ref[0, :, lanes], preferred_element_type=F32).astype(BF16)
+        rows = made.shape[0] // pieces
+        for k, out_ref in enumerate(out_refs):
+            out_ref[:, lanes] = made[k * rows : (k + 1) * rows]
+
+
+def expert(arrays, matrices, pieces=1):
     ff, width = matrices[2].shape[1:]
     rows = sum(a.shape[0] for a in arrays)
     held = rows * 2 * (width + ff) + 4 * rows * (2 * FF_TILE + OUT_TILE)
-    return pl.pallas_call(
-        expert_kernel,
+    made = pl.pallas_call(
+        functools.partial(expert_kernel, pieces),
         in_specs=[pl.BlockSpec(memory_space=pltpu.VMEM)] * (len(arrays) + 3),
-        out_specs=pl.BlockSpec(memory_space=pltpu.VMEM),
-        out_shape=jax.ShapeDtypeStruct((rows, width), BF16),
+        out_specs=[pl.BlockSpec(memory_space=pltpu.VMEM)] * pieces,
+        out_shape=[jax.ShapeDtypeStruct((rows // pieces, width), BF16)] * pieces,
         scratch_shapes=[pltpu.VMEM((rows, width), BF16), pltpu.VMEM((rows, ff), BF16)],
         compiler_params=pltpu.CompilerParams(vmem_limit_bytes=held + 20 * MIB),
         cost_estimate=pl.CostEstimate(flops=1, bytes_accessed=1, transcendentals=0),
     )(*arrays, *matrices)
+    return made if pieces > 1 else made[0]
 
 
 def orders(ep):
@@ -279,22 +291,29 @@
     own3, theirs = lax.optimization_barrier((own3, theirs))
     own7 = send(own3, ep, [-1])
     own3, own5, own6, own7, theirs = lax.optimization_barrier((own3, own5, own6, own7, theirs))
-    far = [own3, own5, own6, own7]
+    far = [own5, own7, own3, own6]
     far_crossed = cross(pack(far))
     far_made = expert(far, matrices)
     far_crossed, far_made = lax.optimization_barrier((far_crossed, far_made))
-    far_back = cross(expert([far_crossed], matrices))
+    first_back, last_back = expert([far_crossed], matrices, 2)
+    first_back = cross(first_back)
     near = [held, own1, own2, own4]
     weights = weigh(me, capacity, near + far + [first, crossed, far_crossed], top, tok_rows)
+    weights, theirs, last_back = lax.optimization_barrier((weights, theirs, last_back))
+    last_back = cross(last_back)
 
     def part(mine, back, block, place):
         return [(mine, block, place), (back, block, 8 + place)]
 
-    send7, send5 = combine([far_made, far_back], weights, [part(0, 1, 3, 7), part(0, 1, 1, 5)])
+    send5, send7 = combine(
+        [far_made, first_back], weights, [[(0, 0, 4), (1, 0, 12)], [(0, 1, 5), (1, 1, 13)]]
+    )
     back7 = send(send7, ep, [-1])
     back5 = send(send5, ep, [-1])
     send3, send6 = combine(
-        [far_made, far_back, back7], weights, [part(0, 1, 0, 4) + [(2, 0, None)], part(0, 1, 2, 6)]
+        [far_made, last_back, back7],
+        weights,
+        [[(0, 2, 6), (1, 0, 14), (2, 0, None)], [(0, 3, 7), (1, 1, 15)]],
     )
     back3 = send(send3, ep, [-2])
     near_made = expert(near, matrices)

time: 73.4 us -> 73.7 us (level)
    ppermute x5 -> x6, starting transfers between devices: 1.3 us -> 1.77 us  [cross(): return lax.ppermute(array, 'sub', [(0, 1), (1, 0)])]
  transfers between devices with their start and end apart: 19 -> 20, of which waited for: 12 -> 12; matrix products, arithmetic and copies ran while one was open for 0% -> 0% of each run, Pallas kernels for 16% -> 17%
where the time goes in v9:
time: 73.7 us; the launch traced here: 73.4 us
  waiting for transfers between devices  28.1 us (38%)
  starting transfers between devices  21.7 us (29%)
  Pallas kernels  17.8 us (24%)
  local copies, waits for them, and re-layouts  5.68 us (8%)
    ppermute x14, waiting for transfers between devices, send(): return lax.ppermute(array, ('ep', 'sub'), pairs)  27.6 us
    ppermute x14, starting transfers between devices, send(): return lax.ppermute(array, ('ep', 'sub'), pairs)  19.9 us
    pallas_call x4, Pallas kernels, expert(): pl.pallas_call(functools.partial(expert_kernel, pieces), in_specs=[pl.Blo...  10.5 us
    unnamed x10, local copies, waits for them, and re-layouts  5.68 us
    pallas_call x8, Pallas kernels, combine(): pl.pallas_call(functools.partial(combine_kernel, rows, sums, len(arrays))...  2.34 us
    pallas_call x1, Pallas kernels, weigh(): pl.pallas_call(functools.partial(weigh_kernel, top, tok_rows), in_specs=[...  2.19 us
    pallas_call x1, Pallas kernels, prepare(): pl.pallas_call(prepare_kernel, in_specs=[pl.BlockSpec(memory_space=pltpu....  1.98 us
    ppermute x6, starting transfers between devices, cross(): return lax.ppermute(array, 'sub', [(0, 1), (1, 0)])  1.77 us
  transfers between devices with their start and end apart: 20, of which 12 were waited for; matrix products, arithmetic and copies ran while one was open for 0% of the time, Pallas kernels for 17%

profile of v9, /device:TPU:0, one launch (start us, length us, event | category | flops | bytes accessed | tf_op | source)
XLA Modules:
  0.0 73.4 jit_solution(5861887609360260361)
XLA Ops:
  0.0 2.0 %shard_map.82.refs_0_ = bf16[64,2176]{1,0:T(8,128)(2,1)} custom-call(s32[1]{0:T(128)} %bitcast.me_ref, bf16[64,2048]{1,0:T(8,128)(2,1)} %tokens_ref.1, s32[8,64]{1,0:T(8,128)} %bitcast.4, f32[8,64]{1,0:T(8,128)} %bitcast.5, s32[1,64]{1,0:T(1,128)} %bitcast.6), custom_call_target="tpu_custom_call" | custom-call | tf_op jit(solution)/shard_map/pallas_call | solution.py:52
  2.0 4.0 %collective-permute-start = (bf16[64,2176]{1,0:T(8,128)(2,1)}, bf16[64,2176]{1,0:T(8,128)(2,1)S(1)}, u32[]{:S(2)}, u32[]{:S(2)}) collective-permute-start(bf16[64,2176]{1,0:T(8,128)(2,1)} %shard_map.82.refs_0_), channel_id=1, source_target_pairs={{0,8},{1,9},{2,10},{3,11},{4,12},{5,13},{6,14},{7,15},{8,0},{9,1},... | collective-permute-start | bytes 835592 | tf_op jit(solution)/shard_map/ppermute | solution.py:262
  6.0 1.6 %collective-permute-start.2 = (bf16[64,2176]{1,0:T(8,128)(2,1)}, bf16[64,2176]{1,0:T(8,128)(2,1)S(1)}, u32[]{:S(2)}, u32[]{:S(2)}) collective-permute-start(bf16[64,2176]{1,0:T(8,128)(2,1)} %shard_map.82.refs_0_), channel_id=1, source_target_pairs={{0,4},{1,3},{2,6},{3,1},{4,0},{5,7},{6,2},{7,5},{8,12},{9,11},{10,... | collective-permute-start | bytes 835592 | tf_op jit(solution)/shard_map/ppermute | solution.py:262
  7.6 1.5 %collective-permute-start.3 = (bf16[64,2176]{1,0:T(8,128)(2,1)}, bf16[64,2176]{1,0:T(8,128)(2,1)S(1)}, u32[]{:S(2)}, u32[]{:S(2)}) collective-permute-start(bf16[64,2176]{1,0:T(8,128)(2,1)} %shard_map.82.refs_0_), channel_id=1, source_target_pairs={{0,2},{1,5},{2,0},{3,7},{4,6},{5,1},{6,4},{7,3},{8,10},{9,13},{10,... | collective-permute-start | bytes 835592 | tf_op jit(solution)/shard_map/ppermute | solution.py:262
  9.1 1.9 %copy-done = bf16[1,2048,768]{2,1,0:T(8,128)(2,1)S(1)} copy-done((bf16[1,2048,768]{2,1,0:T(8,128)(2,1)S(1)}, bf16[1,2048,768]{2,1,0:T(8,128)(2,1)}, u32[]{:S(2)}) %copy-start) | copy-done | bytes 3145752
  11.0 1.9 %copy-done.1 = bf16[1,2048,768]{2,1,0:T(8,128)(2,1)S(1)} copy-done((bf16[1,2048,768]{2,1,0:T(8,128)(2,1)S(1)}, bf16[1,2048,768]{2,1,0:T(8,128)(2,1)}, u32[]{:S(2)}) %copy-start.1) | copy-done | bytes 3145752
  12.9 1.9 %copy-done.2 = bf16[1,768,2048]{2,1,0:T(8,128)(2,1)S(1)} copy-done((bf16[1,768,2048]{2,1,0:T(8,128)(2,1)S(1)}, bf16[1,768,2048]{2,1,0:T(8,128)(2,1)}, u32[]{:S(2)}) %copy-start.2) | copy-done | bytes 3145752
  15.5 3.5 %collective-permute-done.refs_1_.refs_0_ = bf16[64,2176]{1,0:T(8,128)(2,1)S(1)} collective-permute-done((bf16[64,2176]{1,0:T(8,128)(2,1)}, bf16[64,2176]{1,0:T(8,128)(2,1)S(1)}, u32[]{:S(2)}, u32[]{:S(2)}) %collective-permute-start) | collective-permute-done | bytes 278560 | tf_op jit(solution)/shard_map/ppermute | solution.py:262
  20.9 1.5 %collective-permute-start.6 = (bf16[64,2176]{1,0:T(8,128)(2,1)S(1)}, bf16[64,2176]{1,0:T(8,128)(2,1)S(1)}, u32[]{:S(2)}, u32[]{:S(2)}) collective-permute-start(bf16[64,2176]{1,0:T(8,128)(2,1)S(1)} %collective-permute-done.refs_1_.refs_0_), channel_id=1, source_target_pairs={{0,2},{1,5},{2,0},{3,7},{4,6},{5,1},{6,4},{7,3},{8,10},{9,13},{10,... | collective-permute-start | bytes 835592 | tf_op jit(solution)/shard_map/ppermute | solution.py:262
  22.9 2.6 %shard_map.86 = bf16[256,2048]{1,0:T(8,128)(2,1)S(1)} custom-call(bf16[64,2176]{1,0:T(8,128)(2,1)S(1)} %collective-permute-done.1.refs_0_.refs_8_, bf16[192,2176]{1,0:T(8,128)(2,1)S(1)} %collective-permute-done.5.refs_1_.refs_9_, bf16[1,2048,768]{2,1,0:T(8,128)(2,1)S(1)} %get-tuple-element.44.refs_4_.refs_2_.refs_1_, ...), custom_call_target="tpu_custom_call" | custom-call | flops 1 | bytes 1 | tf_op jit(solution)/shard_map/pallas_call | solution.py:237
  25.5 3.8 %collective-permute-done.4.refs_2_.refs_6_ = bf16[64,2176]{1,0:T(8,128)(2,1)S(1)} collective-permute-done((bf16[64,2176]{1,0:T(8,128)(2,1)S(1)}, bf16[64,2176]{1,0:T(8,128)(2,1)S(1)}, u32[]{:S(2)}, u32[]{:S(2)}) %collective-permute-start.4) | collective-permute-done | bytes 278560 | tf_op jit(solution)/shard_map/ppermute | solution.py:262
  29.3 2.3 %collective-permute-start.8 = (bf16[64,2176]{1,0:T(8,128)(2,1)S(1)}, bf16[64,2176]{1,0:T(8,128)(2,1)S(1)}, u32[]{:S(2)}, u32[]{:S(2)}) collective-permute-start(bf16[64,2176]{1,0:T(8,128)(2,1)S(1)} %collective-permute-done.4.refs_2_.refs_6_), channel_id=1, source_target_pairs={{0,2},{1,5},{2,0},{3,7},{4,6},{5,1},{6,4},{7,3},{8,10},{9,13},{10,... | collective-permute-start | bytes 835592 | tf_op jit(solution)/shard_map/ppermute | solution.py:262
  32.4 3.8 %collective-permute-done.8.refs_1_.refs_5_ = bf16[64,2176]{1,0:T(8,128)(2,1)S(1)} collective-permute-done((bf16[64,2176]{1,0:T(8,128)(2,1)S(1)}, bf16[64,2176]{1,0:T(8,128)(2,1)S(1)}, u32[]{:S(2)}, u32[]{:S(2)}) %collective-permute-start.8) | collective-permute-done | bytes 278560 | tf_op jit(solution)/shard_map/ppermute | solution.py:262
  36.3 2.6 %shard_map.88.refs_0_ = bf16[256,2048]{1,0:T(8,128)(2,1)S(1)} custom-call(bf16[64,2176]{1,0:T(8,128)(2,1)S(1)} %collective-permute-done.6.refs_0_.refs_4_, bf16[64,2176]{1,0:T(8,128)(2,1)S(1)} %collective-permute-done.8.refs_1_.refs_5_, bf16[64,2176]{1,0:T(8,128)(2,1)S(1)} %collective-permute-done.4.refs_2_.refs_6_, ...), custom_call_target="tpu_custom_call" | custom-call | flops 1 | bytes 1 | tf_op jit(solution)/shard_map/pallas_call | solution.py:237
  39.0 2.6 %shard_map.90 = (bf16[128,2048]{1,0:T(8,128)(2,1)S(1)}, bf16[128,2048]{1,0:T(8,128)(2,1)S(1)}) custom-call(bf16[256,2176]{1,0:T(8,128)(2,1)S(1)} %collective-permute-done.9.refs_10_.refs_0_, bf16[1,2048,768]{2,1,0:T(8,128)(2,1)S(1)} %get-tuple-element.44.refs_4_.refs_2_.refs_1_, bf16[1,2048,768]{2,1,0:T(8,128)(2,1)S(1)} %get-tuple-element.45.refs_5_.refs_3_.refs_2_, ...), custom_call_target="tpu_custom_call" | custom-call | flops 1 | bytes 1 | tf_op jit(solution)/shard_map/pallas_call | solution.py:237
  42.1 2.2 %shard_map.89.refs_2_.refs_3_.refs_4_ = f32[1024,128]{1,0:T(8,128)S(1)} custom-call(s32[1]{0:T(128)} %bitcast.me_ref, s32[16]{0:T(128)S(1)} %copy-done.4, bf16[64,2176]{1,0:T(8,128)(2,1)S(1)} %copy-done.3, bf16[64,2176]{1,0:T(8,128)(2,1)S(1)} %collective-permute-done.refs_1_.refs_0_, bf16[64,2176]{1,0:T(8,128)(2,1)S(1)} %collective-permute-done.2.refs_2_.refs_1_, ...), custom_call_target="tpu_custom_call" | custom-call | flops 1 | bytes 1 | tf_op jit(solution)/shard_map/pallas_call | solution.py:125
  45.2 2.1 %collective-permute-start.12 = (bf16[64,2048]{1,0:T(8,128)(2,1)S(1)}, bf16[64,2048]{1,0:T(8,128)(2,1)S(1)}, u32[]{:S(2)}, u32[]{:S(2)}) collective-permute-start(bf16[64,2048]{1,0:T(8,128)(2,1)S(1)} %get-tuple-element.61), channel_id=1, source_target_pairs={{0,2},{1,5},{2,0},{3,7},{4,6},{5,1},{6,4},{7,3},{8,10},{9,13},{10,... | collective-permute-start | bytes 786440 | tf_op jit(solution)/shard_map/ppermute | solution.py:262
  47.8 3.9 %collective-permute-done.12.refs_2_ = bf16[64,2048]{1,0:T(8,128)(2,1)S(1)} collective-permute-done((bf16[64,2048]{1,0:T(8,128)(2,1)S(1)}, bf16[64,2048]{1,0:T(8,128)(2,1)S(1)}, u32[]{:S(2)}, u32[]{:S(2)}) %collective-permute-start.12) | collective-permute-done | bytes 262176 | tf_op jit(solution)/shard_map/ppermute | solution.py:262
  52.4 2.6 %shard_map.84.refs_0_ = bf16[256,2048]{1,0:T(8,128)(2,1)S(1)} custom-call(bf16[64,2176]{1,0:T(8,128)(2,1)S(1)} %copy-done.3, bf16[64,2176]{1,0:T(8,128)(2,1)S(1)} %collective-permute-done.refs_1_.refs_0_, bf16[64,2176]{1,0:T(8,128)(2,1)S(1)} %collective-permute-done.2.refs_2_.refs_1_, bf16[64,2176]{1,0:T(8,128)(2,1)S(1)} %collective-permute-done.3.refs_3_.refs_2_, ...), custom_call_target="tpu_custom_call" | custom-call | flops 1 | bytes 1 | tf_op jit(solution)/shard_map/pallas_call | solution.py:237
  55.0 2.1 %collective-permute-start.14 = (bf16[64,2048]{1,0:T(8,128)(2,1)S(1)}, bf16[64,2048]{1,0:T(8,128)(2,1)S(1)}, u32[]{:S(2)}, u32[]{:S(2)}) collective-permute-start(bf16[64,2048]{1,0:T(8,128)(2,1)S(1)} %get-tuple-element.65), channel_id=1, source_target_pairs={{0,2},{1,5},{2,0},{3,7},{4,6},{5,1},{6,4},{7,3},{8,10},{9,13},{10,... | collective-permute-start | bytes 786440 | tf_op jit(solution)/shard_map/ppermute | solution.py:262
  57.4 1.1 %collective-permute-done.15.refs_2_ = bf16[64,2048]{1,0:T(8,128)(2,1)S(1)} collective-permute-done((bf16[64,2048]{1,0:T(8,128)(2,1)S(1)}, bf16[64,2048]{1,0:T(8,128)(2,1)S(1)}, u32[]{:S(2)}, u32[]{:S(2)}) %collective-permute-start.15) | collective-permute-done | bytes 262176 | tf_op jit(solution)/shard_map/ppermute | solution.py:262
  58.8 1.7 %collective-permute-start.18 = (bf16[64,2048]{1,0:T(8,128)(2,1)S(1)}, bf16[64,2048]{1,0:T(8,128)(2,1)S(1)}, u32[]{:S(2)}, u32[]{:S(2)}) collective-permute-start(bf16[64,2048]{1,0:T(8,128)(2,1)S(1)} %shard_map.94), channel_id=1, source_target_pairs={{0,8},{1,9},{2,10},{3,11},{4,12},{5,13},{6,14},{7,15},{8,0},{9,1},... | collective-permute-start | bytes 786440 | tf_op jit(solution)/shard_map/ppermute | solution.py:262
  61.7 1.8 %collective-permute-start.17 = (bf16[64,2048]{1,0:T(8,128)(2,1)S(1)}, bf16[64,2048]{1,0:T(8,128)(2,1)S(1)}, u32[]{:S(2)}, u32[]{:S(2)}) collective-permute-start(bf16[64,2048]{1,0:T(8,128)(2,1)S(1)} %shard_map.95), channel_id=1, source_target_pairs={{0,4},{1,3},{2,6},{3,1},{4,0},{5,7},{6,2},{7,5},{8,12},{9,11},{10,... | collective-permute-start | bytes 786440 | tf_op jit(solution)/shard_map/ppermute | solution.py:262
  64.5 8.1 %collective-permute-done.18.refs_1_ = bf16[64,2048]{1,0:T(8,128)(2,1)S(1)} collective-permute-done((bf16[64,2048]{1,0:T(8,128)(2,1)S(1)}, bf16[64,2048]{1,0:T(8,128)(2,1)S(1)}, u32[]{:S(2)}, u32[]{:S(2)}) %collective-permute-start.18) | collective-permute-done | bytes 262176 | tf_op jit(solution)/shard_map/ppermute | solution.py:262
  (43 shorter events, 10.3 us)
Async XLA Ops:
  2.0 17.0 %collective-permute-start = (bf16[64,2176]{1,0:T(8,128)(2,1)}, bf16[64,2176]{1,0:T(8,128)(2,1)S(1)}, u32[]{:S(2)}, u32[]{:S(2)}) collective-permute-start(bf16[64,2176]{1,0:T(8,128)(2,1)} %shard_map.82.refs_0_), channel_id=1, source_target_pairs={{0,8},{1,9},{2,10},{3,11},{4,12},{5,13},{6,14},{7,15},{8,0},{9,1},... | collective-permute-start | bytes 835592 | tf_op jit(solution)/shard_map/ppermute | solution.py:262
  6.0 12.9 %collective-permute-start.1 = (bf16[64,2176]{1,0:T(8,128)(2,1)}, bf16[64,2176]{1,0:T(8,128)(2,1)S(1)}, u32[]{:S(2)}, u32[]{:S(2)}) collective-permute-start(bf16[64,2176]{1,0:T(8,128)(2,1)} %shard_map.82.refs_0_), channel_id=1, source_target_pairs={{0,1},{1,0},{2,3},{3,2},{4,5},{5,4},{6,7},{7,6},{8,9},{9,8},{10,11... | collective-permute-start | bytes 835592 | tf_op jit(solution)/shard_map/ppermute | solution.py:266
  6.0 13.8 %collective-permute-start.2 = (bf16[64,2176]{1,0:T(8,128)(2,1)}, bf16[64,2176]{1,0:T(8,128)(2,1)S(1)}, u32[]{:S(2)}, u32[]{:S(2)}) collective-permute-start(bf16[64,2176]{1,0:T(8,128)(2,1)} %shard_map.82.refs_0_), channel_id=1, source_target_pairs={{0,4},{1,3},{2,6},{3,1},{4,0},{5,7},{6,2},{7,5},{8,12},{9,11},{10,... | collective-permute-start | bytes 835592 | tf_op jit(solution)/shard_map/ppermute | solution.py:262
  7.6 12.2 %collective-permute-start.3 = (bf16[64,2176]{1,0:T(8,128)(2,1)}, bf16[64,2176]{1,0:T(8,128)(2,1)S(1)}, u32[]{:S(2)}, u32[]{:S(2)}) collective-permute-start(bf16[64,2176]{1,0:T(8,128)(2,1)} %shard_map.82.refs_0_), channel_id=1, source_target_pairs={{0,2},{1,5},{2,0},{3,7},{4,6},{5,1},{6,4},{7,3},{8,10},{9,13},{10,... | collective-permute-start | bytes 835592 | tf_op jit(solution)/shard_map/ppermute | solution.py:262
  9.1 1.9 %copy-start = (bf16[1,2048,768]{2,1,0:T(8,128)(2,1)S(1)}, bf16[1,2048,768]{2,1,0:T(8,128)(2,1)}, u32[]{:S(2)}) copy-start(bf16[1,2048,768]{2,1,0:T(8,128)(2,1)} %refs_0_.1) | copy-start | bytes 9437188
  11.0 1.9 %copy-start.1 = (bf16[1,2048,768]{2,1,0:T(8,128)(2,1)S(1)}, bf16[1,2048,768]{2,1,0:T(8,128)(2,1)}, u32[]{:S(2)}) copy-start(bf16[1,2048,768]{2,1,0:T(8,128)(2,1)} %refs_1_.1) | copy-start | bytes 9437188
  19.9 3.0 %collective-permute-start.5 = (bf16[192,2176]{1,0:T(8,128)(2,1)S(1)}, bf16[192,2176]{1,0:T(8,128)(2,1)S(1)}, u32[]{:S(2)}, u32[]{:S(2)}) collective-permute-start(bf16[192,2176]{1,0:T(8,128)(2,1)S(1)} %shard_map.85), channel_id=1, source_target_pairs={{0,1},{1,0},{2,3},{3,2},{4,5},{5,4},{6,7},{7,6},{8,9},{9,8},{10,11... | collective-permute-start | bytes 2506760 | tf_op jit(solution)/shard_map/ppermute | solution.py:266
  20.5 8.8 %collective-permute-start.4 = (bf16[64,2176]{1,0:T(8,128)(2,1)S(1)}, bf16[64,2176]{1,0:T(8,128)(2,1)S(1)}, u32[]{:S(2)}, u32[]{:S(2)}) collective-permute-start(bf16[64,2176]{1,0:T(8,128)(2,1)S(1)} %collective-permute-done.refs_1_.refs_0_), channel_id=1, source_target_pairs={{0,4},{1,3},{2,6},{3,1},{4,0},{5,7},{6,2},{7,5},{8,12},{9,11},{10,... | collective-permute-start | bytes 835592 | tf_op jit(solution)/shard_map/ppermute | solution.py:262
  20.9 10.7 %collective-permute-start.6 = (bf16[64,2176]{1,0:T(8,128)(2,1)S(1)}, bf16[64,2176]{1,0:T(8,128)(2,1)S(1)}, u32[]{:S(2)}, u32[]{:S(2)}) collective-permute-start(bf16[64,2176]{1,0:T(8,128)(2,1)S(1)} %collective-permute-done.refs_1_.refs_0_), channel_id=1, source_target_pairs={{0,2},{1,5},{2,0},{3,7},{4,6},{5,1},{6,4},{7,3},{8,10},{9,13},{10,... | collective-permute-start | bytes 835592 | tf_op jit(solution)/shard_map/ppermute | solution.py:262
  22.4 10.0 %collective-permute-start.7 = (bf16[64,2176]{1,0:T(8,128)(2,1)S(1)}, bf16[64,2176]{1,0:T(8,128)(2,1)S(1)}, u32[]{:S(2)}, u32[]{:S(2)}) collective-permute-start(bf16[64,2176]{1,0:T(8,128)(2,1)S(1)} %collective-permute-done.2.refs_2_.refs_1_), channel_id=1, source_target_pairs={{0,2},{1,5},{2,0},{3,7},{4,6},{5,1},{6,4},{7,3},{8,10},{9,13},{10,... | collective-permute-start | bytes 835592 | tf_op jit(solution)/shard_map/ppermute | solution.py:262
  29.3 6.8 %collective-permute-start.8 = (bf16[64,2176]{1,0:T(8,128)(2,1)S(1)}, bf16[64,2176]{1,0:T(8,128)(2,1)S(1)}, u32[]{:S(2)}, u32[]{:S(2)}) collective-permute-start(bf16[64,2176]{1,0:T(8,128)(2,1)S(1)} %collective-permute-done.4.refs_2_.refs_6_), channel_id=1, source_target_pairs={{0,2},{1,5},{2,0},{3,7},{4,6},{5,1},{6,4},{7,3},{8,10},{9,13},{10,... | collective-permute-start | bytes 835592 | tf_op jit(solution)/shard_map/ppermute | solution.py:262
  36.2 2.8 %collective-permute-start.9 = (bf16[256,2176]{1,0:T(8,128)(2,1)S(1)}, bf16[256,2176]{1,0:T(8,128)(2,1)S(1)}, u32[]{:S(2)}, u32[]{:S(2)}) collective-permute-start(bf16[256,2176]{1,0:T(8,128)(2,1)S(1)} %shard_map.87), channel_id=1, source_target_pairs={{0,1},{1,0},{2,3},{3,2},{4,5},{5,4},{6,7},{7,6},{8,9},{9,8},{10,11... | collective-permute-start | bytes 3342344 | tf_op jit(solution)/shard_map/ppermute | solution.py:266
  38.9 3.2 %copy-start.3 = (bf16[64,2176]{1,0:T(8,128)(2,1)S(1)}, bf16[64,2176]{1,0:T(8,128)(2,1)}, u32[]{:S(2)}) copy-start(bf16[64,2176]{1,0:T(8,128)(2,1)} %shard_map.82.refs_0_) | copy-start | bytes 835588
  38.9 3.2 %copy-start.4 = (s32[16]{0:T(128)S(1)}, s32[16]{0:T(128)}, u32[]{:S(2)}) copy-start(s32[16]{0:T(128)} %capacity_ref.1) | copy-start | bytes 196
  41.6 3.3 %collective-permute-start.11 = (bf16[128,2048]{1,0:T(8,128)(2,1)S(1)}, bf16[128,2048]{1,0:T(8,128)(2,1)S(1)}, u32[]{:S(2)}, u32[]{:S(2)}) collective-permute-start(bf16[128,2048]{1,0:T(8,128)(2,1)S(1)} %get-tuple-element.59), channel_id=1, source_target_pairs={{0,1},{1,0},{2,3},{3,2},{4,5},{5,4},{6,7},{7,6},{8,9},{9,8},{10,11... | collective-permute-start | bytes 1572872 | tf_op jit(solution)/shard_map/ppermute | solution.py:266
  44.3 12.8 %collective-permute-start.13 = (bf16[256,2048]{1,0:T(8,128)(2,1)S(1)}, bf16[256,2048]{1,0:T(8,128)(2,1)S(1)}, u32[]{:S(2)}, u32[]{:S(2)}) collective-permute-start(bf16[256,2048]{1,0:T(8,128)(2,1)S(1)} %shard_map.86), channel_id=1, source_target_pairs={{0,1},{1,0},{2,3},{3,2},{4,5},{5,4},{6,7},{7,6},{8,9},{9,8},{10,11... | collective-permute-start | bytes 3145736 | tf_op jit(solution)/shard_map/ppermute | solution.py:266
  44.5 3.3 %collective-permute-start.10 = (bf16[128,2048]{1,0:T(8,128)(2,1)S(1)}, bf16[128,2048]{1,0:T(8,128)(2,1)S(1)}, u32[]{:S(2)}, u32[]{:S(2)}) collective-permute-start(bf16[128,2048]{1,0:T(8,128)(2,1)S(1)} %get-tuple-element.58), channel_id=1, source_target_pairs={{0,1},{1,0},{2,3},{3,2},{4,5},{5,4},{6,7},{7,6},{8,9},{9,8},{10,11... | collective-permute-start | bytes 1572872 | tf_op jit(solution)/shard_map/ppermute | solution.py:266
  45.2 6.4 %collective-permute-start.12 = (bf16[64,2048]{1,0:T(8,128)(2,1)S(1)}, bf16[64,2048]{1,0:T(8,128)(2,1)S(1)}, u32[]{:S(2)}, u32[]{:S(2)}) collective-permute-start(bf16[64,2048]{1,0:T(8,128)(2,1)S(1)} %get-tuple-element.61), channel_id=1, source_target_pairs={{0,2},{1,5},{2,0},{3,7},{4,6},{5,1},{6,4},{7,3},{8,10},{9,13},{10,... | collective-permute-start | bytes 786440 | tf_op jit(solution)/shard_map/ppermute | solution.py:262
  47.3 10.1 %collective-permute-start.16 = (bf16[64,2048]{1,0:T(8,128)(2,1)S(1)}, bf16[64,2048]{1,0:T(8,128)(2,1)S(1)}, u32[]{:S(2)}, u32[]{:S(2)}) collective-permute-start(bf16[64,2048]{1,0:T(8,128)(2,1)S(1)} %get-tuple-element.67), channel_id=1, source_target_pairs={{0,2},{1,5},{2,0},{3,7},{4,6},{5,1},{6,4},{7,3},{8,10},{9,13},{10,... | collective-permute-start | bytes 786440 | tf_op jit(solution)/shard_map/ppermute | solution.py:262
  52.0 6.5 %collective-permute-start.15 = (bf16[64,2048]{1,0:T(8,128)(2,1)S(1)}, bf16[64,2048]{1,0:T(8,128)(2,1)S(1)}, u32[]{:S(2)}, u32[]{:S(2)}) collective-permute-start(bf16[64,2048]{1,0:T(8,128)(2,1)S(1)} %get-tuple-element.66), channel_id=1, source_target_pairs={{0,4},{1,3},{2,6},{3,1},{4,0},{5,7},{6,2},{7,5},{8,12},{9,11},{10,... | collective-permute-start | bytes 786440 | tf_op jit(solution)/shard_map/ppermute | solution.py:262
  55.0 6.4 %collective-permute-start.14 = (bf16[64,2048]{1,0:T(8,128)(2,1)S(1)}, bf16[64,2048]{1,0:T(8,128)(2,1)S(1)}, u32[]{:S(2)}, u32[]{:S(2)}) collective-permute-start(bf16[64,2048]{1,0:T(8,128)(2,1)S(1)} %get-tuple-element.65), channel_id=1, source_target_pairs={{0,2},{1,5},{2,0},{3,7},{4,6},{5,1},{6,4},{7,3},{8,10},{9,13},{10,... | collective-permute-start | bytes 786440 | tf_op jit(solution)/shard_map/ppermute | solution.py:262
  57.3 6.9 %collective-permute-start.19 = (bf16[64,2048]{1,0:T(8,128)(2,1)S(1)}, bf16[64,2048]{1,0:T(8,128)(2,1)S(1)}, u32[]{:S(2)}, u32[]{:S(2)}) collective-permute-start(bf16[64,2048]{1,0:T(8,128)(2,1)S(1)} %shard_map.93), channel_id=1, source_target_pairs={{0,2},{1,5},{2,0},{3,7},{4,6},{5,1},{6,4},{7,3},{8,10},{9,13},{10,... | collective-permute-start | bytes 786440 | tf_op jit(solution)/shard_map/ppermute | solution.py:262
  58.8 13.8 %collective-permute-start.18 = (bf16[64,2048]{1,0:T(8,128)(2,1)S(1)}, bf16[64,2048]{1,0:T(8,128)(2,1)S(1)}, u32[]{:S(2)}, u32[]{:S(2)}) collective-permute-start(bf16[64,2048]{1,0:T(8,128)(2,1)S(1)} %shard_map.94), channel_id=1, source_target_pairs={{0,8},{1,9},{2,10},{3,11},{4,12},{5,13},{6,14},{7,15},{8,0},{9,1},... | collective-permute-start | bytes 786440 | tf_op jit(solution)/shard_map/ppermute | solution.py:262
  61.7 11.0 %collective-permute-start.17 = (bf16[64,2048]{1,0:T(8,128)(2,1)S(1)}, bf16[64,2048]{1,0:T(8,128)(2,1)S(1)}, u32[]{:S(2)}, u32[]{:S(2)}) collective-permute-start(bf16[64,2048]{1,0:T(8,128)(2,1)S(1)} %shard_map.95), channel_id=1, source_target_pairs={{0,4},{1,3},{2,6},{3,1},{4,0},{5,7},{6,2},{7,5},{8,12},{9,11},{10,... | collective-permute-start | bytes 786440 | tf_op jit(solution)/shard_map/ppermute | solution.py:262
  (1 other events, 1.9 us)

commit v10 on v8

--- a/solution.py
+++ b/solution.py
@@ -202,8 +202,9 @@
 FF_TILE, OUT_TILE = 256, 512
 
 
-def expert_kernel(*refs):
-    x_refs, (gate_ref, up_ref, down_ref, out_ref, x, hidden) = refs[:-6], refs[-6:]
+def expert_kernel(pieces, *refs):
+    x_refs, (gate_ref, up_ref, down_ref) = refs[: -5 - pieces], refs[-5 - pieces : -2 - pieces]
+    out_refs, (x, hidden) = refs[-2 - pieces : -2], refs[-2:]
     width, ff = x.shape[1], hidden.shape[1]
     at = 0
     for ref in x_refs:
@@ -216,22 +217,26 @@
         hidden[:, lanes] = (gated / (1.0 + jnp.exp(-gated)) * upward).astype(BF16)
     for k in range(width // OUT_TILE):
         lanes = slice(k * OUT_TILE, (k + 1) * OUT_TILE)
-        out_ref[:, lanes] = jnp.dot(hidden[...], down_ref[0, :, lanes], preferred_element_type=F32).astype(BF16)
-
-
-def expert(arrays, matrices):
+        made = jnp.dot(hidden[...], down_ref[0, :, lanes], preferred_element_type=F32).astype(BF16)
+        rows = made.shape[0] // pieces
+        for k, out_ref in enumerate(out_refs):
+            out_ref[:, lanes] = made[k * rows : (k + 1) * rows]
+
+
+def expert(arrays, matrices, pieces=1):
     ff, width = matrices[2].shape[1:]
     rows = sum(a.shape[0] for a in arrays)
     held = rows * 2 * (width + ff) + 4 * rows * (2 * FF_TILE + OUT_TILE)
-    return pl.pallas_call(
-        expert_kernel,
+    made = pl.pallas_call(
+        functools.partial(expert_kernel, pieces),
         in_specs=[pl.BlockSpec(memory_space=pltpu.VMEM)] * (len(arrays) + 3),
-        out_specs=pl.BlockSpec(memory_space=pltpu.VMEM),
-        out_shape=jax.ShapeDtypeStruct((rows, width), BF16),
+        out_specs=[pl.BlockSpec(memory_space=pltpu.VMEM)] * pieces,
+        out_shape=[jax.ShapeDtypeStruct((rows // pieces, width), BF16)] * pieces,
         scratch_shapes=[pltpu.VMEM((rows, width), BF16), pltpu.VMEM((rows, ff), BF16)],
         compiler_params=pltpu.CompilerParams(vmem_limit_bytes=held + 20 * MIB),
         cost_estimate=pl.CostEstimate(flops=1, bytes_accessed=1, transcendentals=0),
     )(*arrays, *matrices)
+    return made if pieces > 1 else made[0]
 
 
 def orders(ep):
@@ -278,23 +283,31 @@
     theirs = expert([first, crossed], matrices)
     own3, theirs = lax.optimization_barrier((own3, theirs))
     own7 = send(own3, ep, [-1])
-    own3, own5, own6, own7, theirs = lax.optimization_barrier((own3, own5, own6, own7, theirs))
-    far = [own3, own5, own6, own7]
+    far_made = expert([own3, own5, own6], matrices)
+    own3, own5, own6, own7, theirs, far_made = lax.optimization_barrier((own3, own5, own6, own7, theirs, far_made))
+    far = [own5, own7, own3, own6]
     far_crossed = cross(pack(far))
-    far_made = expert(far, matrices)
-    far_crossed, far_made = lax.optimization_barrier((far_crossed, far_made))
-    far_back = cross(expert([far_crossed], matrices))
+    last_made = expert([own7], matrices)
+    far_crossed, last_made = lax.optimization_barrier((far_crossed, last_made))
+    first_back, last_back = expert([far_crossed], matrices, 2)
+    first_back = cross(first_back)
     near = [held, own1, own2, own4]
     weights = weigh(me, capacity, near + far + [first, crossed, far_crossed], top, tok_rows)
+    weights, theirs, last_back = lax.optimization_barrier((weights, theirs, last_back))
+    last_back = cross(last_back)
 
     def part(mine, back, block, place):
         return [(mine, block, place), (back, block, 8 + place)]
 
-    send7, send5 = combine([far_made, far_back], weights, [part(0, 1, 3, 7), part(0, 1, 1, 5)])
+    send5, send7 = combine(
+        [far_made, last_made, first_back], weights, [[(0, 1, 4), (2, 0, 12)], [(1, 0, 5), (2, 1, 13)]]
+    )
     back7 = send(send7, ep, [-1])
     back5 = send(send5, ep, [-1])
     send3, send6 = combine(
-        [far_made, far_back, back7], weights, [part(0, 1, 0, 4) + [(2, 0, None)], part(0, 1, 2, 6)]
+        [far_made, last_back, back7],
+        weights,
+        [[(0, 0, 6), (1, 0, 14), (2, 0, None)], [(0, 2, 7), (1, 1, 15)]],
     )
     back3 = send(send3, ep, [-2])
     near_made = expert(near, matrices)

time: 73.4 us -> 73.4 us (level)
  waiting for transfers between devices: 28.6 us -> 27.2 us
  Pallas kernels: 17.5 us -> 18.6 us
    ppermute x14, waiting for transfers between devices: 28.2 us -> 25.9 us  [send(): return lax.ppermute(array, ('ep', 'sub'), pairs)]
    pallas_call x4 -> x5, Pallas kernels: 10.5 us -> 11.6 us  [expert(): pl.pallas_call(functools.partial(expert_kernel, pieces), in_specs=[pl.Blo...]
    ppermute x5 -> x6, waiting for transfers between devices: 0.38 us -> 1.33 us  [cross(): return lax.ppermute(array, 'sub', [(0, 1), (1, 0)])]
    ppermute x5 -> x6, starting transfers between devices: 1.3 us -> 1.5 us  [cross(): return lax.ppermute(array, 'sub', [(0, 1), (1, 0)])]
  transfers between devices with their start and end apart: 19 -> 20, of which waited for: 12 -> 12; matrix products, arithmetic and copies ran while one was open for 0% -> 0% of each run, Pallas kernels for 16% -> 18%
where the time goes in v10:
time: 73.4 us; the launch traced here: 73.1 us
  waiting for transfers between devices  27.2 us (37%)
  starting transfers between devices  21.5 us (29%)
  Pallas kernels  18.6 us (25%)
  local copies, waits for them, and re-layouts  5.68 us (8%)
    ppermute x14, waiting for transfers between devices, send(): return lax.ppermute(array, ('ep', 'sub'), pairs)  25.9 us
    ppermute x14, starting transfers between devices, send(): return lax.ppermute(array, ('ep', 'sub'), pairs)  20 us
    pallas_call x5, Pallas kernels, expert(): pl.pallas_call(functools.partial(expert_kernel, pieces), in_specs=[pl.Blo...  11.6 us
    unnamed x10, local copies, waits for them, and re-layouts  5.68 us
    pallas_call x8, Pallas kernels, combine(): pl.pallas_call(functools.partial(combine_kernel, rows, sums, len(arrays))...  2.34 us
    pallas_call x1, Pallas kernels, prepare(): pl.pallas_call(prepare_kernel, in_specs=[pl.BlockSpec(memory_space=pltpu....  1.98 us
    pallas_call x1, Pallas kernels, weigh(): pl.pallas_call(functools.partial(weigh_kernel, top, tok_rows), in_specs=[...  1.89 us
    ppermute x6, starting transfers between devices, cross(): return lax.ppermute(array, 'sub', [(0, 1), (1, 0)])  1.5 us
  transfers between devices with their start and end apart: 20, of which 12 were waited for; matrix products, arithmetic and copies ran while one was open for 0% of the time, Pallas kernels for 18%

profile of v10, /device:TPU:0, one launch (start us, length us, event | category | flops | bytes accessed | tf_op | source)
XLA Modules:
  0.0 73.1 jit_solution(10174015512567791518)
XLA Ops:
  0.0 2.0 %shard_map.82.refs_0_ = bf16[64,2176]{1,0:T(8,128)(2,1)} custom-call(s32[1]{0:T(128)} %bitcast.me_ref, bf16[64,2048]{1,0:T(8,128)(2,1)} %tokens_ref.1, s32[8,64]{1,0:T(8,128)} %bitcast.4, f32[8,64]{1,0:T(8,128)} %bitcast.5, s32[1,64]{1,0:T(1,128)} %bitcast.6), custom_call_target="tpu_custom_call" | custom-call | tf_op jit(solution)/shard_map/pallas_call | solution.py:52
  2.0 4.0 %collective-permute-start = (bf16[64,2176]{1,0:T(8,128)(2,1)}, bf16[64,2176]{1,0:T(8,128)(2,1)S(1)}, u32[]{:S(2)}, u32[]{:S(2)}) collective-permute-start(bf16[64,2176]{1,0:T(8,128)(2,1)} %shard_map.82.refs_0_), channel_id=1, source_target_pairs={{0,8},{1,9},{2,10},{3,11},{4,12},{5,13},{6,14},{7,15},{8,0},{9,1},... | collective-permute-start | bytes 835592 | tf_op jit(solution)/shard_map/ppermute | solution.py:255
  6.0 1.6 %collective-permute-start.2 = (bf16[64,2176]{1,0:T(8,128)(2,1)}, bf16[64,2176]{1,0:T(8,128)(2,1)S(1)}, u32[]{:S(2)}, u32[]{:S(2)}) collective-permute-start(bf16[64,2176]{1,0:T(8,128)(2,1)} %shard_map.82.refs_0_), channel_id=1, source_target_pairs={{0,4},{1,3},{2,6},{3,1},{4,0},{5,7},{6,2},{7,5},{8,12},{9,11},{10,... | collective-permute-start | bytes 835592 | tf_op jit(solution)/shard_map/ppermute | solution.py:255
  7.6 1.5 %collective-permute-start.3 = (bf16[64,2176]{1,0:T(8,128)(2,1)}, bf16[64,2176]{1,0:T(8,128)(2,1)S(1)}, u32[]{:S(2)}, u32[]{:S(2)}) collective-permute-start(bf16[64,2176]{1,0:T(8,128)(2,1)} %shard_map.82.refs_0_), channel_id=1, source_target_pairs={{0,2},{1,5},{2,0},{3,7},{4,6},{5,1},{6,4},{7,3},{8,10},{9,13},{10,... | collective-permute-start | bytes 835592 | tf_op jit(solution)/shard_map/ppermute | solution.py:255
  9.1 1.9 %copy-done = bf16[1,2048,768]{2,1,0:T(8,128)(2,1)S(1)} copy-done((bf16[1,2048,768]{2,1,0:T(8,128)(2,1)S(1)}, bf16[1,2048,768]{2,1,0:T(8,128)(2,1)}, u32[]{:S(2)}) %copy-start) | copy-done | bytes 3145752
  11.0 1.9 %copy-done.1 = bf16[1,2048,768]{2,1,0:T(8,128)(2,1)S(1)} copy-done((bf16[1,2048,768]{2,1,0:T(8,128)(2,1)S(1)}, bf16[1,2048,768]{2,1,0:T(8,128)(2,1)}, u32[]{:S(2)}) %copy-start.1) | copy-done | bytes 3145752
  12.9 1.9 %copy-done.2 = bf16[1,768,2048]{2,1,0:T(8,128)(2,1)S(1)} copy-done((bf16[1,768,2048]{2,1,0:T(8,128)(2,1)S(1)}, bf16[1,768,2048]{2,1,0:T(8,128)(2,1)}, u32[]{:S(2)}) %copy-start.2) | copy-done | bytes 3145752
  15.5 3.5 %collective-permute-done.refs_1_.refs_0_ = bf16[64,2176]{1,0:T(8,128)(2,1)S(1)} collective-permute-done((bf16[64,2176]{1,0:T(8,128)(2,1)}, bf16[64,2176]{1,0:T(8,128)(2,1)S(1)}, u32[]{:S(2)}, u32[]{:S(2)}) %collective-permute-start) | collective-permute-done | bytes 278560 | tf_op jit(solution)/shard_map/ppermute | solution.py:255
  20.9 1.5 %collective-permute-start.6 = (bf16[64,2176]{1,0:T(8,128)(2,1)S(1)}, bf16[64,2176]{1,0:T(8,128)(2,1)S(1)}, u32[]{:S(2)}, u32[]{:S(2)}) collective-permute-start(bf16[64,2176]{1,0:T(8,128)(2,1)S(1)} %collective-permute-done.refs_1_.refs_0_), channel_id=1, source_target_pairs={{0,2},{1,5},{2,0},{3,7},{4,6},{5,1},{6,4},{7,3},{8,10},{9,13},{10,... | collective-permute-start | bytes 835592 | tf_op jit(solution)/shard_map/ppermute | solution.py:255
  22.9 2.6 %shard_map.86 = bf16[256,2048]{1,0:T(8,128)(2,1)S(1)} custom-call(bf16[64,2176]{1,0:T(8,128)(2,1)S(1)} %collective-permute-done.1.refs_0_.refs_8_, bf16[192,2176]{1,0:T(8,128)(2,1)S(1)} %collective-permute-done.5.refs_1_.refs_9_, bf16[1,2048,768]{2,1,0:T(8,128)(2,1)S(1)} %get-tuple-element.45.refs_4_.refs_2_.refs_3_.refs_1_, ...), custom_call_target="tpu_custom_call" | custom-call | flops 1 | bytes 1 | tf_op jit(solution)/shard_map/pallas_call | solution.py:230
  25.5 3.8 %collective-permute-done.4.refs_0_.refs_2_.refs_6_ = bf16[64,2176]{1,0:T(8,128)(2,1)S(1)} collective-permute-done((bf16[64,2176]{1,0:T(8,128)(2,1)S(1)}, bf16[64,2176]{1,0:T(8,128)(2,1)S(1)}, u32[]{:S(2)}, u32[]{:S(2)}) %collective-permute-start.4) | collective-permute-done | bytes 278560 | tf_op jit(solution)/shard_map/ppermute | solution.py:255
  29.3 2.3 %collective-permute-start.8 = (bf16[64,2176]{1,0:T(8,128)(2,1)S(1)}, bf16[64,2176]{1,0:T(8,128)(2,1)S(1)}, u32[]{:S(2)}, u32[]{:S(2)}) collective-permute-start(bf16[64,2176]{1,0:T(8,128)(2,1)S(1)} %collective-permute-done.4.refs_0_.refs_2_.refs_6_), channel_id=1, source_target_pairs={{0,2},{1,5},{2,0},{3,7},{4,6},{5,1},{6,4},{7,3},{8,10},{9,13},{10,... | collective-permute-start | bytes 835592 | tf_op jit(solution)/shard_map/ppermute | solution.py:255
  32.4 2.0 %shard_map.87.refs_0_ = bf16[192,2048]{1,0:T(8,128)(2,1)S(1)} custom-call(bf16[64,2176]{1,0:T(8,128)(2,1)S(1)} %collective-permute-done.4.refs_0_.refs_2_.refs_6_, bf16[64,2176]{1,0:T(8,128)(2,1)S(1)} %collective-permute-done.6.refs_1_.refs_0_.refs_4_, bf16[64,2176]{1,0:T(8,128)(2,1)S(1)} %collective-permute-done.7.refs_2_.refs_3_.refs_7_, ...), custom_call_target="tpu_custom_call" | custom-call | flops 1 | bytes 1 | tf_op jit(solution)/shard_map/pallas_call | solution.py:230
  34.4 1.7 %collective-permute-done.8.refs_1_.refs_0_.refs_5_ = bf16[64,2176]{1,0:T(8,128)(2,1)S(1)} collective-permute-done((bf16[64,2176]{1,0:T(8,128)(2,1)S(1)}, bf16[64,2176]{1,0:T(8,128)(2,1)S(1)}, u32[]{:S(2)}, u32[]{:S(2)}) %collective-permute-start.8) | collective-permute-done | bytes 278560 | tf_op jit(solution)/shard_map/ppermute | solution.py:255
  36.3 1.8 %shard_map.89.refs_1_ = bf16[64,2048]{1,0:T(8,128)(2,1)S(1)} custom-call(bf16[64,2176]{1,0:T(8,128)(2,1)S(1)} %collective-permute-done.8.refs_1_.refs_0_.refs_5_, bf16[1,2048,768]{2,1,0:T(8,128)(2,1)S(1)} %get-tuple-element.45.refs_4_.refs_2_.refs_3_.refs_1_, bf16[1,2048,768]{2,1,0:T(8,128)(2,1)S(1)} %get-tuple-element.46.refs_5_.refs_3_.refs_4_.refs_2_, ...), custom_call_target="tpu_custom_call" | custom-call | flops 1 | bytes 1 | tf_op jit(solution)/shard_map/pallas_call | solution.py:230
  39.0 2.6 %shard_map.91 = (bf16[128,2048]{1,0:T(8,128)(2,1)S(1)}, bf16[128,2048]{1,0:T(8,128)(2,1)S(1)}) custom-call(bf16[256,2176]{1,0:T(8,128)(2,1)S(1)} %collective-permute-done.9.refs_10_.refs_0_, bf16[1,2048,768]{2,1,0:T(8,128)(2,1)S(1)} %get-tuple-element.45.refs_4_.refs_2_.refs_3_.refs_1_, ...), custom_call_target="tpu_custom_call" | custom-call | flops 1 | bytes 1 | tf_op jit(solution)/shard_map/pallas_call | solution.py:230
  41.8 1.9 %shard_map.90.refs_3_.refs_2_.refs_4_ = f32[1024,128]{1,0:T(8,128)S(1)} custom-call(s32[1]{0:T(128)} %bitcast.me_ref, s32[16]{0:T(128)S(1)} %copy-done.4, bf16[64,2176]{1,0:T(8,128)(2,1)S(1)} %copy-done.3, bf16[64,2176]{1,0:T(8,128)(2,1)S(1)} %collective-permute-done.refs_1_.refs_0_, bf16[64,2176]{1,0:T(8,128)(2,1)S(1)} %collective-permute-done.2.refs_2_.refs_1_, ...), custom_call_target="tpu_custom_call" | custom-call | flops 1 | bytes 1 | tf_op jit(solution)/shard_map/pallas_call | solution.py:118
  44.7 2.1 %collective-permute-start.12 = (bf16[64,2048]{1,0:T(8,128)(2,1)S(1)}, bf16[64,2048]{1,0:T(8,128)(2,1)S(1)}, u32[]{:S(2)}, u32[]{:S(2)}) collective-permute-start(bf16[64,2048]{1,0:T(8,128)(2,1)S(1)} %get-tuple-element.63), channel_id=1, source_target_pairs={{0,2},{1,5},{2,0},{3,7},{4,6},{5,1},{6,4},{7,3},{8,10},{9,13},{10,... | collective-permute-start | bytes 786440 | tf_op jit(solution)/shard_map/ppermute | solution.py:255
  47.2 3.9 %collective-permute-done.12.refs_2_ = bf16[64,2048]{1,0:T(8,128)(2,1)S(1)} collective-permute-done((bf16[64,2048]{1,0:T(8,128)(2,1)S(1)}, bf16[64,2048]{1,0:T(8,128)(2,1)S(1)}, u32[]{:S(2)}, u32[]{:S(2)}) %collective-permute-start.12) | collective-permute-done | bytes 262176 | tf_op jit(solution)/shard_map/ppermute | solution.py:255
  51.8 2.6 %shard_map.84.refs_0_ = bf16[256,2048]{1,0:T(8,128)(2,1)S(1)} custom-call(bf16[64,2176]{1,0:T(8,128)(2,1)S(1)} %copy-done.3, bf16[64,2176]{1,0:T(8,128)(2,1)S(1)} %collective-permute-done.refs_1_.refs_0_, bf16[64,2176]{1,0:T(8,128)(2,1)S(1)} %collective-permute-done.2.refs_2_.refs_1_, bf16[64,2176]{1,0:T(8,128)(2,1)S(1)} %collective-permute-done.3.refs_3_.refs_2_, ...), custom_call_target="tpu_custom_call" | custom-call | flops 1 | bytes 1 | tf_op jit(solution)/shard_map/pallas_call | solution.py:230
  54.4 2.1 %collective-permute-start.14 = (bf16[64,2048]{1,0:T(8,128)(2,1)S(1)}, bf16[64,2048]{1,0:T(8,128)(2,1)S(1)}, u32[]{:S(2)}, u32[]{:S(2)}) collective-permute-start(bf16[64,2048]{1,0:T(8,128)(2,1)S(1)} %get-tuple-element.67), channel_id=1, source_target_pairs={{0,2},{1,5},{2,0},{3,7},{4,6},{5,1},{6,4},{7,3},{8,10},{9,13},{10,... | collective-permute-start | bytes 786440 | tf_op jit(solution)/shard_map/ppermute | solution.py:255
  58.1 1.7 %collective-permute-start.18 = (bf16[64,2048]{1,0:T(8,128)(2,1)S(1)}, bf16[64,2048]{1,0:T(8,128)(2,1)S(1)}, u32[]{:S(2)}, u32[]{:S(2)}) collective-permute-start(bf16[64,2048]{1,0:T(8,128)(2,1)S(1)} %shard_map.95), channel_id=1, source_target_pairs={{0,8},{1,9},{2,10},{3,11},{4,12},{5,13},{6,14},{7,15},{8,0},{9,1},... | collective-permute-start | bytes 786440 | tf_op jit(solution)/shard_map/ppermute | solution.py:255
  61.1 1.8 %collective-permute-start.17 = (bf16[64,2048]{1,0:T(8,128)(2,1)S(1)}, bf16[64,2048]{1,0:T(8,128)(2,1)S(1)}, u32[]{:S(2)}, u32[]{:S(2)}) collective-permute-start(bf16[64,2048]{1,0:T(8,128)(2,1)S(1)} %shard_map.96), channel_id=1, source_target_pairs={{0,4},{1,3},{2,6},{3,1},{4,0},{5,7},{6,2},{7,5},{8,12},{9,11},{10,... | collective-permute-start | bytes 786440 | tf_op jit(solution)/shard_map/ppermute | solution.py:255
  63.9 8.4 %collective-permute-done.18.refs_1_ = bf16[64,2048]{1,0:T(8,128)(2,1)S(1)} collective-permute-done((bf16[64,2048]{1,0:T(8,128)(2,1)S(1)}, bf16[64,2048]{1,0:T(8,128)(2,1)S(1)}, u32[]{:S(2)}, u32[]{:S(2)}) %collective-permute-start.18) | collective-permute-done | bytes 262176 | tf_op jit(solution)/shard_map/ppermute | solution.py:255
  (44 shorter events, 11.9 us)
Async XLA Ops:
  2.0 17.0 %collective-permute-start = (bf16[64,2176]{1,0:T(8,128)(2,1)}, bf16[64,2176]{1,0:T(8,128)(2,1)S(1)}, u32[]{:S(2)}, u32[]{:S(2)}) collective-permute-start(bf16[64,2176]{1,0:T(8,128)(2,1)} %shard_map.82.refs_0_), channel_id=1, source_target_pairs={{0,8},{1,9},{2,10},{3,11},{4,12},{5,13},{6,14},{7,15},{8,0},{9,1},... | collective-permute-start | bytes 835592 | tf_op jit(solution)/shard_map/ppermute | solution.py:255
  6.0 12.9 %collective-permute-start.1 = (bf16[64,2176]{1,0:T(8,128)(2,1)}, bf16[64,2176]{1,0:T(8,128)(2,1)S(1)}, u32[]{:S(2)}, u32[]{:S(2)}) collective-permute-start(bf16[64,2176]{1,0:T(8,128)(2,1)} %shard_map.82.refs_0_), channel_id=1, source_target_pairs={{0,1},{1,0},{2,3},{3,2},{4,5},{5,4},{6,7},{7,6},{8,9},{9,8},{10,11... | collective-permute-start | bytes 835592 | tf_op jit(solution)/shard_map/ppermute | solution.py:259
  6.0 13.8 %collective-permute-start.2 = (bf16[64,2176]{1,0:T(8,128)(2,1)}, bf16[64,2176]{1,0:T(8,128)(2,1)S(1)}, u32[]{:S(2)}, u32[]{:S(2)}) collective-permute-start(bf16[64,2176]{1,0:T(8,128)(2,1)} %shard_map.82.refs_0_), channel_id=1, source_target_pairs={{0,4},{1,3},{2,6},{3,1},{4,0},{5,7},{6,2},{7,5},{8,12},{9,11},{10,... | collective-permute-start | bytes 835592 | tf_op jit(solution)/shard_map/ppermute | solution.py:255
  7.6 12.2 %collective-permute-start.3 = (bf16[64,2176]{1,0:T(8,128)(2,1)}, bf16[64,2176]{1,0:T(8,128)(2,1)S(1)}, u32[]{:S(2)}, u32[]{:S(2)}) collective-permute-start(bf16[64,2176]{1,0:T(8,128)(2,1)} %shard_map.82.refs_0_), channel_id=1, source_target_pairs={{0,2},{1,5},{2,0},{3,7},{4,6},{5,1},{6,4},{7,3},{8,10},{9,13},{10,... | collective-permute-start | bytes 835592 | tf_op jit(solution)/shard_map/ppermute | solution.py:255
  9.1 1.9 %copy-start = (bf16[1,2048,768]{2,1,0:T(8,128)(2,1)S(1)}, bf16[1,2048,768]{2,1,0:T(8,128)(2,1)}, u32[]{:S(2)}) copy-start(bf16[1,2048,768]{2,1,0:T(8,128)(2,1)} %refs_0_.1) | copy-start | bytes 9437188
  11.0 1.9 %copy-start.1 = (bf16[1,2048,768]{2,1,0:T(8,128)(2,1)S(1)}, bf16[1,2048,768]{2,1,0:T(8,128)(2,1)}, u32[]{:S(2)}) copy-start(bf16[1,2048,768]{2,1,0:T(8,128)(2,1)} %refs_1_.1) | copy-start | bytes 9437188
  19.9 3.0 %collective-permute-start.5 = (bf16[192,2176]{1,0:T(8,128)(2,1)S(1)}, bf16[192,2176]{1,0:T(8,128)(2,1)S(1)}, u32[]{:S(2)}, u32[]{:S(2)}) collective-permute-start(bf16[192,2176]{1,0:T(8,128)(2,1)S(1)} %shard_map.85), channel_id=1, source_target_pairs={{0,1},{1,0},{2,3},{3,2},{4,5},{5,4},{6,7},{7,6},{8,9},{9,8},{10,11... | collective-permute-start | bytes 2506760 | tf_op jit(solution)/shard_map/ppermute | solution.py:259
  20.5 8.8 %collective-permute-start.4 = (bf16[64,2176]{1,0:T(8,128)(2,1)S(1)}, bf16[64,2176]{1,0:T(8,128)(2,1)S(1)}, u32[]{:S(2)}, u32[]{:S(2)}) collective-permute-start(bf16[64,2176]{1,0:T(8,128)(2,1)S(1)} %collective-permute-done.refs_1_.refs_0_), channel_id=1, source_target_pairs={{0,4},{1,3},{2,6},{3,1},{4,0},{5,7},{6,2},{7,5},{8,12},{9,11},{10,... | collective-permute-start | bytes 835592 | tf_op jit(solution)/shard_map/ppermute | solution.py:255
  20.9 10.7 %collective-permute-start.6 = (bf16[64,2176]{1,0:T(8,128)(2,1)S(1)}, bf16[64,2176]{1,0:T(8,128)(2,1)S(1)}, u32[]{:S(2)}, u32[]{:S(2)}) collective-permute-start(bf16[64,2176]{1,0:T(8,128)(2,1)S(1)} %collective-permute-done.refs_1_.refs_0_), channel_id=1, source_target_pairs={{0,2},{1,5},{2,0},{3,7},{4,6},{5,1},{6,4},{7,3},{8,10},{9,13},{10,... | collective-permute-start | bytes 835592 | tf_op jit(solution)/shard_map/ppermute | solution.py:255
  22.4 10.0 %collective-permute-start.7 = (bf16[64,2176]{1,0:T(8,128)(2,1)S(1)}, bf16[64,2176]{1,0:T(8,128)(2,1)S(1)}, u32[]{:S(2)}, u32[]{:S(2)}) collective-permute-start(bf16[64,2176]{1,0:T(8,128)(2,1)S(1)} %collective-permute-done.2.refs_2_.refs_1_), channel_id=1, source_target_pairs={{0,2},{1,5},{2,0},{3,7},{4,6},{5,1},{6,4},{7,3},{8,10},{9,13},{10,... | collective-permute-start | bytes 835592 | tf_op jit(solution)/shard_map/ppermute | solution.py:255
  29.3 6.8 %collective-permute-start.8 = (bf16[64,2176]{1,0:T(8,128)(2,1)S(1)}, bf16[64,2176]{1,0:T(8,128)(2,1)S(1)}, u32[]{:S(2)}, u32[]{:S(2)}) collective-permute-start(bf16[64,2176]{1,0:T(8,128)(2,1)S(1)} %collective-permute-done.4.refs_0_.refs_2_.refs_6_), channel_id=1, source_target_pairs={{0,2},{1,5},{2,0},{3,7},{4,6},{5,1},{6,4},{7,3},{8,10},{9,13},{10,... | collective-permute-start | bytes 835592 | tf_op jit(solution)/shard_map/ppermute | solution.py:255
  36.2 2.8 %collective-permute-start.9 = (bf16[256,2176]{1,0:T(8,128)(2,1)S(1)}, bf16[256,2176]{1,0:T(8,128)(2,1)S(1)}, u32[]{:S(2)}, u32[]{:S(2)}) collective-permute-start(bf16[256,2176]{1,0:T(8,128)(2,1)S(1)} %shard_map.88), channel_id=1, source_target_pairs={{0,1},{1,0},{2,3},{3,2},{4,5},{5,4},{6,7},{7,6},{8,9},{9,8},{10,11... | collective-permute-start | bytes 3342344 | tf_op jit(solution)/shard_map/ppermute | solution.py:259
  38.1 3.8 %copy-start.3 = (bf16[64,2176]{1,0:T(8,128)(2,1)S(1)}, bf16[64,2176]{1,0:T(8,128)(2,1)}, u32[]{:S(2)}) copy-start(bf16[64,2176]{1,0:T(8,128)(2,1)} %shard_map.82.refs_0_) | copy-start | bytes 835588
  38.1 3.8 %copy-start.4 = (s32[16]{0:T(128)S(1)}, s32[16]{0:T(128)}, u32[]{:S(2)}) copy-start(s32[16]{0:T(128)} %capacity_ref.1) | copy-start | bytes 196
  41.6 2.7 %collective-permute-start.11 = (bf16[128,2048]{1,0:T(8,128)(2,1)S(1)}, bf16[128,2048]{1,0:T(8,128)(2,1)S(1)}, u32[]{:S(2)}, u32[]{:S(2)}) collective-permute-start(bf16[128,2048]{1,0:T(8,128)(2,1)S(1)} %get-tuple-element.61), channel_id=1, source_target_pairs={{0,1},{1,0},{2,3},{3,2},{4,5},{5,4},{6,7},{7,6},{8,9},{9,8},{10,11... | collective-permute-start | bytes 1572872 | tf_op jit(solution)/shard_map/ppermute | solution.py:259
  43.7 12.8 %collective-permute-start.13 = (bf16[256,2048]{1,0:T(8,128)(2,1)S(1)}, bf16[256,2048]{1,0:T(8,128)(2,1)S(1)}, u32[]{:S(2)}, u32[]{:S(2)}) collective-permute-start(bf16[256,2048]{1,0:T(8,128)(2,1)S(1)} %shard_map.86), channel_id=1, source_target_pairs={{0,1},{1,0},{2,3},{3,2},{4,5},{5,4},{6,7},{7,6},{8,9},{9,8},{10,11... | collective-permute-start | bytes 3145736 | tf_op jit(solution)/shard_map/ppermute | solution.py:259
  44.2 3.0 %collective-permute-start.10 = (bf16[128,2048]{1,0:T(8,128)(2,1)S(1)}, bf16[128,2048]{1,0:T(8,128)(2,1)S(1)}, u32[]{:S(2)}, u32[]{:S(2)}) collective-permute-start(bf16[128,2048]{1,0:T(8,128)(2,1)S(1)} %get-tuple-element.59), channel_id=1, source_target_pairs={{0,1},{1,0},{2,3},{3,2},{4,5},{5,4},{6,7},{7,6},{8,9},{9,8},{10,11... | collective-permute-start | bytes 1572872 | tf_op jit(solution)/shard_map/ppermute | solution.py:259
  44.7 6.4 %collective-permute-start.12 = (bf16[64,2048]{1,0:T(8,128)(2,1)S(1)}, bf16[64,2048]{1,0:T(8,128)(2,1)S(1)}, u32[]{:S(2)}, u32[]{:S(2)}) collective-permute-start(bf16[64,2048]{1,0:T(8,128)(2,1)S(1)} %get-tuple-element.63), channel_id=1, source_target_pairs={{0,2},{1,5},{2,0},{3,7},{4,6},{5,1},{6,4},{7,3},{8,10},{9,13},{10,... | collective-permute-start | bytes 786440 | tf_op jit(solution)/shard_map/ppermute | solution.py:255
  46.7 10.1 %collective-permute-start.16 = (bf16[64,2048]{1,0:T(8,128)(2,1)S(1)}, bf16[64,2048]{1,0:T(8,128)(2,1)S(1)}, u32[]{:S(2)}, u32[]{:S(2)}) collective-permute-start(bf16[64,2048]{1,0:T(8,128)(2,1)S(1)} %get-tuple-element.69), channel_id=1, source_target_pairs={{0,2},{1,5},{2,0},{3,7},{4,6},{5,1},{6,4},{7,3},{8,10},{9,13},{10,... | collective-permute-start | bytes 786440 | tf_op jit(solution)/shard_map/ppermute | solution.py:255
  51.4 6.4 %collective-permute-start.15 = (bf16[64,2048]{1,0:T(8,128)(2,1)S(1)}, bf16[64,2048]{1,0:T(8,128)(2,1)S(1)}, u32[]{:S(2)}, u32[]{:S(2)}) collective-permute-start(bf16[64,2048]{1,0:T(8,128)(2,1)S(1)} %get-tuple-element.68), channel_id=1, source_target_pairs={{0,4},{1,3},{2,6},{3,1},{4,0},{5,7},{6,2},{7,5},{8,12},{9,11},{10,... | collective-permute-start | bytes 786440 | tf_op jit(solution)/shard_map/ppermute | solution.py:255
  54.4 6.4 %collective-permute-start.14 = (bf16[64,2048]{1,0:T(8,128)(2,1)S(1)}, bf16[64,2048]{1,0:T(8,128)(2,1)S(1)}, u32[]{:S(2)}, u32[]{:S(2)}) collective-permute-start(bf16[64,2048]{1,0:T(8,128)(2,1)S(1)} %get-tuple-element.67), channel_id=1, source_target_pairs={{0,2},{1,5},{2,0},{3,7},{4,6},{5,1},{6,4},{7,3},{8,10},{9,13},{10,... | collective-permute-start | bytes 786440 | tf_op jit(solution)/shard_map/ppermute | solution.py:255
  56.7 6.9 %collective-permute-start.19 = (bf16[64,2048]{1,0:T(8,128)(2,1)S(1)}, bf16[64,2048]{1,0:T(8,128)(2,1)S(1)}, u32[]{:S(2)}, u32[]{:S(2)}) collective-permute-start(bf16[64,2048]{1,0:T(8,128)(2,1)S(1)} %shard_map.94), channel_id=1, source_target_pairs={{0,2},{1,5},{2,0},{3,7},{4,6},{5,1},{6,4},{7,3},{8,10},{9,13},{10,... | collective-permute-start | bytes 786440 | tf_op jit(solution)/shard_map/ppermute | solution.py:255
  58.1 14.2 %collective-permute-start.18 = (bf16[64,2048]{1,0:T(8,128)(2,1)S(1)}, bf16[64,2048]{1,0:T(8,128)(2,1)S(1)}, u32[]{:S(2)}, u32[]{:S(2)}) collective-permute-start(bf16[64,2048]{1,0:T(8,128)(2,1)S(1)} %shard_map.95), channel_id=1, source_target_pairs={{0,8},{1,9},{2,10},{3,11},{4,12},{5,13},{6,14},{7,15},{8,0},{9,1},... | collective-permute-start | bytes 786440 | tf_op jit(solution)/shard_map/ppermute | solution.py:255
  61.1 11.3 %collective-permute-start.17 = (bf16[64,2048]{1,0:T(8,128)(2,1)S(1)}, bf16[64,2048]{1,0:T(8,128)(2,1)S(1)}, u32[]{:S(2)}, u32[]{:S(2)}) collective-permute-start(bf16[64,2048]{1,0:T(8,128)(2,1)S(1)} %shard_map.96), channel_id=1, source_target_pairs={{0,4},{1,3},{2,6},{3,1},{4,0},{5,7},{6,2},{7,5},{8,12},{9,11},{10,... | collective-permute-start | bytes 786440 | tf_op jit(solution)/shard_map/ppermute | solution.py:255
  (1 other events, 1.9 us)

commit v11 on v10

--- a/solution.py
+++ b/solution.py
@@ -35,15 +35,11 @@
     place, token = iota((top, rows), 0), iota((top, rows), 1)
     other = jnp.where(place == 0, prio_ref[...], jnp.where(place == 1, me_ref[0], token))
     fields = [routes_ref[...].astype(F32), high.astype(F32), middle.astype(F32), low.astype(F32), other.astype(F32)]
-    facts = jnp.zeros((rows, LANES), F32)
-    for k, field in enumerate(fields):
-        spot = iota((top, LANES), 1) == iota((top, LANES), 0) + k * top
-        facts += lax.dot_general(
-            field.astype(BF16),
-            spot.astype(F32).astype(BF16),
-            (((0,), (0,)), ((), ())),
-            preferred_element_type=F32,
-        )
+    stacked = jnp.concatenate(fields, axis=0)
+    place = iota((stacked.shape[0], LANES), 0) == iota((stacked.shape[0], LANES), 1)
+    facts = lax.dot_general(
+        stacked.astype(BF16), place.astype(F32).astype(BF16), (((0,), (0,)), ((), ())), preferred_element_type=F32
+    )
     rows_ref[:, width:] = facts.astype(BF16)
 
 
@@ -223,7 +219,7 @@
             out_ref[:, lanes] = made[k * rows : (k + 1) * rows]
 
 
-def expert(arrays, matrices, pieces=1):
+def expert(arrays, matrices, pieces=1, flops=1):
     ff, width = matrices[2].shape[1:]
     rows = sum(a.shape[0] for a in arrays)
     held = rows * 2 * (width + ff) + 4 * rows * (2 * FF_TILE + OUT_TILE)
@@ -234,7 +230,7 @@
         out_shape=[jax.ShapeDtypeStruct((rows // pieces, width), BF16)] * pieces,
         scratch_shapes=[pltpu.VMEM((rows, width), BF16), pltpu.VMEM((rows, ff), BF16)],
         compiler_params=pltpu.CompilerParams(vmem_limit_bytes=held + 20 * MIB),
-        cost_estimate=pl.CostEstimate(flops=1, bytes_accessed=1, transcendentals=0),
+        cost_estimate=pl.CostEstimate(flops=flops, bytes_accessed=1, transcendentals=0),
     )(*arrays, *matrices)
     return made if pieces > 1 else made[0]
 
@@ -283,16 +279,17 @@
     theirs = expert([first, crossed], matrices)
     own3, theirs = lax.optimization_barrier((own3, theirs))
     own7 = send(own3, ep, [-1])
+    far_crossed = [cross(o) for o in (own3, own6, own5)]
     far_made = expert([own3, own5, own6], matrices)
     own3, own5, own6, own7, theirs, far_made = lax.optimization_barrier((own3, own5, own6, own7, theirs, far_made))
     far = [own5, own7, own3, own6]
-    far_crossed = cross(pack(far))
+    last_crossed = cross(own7)
     last_made = expert([own7], matrices)
-    far_crossed, last_made = lax.optimization_barrier((far_crossed, last_made))
-    first_back, last_back = expert([far_crossed], matrices, 2)
+    far_crossed, last_crossed, last_made = lax.optimization_barrier((far_crossed, last_crossed, last_made))
+    last_back, first_back = expert([*far_crossed, last_crossed], matrices, 2)
     first_back = cross(first_back)
     near = [held, own1, own2, own4]
-    weights = weigh(me, capacity, near + far + [first, crossed, far_crossed], top, tok_rows)
+    weights = weigh(me, capacity, near + far + [first, crossed, *far_crossed, last_crossed], top, tok_rows)
     weights, theirs, last_back = lax.optimization_barrier((weights, theirs, last_back))
     last_back = cross(last_back)
 

time: 73.4 us -> 72 us (0.981)
  waiting for transfers between devices: 27.2 us -> 23.2 us
  starting transfers between devices: 21.5 us -> 23.9 us
    ppermute x14, waiting for transfers between devices: 25.9 us -> 22.8 us  [send(): return lax.ppermute(array, ('ep', 'sub'), pairs)]
    ppermute x14, starting transfers between devices: 20 us -> 21.3 us  [send(): return lax.ppermute(array, ('ep', 'sub'), pairs)]
    ppermute x6 -> x9, starting transfers between devices: 1.5 us -> 2.55 us  [cross(): return lax.ppermute(array, 'sub', [(0, 1), (1, 0)])]
    ppermute x6 -> x9, waiting for transfers between devices: 1.33 us -> 0.4 us  [cross(): return lax.ppermute(array, 'sub', [(0, 1), (1, 0)])]
  transfers between devices with their start and end apart: 20 -> 23, of which waited for: 12 -> 10; matrix products, arithmetic and copies ran while one was open for 0% -> 0% of each run, Pallas kernels for 18% -> 19%
where the time goes in v11:
time: 72 us; the launch traced here: 71.7 us
  starting transfers between devices  23.9 us (33%)
  waiting for transfers between devices  23.2 us (32%)
  Pallas kernels  18.7 us (26%)
  local copies, waits for them, and re-layouts  5.68 us (8%)
    ppermute x14, waiting for transfers between devices, send(): return lax.ppermute(array, ('ep', 'sub'), pairs)  22.8 us
    ppermute x14, starting transfers between devices, send(): return lax.ppermute(array, ('ep', 'sub'), pairs)  21.3 us
    pallas_call x5, Pallas kernels, expert(): pl.pallas_call(functools.partial(expert_kernel, pieces), in_specs=[pl.Blo...  11.8 us
    unnamed x10, local copies, waits for them, and re-layouts  5.68 us
    ppermute x9, starting transfers between devices, cross(): return lax.ppermute(array, 'sub', [(0, 1), (1, 0)])  2.55 us
    pallas_call x8, Pallas kernels, combine(): pl.pallas_call(functools.partial(combine_kernel, rows, sums, len(arrays))...  2.37 us
    pallas_call x1, Pallas kernels, prepare(): pl.pallas_call(prepare_kernel, in_specs=[pl.BlockSpec(memory_space=pltpu....  1.95 us
    pallas_call x1, Pallas kernels, weigh(): pl.pallas_call(functools.partial(weigh_kernel, top, tok_rows), in_specs=[...  1.89 us
  transfers between devices with their start and end apart: 23, of which 10 were waited for; matrix products, arithmetic and copies ran while one was open for 0% of the time, Pallas kernels for 19%

profile of v11, /device:TPU:0, one launch (start us, length us, event | category | flops | bytes accessed | tf_op | source)
XLA Modules:
  0.0 71.7 jit_solution(3897257748619023588)
XLA Ops:
  0.0 1.9 %shard_map.82.refs_0_ = bf16[64,2176]{1,0:T(8,128)(2,1)} custom-call(s32[1]{0:T(128)} %bitcast.me_ref, bf16[64,2048]{1,0:T(8,128)(2,1)} %tokens_ref.1, s32[8,64]{1,0:T(8,128)} %bitcast.4, f32[8,64]{1,0:T(8,128)} %bitcast.5, s32[1,64]{1,0:T(1,128)} %bitcast.6), custom_call_target="tpu_custom_call" | custom-call | tf_op jit(solution)/shard_map/pallas_call | solution.py:48
  2.4 3.6 %collective-permute-start = (bf16[64,2176]{1,0:T(8,128)(2,1)}, bf16[64,2176]{1,0:T(8,128)(2,1)S(1)}, u32[]{:S(2)}, u32[]{:S(2)}) collective-permute-start(bf16[64,2176]{1,0:T(8,128)(2,1)} %shard_map.82.refs_0_), channel_id=1, source_target_pairs={{0,8},{1,9},{2,10},{3,11},{4,12},{5,13},{6,14},{7,15},{8,0},{9,1},... | collective-permute-start | bytes 835592 | tf_op jit(solution)/shard_map/ppermute | solution.py:251
  6.0 1.5 %collective-permute-start.3 = (bf16[64,2176]{1,0:T(8,128)(2,1)}, bf16[64,2176]{1,0:T(8,128)(2,1)S(1)}, u32[]{:S(2)}, u32[]{:S(2)}) collective-permute-start(bf16[64,2176]{1,0:T(8,128)(2,1)} %shard_map.82.refs_0_), channel_id=1, source_target_pairs={{0,2},{1,5},{2,0},{3,7},{4,6},{5,1},{6,4},{7,3},{8,10},{9,13},{10,... | collective-permute-start | bytes 835592 | tf_op jit(solution)/shard_map/ppermute | solution.py:251
  7.5 1.6 %collective-permute-start.2 = (bf16[64,2176]{1,0:T(8,128)(2,1)}, bf16[64,2176]{1,0:T(8,128)(2,1)S(1)}, u32[]{:S(2)}, u32[]{:S(2)}) collective-permute-start(bf16[64,2176]{1,0:T(8,128)(2,1)} %shard_map.82.refs_0_), channel_id=1, source_target_pairs={{0,4},{1,3},{2,6},{3,1},{4,0},{5,7},{6,2},{7,5},{8,12},{9,11},{10,... | collective-permute-start | bytes 835592 | tf_op jit(solution)/shard_map/ppermute | solution.py:251
  9.1 1.9 %copy-done = bf16[1,2048,768]{2,1,0:T(8,128)(2,1)S(1)} copy-done((bf16[1,2048,768]{2,1,0:T(8,128)(2,1)S(1)}, bf16[1,2048,768]{2,1,0:T(8,128)(2,1)}, u32[]{:S(2)}) %copy-start) | copy-done | bytes 3145752
  11.0 1.9 %copy-done.1 = bf16[1,2048,768]{2,1,0:T(8,128)(2,1)S(1)} copy-done((bf16[1,2048,768]{2,1,0:T(8,128)(2,1)S(1)}, bf16[1,2048,768]{2,1,0:T(8,128)(2,1)}, u32[]{:S(2)}) %copy-start.1) | copy-done | bytes 3145752
  12.9 1.9 %copy-done.2 = bf16[1,768,2048]{2,1,0:T(8,128)(2,1)S(1)} copy-done((bf16[1,768,2048]{2,1,0:T(8,128)(2,1)S(1)}, bf16[1,768,2048]{2,1,0:T(8,128)(2,1)}, u32[]{:S(2)}) %copy-start.2) | copy-done | bytes 3145752
  15.4 4.2 %collective-permute-done.refs_1_.refs_0_ = bf16[64,2176]{1,0:T(8,128)(2,1)S(1)} collective-permute-done((bf16[64,2176]{1,0:T(8,128)(2,1)}, bf16[64,2176]{1,0:T(8,128)(2,1)S(1)}, u32[]{:S(2)}, u32[]{:S(2)}) %collective-permute-start) | collective-permute-done | bytes 278560 | tf_op jit(solution)/shard_map/ppermute | solution.py:251
  19.9 1.6 %collective-permute-start.4 = (bf16[64,2176]{1,0:T(8,128)(2,1)S(1)}, bf16[64,2176]{1,0:T(8,128)(2,1)S(1)}, u32[]{:S(2)}, u32[]{:S(2)}) collective-permute-start(bf16[64,2176]{1,0:T(8,128)(2,1)S(1)} %collective-permute-done.refs_1_.refs_0_), channel_id=1, source_target_pairs={{0,4},{1,3},{2,6},{3,1},{4,0},{5,7},{6,2},{7,5},{8,12},{9,11},{10,... | collective-permute-start | bytes 835592 | tf_op jit(solution)/shard_map/ppermute | solution.py:251
  23.5 2.6 %shard_map.86 = bf16[256,2048]{1,0:T(8,128)(2,1)S(1)} custom-call(bf16[64,2176]{1,0:T(8,128)(2,1)S(1)} %collective-permute-done.1.refs_0_.refs_8_, bf16[192,2176]{1,0:T(8,128)(2,1)S(1)} %collective-permute-done.5.refs_1_.refs_9_, bf16[1,2048,768]{2,1,0:T(8,128)(2,1)S(1)} %get-tuple-element.48.refs_4_.refs_2_.refs_3_.refs_1_, ...), custom_call_target="tpu_custom_call" | custom-call | flops 1 | bytes 1 | tf_op jit(solution)/shard_map/pallas_call | solution.py:226
  26.1 2.7 %collective-permute-done.4.refs_0_.refs_6_ = bf16[64,2176]{1,0:T(8,128)(2,1)S(1)} collective-permute-done((bf16[64,2176]{1,0:T(8,128)(2,1)S(1)}, bf16[64,2176]{1,0:T(8,128)(2,1)S(1)}, u32[]{:S(2)}, u32[]{:S(2)}) %collective-permute-start.4) | collective-permute-done | bytes 278560 | tf_op jit(solution)/shard_map/ppermute | solution.py:251
  28.8 2.2 %collective-permute-start.8 = (bf16[64,2176]{1,0:T(8,128)(2,1)S(1)}, bf16[64,2176]{1,0:T(8,128)(2,1)S(1)}, u32[]{:S(2)}, u32[]{:S(2)}) collective-permute-start(bf16[64,2176]{1,0:T(8,128)(2,1)S(1)} %collective-permute-done.4.refs_0_.refs_6_), channel_id=1, source_target_pairs={{0,2},{1,5},{2,0},{3,7},{4,6},{5,1},{6,4},{7,3},{8,10},{9,13},{10,... | collective-permute-start | bytes 835592 | tf_op jit(solution)/shard_map/ppermute | solution.py:251
  32.8 2.0 %shard_map.87.refs_0_ = bf16[192,2048]{1,0:T(8,128)(2,1)S(1)} custom-call(bf16[64,2176]{1,0:T(8,128)(2,1)S(1)} %collective-permute-done.4.refs_0_.refs_6_, bf16[64,2176]{1,0:T(8,128)(2,1)S(1)} %collective-permute-done.6.refs_1_.refs_4_, bf16[64,2176]{1,0:T(8,128)(2,1)S(1)} %collective-permute-done.7.refs_2_.refs_7_, ...), custom_call_target="tpu_custom_call" | custom-call | flops 1 | bytes 1 | tf_op jit(solution)/shard_map/pallas_call | solution.py:226
  35.6 1.8 %shard_map.88.refs_1_ = bf16[64,2048]{1,0:T(8,128)(2,1)S(1)} custom-call(bf16[64,2176]{1,0:T(8,128)(2,1)S(1)} %collective-permute-done.8.refs_0_.refs_5_, bf16[1,2048,768]{2,1,0:T(8,128)(2,1)S(1)} %get-tuple-element.48.refs_4_.refs_2_.refs_3_.refs_1_, bf16[1,2048,768]{2,1,0:T(8,128)(2,1)S(1)} %get-tuple-element.49.refs_5_.refs_3_.refs_4_.refs_2_, ...), custom_call_target="tpu_custom_call" | custom-call | flops 1 | bytes 1 | tf_op jit(solution)/shard_map/pallas_call | solution.py:226
  37.5 2.7 %shard_map.90 = (bf16[128,2048]{1,0:T(8,128)(2,1)S(1)}, bf16[128,2048]{1,0:T(8,128)(2,1)S(1)}) custom-call(bf16[64,2176]{1,0:T(8,128)(2,1)S(1)} %collective-permute-done.9.refs_10_.refs_0_, bf16[64,2176]{1,0:T(8,128)(2,1)S(1)} %collective-permute-done.10.refs_11_.refs_1_, bf16[64,2176]{1,0:T(8,128)(2,1)S(1)} %collective-permute-done.11.refs_12_.refs_2_, ...), custom_call_target="tpu_custom_call" | custom-call | flops 1 | bytes 1 | tf_op jit(solution)/shard_map/pallas_call | solution.py:226
  40.7 1.9 %shard_map.89.refs_3_.refs_2_.refs_4_ = f32[1024,128]{1,0:T(8,128)S(1)} custom-call(s32[1]{0:T(128)} %bitcast.me_ref, s32[16]{0:T(128)S(1)} %copy-done.4, bf16[64,2176]{1,0:T(8,128)(2,1)S(1)} %copy-done.3, bf16[64,2176]{1,0:T(8,128)(2,1)S(1)} %collective-permute-done.refs_1_.refs_0_, bf16[64,2176]{1,0:T(8,128)(2,1)S(1)} %collective-permute-done.2.refs_2_.refs_1_, ...), custom_call_target="tpu_custom_call" | custom-call | flops 1 | bytes 1 | tf_op jit(solution)/shard_map/pallas_call | solution.py:114
  43.5 2.1 %collective-permute-start.15 = (bf16[64,2048]{1,0:T(8,128)(2,1)S(1)}, bf16[64,2048]{1,0:T(8,128)(2,1)S(1)}, u32[]{:S(2)}, u32[]{:S(2)}) collective-permute-start(bf16[64,2048]{1,0:T(8,128)(2,1)S(1)} %get-tuple-element.69), channel_id=1, source_target_pairs={{0,2},{1,5},{2,0},{3,7},{4,6},{5,1},{6,4},{7,3},{8,10},{9,13},{10,... | collective-permute-start | bytes 786440 | tf_op jit(solution)/shard_map/ppermute | solution.py:251
  46.0 3.9 %collective-permute-done.15.refs_2_ = bf16[64,2048]{1,0:T(8,128)(2,1)S(1)} collective-permute-done((bf16[64,2048]{1,0:T(8,128)(2,1)S(1)}, bf16[64,2048]{1,0:T(8,128)(2,1)S(1)}, u32[]{:S(2)}, u32[]{:S(2)}) %collective-permute-start.15) | collective-permute-done | bytes 262176 | tf_op jit(solution)/shard_map/ppermute | solution.py:251
  50.3 1.6 %collective-permute-start.18 = (bf16[64,2048]{1,0:T(8,128)(2,1)S(1)}, bf16[64,2048]{1,0:T(8,128)(2,1)S(1)}, u32[]{:S(2)}, u32[]{:S(2)}) collective-permute-start(bf16[64,2048]{1,0:T(8,128)(2,1)S(1)} %get-tuple-element.74), channel_id=1, source_target_pairs={{0,4},{1,3},{2,6},{3,1},{4,0},{5,7},{6,2},{7,5},{8,12},{9,11},{10,... | collective-permute-start | bytes 786440 | tf_op jit(solution)/shard_map/ppermute | solution.py:251
  51.9 2.6 %shard_map.84.refs_0_ = bf16[256,2048]{1,0:T(8,128)(2,1)S(1)} custom-call(bf16[64,2176]{1,0:T(8,128)(2,1)S(1)} %copy-done.3, bf16[64,2176]{1,0:T(8,128)(2,1)S(1)} %collective-permute-done.refs_1_.refs_0_, bf16[64,2176]{1,0:T(8,128)(2,1)S(1)} %collective-permute-done.2.refs_2_.refs_1_, bf16[64,2176]{1,0:T(8,128)(2,1)S(1)} %collective-permute-done.3.refs_3_.refs_2_, ...), custom_call_target="tpu_custom_call" | custom-call | flops 1 | bytes 1 | tf_op jit(solution)/shard_map/pallas_call | solution.py:226
  54.5 2.1 %collective-permute-start.17 = (bf16[64,2048]{1,0:T(8,128)(2,1)S(1)}, bf16[64,2048]{1,0:T(8,128)(2,1)S(1)}, u32[]{:S(2)}, u32[]{:S(2)}) collective-permute-start(bf16[64,2048]{1,0:T(8,128)(2,1)S(1)} %get-tuple-element.73), channel_id=1, source_target_pairs={{0,2},{1,5},{2,0},{3,7},{4,6},{5,1},{6,4},{7,3},{8,10},{9,13},{10,... | collective-permute-start | bytes 786440 | tf_op jit(solution)/shard_map/ppermute | solution.py:251
  57.2 2.4 %collective-permute-start.21 = (bf16[64,2048]{1,0:T(8,128)(2,1)S(1)}, bf16[64,2048]{1,0:T(8,128)(2,1)S(1)}, u32[]{:S(2)}, u32[]{:S(2)}) collective-permute-start(bf16[64,2048]{1,0:T(8,128)(2,1)S(1)} %shard_map.94), channel_id=1, source_target_pairs={{0,8},{1,9},{2,10},{3,11},{4,12},{5,13},{6,14},{7,15},{8,0},{9,1},... | collective-permute-start | bytes 786440 | tf_op jit(solution)/shard_map/ppermute | solution.py:251
  61.8 2.9 %collective-permute-done.22.refs_2_ = bf16[64,2048]{1,0:T(8,128)(2,1)S(1)} collective-permute-done((bf16[64,2048]{1,0:T(8,128)(2,1)S(1)}, bf16[64,2048]{1,0:T(8,128)(2,1)S(1)}, u32[]{:S(2)}, u32[]{:S(2)}) %collective-permute-start.22) | collective-permute-done | bytes 262176 | tf_op jit(solution)/shard_map/ppermute | solution.py:251
  64.9 6.0 %collective-permute-done.21.refs_1_ = bf16[64,2048]{1,0:T(8,128)(2,1)S(1)} collective-permute-done((bf16[64,2048]{1,0:T(8,128)(2,1)S(1)}, bf16[64,2048]{1,0:T(8,128)(2,1)S(1)}, u32[]{:S(2)}, u32[]{:S(2)}) %collective-permute-start.21) | collective-permute-done | bytes 262176 | tf_op jit(solution)/shard_map/ppermute | solution.py:251
  (49 shorter events, 12.0 us)
Async XLA Ops:
  1.9 13.5 %collective-permute-start.1 = (bf16[64,2176]{1,0:T(8,128)(2,1)}, bf16[64,2176]{1,0:T(8,128)(2,1)S(1)}, u32[]{:S(2)}, u32[]{:S(2)}) collective-permute-start(bf16[64,2176]{1,0:T(8,128)(2,1)} %shard_map.82.refs_0_), channel_id=1, source_target_pairs={{0,1},{1,0},{2,3},{3,2},{4,5},{5,4},{6,7},{7,6},{8,9},{9,8},{10,11... | collective-permute-start | bytes 835592 | tf_op jit(solution)/shard_map/ppermute | solution.py:255
  2.4 17.2 %collective-permute-start = (bf16[64,2176]{1,0:T(8,128)(2,1)}, bf16[64,2176]{1,0:T(8,128)(2,1)S(1)}, u32[]{:S(2)}, u32[]{:S(2)}) collective-permute-start(bf16[64,2176]{1,0:T(8,128)(2,1)} %shard_map.82.refs_0_), channel_id=1, source_target_pairs={{0,8},{1,9},{2,10},{3,11},{4,12},{5,13},{6,14},{7,15},{8,0},{9,1},... | collective-permute-start | bytes 835592 | tf_op jit(solution)/shard_map/ppermute | solution.py:251
  6.0 13.6 %collective-permute-start.3 = (bf16[64,2176]{1,0:T(8,128)(2,1)}, bf16[64,2176]{1,0:T(8,128)(2,1)S(1)}, u32[]{:S(2)}, u32[]{:S(2)}) collective-permute-start(bf16[64,2176]{1,0:T(8,128)(2,1)} %shard_map.82.refs_0_), channel_id=1, source_target_pairs={{0,2},{1,5},{2,0},{3,7},{4,6},{5,1},{6,4},{7,3},{8,10},{9,13},{10,... | collective-permute-start | bytes 835592 | tf_op jit(solution)/shard_map/ppermute | solution.py:251
  7.5 12.3 %collective-permute-start.2 = (bf16[64,2176]{1,0:T(8,128)(2,1)}, bf16[64,2176]{1,0:T(8,128)(2,1)S(1)}, u32[]{:S(2)}, u32[]{:S(2)}) collective-permute-start(bf16[64,2176]{1,0:T(8,128)(2,1)} %shard_map.82.refs_0_), channel_id=1, source_target_pairs={{0,4},{1,3},{2,6},{3,1},{4,0},{5,7},{6,2},{7,5},{8,12},{9,11},{10,... | collective-permute-start | bytes 835592 | tf_op jit(solution)/shard_map/ppermute | solution.py:251
  19.9 3.7 %collective-permute-start.5 = (bf16[192,2176]{1,0:T(8,128)(2,1)S(1)}, bf16[192,2176]{1,0:T(8,128)(2,1)S(1)}, u32[]{:S(2)}, u32[]{:S(2)}) collective-permute-start(bf16[192,2176]{1,0:T(8,128)(2,1)S(1)} %shard_map.85), channel_id=1, source_target_pairs={{0,1},{1,0},{2,3},{3,2},{4,5},{5,4},{6,7},{7,6},{8,9},{9,8},{10,11... | collective-permute-start | bytes 2506760 | tf_op jit(solution)/shard_map/ppermute | solution.py:255
  19.9 8.9 %collective-permute-start.4 = (bf16[64,2176]{1,0:T(8,128)(2,1)S(1)}, bf16[64,2176]{1,0:T(8,128)(2,1)S(1)}, u32[]{:S(2)}, u32[]{:S(2)}) collective-permute-start(bf16[64,2176]{1,0:T(8,128)(2,1)S(1)} %collective-permute-done.refs_1_.refs_0_), channel_id=1, source_target_pairs={{0,4},{1,3},{2,6},{3,1},{4,0},{5,7},{6,2},{7,5},{8,12},{9,11},{10,... | collective-permute-start | bytes 835592 | tf_op jit(solution)/shard_map/ppermute | solution.py:251
  21.5 10.8 %collective-permute-start.6 = (bf16[64,2176]{1,0:T(8,128)(2,1)S(1)}, bf16[64,2176]{1,0:T(8,128)(2,1)S(1)}, u32[]{:S(2)}, u32[]{:S(2)}) collective-permute-start(bf16[64,2176]{1,0:T(8,128)(2,1)S(1)} %collective-permute-done.refs_1_.refs_0_), channel_id=1, source_target_pairs={{0,2},{1,5},{2,0},{3,7},{4,6},{5,1},{6,4},{7,3},{8,10},{9,13},{10,... | collective-permute-start | bytes 835592 | tf_op jit(solution)/shard_map/ppermute | solution.py:251
  23.0 9.0 %collective-permute-start.7 = (bf16[64,2176]{1,0:T(8,128)(2,1)S(1)}, bf16[64,2176]{1,0:T(8,128)(2,1)S(1)}, u32[]{:S(2)}, u32[]{:S(2)}) collective-permute-start(bf16[64,2176]{1,0:T(8,128)(2,1)S(1)} %collective-permute-done.2.refs_2_.refs_1_), channel_id=1, source_target_pairs={{0,2},{1,5},{2,0},{3,7},{4,6},{5,1},{6,4},{7,3},{8,10},{9,13},{10,... | collective-permute-start | bytes 835592 | tf_op jit(solution)/shard_map/ppermute | solution.py:251
  28.8 6.7 %collective-permute-start.8 = (bf16[64,2176]{1,0:T(8,128)(2,1)S(1)}, bf16[64,2176]{1,0:T(8,128)(2,1)S(1)}, u32[]{:S(2)}, u32[]{:S(2)}) collective-permute-start(bf16[64,2176]{1,0:T(8,128)(2,1)S(1)} %collective-permute-done.4.refs_0_.refs_6_), channel_id=1, source_target_pairs={{0,2},{1,5},{2,0},{3,7},{4,6},{5,1},{6,4},{7,3},{8,10},{9,13},{10,... | collective-permute-start | bytes 835592 | tf_op jit(solution)/shard_map/ppermute | solution.py:251
  32.0 5.5 %collective-permute-start.10 = (bf16[64,2176]{1,0:T(8,128)(2,1)S(1)}, bf16[64,2176]{1,0:T(8,128)(2,1)S(1)}, u32[]{:S(2)}, u32[]{:S(2)}) collective-permute-start(bf16[64,2176]{1,0:T(8,128)(2,1)S(1)} %collective-permute-done.7.refs_2_.refs_7_), channel_id=1, source_target_pairs={{0,1},{1,0},{2,3},{3,2},{4,5},{5,4},{6,7},{7,6},{8,9},{9,8},{10,11... | collective-permute-start | bytes 835592 | tf_op jit(solution)/shard_map/ppermute | solution.py:255
  32.3 5.1 %collective-permute-start.11 = (bf16[64,2176]{1,0:T(8,128)(2,1)S(1)}, bf16[64,2176]{1,0:T(8,128)(2,1)S(1)}, u32[]{:S(2)}, u32[]{:S(2)}) collective-permute-start(bf16[64,2176]{1,0:T(8,128)(2,1)S(1)} %collective-permute-done.6.refs_1_.refs_4_), channel_id=1, source_target_pairs={{0,1},{1,0},{2,3},{3,2},{4,5},{5,4},{6,7},{7,6},{8,9},{9,8},{10,11... | collective-permute-start | bytes 835592 | tf_op jit(solution)/shard_map/ppermute | solution.py:255
  32.5 5.0 %collective-permute-start.9 = (bf16[64,2176]{1,0:T(8,128)(2,1)S(1)}, bf16[64,2176]{1,0:T(8,128)(2,1)S(1)}, u32[]{:S(2)}, u32[]{:S(2)}) collective-permute-start(bf16[64,2176]{1,0:T(8,128)(2,1)S(1)} %collective-permute-done.4.refs_0_.refs_6_), channel_id=1, source_target_pairs={{0,1},{1,0},{2,3},{3,2},{4,5},{5,4},{6,7},{7,6},{8,9},{9,8},{10,11... | collective-permute-start | bytes 835592 | tf_op jit(solution)/shard_map/ppermute | solution.py:255
  35.5 1.9 %collective-permute-start.12 = (bf16[64,2176]{1,0:T(8,128)(2,1)S(1)}, bf16[64,2176]{1,0:T(8,128)(2,1)S(1)}, u32[]{:S(2)}, u32[]{:S(2)}) collective-permute-start(bf16[64,2176]{1,0:T(8,128)(2,1)S(1)} %collective-permute-done.8.refs_0_.refs_5_), channel_id=1, source_target_pairs={{0,1},{1,0},{2,3},{3,2},{4,5},{5,4},{6,7},{7,6},{8,9},{9,8},{10,11... | collective-permute-start | bytes 835592 | tf_op jit(solution)/shard_map/ppermute | solution.py:255
  37.4 3.2 %copy-start.3 = (bf16[64,2176]{1,0:T(8,128)(2,1)S(1)}, bf16[64,2176]{1,0:T(8,128)(2,1)}, u32[]{:S(2)}) copy-start(bf16[64,2176]{1,0:T(8,128)(2,1)} %shard_map.82.refs_0_) | copy-start | bytes 835588
  40.2 3.0 %collective-permute-start.14 = (bf16[128,2048]{1,0:T(8,128)(2,1)S(1)}, bf16[128,2048]{1,0:T(8,128)(2,1)S(1)}, u32[]{:S(2)}, u32[]{:S(2)}) collective-permute-start(bf16[128,2048]{1,0:T(8,128)(2,1)S(1)} %get-tuple-element.67), channel_id=1, source_target_pairs={{0,1},{1,0},{2,3},{3,2},{4,5},{5,4},{6,7},{7,6},{8,9},{9,8},{10,11... | collective-permute-start | bytes 1572872 | tf_op jit(solution)/shard_map/ppermute | solution.py:255
  42.6 14.1 %collective-permute-start.16 = (bf16[256,2048]{1,0:T(8,128)(2,1)S(1)}, bf16[256,2048]{1,0:T(8,128)(2,1)S(1)}, u32[]{:S(2)}, u32[]{:S(2)}) collective-permute-start(bf16[256,2048]{1,0:T(8,128)(2,1)S(1)} %shard_map.86), channel_id=1, source_target_pairs={{0,1},{1,0},{2,3},{3,2},{4,5},{5,4},{6,7},{7,6},{8,9},{9,8},{10,11... | collective-permute-start | bytes 3145736 | tf_op jit(solution)/shard_map/ppermute | solution.py:255
  42.7 3.3 %collective-permute-start.13 = (bf16[128,2048]{1,0:T(8,128)(2,1)S(1)}, bf16[128,2048]{1,0:T(8,128)(2,1)S(1)}, u32[]{:S(2)}, u32[]{:S(2)}) collective-permute-start(bf16[128,2048]{1,0:T(8,128)(2,1)S(1)} %get-tuple-element.65), channel_id=1, source_target_pairs={{0,1},{1,0},{2,3},{3,2},{4,5},{5,4},{6,7},{7,6},{8,9},{9,8},{10,11... | collective-permute-start | bytes 1572872 | tf_op jit(solution)/shard_map/ppermute | solution.py:255
  43.5 6.4 %collective-permute-start.15 = (bf16[64,2048]{1,0:T(8,128)(2,1)S(1)}, bf16[64,2048]{1,0:T(8,128)(2,1)S(1)}, u32[]{:S(2)}, u32[]{:S(2)}) collective-permute-start(bf16[64,2048]{1,0:T(8,128)(2,1)S(1)} %get-tuple-element.69), channel_id=1, source_target_pairs={{0,2},{1,5},{2,0},{3,7},{4,6},{5,1},{6,4},{7,3},{8,10},{9,13},{10,... | collective-permute-start | bytes 786440 | tf_op jit(solution)/shard_map/ppermute | solution.py:251
  45.6 11.3 %collective-permute-start.19 = (bf16[64,2048]{1,0:T(8,128)(2,1)S(1)}, bf16[64,2048]{1,0:T(8,128)(2,1)S(1)}, u32[]{:S(2)}, u32[]{:S(2)}) collective-permute-start(bf16[64,2048]{1,0:T(8,128)(2,1)S(1)} %get-tuple-element.75), channel_id=1, source_target_pairs={{0,2},{1,5},{2,0},{3,7},{4,6},{5,1},{6,4},{7,3},{8,10},{9,13},{10,... | collective-permute-start | bytes 786440 | tf_op jit(solution)/shard_map/ppermute | solution.py:251
  50.3 6.6 %collective-permute-start.18 = (bf16[64,2048]{1,0:T(8,128)(2,1)S(1)}, bf16[64,2048]{1,0:T(8,128)(2,1)S(1)}, u32[]{:S(2)}, u32[]{:S(2)}) collective-permute-start(bf16[64,2048]{1,0:T(8,128)(2,1)S(1)} %get-tuple-element.74), channel_id=1, source_target_pairs={{0,4},{1,3},{2,6},{3,1},{4,0},{5,7},{6,2},{7,5},{8,12},{9,11},{10,... | collective-permute-start | bytes 786440 | tf_op jit(solution)/shard_map/ppermute | solution.py:251
  54.5 6.4 %collective-permute-start.17 = (bf16[64,2048]{1,0:T(8,128)(2,1)S(1)}, bf16[64,2048]{1,0:T(8,128)(2,1)S(1)}, u32[]{:S(2)}, u32[]{:S(2)}) collective-permute-start(bf16[64,2048]{1,0:T(8,128)(2,1)S(1)} %get-tuple-element.73), channel_id=1, source_target_pairs={{0,2},{1,5},{2,0},{3,7},{4,6},{5,1},{6,4},{7,3},{8,10},{9,13},{10,... | collective-permute-start | bytes 786440 | tf_op jit(solution)/shard_map/ppermute | solution.py:251
  56.8 7.8 %collective-permute-start.22 = (bf16[64,2048]{1,0:T(8,128)(2,1)S(1)}, bf16[64,2048]{1,0:T(8,128)(2,1)S(1)}, u32[]{:S(2)}, u32[]{:S(2)}) collective-permute-start(bf16[64,2048]{1,0:T(8,128)(2,1)S(1)} %shard_map.93), channel_id=1, source_target_pairs={{0,2},{1,5},{2,0},{3,7},{4,6},{5,1},{6,4},{7,3},{8,10},{9,13},{10,... | collective-permute-start | bytes 786440 | tf_op jit(solution)/shard_map/ppermute | solution.py:251
  57.2 13.7 %collective-permute-start.21 = (bf16[64,2048]{1,0:T(8,128)(2,1)S(1)}, bf16[64,2048]{1,0:T(8,128)(2,1)S(1)}, u32[]{:S(2)}, u32[]{:S(2)}) collective-permute-start(bf16[64,2048]{1,0:T(8,128)(2,1)S(1)} %shard_map.94), channel_id=1, source_target_pairs={{0,8},{1,9},{2,10},{3,11},{4,12},{5,13},{6,14},{7,15},{8,0},{9,1},... | collective-permute-start | bytes 786440 | tf_op jit(solution)/shard_map/ppermute | solution.py:251
  61.2 9.8 %collective-permute-start.20 = (bf16[64,2048]{1,0:T(8,128)(2,1)S(1)}, bf16[64,2048]{1,0:T(8,128)(2,1)S(1)}, u32[]{:S(2)}, u32[]{:S(2)}) collective-permute-start(bf16[64,2048]{1,0:T(8,128)(2,1)S(1)} %shard_map.95), channel_id=1, source_target_pairs={{0,4},{1,3},{2,6},{3,1},{4,0},{5,7},{6,2},{7,5},{8,12},{9,11},{10,... | collective-permute-start | bytes 786440 | tf_op jit(solution)/shard_map/ppermute | solution.py:251
  (4 other events, 8.9 us)

commit v12 on v11

--- a/solution.py
+++ b/solution.py
@@ -145,32 +145,53 @@
     )(*blocks)
 
 
-def combine_kernel(rows, sums, weighted, *refs):
+def combine_kernel(rows, sums, spans, offsets, weighted, *refs):
     ins, outs = refs[: -len(sums)], refs[-len(sums) :]
-    width = outs[0].shape[1]
-    for lanes in range(0, width, 256):
-        for terms, out in zip(sums, outs):
+    for terms, (start, size), out in zip(sums, spans, outs):
+        for lane in range(start, start + size, 256):
             total = None
             for which, first, place in terms:
-                value = ins[which][first : first + rows, lanes : lanes + 256].astype(F32)
+                at = lane - offsets[which]
+                value = ins[which][first : first + rows, at : at + 256].astype(F32)
                 if place is not None:
                     value = value * ins[weighted][place : place + rows, :1]
                 total = value if total is None else total + value
-            out[:, lanes : lanes + 256] = total.astype(out.dtype)
-
-
-def combine(arrays, weights, sums, kind=BF16):
+            out[:, lane - start : lane - start + 256] = total.astype(out.dtype)
+
+
+def combine(arrays, weights, sums, kind=BF16, spans=None, offsets=None):
     rows = weights.shape[0] // 16
-    width = arrays[0].shape[1]
+    spans = spans or [(0, arrays[0].shape[1])] * len(sums)
+    offsets = offsets or [0] * len(arrays)
     sums = [[(a, b * rows, None if p is None else p * rows) for a, b, p in terms] for terms in sums]
     return pl.pallas_call(
-        functools.partial(combine_kernel, rows, sums, len(arrays)),
+        functools.partial(combine_kernel, rows, sums, spans, offsets, len(arrays)),
         in_specs=[pl.BlockSpec(memory_space=pltpu.VMEM)] * (len(arrays) + 1),
         out_specs=[pl.BlockSpec(memory_space=pltpu.VMEM)] * len(sums),
-        out_shape=[jax.ShapeDtypeStruct((rows, width), kind)] * len(sums),
+        out_shape=[jax.ShapeDtypeStruct((rows, size), kind) for start, size in spans],
         compiler_params=pltpu.CompilerParams(vmem_limit_bytes=24 * MIB),
         cost_estimate=pl.CostEstimate(flops=1, bytes_accessed=1, transcendentals=0),
     )(*arrays, weights)
+
+
+def merge_kernel(low_ref, high_ref, low_last_ref, high_last_ref, out_ref):
+    half = low_ref.shape[1]
+    for ref, last, first in ((low_ref, low_last_ref, 0), (high_ref, high_last_ref, half)):
+        for lane in range(0, half, 256):
+            lanes = slice(lane, lane + 256)
+            out_ref[:, first + lane : first + lane + 256] = (ref[:, lanes] + last[:, lanes].astype(F32)).astype(BF16)
+
+
+def merge(halves, last):
+    rows, half = last[0].shape
+    return pl.pallas_call(
+        merge_kernel,
+        in_specs=[pl.BlockSpec(memory_space=pltpu.VMEM)] * 4,
+        out_specs=pl.BlockSpec(memory_space=pltpu.VMEM),
+        out_shape=jax.ShapeDtypeStruct((rows, 2 * half), BF16),
+        compiler_params=pltpu.CompilerParams(vmem_limit_bytes=24 * MIB),
+        cost_estimate=pl.CostEstimate(flops=1, bytes_accessed=1, transcendentals=0),
+    )(*halves, *last)
 
 
 def load_kernel(*refs):
@@ -296,37 +317,72 @@
     def part(mine, back, block, place):
         return [(mine, block, place), (back, block, 8 + place)]
 
-    send5, send7 = combine(
-        [far_made, last_made, first_back], weights, [[(0, 1, 4), (2, 0, 12)], [(1, 0, 5), (2, 1, 13)]]
+    half = width // 2
+    spans = [(0, half), (half, half)]
+    sends = combine(
+        [far_made, last_made, first_back],
+        weights,
+        [[(1, 0, 5), (2, 1, 13)]] * 2 + [[(0, 1, 4), (2, 0, 12)]] * 2,
+        spans=spans * 2,
     )
-    back7 = send(send7, ep, [-1])
-    back5 = send(send5, ep, [-1])
-    send3, send6 = combine(
-        [far_made, last_back, back7],
-        weights,
-        [[(0, 0, 6), (1, 0, 14), (2, 0, None)], [(0, 2, 7), (1, 1, 15)]],
-    )
-    back3 = send(send3, ep, [-2])
+    back7 = [send(s, ep, [-1]) for s in sends[:2]]
+    back5 = [send(s, ep, [-1]) for s in sends[2:]]
     near_made = expert(near, matrices)
-    near_made, send6 = lax.optimization_barrier((near_made, send6))
-    back6 = send(send6, ep, [-1])
+    near_made, back7[0] = lax.optimization_barrier((near_made, back7[0]))
+    back3 = []
+    for k, span in enumerate(spans):
+        (send3,) = combine(
+            [far_made, last_back, back7[k]],
+            weights,
+            [[(0, 0, 6), (1, 0, 14), (2, 0, None)]],
+            spans=[span],
+            offsets=[0, 0, span[0]],
+        )
+        back3.append(send(send3, ep, [-2]))
+        if k == 0:
+            back7[1], send3 = lax.optimization_barrier((back7[1], send3))
+    send3, last_back = lax.optimization_barrier((send3, last_back))
+    send6 = combine([far_made, last_back], weights, [[(0, 2, 7), (1, 1, 15)]] * 2, spans=spans)
+    back6 = [send(s, ep, [-1]) for s in send6]
     near_back = cross(theirs)
     (send4,) = combine([near_made, near_back], weights, [part(0, 1, 3, 3)])
     back4 = send(send4, ep, [-1])
-    back3, back5, send4 = lax.optimization_barrier((back3, back5, send4))
-    (send1,) = combine([near_made, near_back, back3, back5], weights, [part(0, 1, 1, 1) + [(2, 0, None), (3, 0, None)]])
-    back1 = send(send1, ep, [-3])
+    back1 = []
+    for k, span in enumerate(spans):
+        (send1,) = combine(
+            [near_made, near_back, back3[k], back5[k]],
+            weights,
+            [part(0, 1, 1, 1) + [(2, 0, None), (3, 0, None)]],
+            spans=[span],
+            offsets=[0, 0, span[0], span[0]],
+        )
+        back1.append(send(send1, ep, [-3]))
+        if k == 0:
+            back3[1], send1 = lax.optimization_barrier((back3[1], send1))
     back6, send1 = lax.optimization_barrier((back6, send1))
-    (send2,) = combine([near_made, near_back, back6], weights, [part(0, 1, 2, 2) + [(2, 0, None)]])
-    back2 = send(send2, ep, [-2])
+    send2 = combine(
+        [near_made, near_back, *back6],
+        weights,
+        [part(0, 1, 2, 2) + [(2, 0, None)], part(0, 1, 2, 2) + [(3, 0, None)]],
+        spans=spans,
+        offsets=[0, 0, 0, half],
+    )
+    back2 = [send(s, ep, [-2]) for s in send2]
     (total,) = combine([near_made, near_back, back4], weights, [part(0, 1, 0, 0) + [(2, 0, None)]], F32)
-    back1, total = lax.optimization_barrier((back1, total))
-    (total,) = combine([total, back1], weights, [[(0, 0, None), (1, 0, None)]], F32)
-    back2, total = lax.optimization_barrier((back2, total))
-    (total,) = combine([total, back2], weights, [[(0, 0, None), (1, 0, None)]])
+    halves = []
+    for k, span in enumerate(spans):
+        back1[k], total = lax.optimization_barrier((back1[k], total))
+        (sums,) = combine(
+            [total, back1[k]], weights, [[(0, 0, None), (1, 0, None)]], F32, spans=[span], offsets=[0, span[0]]
+        )
+        halves.append(sums)
+        if k == 0:
+            total, sums = lax.optimization_barrier((total, sums))
+    back2, halves = lax.optimization_barrier((back2, halves))
+    total = merge(halves, back2)
     for step in range(steps - 3)[::-1]:
-        half = total.shape[0] // 2
-        total = add(total[:half], send(total[half:], ep, [step]))
+        count = total.shape[0] // 2
+        total = add(total[:count], send(total[count:], ep, [step]))
     return total
 
 

time: 72 us -> 76.8 us (1.067)
  starting transfers between devices: 23.9 us -> 30 us
  waiting for transfers between devices: 23.2 us -> 21.1 us
    ppermute x14 -> x20, starting transfers between devices: 21.3 us -> 27.5 us  [send(): return lax.ppermute(array, ('ep', 'sub'), pairs)]
    ppermute x14 -> x20, waiting for transfers between devices: 22.8 us -> 18.5 us  [send(): return lax.ppermute(array, ('ep', 'sub'), pairs)]
    ppermute x9, waiting for transfers between devices: 0.4 us -> 2.55 us  [cross(): return lax.ppermute(array, 'sub', [(0, 1), (1, 0)])]
    pallas_call x8 -> x12, Pallas kernels: 2.37 us -> 2.55 us  [the longest x11 1.79 us: combine(): pl.pallas_call(functools.partial(combine_kernel, rows, sums, spans, offse...]
  transfers between devices with their start and end apart: 23 -> 29, of which waited for: 10 -> 11; matrix products, arithmetic and copies ran while one was open for 0% -> 0% of each run, Pallas kernels for 19% -> 15%
where the time goes in v12:
time: 76.8 us; the launch traced here: 75.8 us
  starting transfers between devices  30 us (39%)
  waiting for transfers between devices  21.1 us (27%)
  Pallas kernels  18.7 us (24%)
  local copies, waits for them, and re-layouts  5.68 us (7%)
    ppermute x20, starting transfers between devices, send(): return lax.ppermute(array, ('ep', 'sub'), pairs)  27.5 us
    ppermute x20, waiting for transfers between devices, send(): return lax.ppermute(array, ('ep', 'sub'), pairs)  18.5 us
    pallas_call x5, Pallas kernels, expert(): pl.pallas_call(functools.partial(expert_kernel, pieces), in_specs=[pl.Blo...  11.6 us
    unnamed x10, local copies, waits for them, and re-layouts  5.68 us
    ppermute x9, waiting for transfers between devices, cross(): return lax.ppermute(array, 'sub', [(0, 1), (1, 0)])  2.55 us
    ppermute x9, starting transfers between devices, cross(): return lax.ppermute(array, 'sub', [(0, 1), (1, 0)])  2.48 us
    pallas_call x1, Pallas kernels, prepare(): pl.pallas_call(prepare_kernel, in_specs=[pl.BlockSpec(memory_space=pltpu....  1.94 us
    pallas_call x1, Pallas kernels, weigh(): pl.pallas_call(functools.partial(weigh_kernel, top, tok_rows), in_specs=[...  1.89 us
  transfers between devices with their start and end apart: 29, of which 11 were waited for; matrix products, arithmetic and copies ran while one was open for 0% of the time, Pallas kernels for 15%

profile of v12, /device:TPU:0, one launch (start us, length us, event | category | flops | bytes accessed | tf_op | source)
XLA Modules:
  0.0 75.8 jit_solution(2595120923507244800)
XLA Ops:
  0.0 1.9 %shard_map.82.refs_0_ = bf16[64,2176]{1,0:T(8,128)(2,1)} custom-call(s32[1]{0:T(128)} %bitcast.me_ref, bf16[64,2048]{1,0:T(8,128)(2,1)} %tokens_ref.1, s32[8,64]{1,0:T(8,128)} %bitcast.4, f32[8,64]{1,0:T(8,128)} %bitcast.5, s32[1,64]{1,0:T(1,128)} %bitcast.6), custom_call_target="tpu_custom_call" | custom-call | tf_op jit(solution)/shard_map/pallas_call | solution.py:48
  2.4 3.6 %collective-permute-start = (bf16[64,2176]{1,0:T(8,128)(2,1)}, bf16[64,2176]{1,0:T(8,128)(2,1)S(1)}, u32[]{:S(2)}, u32[]{:S(2)}) collective-permute-start(bf16[64,2176]{1,0:T(8,128)(2,1)} %shard_map.82.refs_0_), channel_id=1, source_target_pairs={{0,8},{1,9},{2,10},{3,11},{4,12},{5,13},{6,14},{7,15},{8,0},{9,1},... | collective-permute-start | bytes 835592 | tf_op jit(solution)/shard_map/ppermute | solution.py:272
  7.5 1.6 %collective-permute-start.2 = (bf16[64,2176]{1,0:T(8,128)(2,1)}, bf16[64,2176]{1,0:T(8,128)(2,1)S(1)}, u32[]{:S(2)}, u32[]{:S(2)}) collective-permute-start(bf16[64,2176]{1,0:T(8,128)(2,1)} %shard_map.82.refs_0_), channel_id=1, source_target_pairs={{0,4},{1,3},{2,6},{3,1},{4,0},{5,7},{6,2},{7,5},{8,12},{9,11},{10,... | collective-permute-start | bytes 835592 | tf_op jit(solution)/shard_map/ppermute | solution.py:272
  9.1 1.9 %copy-done = bf16[1,2048,768]{2,1,0:T(8,128)(2,1)S(1)} copy-done((bf16[1,2048,768]{2,1,0:T(8,128)(2,1)S(1)}, bf16[1,2048,768]{2,1,0:T(8,128)(2,1)}, u32[]{:S(2)}) %copy-start) | copy-done | bytes 3145752
  11.0 1.9 %copy-done.1 = bf16[1,2048,768]{2,1,0:T(8,128)(2,1)S(1)} copy-done((bf16[1,2048,768]{2,1,0:T(8,128)(2,1)S(1)}, bf16[1,2048,768]{2,1,0:T(8,128)(2,1)}, u32[]{:S(2)}) %copy-start.1) | copy-done | bytes 3145752
  12.9 1.9 %copy-done.2 = bf16[1,768,2048]{2,1,0:T(8,128)(2,1)S(1)} copy-done((bf16[1,768,2048]{2,1,0:T(8,128)(2,1)S(1)}, bf16[1,768,2048]{2,1,0:T(8,128)(2,1)}, u32[]{:S(2)}) %copy-start.2) | copy-done | bytes 3145752
  15.4 4.2 %collective-permute-done.refs_1_.refs_0_ = bf16[64,2176]{1,0:T(8,128)(2,1)S(1)} collective-permute-done((bf16[64,2176]{1,0:T(8,128)(2,1)}, bf16[64,2176]{1,0:T(8,128)(2,1)S(1)}, u32[]{:S(2)}, u32[]{:S(2)}) %collective-permute-start) | collective-permute-done | bytes 278560 | tf_op jit(solution)/shard_map/ppermute | solution.py:272
  19.9 1.6 %collective-permute-start.4 = (bf16[64,2176]{1,0:T(8,128)(2,1)S(1)}, bf16[64,2176]{1,0:T(8,128)(2,1)S(1)}, u32[]{:S(2)}, u32[]{:S(2)}) collective-permute-start(bf16[64,2176]{1,0:T(8,128)(2,1)S(1)} %collective-permute-done.refs_1_.refs_0_), channel_id=1, source_target_pairs={{0,4},{1,3},{2,6},{3,1},{4,0},{5,7},{6,2},{7,5},{8,12},{9,11},{10,... | collective-permute-start | bytes 835592 | tf_op jit(solution)/shard_map/ppermute | solution.py:272
  23.5 2.6 %shard_map.86 = bf16[256,2048]{1,0:T(8,128)(2,1)S(1)} custom-call(bf16[64,2176]{1,0:T(8,128)(2,1)S(1)} %collective-permute-done.1.refs_0_.refs_8_, bf16[192,2176]{1,0:T(8,128)(2,1)S(1)} %collective-permute-done.5.refs_1_.refs_9_, bf16[1,2048,768]{2,1,0:T(8,128)(2,1)S(1)} %get-tuple-element.59.refs_4_.refs_2_.refs_3_.refs_1_, ...), custom_call_target="tpu_custom_call" | custom-call | flops 1 | bytes 1 | tf_op jit(solution)/shard_map/pallas_call | solution.py:247
  26.1 2.7 %collective-permute-done.4.refs_0_.refs_6_ = bf16[64,2176]{1,0:T(8,128)(2,1)S(1)} collective-permute-done((bf16[64,2176]{1,0:T(8,128)(2,1)S(1)}, bf16[64,2176]{1,0:T(8,128)(2,1)S(1)}, u32[]{:S(2)}, u32[]{:S(2)}) %collective-permute-start.4) | collective-permute-done | bytes 278560 | tf_op jit(solution)/shard_map/ppermute | solution.py:272
  28.8 2.2 %collective-permute-start.8 = (bf16[64,2176]{1,0:T(8,128)(2,1)S(1)}, bf16[64,2176]{1,0:T(8,128)(2,1)S(1)}, u32[]{:S(2)}, u32[]{:S(2)}) collective-permute-start(bf16[64,2176]{1,0:T(8,128)(2,1)S(1)} %collective-permute-done.4.refs_0_.refs_6_), channel_id=1, source_target_pairs={{0,2},{1,5},{2,0},{3,7},{4,6},{5,1},{6,4},{7,3},{8,10},{9,13},{10,... | collective-permute-start | bytes 835592 | tf_op jit(solution)/shard_map/ppermute | solution.py:272
  32.8 2.0 %shard_map.87.refs_0_ = bf16[192,2048]{1,0:T(8,128)(2,1)S(1)} custom-call(bf16[64,2176]{1,0:T(8,128)(2,1)S(1)} %collective-permute-done.4.refs_0_.refs_6_, bf16[64,2176]{1,0:T(8,128)(2,1)S(1)} %collective-permute-done.6.refs_1_.refs_4_, bf16[64,2176]{1,0:T(8,128)(2,1)S(1)} %collective-permute-done.7.refs_2_.refs_7_, ...), custom_call_target="tpu_custom_call" | custom-call | flops 1 | bytes 1 | tf_op jit(solution)/shard_map/pallas_call | solution.py:247
  35.6 1.8 %shard_map.88.refs_1_ = bf16[64,2048]{1,0:T(8,128)(2,1)S(1)} custom-call(bf16[64,2176]{1,0:T(8,128)(2,1)S(1)} %collective-permute-done.8.refs_0_.refs_5_, bf16[1,2048,768]{2,1,0:T(8,128)(2,1)S(1)} %get-tuple-element.59.refs_4_.refs_2_.refs_3_.refs_1_, bf16[1,2048,768]{2,1,0:T(8,128)(2,1)S(1)} %get-tuple-element.60.refs_5_.refs_3_.refs_4_.refs_2_, ...), custom_call_target="tpu_custom_call" | custom-call | flops 1 | bytes 1 | tf_op jit(solution)/shard_map/pallas_call | solution.py:247
  37.4 2.6 %shard_map.89 = (bf16[128,2048]{1,0:T(8,128)(2,1)S(1)}, bf16[128,2048]{1,0:T(8,128)(2,1)S(1)}) custom-call(bf16[64,2176]{1,0:T(8,128)(2,1)S(1)} %collective-permute-done.9.refs_0_.refs_10_, bf16[64,2176]{1,0:T(8,128)(2,1)S(1)} %collective-permute-done.10.refs_1_.refs_11_, bf16[64,2176]{1,0:T(8,128)(2,1)S(1)} %collective-permute-done.11.refs_2_.refs_12_, ...), custom_call_target="tpu_custom_call" | custom-call | flops 1 | bytes 1 | tf_op jit(solution)/shard_map/pallas_call | solution.py:247
  40.1 1.9 %shard_map.90.refs_3_.refs_2_.refs_4_ = f32[1024,128]{1,0:T(8,128)S(1)} custom-call(s32[1]{0:T(128)} %bitcast.me_ref, s32[16]{0:T(128)S(1)} %copy-done.4, bf16[64,2176]{1,0:T(8,128)(2,1)S(1)} %copy-done.3, bf16[64,2176]{1,0:T(8,128)(2,1)S(1)} %collective-permute-done.refs_1_.refs_0_, bf16[64,2176]{1,0:T(8,128)(2,1)S(1)} %collective-permute-done.2.refs_2_.refs_1_, ...), custom_call_target="tpu_custom_call" | custom-call | flops 1 | bytes 1 | tf_op jit(solution)/shard_map/pallas_call | solution.py:114
  43.0 2.5 %collective-permute-done.13.refs_2_ = bf16[128,2048]{1,0:T(8,128)(2,1)S(1)} collective-permute-done((bf16[128,2048]{1,0:T(8,128)(2,1)S(1)}, bf16[128,2048]{1,0:T(8,128)(2,1)S(1)}, u32[]{:S(2)}, u32[]{:S(2)}) %collective-permute-start.13) | collective-permute-done | bytes 524320 | tf_op jit(solution)/shard_map/ppermute | solution.py:276
  45.9 2.1 %collective-permute-start.14 = (bf16[64,1024]{1,0:T(8,128)(2,1)S(1)}, bf16[64,1024]{1,0:T(8,128)(2,1)S(1)}, u32[]{:S(2)}, u32[]{:S(2)}) collective-permute-start(bf16[64,1024]{1,0:T(8,128)(2,1)S(1)} %get-tuple-element.79), channel_id=1, source_target_pairs={{0,2},{1,5},{2,0},{3,7},{4,6},{5,1},{6,4},{7,3},{8,10},{9,13},{10,... | collective-permute-start | bytes 393224 | tf_op jit(solution)/shard_map/ppermute | solution.py:272
  48.0 2.6 %shard_map.84.refs_0_ = bf16[256,2048]{1,0:T(8,128)(2,1)S(1)} custom-call(bf16[64,2176]{1,0:T(8,128)(2,1)S(1)} %copy-done.3, bf16[64,2176]{1,0:T(8,128)(2,1)S(1)} %collective-permute-done.refs_1_.refs_0_, bf16[64,2176]{1,0:T(8,128)(2,1)S(1)} %collective-permute-done.2.refs_2_.refs_1_, bf16[64,2176]{1,0:T(8,128)(2,1)S(1)} %collective-permute-done.3.refs_3_.refs_2_, ...), custom_call_target="tpu_custom_call" | custom-call | flops 1 | bytes 1 | tf_op jit(solution)/shard_map/pallas_call | solution.py:247
  50.7 2.0 %collective-permute-start.22 = (bf16[64,1024]{1,0:T(8,128)(2,1)S(1)}, bf16[64,1024]{1,0:T(8,128)(2,1)S(1)}, u32[]{:S(2)}, u32[]{:S(2)}) collective-permute-start(bf16[64,1024]{1,0:T(8,128)(2,1)S(1)} %get-tuple-element.89), channel_id=1, source_target_pairs={{0,2},{1,5},{2,0},{3,7},{4,6},{5,1},{6,4},{7,3},{8,10},{9,13},{10,... | collective-permute-start | bytes 393224 | tf_op jit(solution)/shard_map/ppermute | solution.py:272
  52.8 1.6 %collective-permute-start.21 = (bf16[64,1024]{1,0:T(8,128)(2,1)S(1)}, bf16[64,1024]{1,0:T(8,128)(2,1)S(1)}, u32[]{:S(2)}, u32[]{:S(2)}) collective-permute-start(bf16[64,1024]{1,0:T(8,128)(2,1)S(1)} %shard_map.92), channel_id=1, source_target_pairs={{0,4},{1,3},{2,6},{3,1},{4,0},{5,7},{6,2},{7,5},{8,12},{9,11},{10,... | collective-permute-start | bytes 393224 | tf_op jit(solution)/shard_map/ppermute | solution.py:272
  55.6 1.8 %collective-permute-start.27 = (bf16[64,2048]{1,0:T(8,128)(2,1)S(1)}, bf16[64,2048]{1,0:T(8,128)(2,1)S(1)}, u32[]{:S(2)}, u32[]{:S(2)}) collective-permute-start(bf16[64,2048]{1,0:T(8,128)(2,1)S(1)} %shard_map.98), channel_id=1, source_target_pairs={{0,2},{1,5},{2,0},{3,7},{4,6},{5,1},{6,4},{7,3},{8,10},{9,13},{10,... | collective-permute-start | bytes 786440 | tf_op jit(solution)/shard_map/ppermute | solution.py:272
  59.9 2.2 %collective-permute-done.20.refs_2_ = bf16[64,1024]{1,0:T(8,128)(2,1)S(1)} collective-permute-done((bf16[64,1024]{1,0:T(8,128)(2,1)S(1)}, bf16[64,1024]{1,0:T(8,128)(2,1)S(1)}, u32[]{:S(2)}, u32[]{:S(2)}) %collective-permute-start.20) | collective-permute-done | bytes 131104 | tf_op jit(solution)/shard_map/ppermute | solution.py:272
  62.1 1.5 %collective-permute-start.26 = (bf16[64,1024]{1,0:T(8,128)(2,1)S(1)}, bf16[64,1024]{1,0:T(8,128)(2,1)S(1)}, u32[]{:S(2)}, u32[]{:S(2)}) collective-permute-start(bf16[64,1024]{1,0:T(8,128)(2,1)S(1)} %shard_map.95), channel_id=1, source_target_pairs={{0,8},{1,9},{2,10},{3,11},{4,12},{5,13},{6,14},{7,15},{8,0},{9,1},... | collective-permute-start | bytes 393224 | tf_op jit(solution)/shard_map/ppermute | solution.py:272
  68.0 5.5 %collective-permute-done.26.refs_1_ = bf16[64,1024]{1,0:T(8,128)(2,1)S(1)} collective-permute-done((bf16[64,1024]{1,0:T(8,128)(2,1)S(1)}, bf16[64,1024]{1,0:T(8,128)(2,1)S(1)}, u32[]{:S(2)}, u32[]{:S(2)}) %collective-permute-start.26) | collective-permute-done | bytes 131104 | tf_op jit(solution)/shard_map/ppermute | solution.py:272
  (65 shorter events, 19.4 us)
Async XLA Ops:
  1.9 13.5 %collective-permute-start.1 = (bf16[64,2176]{1,0:T(8,128)(2,1)}, bf16[64,2176]{1,0:T(8,128)(2,1)S(1)}, u32[]{:S(2)}, u32[]{:S(2)}) collective-permute-start(bf16[64,2176]{1,0:T(8,128)(2,1)} %shard_map.82.refs_0_), channel_id=1, source_target_pairs={{0,1},{1,0},{2,3},{3,2},{4,5},{5,4},{6,7},{7,6},{8,9},{9,8},{10,11... | collective-permute-start | bytes 835592 | tf_op jit(solution)/shard_map/ppermute | solution.py:276
  2.4 17.2 %collective-permute-start = (bf16[64,2176]{1,0:T(8,128)(2,1)}, bf16[64,2176]{1,0:T(8,128)(2,1)S(1)}, u32[]{:S(2)}, u32[]{:S(2)}) collective-permute-start(bf16[64,2176]{1,0:T(8,128)(2,1)} %shard_map.82.refs_0_), channel_id=1, source_target_pairs={{0,8},{1,9},{2,10},{3,11},{4,12},{5,13},{6,14},{7,15},{8,0},{9,1},... | collective-permute-start | bytes 835592 | tf_op jit(solution)/shard_map/ppermute | solution.py:272
  6.0 13.6 %collective-permute-start.3 = (bf16[64,2176]{1,0:T(8,128)(2,1)}, bf16[64,2176]{1,0:T(8,128)(2,1)S(1)}, u32[]{:S(2)}, u32[]{:S(2)}) collective-permute-start(bf16[64,2176]{1,0:T(8,128)(2,1)} %shard_map.82.refs_0_), channel_id=1, source_target_pairs={{0,2},{1,5},{2,0},{3,7},{4,6},{5,1},{6,4},{7,3},{8,10},{9,13},{10,... | collective-permute-start | bytes 835592 | tf_op jit(solution)/shard_map/ppermute | solution.py:272
  7.5 12.3 %collective-permute-start.2 = (bf16[64,2176]{1,0:T(8,128)(2,1)}, bf16[64,2176]{1,0:T(8,128)(2,1)S(1)}, u32[]{:S(2)}, u32[]{:S(2)}) collective-permute-start(bf16[64,2176]{1,0:T(8,128)(2,1)} %shard_map.82.refs_0_), channel_id=1, source_target_pairs={{0,4},{1,3},{2,6},{3,1},{4,0},{5,7},{6,2},{7,5},{8,12},{9,11},{10,... | collective-permute-start | bytes 835592 | tf_op jit(solution)/shard_map/ppermute | solution.py:272
  19.9 8.9 %collective-permute-start.4 = (bf16[64,2176]{1,0:T(8,128)(2,1)S(1)}, bf16[64,2176]{1,0:T(8,128)(2,1)S(1)}, u32[]{:S(2)}, u32[]{:S(2)}) collective-permute-start(bf16[64,2176]{1,0:T(8,128)(2,1)S(1)} %collective-permute-done.refs_1_.refs_0_), channel_id=1, source_target_pairs={{0,4},{1,3},{2,6},{3,1},{4,0},{5,7},{6,2},{7,5},{8,12},{9,11},{10,... | collective-permute-start | bytes 835592 | tf_op jit(solution)/shard_map/ppermute | solution.py:272
  21.5 10.8 %collective-permute-start.6 = (bf16[64,2176]{1,0:T(8,128)(2,1)S(1)}, bf16[64,2176]{1,0:T(8,128)(2,1)S(1)}, u32[]{:S(2)}, u32[]{:S(2)}) collective-permute-start(bf16[64,2176]{1,0:T(8,128)(2,1)S(1)} %collective-permute-done.refs_1_.refs_0_), channel_id=1, source_target_pairs={{0,2},{1,5},{2,0},{3,7},{4,6},{5,1},{6,4},{7,3},{8,10},{9,13},{10,... | collective-permute-start | bytes 835592 | tf_op jit(solution)/shard_map/ppermute | solution.py:272
  23.0 9.0 %collective-permute-start.7 = (bf16[64,2176]{1,0:T(8,128)(2,1)S(1)}, bf16[64,2176]{1,0:T(8,128)(2,1)S(1)}, u32[]{:S(2)}, u32[]{:S(2)}) collective-permute-start(bf16[64,2176]{1,0:T(8,128)(2,1)S(1)} %collective-permute-done.2.refs_2_.refs_1_), channel_id=1, source_target_pairs={{0,2},{1,5},{2,0},{3,7},{4,6},{5,1},{6,4},{7,3},{8,10},{9,13},{10,... | collective-permute-start | bytes 835592 | tf_op jit(solution)/shard_map/ppermute | solution.py:272
  28.8 6.7 %collective-permute-start.8 = (bf16[64,2176]{1,0:T(8,128)(2,1)S(1)}, bf16[64,2176]{1,0:T(8,128)(2,1)S(1)}, u32[]{:S(2)}, u32[]{:S(2)}) collective-permute-start(bf16[64,2176]{1,0:T(8,128)(2,1)S(1)} %collective-permute-done.4.refs_0_.refs_6_), channel_id=1, source_target_pairs={{0,2},{1,5},{2,0},{3,7},{4,6},{5,1},{6,4},{7,3},{8,10},{9,13},{10,... | collective-permute-start | bytes 835592 | tf_op jit(solution)/shard_map/ppermute | solution.py:272
  32.0 5.4 %collective-permute-start.10 = (bf16[64,2176]{1,0:T(8,128)(2,1)S(1)}, bf16[64,2176]{1,0:T(8,128)(2,1)S(1)}, u32[]{:S(2)}, u32[]{:S(2)}) collective-permute-start(bf16[64,2176]{1,0:T(8,128)(2,1)S(1)} %collective-permute-done.7.refs_2_.refs_7_), channel_id=1, source_target_pairs={{0,1},{1,0},{2,3},{3,2},{4,5},{5,4},{6,7},{7,6},{8,9},{9,8},{10,11... | collective-permute-start | bytes 835592 | tf_op jit(solution)/shard_map/ppermute | solution.py:276
  42.0 13.4 %collective-permute-start.15 = (bf16[256,2048]{1,0:T(8,128)(2,1)S(1)}, bf16[256,2048]{1,0:T(8,128)(2,1)S(1)}, u32[]{:S(2)}, u32[]{:S(2)}) collective-permute-start(bf16[256,2048]{1,0:T(8,128)(2,1)S(1)} %shard_map.86), channel_id=1, source_target_pairs={{0,1},{1,0},{2,3},{3,2},{4,5},{5,4},{6,7},{7,6},{8,9},{9,8},{10,11... | collective-permute-start | bytes 3145736 | tf_op jit(solution)/shard_map/ppermute | solution.py:276
  42.6 10.1 %collective-permute-start.16 = (bf16[128,2048]{1,0:T(8,128)(2,1)S(1)}, bf16[128,2048]{1,0:T(8,128)(2,1)S(1)}, u32[]{:S(2)}, u32[]{:S(2)}) collective-permute-start(bf16[128,2048]{1,0:T(8,128)(2,1)S(1)} %get-tuple-element.82), channel_id=1, source_target_pairs={{0,1},{1,0},{2,3},{3,2},{4,5},{5,4},{6,7},{7,6},{8,9},{9,8},{10,11... | collective-permute-start | bytes 1572872 | tf_op jit(solution)/shard_map/ppermute | solution.py:276
  45.9 6.8 %collective-permute-start.14 = (bf16[64,1024]{1,0:T(8,128)(2,1)S(1)}, bf16[64,1024]{1,0:T(8,128)(2,1)S(1)}, u32[]{:S(2)}, u32[]{:S(2)}) collective-permute-start(bf16[64,1024]{1,0:T(8,128)(2,1)S(1)} %get-tuple-element.79), channel_id=1, source_target_pairs={{0,2},{1,5},{2,0},{3,7},{4,6},{5,1},{6,4},{7,3},{8,10},{9,13},{10,... | collective-permute-start | bytes 393224 | tf_op jit(solution)/shard_map/ppermute | solution.py:272
  48.0 6.7 %collective-permute-start.17 = (bf16[64,1024]{1,0:T(8,128)(2,1)S(1)}, bf16[64,1024]{1,0:T(8,128)(2,1)S(1)}, u32[]{:S(2)}, u32[]{:S(2)}) collective-permute-start(bf16[64,1024]{1,0:T(8,128)(2,1)S(1)} %get-tuple-element.83), channel_id=1, source_target_pairs={{0,2},{1,5},{2,0},{3,7},{4,6},{5,1},{6,4},{7,3},{8,10},{9,13},{10,... | collective-permute-start | bytes 393224 | tf_op jit(solution)/shard_map/ppermute | solution.py:272
  50.7 7.0 %collective-permute-start.22 = (bf16[64,1024]{1,0:T(8,128)(2,1)S(1)}, bf16[64,1024]{1,0:T(8,128)(2,1)S(1)}, u32[]{:S(2)}, u32[]{:S(2)}) collective-permute-start(bf16[64,1024]{1,0:T(8,128)(2,1)S(1)} %get-tuple-element.89), channel_id=1, source_target_pairs={{0,2},{1,5},{2,0},{3,7},{4,6},{5,1},{6,4},{7,3},{8,10},{9,13},{10,... | collective-permute-start | bytes 393224 | tf_op jit(solution)/shard_map/ppermute | solution.py:272
  52.8 6.4 %collective-permute-start.21 = (bf16[64,1024]{1,0:T(8,128)(2,1)S(1)}, bf16[64,1024]{1,0:T(8,128)(2,1)S(1)}, u32[]{:S(2)}, u32[]{:S(2)}) collective-permute-start(bf16[64,1024]{1,0:T(8,128)(2,1)S(1)} %shard_map.92), channel_id=1, source_target_pairs={{0,4},{1,3},{2,6},{3,1},{4,0},{5,7},{6,2},{7,5},{8,12},{9,11},{10,... | collective-permute-start | bytes 393224 | tf_op jit(solution)/shard_map/ppermute | solution.py:272
  54.4 9.2 %collective-permute-start.23 = (bf16[64,1024]{1,0:T(8,128)(2,1)S(1)}, bf16[64,1024]{1,0:T(8,128)(2,1)S(1)}, u32[]{:S(2)}, u32[]{:S(2)}) collective-permute-start(bf16[64,1024]{1,0:T(8,128)(2,1)S(1)} %get-tuple-element.91), channel_id=1, source_target_pairs={{0,2},{1,5},{2,0},{3,7},{4,6},{5,1},{6,4},{7,3},{8,10},{9,13},{10,... | collective-permute-start | bytes 393224 | tf_op jit(solution)/shard_map/ppermute | solution.py:272
  54.8 7.2 %collective-permute-start.20 = (bf16[64,1024]{1,0:T(8,128)(2,1)S(1)}, bf16[64,1024]{1,0:T(8,128)(2,1)S(1)}, u32[]{:S(2)}, u32[]{:S(2)}) collective-permute-start(bf16[64,1024]{1,0:T(8,128)(2,1)S(1)} %shard_map.93), channel_id=1, source_target_pairs={{0,4},{1,3},{2,6},{3,1},{4,0},{5,7},{6,2},{7,5},{8,12},{9,11},{10,... | collective-permute-start | bytes 393224 | tf_op jit(solution)/shard_map/ppermute | solution.py:272
  55.6 12.2 %collective-permute-start.27 = (bf16[64,2048]{1,0:T(8,128)(2,1)S(1)}, bf16[64,2048]{1,0:T(8,128)(2,1)S(1)}, u32[]{:S(2)}, u32[]{:S(2)}) collective-permute-start(bf16[64,2048]{1,0:T(8,128)(2,1)S(1)} %shard_map.98), channel_id=1, source_target_pairs={{0,2},{1,5},{2,0},{3,7},{4,6},{5,1},{6,4},{7,3},{8,10},{9,13},{10,... | collective-permute-start | bytes 786440 | tf_op jit(solution)/shard_map/ppermute | solution.py:272
  57.7 7.6 %collective-permute-start.18 = (bf16[64,1024]{1,0:T(8,128)(2,1)S(1)}, bf16[64,1024]{1,0:T(8,128)(2,1)S(1)}, u32[]{:S(2)}, u32[]{:S(2)}) collective-permute-start(bf16[64,1024]{1,0:T(8,128)(2,1)S(1)} %get-tuple-element.87), channel_id=1, source_target_pairs={{0,2},{1,5},{2,0},{3,7},{4,6},{5,1},{6,4},{7,3},{8,10},{9,13},{10,... | collective-permute-start | bytes 393224 | tf_op jit(solution)/shard_map/ppermute | solution.py:272
  59.3 6.3 %collective-permute-start.19 = (bf16[64,1024]{1,0:T(8,128)(2,1)S(1)}, bf16[64,1024]{1,0:T(8,128)(2,1)S(1)}, u32[]{:S(2)}, u32[]{:S(2)}) collective-permute-start(bf16[64,1024]{1,0:T(8,128)(2,1)S(1)} %get-tuple-element.88), channel_id=1, source_target_pairs={{0,2},{1,5},{2,0},{3,7},{4,6},{5,1},{6,4},{7,3},{8,10},{9,13},{10,... | collective-permute-start | bytes 393224 | tf_op jit(solution)/shard_map/ppermute | solution.py:272
  62.1 11.5 %collective-permute-start.26 = (bf16[64,1024]{1,0:T(8,128)(2,1)S(1)}, bf16[64,1024]{1,0:T(8,128)(2,1)S(1)}, u32[]{:S(2)}, u32[]{:S(2)}) collective-permute-start(bf16[64,1024]{1,0:T(8,128)(2,1)S(1)} %shard_map.95), channel_id=1, source_target_pairs={{0,8},{1,9},{2,10},{3,11},{4,12},{5,13},{6,14},{7,15},{8,0},{9,1},... | collective-permute-start | bytes 393224 | tf_op jit(solution)/shard_map/ppermute | solution.py:272
  63.8 11.2 %collective-permute-start.28 = (bf16[64,1024]{1,0:T(8,128)(2,1)S(1)}, bf16[64,1024]{1,0:T(8,128)(2,1)S(1)}, u32[]{:S(2)}, u32[]{:S(2)}) collective-permute-start(bf16[64,1024]{1,0:T(8,128)(2,1)S(1)} %shard_map.96), channel_id=1, source_target_pairs={{0,8},{1,9},{2,10},{3,11},{4,12},{5,13},{6,14},{7,15},{8,0},{9,1},... | collective-permute-start | bytes 393224 | tf_op jit(solution)/shard_map/ppermute | solution.py:272
  65.7 9.3 %collective-permute-start.24 = (bf16[64,1024]{1,0:T(8,128)(2,1)S(1)}, bf16[64,1024]{1,0:T(8,128)(2,1)S(1)}, u32[]{:S(2)}, u32[]{:S(2)}) collective-permute-start(bf16[64,1024]{1,0:T(8,128)(2,1)S(1)} %get-tuple-element.94), channel_id=1, source_target_pairs={{0,4},{1,3},{2,6},{3,1},{4,0},{5,7},{6,2},{7,5},{8,12},{9,11},{10,... | collective-permute-start | bytes 393224 | tf_op jit(solution)/shard_map/ppermute | solution.py:272
  66.9 8.1 %collective-permute-start.25 = (bf16[64,1024]{1,0:T(8,128)(2,1)S(1)}, bf16[64,1024]{1,0:T(8,128)(2,1)S(1)}, u32[]{:S(2)}, u32[]{:S(2)}) collective-permute-start(bf16[64,1024]{1,0:T(8,128)(2,1)S(1)} %get-tuple-element.95), channel_id=1, source_target_pairs={{0,4},{1,3},{2,6},{3,1},{4,0},{5,7},{6,2},{7,5},{8,12},{9,11},{10,... | collective-permute-start | bytes 393224 | tf_op jit(solution)/shard_map/ppermute | solution.py:272
  (10 other events, 29.7 us)

commit v13 on v11

--- a/solution.py
+++ b/solution.py
@@ -271,7 +271,7 @@
     own1, own2, own4 = send(held, ep, [-3]), send(held, ep, [-2]), send(held, ep, [-1])
     first = cross(held)
     matrices = load(w_gate, w_up, w_down)
-    own1, first, matrices = lax.optimization_barrier((own1, first, matrices))
+    first, own4, own2, own1, matrices = lax.optimization_barrier((first, own4, own2, own1, matrices))
     crossed = cross(pack([own1, own2, own4]))
     own3 = send(own1, ep, [-2])
     own5 = send(own1, ep, [-1])

time: 72 us -> 73.2 us (1.017)
  waiting for transfers between devices: 23.2 us -> 30.6 us
  starting transfers between devices: 23.9 us -> 17.7 us
    ppermute x14, waiting for transfers between devices: 22.8 us -> 30.2 us  [send(): return lax.ppermute(array, ('ep', 'sub'), pairs)]
    ppermute x14, starting transfers between devices: 21.3 us -> 15.9 us  [send(): return lax.ppermute(array, ('ep', 'sub'), pairs)]
    ppermute x9, starting transfers between devices: 2.55 us -> 1.74 us  [cross(): return lax.ppermute(array, 'sub', [(0, 1), (1, 0)])]
  transfers between devices with their start and end apart: 23 -> 23, of which waited for: 10 -> 11; matrix products, arithmetic and copies ran while one was open for 0% -> 0% of each run, Pallas kernels for 19% -> 18%
where the time goes in v13:
time: 73.2 us; the launch traced here: 72.9 us
  waiting for transfers between devices  30.6 us (42%)
  Pallas kernels  18.7 us (26%)
  starting transfers between devices  17.7 us (24%)
  local copies, waits for them, and re-layouts  5.68 us (8%)
    ppermute x14, waiting for transfers between devices, send(): return lax.ppermute(array, ('ep', 'sub'), pairs)  30.2 us
    ppermute x14, starting transfers between devices, send(): return lax.ppermute(array, ('ep', 'sub'), pairs)  15.9 us
    pallas_call x5, Pallas kernels, expert(): pl.pallas_call(functools.partial(expert_kernel, pieces), in_specs=[pl.Blo...  11.8 us
    unnamed x10, local copies, waits for them, and re-layouts  5.68 us
    pallas_call x8, Pallas kernels, combine(): pl.pallas_call(functools.partial(combine_kernel, rows, sums, len(arrays))...  2.37 us
    pallas_call x1, Pallas kernels, prepare(): pl.pallas_call(prepare_kernel, in_specs=[pl.BlockSpec(memory_space=pltpu....  1.95 us
    pallas_call x1, Pallas kernels, weigh(): pl.pallas_call(functools.partial(weigh_kernel, top, tok_rows), in_specs=[...  1.89 us
    ppermute x9, starting transfers between devices, cross(): return lax.ppermute(array, 'sub', [(0, 1), (1, 0)])  1.74 us
  transfers between devices with their start and end apart: 23, of which 11 were waited for; matrix products, arithmetic and copies ran while one was open for 0% of the time, Pallas kernels for 18%

profile of v13, /device:TPU:0, one launch (start us, length us, event | category | flops | bytes accessed | tf_op | source)
XLA Modules:
  0.0 72.9 jit_solution(5677537127452881283)
XLA Ops:
  0.0 1.9 %shard_map.82.refs_0_ = bf16[64,2176]{1,0:T(8,128)(2,1)} custom-call(s32[1]{0:T(128)} %bitcast.me_ref, bf16[64,2048]{1,0:T(8,128)(2,1)} %tokens_ref.1, s32[8,64]{1,0:T(8,128)} %bitcast.4, f32[8,64]{1,0:T(8,128)} %bitcast.5, s32[1,64]{1,0:T(1,128)} %bitcast.6), custom_call_target="tpu_custom_call" | custom-call | tf_op jit(solution)/shard_map/pallas_call | solution.py:48
  1.9 4.0 %collective-permute-start.3 = (bf16[64,2176]{1,0:T(8,128)(2,1)}, bf16[64,2176]{1,0:T(8,128)(2,1)S(1)}, u32[]{:S(2)}, u32[]{:S(2)}) collective-permute-start(bf16[64,2176]{1,0:T(8,128)(2,1)} %shard_map.82.refs_0_), channel_id=1, source_target_pairs={{0,8},{1,9},{2,10},{3,11},{4,12},{5,13},{6,14},{7,15},{8,0},{9,1},... | collective-permute-start | bytes 835592 | tf_op jit(solution)/shard_map/ppermute | solution.py:251
  6.0 1.6 %collective-permute-start.2 = (bf16[64,2176]{1,0:T(8,128)(2,1)}, bf16[64,2176]{1,0:T(8,128)(2,1)S(1)}, u32[]{:S(2)}, u32[]{:S(2)}) collective-permute-start(bf16[64,2176]{1,0:T(8,128)(2,1)} %shard_map.82.refs_0_), channel_id=1, source_target_pairs={{0,4},{1,3},{2,6},{3,1},{4,0},{5,7},{6,2},{7,5},{8,12},{9,11},{10,... | collective-permute-start | bytes 835592 | tf_op jit(solution)/shard_map/ppermute | solution.py:251
  7.6 1.5 %collective-permute-start.1 = (bf16[64,2176]{1,0:T(8,128)(2,1)}, bf16[64,2176]{1,0:T(8,128)(2,1)S(1)}, u32[]{:S(2)}, u32[]{:S(2)}) collective-permute-start(bf16[64,2176]{1,0:T(8,128)(2,1)} %shard_map.82.refs_0_), channel_id=1, source_target_pairs={{0,2},{1,5},{2,0},{3,7},{4,6},{5,1},{6,4},{7,3},{8,10},{9,13},{10,... | collective-permute-start | bytes 835592 | tf_op jit(solution)/shard_map/ppermute | solution.py:251
  9.1 1.9 %copy-done = bf16[1,2048,768]{2,1,0:T(8,128)(2,1)S(1)} copy-done((bf16[1,2048,768]{2,1,0:T(8,128)(2,1)S(1)}, bf16[1,2048,768]{2,1,0:T(8,128)(2,1)}, u32[]{:S(2)}) %copy-start) | copy-done | bytes 3145752
  11.0 1.9 %copy-done.1 = bf16[1,2048,768]{2,1,0:T(8,128)(2,1)S(1)} copy-done((bf16[1,2048,768]{2,1,0:T(8,128)(2,1)S(1)}, bf16[1,2048,768]{2,1,0:T(8,128)(2,1)}, u32[]{:S(2)}) %copy-start.1) | copy-done | bytes 3145752
  12.9 1.9 %copy-done.2 = bf16[1,768,2048]{2,1,0:T(8,128)(2,1)S(1)} copy-done((bf16[1,768,2048]{2,1,0:T(8,128)(2,1)S(1)}, bf16[1,768,2048]{2,1,0:T(8,128)(2,1)}, u32[]{:S(2)}) %copy-start.2) | copy-done | bytes 3145752
  15.4 3.5 %collective-permute-done.3.refs_1_.refs_0_ = bf16[64,2176]{1,0:T(8,128)(2,1)S(1)} collective-permute-done((bf16[64,2176]{1,0:T(8,128)(2,1)}, bf16[64,2176]{1,0:T(8,128)(2,1)S(1)}, u32[]{:S(2)}, u32[]{:S(2)}) %collective-permute-start.3) | collective-permute-done | bytes 278560 | tf_op jit(solution)/shard_map/ppermute | solution.py:251
  20.8 1.5 %collective-permute-start.7 = (bf16[64,2176]{1,0:T(8,128)(2,1)S(1)}, bf16[64,2176]{1,0:T(8,128)(2,1)S(1)}, u32[]{:S(2)}, u32[]{:S(2)}) collective-permute-start(bf16[64,2176]{1,0:T(8,128)(2,1)S(1)} %collective-permute-done.2.refs_2_.refs_1_), channel_id=1, source_target_pairs={{0,2},{1,5},{2,0},{3,7},{4,6},{5,1},{6,4},{7,3},{8,10},{9,13},{10,... | collective-permute-start | bytes 835592 | tf_op jit(solution)/shard_map/ppermute | solution.py:251
  22.9 2.6 %shard_map.86 = bf16[256,2048]{1,0:T(8,128)(2,1)S(1)} custom-call(bf16[64,2176]{1,0:T(8,128)(2,1)S(1)} %collective-permute-done.refs_0_.refs_8_, bf16[192,2176]{1,0:T(8,128)(2,1)S(1)} %collective-permute-done.5.refs_1_.refs_9_, bf16[1,2048,768]{2,1,0:T(8,128)(2,1)S(1)} %get-tuple-element.52.refs_4_.refs_2_.refs_3_.refs_1_, ...), custom_call_target="tpu_custom_call" | custom-call | flops 1 | bytes 1 | tf_op jit(solution)/shard_map/pallas_call | solution.py:226
  25.5 4.6 %collective-permute-done.4.refs_0_.refs_6_ = bf16[64,2176]{1,0:T(8,128)(2,1)S(1)} collective-permute-done((bf16[64,2176]{1,0:T(8,128)(2,1)S(1)}, bf16[64,2176]{1,0:T(8,128)(2,1)S(1)}, u32[]{:S(2)}, u32[]{:S(2)}) %collective-permute-start.4) | collective-permute-done | bytes 278560 | tf_op jit(solution)/shard_map/ppermute | solution.py:251
  30.1 2.4 %collective-permute-done.6.refs_1_.refs_4_ = bf16[64,2176]{1,0:T(8,128)(2,1)S(1)} collective-permute-done((bf16[64,2176]{1,0:T(8,128)(2,1)S(1)}, bf16[64,2176]{1,0:T(8,128)(2,1)S(1)}, u32[]{:S(2)}, u32[]{:S(2)}) %collective-permute-start.6) | collective-permute-done | bytes 278560 | tf_op jit(solution)/shard_map/ppermute | solution.py:251
  33.1 2.0 %shard_map.87.refs_0_ = bf16[192,2048]{1,0:T(8,128)(2,1)S(1)} custom-call(bf16[64,2176]{1,0:T(8,128)(2,1)S(1)} %collective-permute-done.4.refs_0_.refs_6_, bf16[64,2176]{1,0:T(8,128)(2,1)S(1)} %collective-permute-done.6.refs_1_.refs_4_, bf16[64,2176]{1,0:T(8,128)(2,1)S(1)} %collective-permute-done.7.refs_2_.refs_7_, ...), custom_call_target="tpu_custom_call" | custom-call | flops 1 | bytes 1 | tf_op jit(solution)/shard_map/pallas_call | solution.py:226
  35.1 1.5 %collective-permute-done.8.refs_0_.refs_5_ = bf16[64,2176]{1,0:T(8,128)(2,1)S(1)} collective-permute-done((bf16[64,2176]{1,0:T(8,128)(2,1)S(1)}, bf16[64,2176]{1,0:T(8,128)(2,1)S(1)}, u32[]{:S(2)}, u32[]{:S(2)}) %collective-permute-start.8) | collective-permute-done | bytes 278560 | tf_op jit(solution)/shard_map/ppermute | solution.py:251
  36.6 1.8 %shard_map.88.refs_1_ = bf16[64,2048]{1,0:T(8,128)(2,1)S(1)} custom-call(bf16[64,2176]{1,0:T(8,128)(2,1)S(1)} %collective-permute-done.8.refs_0_.refs_5_, bf16[1,2048,768]{2,1,0:T(8,128)(2,1)S(1)} %get-tuple-element.52.refs_4_.refs_2_.refs_3_.refs_1_, bf16[1,2048,768]{2,1,0:T(8,128)(2,1)S(1)} %get-tuple-element.53.refs_5_.refs_3_.refs_4_.refs_2_, ...), custom_call_target="tpu_custom_call" | custom-call | flops 1 | bytes 1 | tf_op jit(solution)/shard_map/pallas_call | solution.py:226
  38.5 2.7 %shard_map.90 = (bf16[128,2048]{1,0:T(8,128)(2,1)S(1)}, bf16[128,2048]{1,0:T(8,128)(2,1)S(1)}) custom-call(bf16[64,2176]{1,0:T(8,128)(2,1)S(1)} %collective-permute-done.9.refs_10_.refs_0_, bf16[64,2176]{1,0:T(8,128)(2,1)S(1)} %collective-permute-done.10.refs_11_.refs_1_, bf16[64,2176]{1,0:T(8,128)(2,1)S(1)} %collective-permute-done.11.refs_12_.refs_2_, ...), custom_call_target="tpu_custom_call" | custom-call | flops 1 | bytes 1 | tf_op jit(solution)/shard_map/pallas_call | solution.py:226
  41.8 1.9 %shard_map.89.refs_3_.refs_2_.refs_4_ = f32[1024,128]{1,0:T(8,128)S(1)} custom-call(s32[1]{0:T(128)} %bitcast.me_ref, s32[16]{0:T(128)S(1)} %copy-done.4, bf16[64,2176]{1,0:T(8,128)(2,1)S(1)} %copy-done.3, bf16[64,2176]{1,0:T(8,128)(2,1)S(1)} %collective-permute-done.3.refs_1_.refs_0_, bf16[64,2176]{1,0:T(8,128)(2,1)S(1)} %collective-permute-done.2.refs_2_.refs_1_, ...), custom_call_target="tpu_custom_call" | custom-call | flops 1 | bytes 1 | tf_op jit(solution)/shard_map/pallas_call | solution.py:114
  44.7 2.0 %collective-permute-start.19 = (bf16[64,2048]{1,0:T(8,128)(2,1)S(1)}, bf16[64,2048]{1,0:T(8,128)(2,1)S(1)}, u32[]{:S(2)}, u32[]{:S(2)}) collective-permute-start(bf16[64,2048]{1,0:T(8,128)(2,1)S(1)} %get-tuple-element.79), channel_id=1, source_target_pairs={{0,2},{1,5},{2,0},{3,7},{4,6},{5,1},{6,4},{7,3},{8,10},{9,13},{10,... | collective-permute-start | bytes 786440 | tf_op jit(solution)/shard_map/ppermute | solution.py:251
  47.2 3.9 %collective-permute-done.15.refs_2_ = bf16[64,2048]{1,0:T(8,128)(2,1)S(1)} collective-permute-done((bf16[64,2048]{1,0:T(8,128)(2,1)S(1)}, bf16[64,2048]{1,0:T(8,128)(2,1)S(1)}, u32[]{:S(2)}, u32[]{:S(2)}) %collective-permute-start.15) | collective-permute-done | bytes 262176 | tf_op jit(solution)/shard_map/ppermute | solution.py:251
  51.5 2.6 %shard_map.84.refs_0_ = bf16[256,2048]{1,0:T(8,128)(2,1)S(1)} custom-call(bf16[64,2176]{1,0:T(8,128)(2,1)S(1)} %copy-done.3, bf16[64,2176]{1,0:T(8,128)(2,1)S(1)} %collective-permute-done.3.refs_1_.refs_0_, bf16[64,2176]{1,0:T(8,128)(2,1)S(1)} %collective-permute-done.2.refs_2_.refs_1_, bf16[64,2176]{1,0:T(8,128)(2,1)S(1)} %collective-permute-done.1.refs_3_.refs_2_, ...), custom_call_target="tpu_custom_call" | custom-call | flops 1 | bytes 1 | tf_op jit(solution)/shard_map/pallas_call | solution.py:226
  54.1 1.8 %collective-permute-start.17 = (bf16[64,2048]{1,0:T(8,128)(2,1)S(1)}, bf16[64,2048]{1,0:T(8,128)(2,1)S(1)}, u32[]{:S(2)}, u32[]{:S(2)}) collective-permute-start(bf16[64,2048]{1,0:T(8,128)(2,1)S(1)} %get-tuple-element.77), channel_id=1, source_target_pairs={{0,2},{1,5},{2,0},{3,7},{4,6},{5,1},{6,4},{7,3},{8,10},{9,13},{10,... | collective-permute-start | bytes 786440 | tf_op jit(solution)/shard_map/ppermute | solution.py:251
  56.5 3.2 %collective-permute-done.18.refs_2_ = bf16[64,2048]{1,0:T(8,128)(2,1)S(1)} collective-permute-done((bf16[64,2048]{1,0:T(8,128)(2,1)S(1)}, bf16[64,2048]{1,0:T(8,128)(2,1)S(1)}, u32[]{:S(2)}, u32[]{:S(2)}) %collective-permute-start.18) | collective-permute-done | bytes 262176 | tf_op jit(solution)/shard_map/ppermute | solution.py:251
  60.8 2.1 %collective-permute-start.20 = (bf16[64,2048]{1,0:T(8,128)(2,1)S(1)}, bf16[64,2048]{1,0:T(8,128)(2,1)S(1)}, u32[]{:S(2)}, u32[]{:S(2)}) collective-permute-start(bf16[64,2048]{1,0:T(8,128)(2,1)S(1)} %shard_map.95), channel_id=1, source_target_pairs={{0,4},{1,3},{2,6},{3,1},{4,0},{5,7},{6,2},{7,5},{8,12},{9,11},{10,... | collective-permute-start | bytes 786440 | tf_op jit(solution)/shard_map/ppermute | solution.py:251
  64.0 8.1 %collective-permute-done.21.refs_1_ = bf16[64,2048]{1,0:T(8,128)(2,1)S(1)} collective-permute-done((bf16[64,2048]{1,0:T(8,128)(2,1)S(1)}, bf16[64,2048]{1,0:T(8,128)(2,1)S(1)}, u32[]{:S(2)}, u32[]{:S(2)}) %collective-permute-start.21) | collective-permute-done | bytes 262176 | tf_op jit(solution)/shard_map/ppermute | solution.py:251
  (49 shorter events, 9.6 us)
Async XLA Ops:
  1.9 17.0 %collective-permute-start.3 = (bf16[64,2176]{1,0:T(8,128)(2,1)}, bf16[64,2176]{1,0:T(8,128)(2,1)S(1)}, u32[]{:S(2)}, u32[]{:S(2)}) collective-permute-start(bf16[64,2176]{1,0:T(8,128)(2,1)} %shard_map.82.refs_0_), channel_id=1, source_target_pairs={{0,8},{1,9},{2,10},{3,11},{4,12},{5,13},{6,14},{7,15},{8,0},{9,1},... | collective-permute-start | bytes 835592 | tf_op jit(solution)/shard_map/ppermute | solution.py:251
  6.0 14.4 %collective-permute-start.2 = (bf16[64,2176]{1,0:T(8,128)(2,1)}, bf16[64,2176]{1,0:T(8,128)(2,1)S(1)}, u32[]{:S(2)}, u32[]{:S(2)}) collective-permute-start(bf16[64,2176]{1,0:T(8,128)(2,1)} %shard_map.82.refs_0_), channel_id=1, source_target_pairs={{0,4},{1,3},{2,6},{3,1},{4,0},{5,7},{6,2},{7,5},{8,12},{9,11},{10,... | collective-permute-start | bytes 835592 | tf_op jit(solution)/shard_map/ppermute | solution.py:251
  7.6 12.8 %collective-permute-start.1 = (bf16[64,2176]{1,0:T(8,128)(2,1)}, bf16[64,2176]{1,0:T(8,128)(2,1)S(1)}, u32[]{:S(2)}, u32[]{:S(2)}) collective-permute-start(bf16[64,2176]{1,0:T(8,128)(2,1)} %shard_map.82.refs_0_), channel_id=1, source_target_pairs={{0,2},{1,5},{2,0},{3,7},{4,6},{5,1},{6,4},{7,3},{8,10},{9,13},{10,... | collective-permute-start | bytes 835592 | tf_op jit(solution)/shard_map/ppermute | solution.py:251
  9.1 11.3 %collective-permute-start = (bf16[64,2176]{1,0:T(8,128)(2,1)}, bf16[64,2176]{1,0:T(8,128)(2,1)S(1)}, u32[]{:S(2)}, u32[]{:S(2)}) collective-permute-start(bf16[64,2176]{1,0:T(8,128)(2,1)} %shard_map.82.refs_0_), channel_id=1, source_target_pairs={{0,1},{1,0},{2,3},{3,2},{4,5},{5,4},{6,7},{7,6},{8,9},{9,8},{10,11... | collective-permute-start | bytes 835592 | tf_op jit(solution)/shard_map/ppermute | solution.py:255
  20.4 2.4 %collective-permute-start.5 = (bf16[192,2176]{1,0:T(8,128)(2,1)S(1)}, bf16[192,2176]{1,0:T(8,128)(2,1)S(1)}, u32[]{:S(2)}, u32[]{:S(2)}) collective-permute-start(bf16[192,2176]{1,0:T(8,128)(2,1)S(1)} %shard_map.85), channel_id=1, source_target_pairs={{0,1},{1,0},{2,3},{3,2},{4,5},{5,4},{6,7},{7,6},{8,9},{9,8},{10,11... | collective-permute-start | bytes 2506760 | tf_op jit(solution)/shard_map/ppermute | solution.py:255
  20.5 9.6 %collective-permute-start.4 = (bf16[64,2176]{1,0:T(8,128)(2,1)S(1)}, bf16[64,2176]{1,0:T(8,128)(2,1)S(1)}, u32[]{:S(2)}, u32[]{:S(2)}) collective-permute-start(bf16[64,2176]{1,0:T(8,128)(2,1)S(1)} %collective-permute-done.3.refs_1_.refs_0_), channel_id=1, source_target_pairs={{0,4},{1,3},{2,6},{3,1},{4,0},{5,7},{6,2},{7,5},{8,12},{9,11},{10,... | collective-permute-start | bytes 835592 | tf_op jit(solution)/shard_map/ppermute | solution.py:251
  20.8 9.3 %collective-permute-start.7 = (bf16[64,2176]{1,0:T(8,128)(2,1)S(1)}, bf16[64,2176]{1,0:T(8,128)(2,1)S(1)}, u32[]{:S(2)}, u32[]{:S(2)}) collective-permute-start(bf16[64,2176]{1,0:T(8,128)(2,1)S(1)} %collective-permute-done.2.refs_2_.refs_1_), channel_id=1, source_target_pairs={{0,2},{1,5},{2,0},{3,7},{4,6},{5,1},{6,4},{7,3},{8,10},{9,13},{10,... | collective-permute-start | bytes 835592 | tf_op jit(solution)/shard_map/ppermute | solution.py:251
  22.3 10.2 %collective-permute-start.6 = (bf16[64,2176]{1,0:T(8,128)(2,1)S(1)}, bf16[64,2176]{1,0:T(8,128)(2,1)S(1)}, u32[]{:S(2)}, u32[]{:S(2)}) collective-permute-start(bf16[64,2176]{1,0:T(8,128)(2,1)S(1)} %collective-permute-done.3.refs_1_.refs_0_), channel_id=1, source_target_pairs={{0,2},{1,5},{2,0},{3,7},{4,6},{5,1},{6,4},{7,3},{8,10},{9,13},{10,... | collective-permute-start | bytes 835592 | tf_op jit(solution)/shard_map/ppermute | solution.py:251
  30.1 6.5 %collective-permute-start.8 = (bf16[64,2176]{1,0:T(8,128)(2,1)S(1)}, bf16[64,2176]{1,0:T(8,128)(2,1)S(1)}, u32[]{:S(2)}, u32[]{:S(2)}) collective-permute-start(bf16[64,2176]{1,0:T(8,128)(2,1)S(1)} %collective-permute-done.4.refs_0_.refs_6_), channel_id=1, source_target_pairs={{0,2},{1,5},{2,0},{3,7},{4,6},{5,1},{6,4},{7,3},{8,10},{9,13},{10,... | collective-permute-start | bytes 835592 | tf_op jit(solution)/shard_map/ppermute | solution.py:251
  30.1 8.4 %collective-permute-start.10 = (bf16[64,2176]{1,0:T(8,128)(2,1)S(1)}, bf16[64,2176]{1,0:T(8,128)(2,1)S(1)}, u32[]{:S(2)}, u32[]{:S(2)}) collective-permute-start(bf16[64,2176]{1,0:T(8,128)(2,1)S(1)} %collective-permute-done.7.refs_2_.refs_7_), channel_id=1, source_target_pairs={{0,1},{1,0},{2,3},{3,2},{4,5},{5,4},{6,7},{7,6},{8,9},{9,8},{10,11... | collective-permute-start | bytes 835592 | tf_op jit(solution)/shard_map/ppermute | solution.py:255
  32.5 5.9 %collective-permute-start.11 = (bf16[64,2176]{1,0:T(8,128)(2,1)S(1)}, bf16[64,2176]{1,0:T(8,128)(2,1)S(1)}, u32[]{:S(2)}, u32[]{:S(2)}) collective-permute-start(bf16[64,2176]{1,0:T(8,128)(2,1)S(1)} %collective-permute-done.6.refs_1_.refs_4_), channel_id=1, source_target_pairs={{0,1},{1,0},{2,3},{3,2},{4,5},{5,4},{6,7},{7,6},{8,9},{9,8},{10,11... | collective-permute-start | bytes 835592 | tf_op jit(solution)/shard_map/ppermute | solution.py:255
  32.7 5.8 %collective-permute-start.9 = (bf16[64,2176]{1,0:T(8,128)(2,1)S(1)}, bf16[64,2176]{1,0:T(8,128)(2,1)S(1)}, u32[]{:S(2)}, u32[]{:S(2)}) collective-permute-start(bf16[64,2176]{1,0:T(8,128)(2,1)S(1)} %collective-permute-done.4.refs_0_.refs_6_), channel_id=1, source_target_pairs={{0,1},{1,0},{2,3},{3,2},{4,5},{5,4},{6,7},{7,6},{8,9},{9,8},{10,11... | collective-permute-start | bytes 835592 | tf_op jit(solution)/shard_map/ppermute | solution.py:255
  36.6 1.9 %collective-permute-start.12 = (bf16[64,2176]{1,0:T(8,128)(2,1)S(1)}, bf16[64,2176]{1,0:T(8,128)(2,1)S(1)}, u32[]{:S(2)}, u32[]{:S(2)}) collective-permute-start(bf16[64,2176]{1,0:T(8,128)(2,1)S(1)} %collective-permute-done.8.refs_0_.refs_5_), channel_id=1, source_target_pairs={{0,1},{1,0},{2,3},{3,2},{4,5},{5,4},{6,7},{7,6},{8,9},{9,8},{10,11... | collective-permute-start | bytes 835592 | tf_op jit(solution)/shard_map/ppermute | solution.py:255
  38.5 3.3 %copy-start.3 = (bf16[64,2176]{1,0:T(8,128)(2,1)S(1)}, bf16[64,2176]{1,0:T(8,128)(2,1)}, u32[]{:S(2)}) copy-start(bf16[64,2176]{1,0:T(8,128)(2,1)} %shard_map.82.refs_0_) | copy-start | bytes 835588
  41.2 3.1 %collective-permute-start.14 = (bf16[128,2048]{1,0:T(8,128)(2,1)S(1)}, bf16[128,2048]{1,0:T(8,128)(2,1)S(1)}, u32[]{:S(2)}, u32[]{:S(2)}) collective-permute-start(bf16[128,2048]{1,0:T(8,128)(2,1)S(1)} %get-tuple-element.71), channel_id=1, source_target_pairs={{0,1},{1,0},{2,3},{3,2},{4,5},{5,4},{6,7},{7,6},{8,9},{9,8},{10,11... | collective-permute-start | bytes 1572872 | tf_op jit(solution)/shard_map/ppermute | solution.py:255
  43.7 12.3 %collective-permute-start.16 = (bf16[256,2048]{1,0:T(8,128)(2,1)S(1)}, bf16[256,2048]{1,0:T(8,128)(2,1)S(1)}, u32[]{:S(2)}, u32[]{:S(2)}) collective-permute-start(bf16[256,2048]{1,0:T(8,128)(2,1)S(1)} %shard_map.86), channel_id=1, source_target_pairs={{0,1},{1,0},{2,3},{3,2},{4,5},{5,4},{6,7},{7,6},{8,9},{9,8},{10,11... | collective-permute-start | bytes 3145736 | tf_op jit(solution)/shard_map/ppermute | solution.py:255
  43.8 3.4 %collective-permute-start.13 = (bf16[128,2048]{1,0:T(8,128)(2,1)S(1)}, bf16[128,2048]{1,0:T(8,128)(2,1)S(1)}, u32[]{:S(2)}, u32[]{:S(2)}) collective-permute-start(bf16[128,2048]{1,0:T(8,128)(2,1)S(1)} %get-tuple-element.69), channel_id=1, source_target_pairs={{0,1},{1,0},{2,3},{3,2},{4,5},{5,4},{6,7},{7,6},{8,9},{9,8},{10,11... | collective-permute-start | bytes 1572872 | tf_op jit(solution)/shard_map/ppermute | solution.py:255
  44.6 6.4 %collective-permute-start.15 = (bf16[64,2048]{1,0:T(8,128)(2,1)S(1)}, bf16[64,2048]{1,0:T(8,128)(2,1)S(1)}, u32[]{:S(2)}, u32[]{:S(2)}) collective-permute-start(bf16[64,2048]{1,0:T(8,128)(2,1)S(1)} %get-tuple-element.73), channel_id=1, source_target_pairs={{0,2},{1,5},{2,0},{3,7},{4,6},{5,1},{6,4},{7,3},{8,10},{9,13},{10,... | collective-permute-start | bytes 786440 | tf_op jit(solution)/shard_map/ppermute | solution.py:251
  44.7 11.8 %collective-permute-start.19 = (bf16[64,2048]{1,0:T(8,128)(2,1)S(1)}, bf16[64,2048]{1,0:T(8,128)(2,1)S(1)}, u32[]{:S(2)}, u32[]{:S(2)}) collective-permute-start(bf16[64,2048]{1,0:T(8,128)(2,1)S(1)} %get-tuple-element.79), channel_id=1, source_target_pairs={{0,2},{1,5},{2,0},{3,7},{4,6},{5,1},{6,4},{7,3},{8,10},{9,13},{10,... | collective-permute-start | bytes 786440 | tf_op jit(solution)/shard_map/ppermute | solution.py:251
  51.4 8.3 %collective-permute-start.18 = (bf16[64,2048]{1,0:T(8,128)(2,1)S(1)}, bf16[64,2048]{1,0:T(8,128)(2,1)S(1)}, u32[]{:S(2)}, u32[]{:S(2)}) collective-permute-start(bf16[64,2048]{1,0:T(8,128)(2,1)S(1)} %get-tuple-element.78), channel_id=1, source_target_pairs={{0,4},{1,3},{2,6},{3,1},{4,0},{5,7},{6,2},{7,5},{8,12},{9,11},{10,... | collective-permute-start | bytes 786440 | tf_op jit(solution)/shard_map/ppermute | solution.py:251
  54.1 6.4 %collective-permute-start.17 = (bf16[64,2048]{1,0:T(8,128)(2,1)S(1)}, bf16[64,2048]{1,0:T(8,128)(2,1)S(1)}, u32[]{:S(2)}, u32[]{:S(2)}) collective-permute-start(bf16[64,2048]{1,0:T(8,128)(2,1)S(1)} %get-tuple-element.77), channel_id=1, source_target_pairs={{0,2},{1,5},{2,0},{3,7},{4,6},{5,1},{6,4},{7,3},{8,10},{9,13},{10,... | collective-permute-start | bytes 786440 | tf_op jit(solution)/shard_map/ppermute | solution.py:251
  56.2 7.6 %collective-permute-start.22 = (bf16[64,2048]{1,0:T(8,128)(2,1)S(1)}, bf16[64,2048]{1,0:T(8,128)(2,1)S(1)}, u32[]{:S(2)}, u32[]{:S(2)}) collective-permute-start(bf16[64,2048]{1,0:T(8,128)(2,1)S(1)} %shard_map.93), channel_id=1, source_target_pairs={{0,2},{1,5},{2,0},{3,7},{4,6},{5,1},{6,4},{7,3},{8,10},{9,13},{10,... | collective-permute-start | bytes 786440 | tf_op jit(solution)/shard_map/ppermute | solution.py:251
  59.9 12.2 %collective-permute-start.21 = (bf16[64,2048]{1,0:T(8,128)(2,1)S(1)}, bf16[64,2048]{1,0:T(8,128)(2,1)S(1)}, u32[]{:S(2)}, u32[]{:S(2)}) collective-permute-start(bf16[64,2048]{1,0:T(8,128)(2,1)S(1)} %shard_map.94), channel_id=1, source_target_pairs={{0,8},{1,9},{2,10},{3,11},{4,12},{5,13},{6,14},{7,15},{8,0},{9,1},... | collective-permute-start | bytes 786440 | tf_op jit(solution)/shard_map/ppermute | solution.py:251
  60.8 11.4 %collective-permute-start.20 = (bf16[64,2048]{1,0:T(8,128)(2,1)S(1)}, bf16[64,2048]{1,0:T(8,128)(2,1)S(1)}, u32[]{:S(2)}, u32[]{:S(2)}) collective-permute-start(bf16[64,2048]{1,0:T(8,128)(2,1)S(1)} %shard_map.95), channel_id=1, source_target_pairs={{0,4},{1,3},{2,6},{3,1},{4,0},{5,7},{6,2},{7,5},{8,12},{9,11},{10,... | collective-permute-start | bytes 786440 | tf_op jit(solution)/shard_map/ppermute | solution.py:251
  (4 other events, 9.0 us)

commit v14 on v13

--- a/solution.py
+++ b/solution.py
@@ -271,7 +271,7 @@
     own1, own2, own4 = send(held, ep, [-3]), send(held, ep, [-2]), send(held, ep, [-1])
     first = cross(held)
     matrices = load(w_gate, w_up, w_down)
-    first, own4, own2, own1, matrices = lax.optimization_barrier((first, own4, own2, own1, matrices))
+    first, own1, matrices = lax.optimization_barrier((first, own1, matrices))
     crossed = cross(pack([own1, own2, own4]))
     own3 = send(own1, ep, [-2])
     own5 = send(own1, ep, [-1])

time: 73.2 us -> 72.2 us (0.986)
  waiting for transfers between devices: 30.6 us -> 25 us
  starting transfers between devices: 17.7 us -> 22.4 us
    ppermute x14, waiting for transfers between devices: 30.2 us -> 24.6 us  [send(): return lax.ppermute(array, ('ep', 'sub'), pairs)]
    ppermute x14, starting transfers between devices: 15.9 us -> 20.3 us  [send(): return lax.ppermute(array, ('ep', 'sub'), pairs)]
where the time goes in v14:
time: 72.2 us; the launch traced here: 72 us
  waiting for transfers between devices  25 us (35%)
  starting transfers between devices  22.4 us (31%)
  Pallas kernels  18.7 us (26%)
  local copies, waits for them, and re-layouts  5.68 us (8%)
    ppermute x14, waiting for transfers between devices, send(): return lax.ppermute(array, ('ep', 'sub'), pairs)  24.6 us
    ppermute x14, starting transfers between devices, send(): return lax.ppermute(array, ('ep', 'sub'), pairs)  20.3 us
    pallas_call x5, Pallas kernels, expert(): pl.pallas_call(functools.partial(expert_kernel, pieces), in_specs=[pl.Blo...  11.8 us
    unnamed x10, local copies, waits for them, and re-layouts  5.68 us
    pallas_call x8, Pallas kernels, combine(): pl.pallas_call(functools.partial(combine_kernel, rows, sums, len(arrays))...  2.37 us
    ppermute x9, starting transfers between devices, cross(): return lax.ppermute(array, 'sub', [(0, 1), (1, 0)])  2.09 us
    pallas_call x1, Pallas kernels, prepare(): pl.pallas_call(prepare_kernel, in_specs=[pl.BlockSpec(memory_space=pltpu....  1.95 us
    pallas_call x1, Pallas kernels, weigh(): pl.pallas_call(functools.partial(weigh_kernel, top, tok_rows), in_specs=[...  1.89 us
  transfers between devices with their start and end apart: 23, of which 11 were waited for; matrix products, arithmetic and copies ran while one was open for 0% of the time, Pallas kernels for 18%

profile of v14, /device:TPU:0, one launch (start us, length us, event | category | flops | bytes accessed | tf_op | source)
XLA Modules:
  0.0 72.0 jit_solution(14071440927307675192)
XLA Ops:
  0.0 1.9 %shard_map.82.refs_0_ = bf16[64,2176]{1,0:T(8,128)(2,1)} custom-call(s32[1]{0:T(128)} %bitcast.me_ref, bf16[64,2048]{1,0:T(8,128)(2,1)} %tokens_ref.1, s32[8,64]{1,0:T(8,128)} %bitcast.4, f32[8,64]{1,0:T(8,128)} %bitcast.5, s32[1,64]{1,0:T(1,128)} %bitcast.6), custom_call_target="tpu_custom_call" | custom-call | tf_op jit(solution)/shard_map/pallas_call | solution.py:48
  1.9 4.0 %collective-permute-start.1 = (bf16[64,2176]{1,0:T(8,128)(2,1)}, bf16[64,2176]{1,0:T(8,128)(2,1)S(1)}, u32[]{:S(2)}, u32[]{:S(2)}) collective-permute-start(bf16[64,2176]{1,0:T(8,128)(2,1)} %shard_map.82.refs_0_), channel_id=1, source_target_pairs={{0,8},{1,9},{2,10},{3,11},{4,12},{5,13},{6,14},{7,15},{8,0},{9,1},... | collective-permute-start | bytes 835592 | tf_op jit(solution)/shard_map/ppermute | solution.py:251
  6.0 1.5 %collective-permute-start.3 = (bf16[64,2176]{1,0:T(8,128)(2,1)}, bf16[64,2176]{1,0:T(8,128)(2,1)S(1)}, u32[]{:S(2)}, u32[]{:S(2)}) collective-permute-start(bf16[64,2176]{1,0:T(8,128)(2,1)} %shard_map.82.refs_0_), channel_id=1, source_target_pairs={{0,2},{1,5},{2,0},{3,7},{4,6},{5,1},{6,4},{7,3},{8,10},{9,13},{10,... | collective-permute-start | bytes 835592 | tf_op jit(solution)/shard_map/ppermute | solution.py:251
  7.5 1.6 %collective-permute-start.2 = (bf16[64,2176]{1,0:T(8,128)(2,1)}, bf16[64,2176]{1,0:T(8,128)(2,1)S(1)}, u32[]{:S(2)}, u32[]{:S(2)}) collective-permute-start(bf16[64,2176]{1,0:T(8,128)(2,1)} %shard_map.82.refs_0_), channel_id=1, source_target_pairs={{0,4},{1,3},{2,6},{3,1},{4,0},{5,7},{6,2},{7,5},{8,12},{9,11},{10,... | collective-permute-start | bytes 835592 | tf_op jit(solution)/shard_map/ppermute | solution.py:251
  9.1 1.9 %copy-done = bf16[1,2048,768]{2,1,0:T(8,128)(2,1)S(1)} copy-done((bf16[1,2048,768]{2,1,0:T(8,128)(2,1)S(1)}, bf16[1,2048,768]{2,1,0:T(8,128)(2,1)}, u32[]{:S(2)}) %copy-start) | copy-done | bytes 3145752
  11.0 1.9 %copy-done.1 = bf16[1,2048,768]{2,1,0:T(8,128)(2,1)S(1)} copy-done((bf16[1,2048,768]{2,1,0:T(8,128)(2,1)S(1)}, bf16[1,2048,768]{2,1,0:T(8,128)(2,1)}, u32[]{:S(2)}) %copy-start.1) | copy-done | bytes 3145752
  12.9 1.9 %copy-done.2 = bf16[1,768,2048]{2,1,0:T(8,128)(2,1)S(1)} copy-done((bf16[1,768,2048]{2,1,0:T(8,128)(2,1)S(1)}, bf16[1,768,2048]{2,1,0:T(8,128)(2,1)}, u32[]{:S(2)}) %copy-start.2) | copy-done | bytes 3145752
  15.4 3.5 %collective-permute-done.1.refs_1_.refs_0_ = bf16[64,2176]{1,0:T(8,128)(2,1)S(1)} collective-permute-done((bf16[64,2176]{1,0:T(8,128)(2,1)}, bf16[64,2176]{1,0:T(8,128)(2,1)S(1)}, u32[]{:S(2)}, u32[]{:S(2)}) %collective-permute-start.1) | collective-permute-done | bytes 278560 | tf_op jit(solution)/shard_map/ppermute | solution.py:251
  20.8 1.5 %collective-permute-start.6 = (bf16[64,2176]{1,0:T(8,128)(2,1)S(1)}, bf16[64,2176]{1,0:T(8,128)(2,1)S(1)}, u32[]{:S(2)}, u32[]{:S(2)}) collective-permute-start(bf16[64,2176]{1,0:T(8,128)(2,1)S(1)} %collective-permute-done.1.refs_1_.refs_0_), channel_id=1, source_target_pairs={{0,2},{1,5},{2,0},{3,7},{4,6},{5,1},{6,4},{7,3},{8,10},{9,13},{10,... | collective-permute-start | bytes 835592 | tf_op jit(solution)/shard_map/ppermute | solution.py:251
  22.8 2.6 %shard_map.86 = bf16[256,2048]{1,0:T(8,128)(2,1)S(1)} custom-call(bf16[64,2176]{1,0:T(8,128)(2,1)S(1)} %collective-permute-done.refs_0_.refs_8_, bf16[192,2176]{1,0:T(8,128)(2,1)S(1)} %collective-permute-done.5.refs_1_.refs_9_, bf16[1,2048,768]{2,1,0:T(8,128)(2,1)S(1)} %get-tuple-element.48.refs_4_.refs_2_.refs_3_.refs_1_, ...), custom_call_target="tpu_custom_call" | custom-call | flops 1 | bytes 1 | tf_op jit(solution)/shard_map/pallas_call | solution.py:226
  25.5 3.6 %collective-permute-done.4.refs_0_.refs_6_ = bf16[64,2176]{1,0:T(8,128)(2,1)S(1)} collective-permute-done((bf16[64,2176]{1,0:T(8,128)(2,1)S(1)}, bf16[64,2176]{1,0:T(8,128)(2,1)S(1)}, u32[]{:S(2)}, u32[]{:S(2)}) %collective-permute-start.4) | collective-permute-done | bytes 278560 | tf_op jit(solution)/shard_map/ppermute | solution.py:251
  29.1 2.2 %collective-permute-start.8 = (bf16[64,2176]{1,0:T(8,128)(2,1)S(1)}, bf16[64,2176]{1,0:T(8,128)(2,1)S(1)}, u32[]{:S(2)}, u32[]{:S(2)}) collective-permute-start(bf16[64,2176]{1,0:T(8,128)(2,1)S(1)} %collective-permute-done.4.refs_0_.refs_6_), channel_id=1, source_target_pairs={{0,2},{1,5},{2,0},{3,7},{4,6},{5,1},{6,4},{7,3},{8,10},{9,13},{10,... | collective-permute-start | bytes 835592 | tf_op jit(solution)/shard_map/ppermute | solution.py:251
  33.1 2.0 %shard_map.87.refs_0_ = bf16[192,2048]{1,0:T(8,128)(2,1)S(1)} custom-call(bf16[64,2176]{1,0:T(8,128)(2,1)S(1)} %collective-permute-done.4.refs_0_.refs_6_, bf16[64,2176]{1,0:T(8,128)(2,1)S(1)} %collective-permute-done.6.refs_1_.refs_4_, bf16[64,2176]{1,0:T(8,128)(2,1)S(1)} %collective-permute-done.7.refs_2_.refs_7_, ...), custom_call_target="tpu_custom_call" | custom-call | flops 1 | bytes 1 | tf_op jit(solution)/shard_map/pallas_call | solution.py:226
  35.9 1.8 %shard_map.88.refs_1_ = bf16[64,2048]{1,0:T(8,128)(2,1)S(1)} custom-call(bf16[64,2176]{1,0:T(8,128)(2,1)S(1)} %collective-permute-done.8.refs_0_.refs_5_, bf16[1,2048,768]{2,1,0:T(8,128)(2,1)S(1)} %get-tuple-element.48.refs_4_.refs_2_.refs_3_.refs_1_, bf16[1,2048,768]{2,1,0:T(8,128)(2,1)S(1)} %get-tuple-element.49.refs_5_.refs_3_.refs_4_.refs_2_, ...), custom_call_target="tpu_custom_call" | custom-call | flops 1 | bytes 1 | tf_op jit(solution)/shard_map/pallas_call | solution.py:226
  37.8 2.7 %shard_map.90 = (bf16[128,2048]{1,0:T(8,128)(2,1)S(1)}, bf16[128,2048]{1,0:T(8,128)(2,1)S(1)}) custom-call(bf16[64,2176]{1,0:T(8,128)(2,1)S(1)} %collective-permute-done.9.refs_10_.refs_0_, bf16[64,2176]{1,0:T(8,128)(2,1)S(1)} %collective-permute-done.10.refs_11_.refs_1_, bf16[64,2176]{1,0:T(8,128)(2,1)S(1)} %collective-permute-done.11.refs_12_.refs_2_, ...), custom_call_target="tpu_custom_call" | custom-call | flops 1 | bytes 1 | tf_op jit(solution)/shard_map/pallas_call | solution.py:226
  40.9 1.9 %shard_map.89.refs_3_.refs_2_.refs_4_ = f32[1024,128]{1,0:T(8,128)S(1)} custom-call(s32[1]{0:T(128)} %bitcast.me_ref, s32[16]{0:T(128)S(1)} %copy-done.4, bf16[64,2176]{1,0:T(8,128)(2,1)S(1)} %copy-done.3, bf16[64,2176]{1,0:T(8,128)(2,1)S(1)} %collective-permute-done.1.refs_1_.refs_0_, bf16[64,2176]{1,0:T(8,128)(2,1)S(1)} %collective-permute-done.2.refs_2_.refs_1_, ...), custom_call_target="tpu_custom_call" | custom-call | flops 1 | bytes 1 | tf_op jit(solution)/shard_map/pallas_call | solution.py:114
  43.8 2.1 %collective-permute-start.15 = (bf16[64,2048]{1,0:T(8,128)(2,1)S(1)}, bf16[64,2048]{1,0:T(8,128)(2,1)S(1)}, u32[]{:S(2)}, u32[]{:S(2)}) collective-permute-start(bf16[64,2048]{1,0:T(8,128)(2,1)S(1)} %get-tuple-element.69), channel_id=1, source_target_pairs={{0,2},{1,5},{2,0},{3,7},{4,6},{5,1},{6,4},{7,3},{8,10},{9,13},{10,... | collective-permute-start | bytes 786440 | tf_op jit(solution)/shard_map/ppermute | solution.py:251
  46.3 3.9 %collective-permute-done.15.refs_2_ = bf16[64,2048]{1,0:T(8,128)(2,1)S(1)} collective-permute-done((bf16[64,2048]{1,0:T(8,128)(2,1)S(1)}, bf16[64,2048]{1,0:T(8,128)(2,1)S(1)}, u32[]{:S(2)}, u32[]{:S(2)}) %collective-permute-start.15) | collective-permute-done | bytes 262176 | tf_op jit(solution)/shard_map/ppermute | solution.py:251
  51.2 2.6 %shard_map.84.refs_0_ = bf16[256,2048]{1,0:T(8,128)(2,1)S(1)} custom-call(bf16[64,2176]{1,0:T(8,128)(2,1)S(1)} %copy-done.3, bf16[64,2176]{1,0:T(8,128)(2,1)S(1)} %collective-permute-done.1.refs_1_.refs_0_, bf16[64,2176]{1,0:T(8,128)(2,1)S(1)} %collective-permute-done.2.refs_2_.refs_1_, bf16[64,2176]{1,0:T(8,128)(2,1)S(1)} %collective-permute-done.3.refs_3_.refs_2_, ...), custom_call_target="tpu_custom_call" | custom-call | flops 1 | bytes 1 | tf_op jit(solution)/shard_map/pallas_call | solution.py:226
  53.9 2.1 %collective-permute-start.17 = (bf16[64,2048]{1,0:T(8,128)(2,1)S(1)}, bf16[64,2048]{1,0:T(8,128)(2,1)S(1)}, u32[]{:S(2)}, u32[]{:S(2)}) collective-permute-start(bf16[64,2048]{1,0:T(8,128)(2,1)S(1)} %get-tuple-element.73), channel_id=1, source_target_pairs={{0,2},{1,5},{2,0},{3,7},{4,6},{5,1},{6,4},{7,3},{8,10},{9,13},{10,... | collective-permute-start | bytes 786440 | tf_op jit(solution)/shard_map/ppermute | solution.py:251
  57.3 1.8 %collective-permute-start.21 = (bf16[64,2048]{1,0:T(8,128)(2,1)S(1)}, bf16[64,2048]{1,0:T(8,128)(2,1)S(1)}, u32[]{:S(2)}, u32[]{:S(2)}) collective-permute-start(bf16[64,2048]{1,0:T(8,128)(2,1)S(1)} %shard_map.94), channel_id=1, source_target_pairs={{0,8},{1,9},{2,10},{3,11},{4,12},{5,13},{6,14},{7,15},{8,0},{9,1},... | collective-permute-start | bytes 786440 | tf_op jit(solution)/shard_map/ppermute | solution.py:251
  59.1 1.2 %collective-permute-done.17.refs_2_ = bf16[64,2048]{1,0:T(8,128)(2,1)S(1)} collective-permute-done((bf16[64,2048]{1,0:T(8,128)(2,1)S(1)}, bf16[64,2048]{1,0:T(8,128)(2,1)S(1)}, u32[]{:S(2)}, u32[]{:S(2)}) %collective-permute-start.17) | collective-permute-done | bytes 262176 | tf_op jit(solution)/shard_map/ppermute | solution.py:251
  60.5 1.5 %collective-permute-start.20 = (bf16[64,2048]{1,0:T(8,128)(2,1)S(1)}, bf16[64,2048]{1,0:T(8,128)(2,1)S(1)}, u32[]{:S(2)}, u32[]{:S(2)}) collective-permute-start(bf16[64,2048]{1,0:T(8,128)(2,1)S(1)} %shard_map.95), channel_id=1, source_target_pairs={{0,4},{1,3},{2,6},{3,1},{4,0},{5,7},{6,2},{7,5},{8,12},{9,11},{10,... | collective-permute-start | bytes 786440 | tf_op jit(solution)/shard_map/ppermute | solution.py:251
  63.3 7.8 %collective-permute-done.21.refs_1_ = bf16[64,2048]{1,0:T(8,128)(2,1)S(1)} collective-permute-done((bf16[64,2048]{1,0:T(8,128)(2,1)S(1)}, bf16[64,2048]{1,0:T(8,128)(2,1)S(1)}, u32[]{:S(2)}, u32[]{:S(2)}) %collective-permute-start.21) | collective-permute-done | bytes 262176 | tf_op jit(solution)/shard_map/ppermute | solution.py:251
  (49 shorter events, 12.1 us)
Async XLA Ops:
  1.9 17.0 %collective-permute-start.1 = (bf16[64,2176]{1,0:T(8,128)(2,1)}, bf16[64,2176]{1,0:T(8,128)(2,1)S(1)}, u32[]{:S(2)}, u32[]{:S(2)}) collective-permute-start(bf16[64,2176]{1,0:T(8,128)(2,1)} %shard_map.82.refs_0_), channel_id=1, source_target_pairs={{0,8},{1,9},{2,10},{3,11},{4,12},{5,13},{6,14},{7,15},{8,0},{9,1},... | collective-permute-start | bytes 835592 | tf_op jit(solution)/shard_map/ppermute | solution.py:251
  6.0 12.9 %collective-permute-start = (bf16[64,2176]{1,0:T(8,128)(2,1)}, bf16[64,2176]{1,0:T(8,128)(2,1)S(1)}, u32[]{:S(2)}, u32[]{:S(2)}) collective-permute-start(bf16[64,2176]{1,0:T(8,128)(2,1)} %shard_map.82.refs_0_), channel_id=1, source_target_pairs={{0,1},{1,0},{2,3},{3,2},{4,5},{5,4},{6,7},{7,6},{8,9},{9,8},{10,11... | collective-permute-start | bytes 835592 | tf_op jit(solution)/shard_map/ppermute | solution.py:255
  6.0 12.9 %collective-permute-start.3 = (bf16[64,2176]{1,0:T(8,128)(2,1)}, bf16[64,2176]{1,0:T(8,128)(2,1)S(1)}, u32[]{:S(2)}, u32[]{:S(2)}) collective-permute-start(bf16[64,2176]{1,0:T(8,128)(2,1)} %shard_map.82.refs_0_), channel_id=1, source_target_pairs={{0,2},{1,5},{2,0},{3,7},{4,6},{5,1},{6,4},{7,3},{8,10},{9,13},{10,... | collective-permute-start | bytes 835592 | tf_op jit(solution)/shard_map/ppermute | solution.py:251
  7.5 12.6 %collective-permute-start.2 = (bf16[64,2176]{1,0:T(8,128)(2,1)}, bf16[64,2176]{1,0:T(8,128)(2,1)S(1)}, u32[]{:S(2)}, u32[]{:S(2)}) collective-permute-start(bf16[64,2176]{1,0:T(8,128)(2,1)} %shard_map.82.refs_0_), channel_id=1, source_target_pairs={{0,4},{1,3},{2,6},{3,1},{4,0},{5,7},{6,2},{7,5},{8,12},{9,11},{10,... | collective-permute-start | bytes 835592 | tf_op jit(solution)/shard_map/ppermute | solution.py:251
  20.1 2.7 %collective-permute-start.5 = (bf16[192,2176]{1,0:T(8,128)(2,1)S(1)}, bf16[192,2176]{1,0:T(8,128)(2,1)S(1)}, u32[]{:S(2)}, u32[]{:S(2)}) collective-permute-start(bf16[192,2176]{1,0:T(8,128)(2,1)S(1)} %shard_map.85), channel_id=1, source_target_pairs={{0,1},{1,0},{2,3},{3,2},{4,5},{5,4},{6,7},{7,6},{8,9},{9,8},{10,11... | collective-permute-start | bytes 2506760 | tf_op jit(solution)/shard_map/ppermute | solution.py:255
  20.2 8.9 %collective-permute-start.4 = (bf16[64,2176]{1,0:T(8,128)(2,1)S(1)}, bf16[64,2176]{1,0:T(8,128)(2,1)S(1)}, u32[]{:S(2)}, u32[]{:S(2)}) collective-permute-start(bf16[64,2176]{1,0:T(8,128)(2,1)S(1)} %collective-permute-done.1.refs_1_.refs_0_), channel_id=1, source_target_pairs={{0,4},{1,3},{2,6},{3,1},{4,0},{5,7},{6,2},{7,5},{8,12},{9,11},{10,... | collective-permute-start | bytes 835592 | tf_op jit(solution)/shard_map/ppermute | solution.py:251
  20.8 11.8 %collective-permute-start.6 = (bf16[64,2176]{1,0:T(8,128)(2,1)S(1)}, bf16[64,2176]{1,0:T(8,128)(2,1)S(1)}, u32[]{:S(2)}, u32[]{:S(2)}) collective-permute-start(bf16[64,2176]{1,0:T(8,128)(2,1)S(1)} %collective-permute-done.1.refs_1_.refs_0_), channel_id=1, source_target_pairs={{0,2},{1,5},{2,0},{3,7},{4,6},{5,1},{6,4},{7,3},{8,10},{9,13},{10,... | collective-permute-start | bytes 835592 | tf_op jit(solution)/shard_map/ppermute | solution.py:251
  22.3 9.9 %collective-permute-start.7 = (bf16[64,2176]{1,0:T(8,128)(2,1)S(1)}, bf16[64,2176]{1,0:T(8,128)(2,1)S(1)}, u32[]{:S(2)}, u32[]{:S(2)}) collective-permute-start(bf16[64,2176]{1,0:T(8,128)(2,1)S(1)} %collective-permute-done.2.refs_2_.refs_1_), channel_id=1, source_target_pairs={{0,2},{1,5},{2,0},{3,7},{4,6},{5,1},{6,4},{7,3},{8,10},{9,13},{10,... | collective-permute-start | bytes 835592 | tf_op jit(solution)/shard_map/ppermute | solution.py:251
  29.1 6.7 %collective-permute-start.8 = (bf16[64,2176]{1,0:T(8,128)(2,1)S(1)}, bf16[64,2176]{1,0:T(8,128)(2,1)S(1)}, u32[]{:S(2)}, u32[]{:S(2)}) collective-permute-start(bf16[64,2176]{1,0:T(8,128)(2,1)S(1)} %collective-permute-done.4.refs_0_.refs_6_), channel_id=1, source_target_pairs={{0,2},{1,5},{2,0},{3,7},{4,6},{5,1},{6,4},{7,3},{8,10},{9,13},{10,... | collective-permute-start | bytes 835592 | tf_op jit(solution)/shard_map/ppermute | solution.py:251
  32.3 5.5 %collective-permute-start.10 = (bf16[64,2176]{1,0:T(8,128)(2,1)S(1)}, bf16[64,2176]{1,0:T(8,128)(2,1)S(1)}, u32[]{:S(2)}, u32[]{:S(2)}) collective-permute-start(bf16[64,2176]{1,0:T(8,128)(2,1)S(1)} %collective-permute-done.7.refs_2_.refs_7_), channel_id=1, source_target_pairs={{0,1},{1,0},{2,3},{3,2},{4,5},{5,4},{6,7},{7,6},{8,9},{9,8},{10,11... | collective-permute-start | bytes 835592 | tf_op jit(solution)/shard_map/ppermute | solution.py:255
  32.6 5.1 %collective-permute-start.11 = (bf16[64,2176]{1,0:T(8,128)(2,1)S(1)}, bf16[64,2176]{1,0:T(8,128)(2,1)S(1)}, u32[]{:S(2)}, u32[]{:S(2)}) collective-permute-start(bf16[64,2176]{1,0:T(8,128)(2,1)S(1)} %collective-permute-done.6.refs_1_.refs_4_), channel_id=1, source_target_pairs={{0,1},{1,0},{2,3},{3,2},{4,5},{5,4},{6,7},{7,6},{8,9},{9,8},{10,11... | collective-permute-start | bytes 835592 | tf_op jit(solution)/shard_map/ppermute | solution.py:255
  32.8 5.0 %collective-permute-start.9 = (bf16[64,2176]{1,0:T(8,128)(2,1)S(1)}, bf16[64,2176]{1,0:T(8,128)(2,1)S(1)}, u32[]{:S(2)}, u32[]{:S(2)}) collective-permute-start(bf16[64,2176]{1,0:T(8,128)(2,1)S(1)} %collective-permute-done.4.refs_0_.refs_6_), channel_id=1, source_target_pairs={{0,1},{1,0},{2,3},{3,2},{4,5},{5,4},{6,7},{7,6},{8,9},{9,8},{10,11... | collective-permute-start | bytes 835592 | tf_op jit(solution)/shard_map/ppermute | solution.py:255
  35.8 1.9 %collective-permute-start.12 = (bf16[64,2176]{1,0:T(8,128)(2,1)S(1)}, bf16[64,2176]{1,0:T(8,128)(2,1)S(1)}, u32[]{:S(2)}, u32[]{:S(2)}) collective-permute-start(bf16[64,2176]{1,0:T(8,128)(2,1)S(1)} %collective-permute-done.8.refs_0_.refs_5_), channel_id=1, source_target_pairs={{0,1},{1,0},{2,3},{3,2},{4,5},{5,4},{6,7},{7,6},{8,9},{9,8},{10,11... | collective-permute-start | bytes 835592 | tf_op jit(solution)/shard_map/ppermute | solution.py:255
  37.7 3.2 %copy-start.3 = (bf16[64,2176]{1,0:T(8,128)(2,1)S(1)}, bf16[64,2176]{1,0:T(8,128)(2,1)}, u32[]{:S(2)}) copy-start(bf16[64,2176]{1,0:T(8,128)(2,1)} %shard_map.82.refs_0_) | copy-start | bytes 835588
  40.5 3.0 %collective-permute-start.14 = (bf16[128,2048]{1,0:T(8,128)(2,1)S(1)}, bf16[128,2048]{1,0:T(8,128)(2,1)S(1)}, u32[]{:S(2)}, u32[]{:S(2)}) collective-permute-start(bf16[128,2048]{1,0:T(8,128)(2,1)S(1)} %get-tuple-element.67), channel_id=1, source_target_pairs={{0,1},{1,0},{2,3},{3,2},{4,5},{5,4},{6,7},{7,6},{8,9},{9,8},{10,11... | collective-permute-start | bytes 1572872 | tf_op jit(solution)/shard_map/ppermute | solution.py:255
  42.8 13.1 %collective-permute-start.16 = (bf16[256,2048]{1,0:T(8,128)(2,1)S(1)}, bf16[256,2048]{1,0:T(8,128)(2,1)S(1)}, u32[]{:S(2)}, u32[]{:S(2)}) collective-permute-start(bf16[256,2048]{1,0:T(8,128)(2,1)S(1)} %shard_map.86), channel_id=1, source_target_pairs={{0,1},{1,0},{2,3},{3,2},{4,5},{5,4},{6,7},{7,6},{8,9},{9,8},{10,11... | collective-permute-start | bytes 3145736 | tf_op jit(solution)/shard_map/ppermute | solution.py:255
  43.0 3.3 %collective-permute-start.13 = (bf16[128,2048]{1,0:T(8,128)(2,1)S(1)}, bf16[128,2048]{1,0:T(8,128)(2,1)S(1)}, u32[]{:S(2)}, u32[]{:S(2)}) collective-permute-start(bf16[128,2048]{1,0:T(8,128)(2,1)S(1)} %get-tuple-element.65), channel_id=1, source_target_pairs={{0,1},{1,0},{2,3},{3,2},{4,5},{5,4},{6,7},{7,6},{8,9},{9,8},{10,11... | collective-permute-start | bytes 1572872 | tf_op jit(solution)/shard_map/ppermute | solution.py:255
  43.8 6.4 %collective-permute-start.15 = (bf16[64,2048]{1,0:T(8,128)(2,1)S(1)}, bf16[64,2048]{1,0:T(8,128)(2,1)S(1)}, u32[]{:S(2)}, u32[]{:S(2)}) collective-permute-start(bf16[64,2048]{1,0:T(8,128)(2,1)S(1)} %get-tuple-element.69), channel_id=1, source_target_pairs={{0,2},{1,5},{2,0},{3,7},{4,6},{5,1},{6,4},{7,3},{8,10},{9,13},{10,... | collective-permute-start | bytes 786440 | tf_op jit(solution)/shard_map/ppermute | solution.py:251
  45.9 10.4 %collective-permute-start.19 = (bf16[64,2048]{1,0:T(8,128)(2,1)S(1)}, bf16[64,2048]{1,0:T(8,128)(2,1)S(1)}, u32[]{:S(2)}, u32[]{:S(2)}) collective-permute-start(bf16[64,2048]{1,0:T(8,128)(2,1)S(1)} %get-tuple-element.75), channel_id=1, source_target_pairs={{0,2},{1,5},{2,0},{3,7},{4,6},{5,1},{6,4},{7,3},{8,10},{9,13},{10,... | collective-permute-start | bytes 786440 | tf_op jit(solution)/shard_map/ppermute | solution.py:251
  50.6 6.5 %collective-permute-start.18 = (bf16[64,2048]{1,0:T(8,128)(2,1)S(1)}, bf16[64,2048]{1,0:T(8,128)(2,1)S(1)}, u32[]{:S(2)}, u32[]{:S(2)}) collective-permute-start(bf16[64,2048]{1,0:T(8,128)(2,1)S(1)} %get-tuple-element.74), channel_id=1, source_target_pairs={{0,4},{1,3},{2,6},{3,1},{4,0},{5,7},{6,2},{7,5},{8,12},{9,11},{10,... | collective-permute-start | bytes 786440 | tf_op jit(solution)/shard_map/ppermute | solution.py:251
  53.9 6.4 %collective-permute-start.17 = (bf16[64,2048]{1,0:T(8,128)(2,1)S(1)}, bf16[64,2048]{1,0:T(8,128)(2,1)S(1)}, u32[]{:S(2)}, u32[]{:S(2)}) collective-permute-start(bf16[64,2048]{1,0:T(8,128)(2,1)S(1)} %get-tuple-element.73), channel_id=1, source_target_pairs={{0,2},{1,5},{2,0},{3,7},{4,6},{5,1},{6,4},{7,3},{8,10},{9,13},{10,... | collective-permute-start | bytes 786440 | tf_op jit(solution)/shard_map/ppermute | solution.py:251
  56.2 6.9 %collective-permute-start.22 = (bf16[64,2048]{1,0:T(8,128)(2,1)S(1)}, bf16[64,2048]{1,0:T(8,128)(2,1)S(1)}, u32[]{:S(2)}, u32[]{:S(2)}) collective-permute-start(bf16[64,2048]{1,0:T(8,128)(2,1)S(1)} %shard_map.93), channel_id=1, source_target_pairs={{0,2},{1,5},{2,0},{3,7},{4,6},{5,1},{6,4},{7,3},{8,10},{9,13},{10,... | collective-permute-start | bytes 786440 | tf_op jit(solution)/shard_map/ppermute | solution.py:251
  57.3 13.9 %collective-permute-start.21 = (bf16[64,2048]{1,0:T(8,128)(2,1)S(1)}, bf16[64,2048]{1,0:T(8,128)(2,1)S(1)}, u32[]{:S(2)}, u32[]{:S(2)}) collective-permute-start(bf16[64,2048]{1,0:T(8,128)(2,1)S(1)} %shard_map.94), channel_id=1, source_target_pairs={{0,8},{1,9},{2,10},{3,11},{4,12},{5,13},{6,14},{7,15},{8,0},{9,1},... | collective-permute-start | bytes 786440 | tf_op jit(solution)/shard_map/ppermute | solution.py:251
  60.5 10.7 %collective-permute-start.20 = (bf16[64,2048]{1,0:T(8,128)(2,1)S(1)}, bf16[64,2048]{1,0:T(8,128)(2,1)S(1)}, u32[]{:S(2)}, u32[]{:S(2)}) collective-permute-start(bf16[64,2048]{1,0:T(8,128)(2,1)S(1)} %shard_map.95), channel_id=1, source_target_pairs={{0,4},{1,3},{2,6},{3,1},{4,0},{5,7},{6,2},{7,5},{8,12},{9,11},{10,... | collective-permute-start | bytes 786440 | tf_op jit(solution)/shard_map/ppermute | solution.py:251
  (4 other events, 8.9 us)

commit v15 on v11

--- a/solution.py
+++ b/solution.py
@@ -301,18 +301,20 @@
     )
     back7 = send(send7, ep, [-1])
     back5 = send(send5, ep, [-1])
+    near_made = expert(near, matrices)
+    near_made, back7 = lax.optimization_barrier((near_made, back7))
     send3, send6 = combine(
         [far_made, last_back, back7],
         weights,
         [[(0, 0, 6), (1, 0, 14), (2, 0, None)], [(0, 2, 7), (1, 1, 15)]],
     )
     back3 = send(send3, ep, [-2])
-    near_made = expert(near, matrices)
-    near_made, send6 = lax.optimization_barrier((near_made, send6))
-    back6 = send(send6, ep, [-1])
     near_back = cross(theirs)
+    near_made, send3 = lax.optimization_barrier((near_made, send3))
     (send4,) = combine([near_made, near_back], weights, [part(0, 1, 3, 3)])
     back4 = send(send4, ep, [-1])
+    send6, send4 = lax.optimization_barrier((send6, send4))
+    back6 = send(send6, ep, [-1])
     back3, back5, send4 = lax.optimization_barrier((back3, back5, send4))
     (send1,) = combine([near_made, near_back, back3, back5], weights, [part(0, 1, 1, 1) + [(2, 0, None), (3, 0, None)]])
     back1 = send(send1, ep, [-3])

time: 72 us -> 78.2 us (1.086)
  waiting for transfers between devices: 23.2 us -> 27.4 us
  starting transfers between devices: 23.9 us -> 26.2 us
    ppermute x14, starting transfers between devices: 21.3 us -> 23.7 us  [send(): return lax.ppermute(array, ('ep', 'sub'), pairs)]
    ppermute x9, waiting for transfers between devices: 0.4 us -> 2.55 us  [cross(): return lax.ppermute(array, 'sub', [(0, 1), (1, 0)])]
    ppermute x14, waiting for transfers between devices: 22.8 us -> 24.9 us  [send(): return lax.ppermute(array, ('ep', 'sub'), pairs)]
  transfers between devices with their start and end apart: 23 -> 23, of which waited for: 10 -> 11; matrix products, arithmetic and copies ran while one was open for 0% -> 0% of each run, Pallas kernels for 19% -> 14%
where the time goes in v15:
time: 78.2 us; the launch traced here: 78 us
  waiting for transfers between devices  27.4 us (35%)
  starting transfers between devices  26.2 us (34%)
  Pallas kernels  18.5 us (24%)
  local copies, waits for them, and re-layouts  5.68 us (7%)
    ppermute x14, waiting for transfers between devices, send(): return lax.ppermute(array, ('ep', 'sub'), pairs)  24.9 us
    ppermute x14, starting transfers between devices, send(): return lax.ppermute(array, ('ep', 'sub'), pairs)  23.7 us
    pallas_call x5, Pallas kernels, expert(): pl.pallas_call(functools.partial(expert_kernel, pieces), in_specs=[pl.Blo...  11.6 us
    unnamed x10, local copies, waits for them, and re-layouts  5.68 us
    ppermute x9, waiting for transfers between devices, cross(): return lax.ppermute(array, 'sub', [(0, 1), (1, 0)])  2.55 us
    ppermute x9, starting transfers between devices, cross(): return lax.ppermute(array, 'sub', [(0, 1), (1, 0)])  2.48 us
    pallas_call x8, Pallas kernels, combine(): pl.pallas_call(functools.partial(combine_kernel, rows, sums, len(arrays))...  2.34 us
    pallas_call x1, Pallas kernels, prepare(): pl.pallas_call(prepare_kernel, in_specs=[pl.BlockSpec(memory_space=pltpu....  1.95 us
  transfers between devices with their start and end apart: 23, of which 11 were waited for; matrix products, arithmetic and copies ran while one was open for 0% of the time, Pallas kernels for 14%

profile of v15, /device:TPU:0, one launch (start us, length us, event | category | flops | bytes accessed | tf_op | source)
XLA Modules:
  0.0 78.0 jit_solution(11295719877824328447)
XLA Ops:
  0.0 1.9 %shard_map.82.refs_0_ = bf16[64,2176]{1,0:T(8,128)(2,1)} custom-call(s32[1]{0:T(128)} %bitcast.me_ref, bf16[64,2048]{1,0:T(8,128)(2,1)} %tokens_ref.1, s32[8,64]{1,0:T(8,128)} %bitcast.4, f32[8,64]{1,0:T(8,128)} %bitcast.5, s32[1,64]{1,0:T(1,128)} %bitcast.6), custom_call_target="tpu_custom_call" | custom-call | tf_op jit(solution)/shard_map/pallas_call | solution.py:48
  2.4 3.6 %collective-permute-start = (bf16[64,2176]{1,0:T(8,128)(2,1)}, bf16[64,2176]{1,0:T(8,128)(2,1)S(1)}, u32[]{:S(2)}, u32[]{:S(2)}) collective-permute-start(bf16[64,2176]{1,0:T(8,128)(2,1)} %shard_map.82.refs_0_), channel_id=1, source_target_pairs={{0,8},{1,9},{2,10},{3,11},{4,12},{5,13},{6,14},{7,15},{8,0},{9,1},... | collective-permute-start | bytes 835592 | tf_op jit(solution)/shard_map/ppermute | solution.py:251
  9.1 1.9 %copy-done = bf16[1,2048,768]{2,1,0:T(8,128)(2,1)S(1)} copy-done((bf16[1,2048,768]{2,1,0:T(8,128)(2,1)S(1)}, bf16[1,2048,768]{2,1,0:T(8,128)(2,1)}, u32[]{:S(2)}) %copy-start) | copy-done | bytes 3145752
  11.0 1.9 %copy-done.1 = bf16[1,2048,768]{2,1,0:T(8,128)(2,1)S(1)} copy-done((bf16[1,2048,768]{2,1,0:T(8,128)(2,1)S(1)}, bf16[1,2048,768]{2,1,0:T(8,128)(2,1)}, u32[]{:S(2)}) %copy-start.1) | copy-done | bytes 3145752
  12.9 1.9 %copy-done.2 = bf16[1,768,2048]{2,1,0:T(8,128)(2,1)S(1)} copy-done((bf16[1,768,2048]{2,1,0:T(8,128)(2,1)S(1)}, bf16[1,768,2048]{2,1,0:T(8,128)(2,1)}, u32[]{:S(2)}) %copy-start.2) | copy-done | bytes 3145752
  15.4 4.2 %collective-permute-done.refs_1_.refs_0_ = bf16[64,2176]{1,0:T(8,128)(2,1)S(1)} collective-permute-done((bf16[64,2176]{1,0:T(8,128)(2,1)}, bf16[64,2176]{1,0:T(8,128)(2,1)S(1)}, u32[]{:S(2)}, u32[]{:S(2)}) %collective-permute-start) | collective-permute-done | bytes 278560 | tf_op jit(solution)/shard_map/ppermute | solution.py:251
  23.5 2.6 %shard_map.86 = bf16[256,2048]{1,0:T(8,128)(2,1)S(1)} custom-call(bf16[64,2176]{1,0:T(8,128)(2,1)S(1)} %collective-permute-done.1.refs_0_.refs_8_, bf16[192,2176]{1,0:T(8,128)(2,1)S(1)} %collective-permute-done.5.refs_1_.refs_9_, bf16[1,2048,768]{2,1,0:T(8,128)(2,1)S(1)} %get-tuple-element.50.refs_4_.refs_2_.refs_3_.refs_1_, ...), custom_call_target="tpu_custom_call" | custom-call | flops 1 | bytes 1 | tf_op jit(solution)/shard_map/pallas_call | solution.py:226
  26.1 2.7 %collective-permute-done.4.refs_0_.refs_6_ = bf16[64,2176]{1,0:T(8,128)(2,1)S(1)} collective-permute-done((bf16[64,2176]{1,0:T(8,128)(2,1)S(1)}, bf16[64,2176]{1,0:T(8,128)(2,1)S(1)}, u32[]{:S(2)}, u32[]{:S(2)}) %collective-permute-start.4) | collective-permute-done | bytes 278560 | tf_op jit(solution)/shard_map/ppermute | solution.py:251
  28.8 2.2 %collective-permute-start.8 = (bf16[64,2176]{1,0:T(8,128)(2,1)S(1)}, bf16[64,2176]{1,0:T(8,128)(2,1)S(1)}, u32[]{:S(2)}, u32[]{:S(2)}) collective-permute-start(bf16[64,2176]{1,0:T(8,128)(2,1)S(1)} %collective-permute-done.4.refs_0_.refs_6_), channel_id=1, source_target_pairs={{0,2},{1,5},{2,0},{3,7},{4,6},{5,1},{6,4},{7,3},{8,10},{9,13},{10,... | collective-permute-start | bytes 835592 | tf_op jit(solution)/shard_map/ppermute | solution.py:251
  32.8 2.0 %shard_map.87.refs_0_ = bf16[192,2048]{1,0:T(8,128)(2,1)S(1)} custom-call(bf16[64,2176]{1,0:T(8,128)(2,1)S(1)} %collective-permute-done.4.refs_0_.refs_6_, bf16[64,2176]{1,0:T(8,128)(2,1)S(1)} %collective-permute-done.6.refs_1_.refs_4_, bf16[64,2176]{1,0:T(8,128)(2,1)S(1)} %collective-permute-done.7.refs_2_.refs_7_, ...), custom_call_target="tpu_custom_call" | custom-call | flops 1 | bytes 1 | tf_op jit(solution)/shard_map/pallas_call | solution.py:226
  35.6 1.8 %shard_map.88.refs_1_ = bf16[64,2048]{1,0:T(8,128)(2,1)S(1)} custom-call(bf16[64,2176]{1,0:T(8,128)(2,1)S(1)} %collective-permute-done.8.refs_0_.refs_5_, bf16[1,2048,768]{2,1,0:T(8,128)(2,1)S(1)} %get-tuple-element.50.refs_4_.refs_2_.refs_3_.refs_1_, bf16[1,2048,768]{2,1,0:T(8,128)(2,1)S(1)} %get-tuple-element.51.refs_5_.refs_3_.refs_4_.refs_2_, ...), custom_call_target="tpu_custom_call" | custom-call | flops 1 | bytes 1 | tf_op jit(solution)/shard_map/pallas_call | solution.py:226
  37.5 2.6 %shard_map.89 = (bf16[128,2048]{1,0:T(8,128)(2,1)S(1)}, bf16[128,2048]{1,0:T(8,128)(2,1)S(1)}) custom-call(bf16[64,2176]{1,0:T(8,128)(2,1)S(1)} %collective-permute-done.9.refs_0_.refs_10_, bf16[64,2176]{1,0:T(8,128)(2,1)S(1)} %collective-permute-done.10.refs_1_.refs_11_, bf16[64,2176]{1,0:T(8,128)(2,1)S(1)} %collective-permute-done.11.refs_2_.refs_12_, ...), custom_call_target="tpu_custom_call" | custom-call | flops 1 | bytes 1 | tf_op jit(solution)/shard_map/pallas_call | solution.py:226
  40.1 1.9 %shard_map.90.refs_3_.refs_2_.refs_4_ = f32[1024,128]{1,0:T(8,128)S(1)} custom-call(s32[1]{0:T(128)} %bitcast.me_ref, s32[16]{0:T(128)S(1)} %copy-done.4, bf16[64,2176]{1,0:T(8,128)(2,1)S(1)} %copy-done.3, bf16[64,2176]{1,0:T(8,128)(2,1)S(1)} %collective-permute-done.refs_1_.refs_0_, bf16[64,2176]{1,0:T(8,128)(2,1)S(1)} %collective-permute-done.2.refs_2_.refs_1_, ...), custom_call_target="tpu_custom_call" | custom-call | flops 1 | bytes 1 | tf_op jit(solution)/shard_map/pallas_call | solution.py:114
  43.0 2.5 %collective-permute-done.13.refs_2_ = bf16[128,2048]{1,0:T(8,128)(2,1)S(1)} collective-permute-done((bf16[128,2048]{1,0:T(8,128)(2,1)S(1)}, bf16[128,2048]{1,0:T(8,128)(2,1)S(1)}, u32[]{:S(2)}, u32[]{:S(2)}) %collective-permute-start.13) | collective-permute-done | bytes 524320 | tf_op jit(solution)/shard_map/ppermute | solution.py:255
  45.9 2.1 %collective-permute-start.14 = (bf16[64,2048]{1,0:T(8,128)(2,1)S(1)}, bf16[64,2048]{1,0:T(8,128)(2,1)S(1)}, u32[]{:S(2)}, u32[]{:S(2)}) collective-permute-start(bf16[64,2048]{1,0:T(8,128)(2,1)S(1)} %get-tuple-element.70), channel_id=1, source_target_pairs={{0,2},{1,5},{2,0},{3,7},{4,6},{5,1},{6,4},{7,3},{8,10},{9,13},{10,... | collective-permute-start | bytes 786440 | tf_op jit(solution)/shard_map/ppermute | solution.py:251
  48.0 2.6 %shard_map.84.refs_0_ = bf16[256,2048]{1,0:T(8,128)(2,1)S(1)} custom-call(bf16[64,2176]{1,0:T(8,128)(2,1)S(1)} %copy-done.3, bf16[64,2176]{1,0:T(8,128)(2,1)S(1)} %collective-permute-done.refs_1_.refs_0_, bf16[64,2176]{1,0:T(8,128)(2,1)S(1)} %collective-permute-done.2.refs_2_.refs_1_, bf16[64,2176]{1,0:T(8,128)(2,1)S(1)} %collective-permute-done.3.refs_3_.refs_2_, ...), custom_call_target="tpu_custom_call" | custom-call | flops 1 | bytes 1 | tf_op jit(solution)/shard_map/pallas_call | solution.py:226
  50.7 1.6 %collective-permute-done.14.refs_2_ = bf16[64,2048]{1,0:T(8,128)(2,1)S(1)} collective-permute-done((bf16[64,2048]{1,0:T(8,128)(2,1)S(1)}, bf16[64,2048]{1,0:T(8,128)(2,1)S(1)}, u32[]{:S(2)}, u32[]{:S(2)}) %collective-permute-start.14) | collective-permute-done | bytes 262176 | tf_op jit(solution)/shard_map/ppermute | solution.py:251
  54.5 2.1 %collective-permute-start.17 = (bf16[64,2048]{1,0:T(8,128)(2,1)S(1)}, bf16[64,2048]{1,0:T(8,128)(2,1)S(1)}, u32[]{:S(2)}, u32[]{:S(2)}) collective-permute-start(bf16[64,2048]{1,0:T(8,128)(2,1)S(1)} %get-tuple-element.78), channel_id=1, source_target_pairs={{0,2},{1,5},{2,0},{3,7},{4,6},{5,1},{6,4},{7,3},{8,10},{9,13},{10,... | collective-permute-start | bytes 786440 | tf_op jit(solution)/shard_map/ppermute | solution.py:251
  56.6 2.4 %collective-permute-done.19.refs_3_ = bf16[64,2048]{1,0:T(8,128)(2,1)S(1)} collective-permute-done((bf16[64,2048]{1,0:T(8,128)(2,1)S(1)}, bf16[64,2048]{1,0:T(8,128)(2,1)S(1)}, u32[]{:S(2)}, u32[]{:S(2)}) %collective-permute-start.19) | collective-permute-done | bytes 262176 | tf_op jit(solution)/shard_map/ppermute | solution.py:251
  58.9 2.5 %collective-permute-done.18.refs_2_ = bf16[64,2048]{1,0:T(8,128)(2,1)S(1)} collective-permute-done((bf16[64,2048]{1,0:T(8,128)(2,1)S(1)}, bf16[64,2048]{1,0:T(8,128)(2,1)S(1)}, u32[]{:S(2)}, u32[]{:S(2)}) %collective-permute-start.18) | collective-permute-done | bytes 262176 | tf_op jit(solution)/shard_map/ppermute | solution.py:251
  61.4 1.9 %collective-permute-start.22 = (bf16[64,2048]{1,0:T(8,128)(2,1)S(1)}, bf16[64,2048]{1,0:T(8,128)(2,1)S(1)}, u32[]{:S(2)}, u32[]{:S(2)}) collective-permute-start(bf16[64,2048]{1,0:T(8,128)(2,1)S(1)} %shard_map.93), channel_id=1, source_target_pairs={{0,2},{1,5},{2,0},{3,7},{4,6},{5,1},{6,4},{7,3},{8,10},{9,13},{10,... | collective-permute-start | bytes 786440 | tf_op jit(solution)/shard_map/ppermute | solution.py:251
  63.5 2.4 %collective-permute-start.21 = (bf16[64,2048]{1,0:T(8,128)(2,1)S(1)}, bf16[64,2048]{1,0:T(8,128)(2,1)S(1)}, u32[]{:S(2)}, u32[]{:S(2)}) collective-permute-start(bf16[64,2048]{1,0:T(8,128)(2,1)S(1)} %shard_map.94), channel_id=1, source_target_pairs={{0,8},{1,9},{2,10},{3,11},{4,12},{5,13},{6,14},{7,15},{8,0},{9,1},... | collective-permute-start | bytes 786440 | tf_op jit(solution)/shard_map/ppermute | solution.py:251
  67.2 1.8 %collective-permute-done.22.refs_2_ = bf16[64,2048]{1,0:T(8,128)(2,1)S(1)} collective-permute-done((bf16[64,2048]{1,0:T(8,128)(2,1)S(1)}, bf16[64,2048]{1,0:T(8,128)(2,1)S(1)}, u32[]{:S(2)}, u32[]{:S(2)}) %collective-permute-start.22) | collective-permute-done | bytes 262176 | tf_op jit(solution)/shard_map/ppermute | solution.py:251
  69.2 7.9 %collective-permute-done.21.refs_1_ = bf16[64,2048]{1,0:T(8,128)(2,1)S(1)} collective-permute-done((bf16[64,2048]{1,0:T(8,128)(2,1)S(1)}, bf16[64,2048]{1,0:T(8,128)(2,1)S(1)}, u32[]{:S(2)}, u32[]{:S(2)}) %collective-permute-start.21) | collective-permute-done | bytes 262176 | tf_op jit(solution)/shard_map/ppermute | solution.py:251
  (49 shorter events, 16.8 us)
Async XLA Ops:
  1.9 13.5 %collective-permute-start.1 = (bf16[64,2176]{1,0:T(8,128)(2,1)}, bf16[64,2176]{1,0:T(8,128)(2,1)S(1)}, u32[]{:S(2)}, u32[]{:S(2)}) collective-permute-start(bf16[64,2176]{1,0:T(8,128)(2,1)} %shard_map.82.refs_0_), channel_id=1, source_target_pairs={{0,1},{1,0},{2,3},{3,2},{4,5},{5,4},{6,7},{7,6},{8,9},{9,8},{10,11... | collective-permute-start | bytes 835592 | tf_op jit(solution)/shard_map/ppermute | solution.py:255
  2.4 17.2 %collective-permute-start = (bf16[64,2176]{1,0:T(8,128)(2,1)}, bf16[64,2176]{1,0:T(8,128)(2,1)S(1)}, u32[]{:S(2)}, u32[]{:S(2)}) collective-permute-start(bf16[64,2176]{1,0:T(8,128)(2,1)} %shard_map.82.refs_0_), channel_id=1, source_target_pairs={{0,8},{1,9},{2,10},{3,11},{4,12},{5,13},{6,14},{7,15},{8,0},{9,1},... | collective-permute-start | bytes 835592 | tf_op jit(solution)/shard_map/ppermute | solution.py:251
  6.0 13.6 %collective-permute-start.3 = (bf16[64,2176]{1,0:T(8,128)(2,1)}, bf16[64,2176]{1,0:T(8,128)(2,1)S(1)}, u32[]{:S(2)}, u32[]{:S(2)}) collective-permute-start(bf16[64,2176]{1,0:T(8,128)(2,1)} %shard_map.82.refs_0_), channel_id=1, source_target_pairs={{0,2},{1,5},{2,0},{3,7},{4,6},{5,1},{6,4},{7,3},{8,10},{9,13},{10,... | collective-permute-start | bytes 835592 | tf_op jit(solution)/shard_map/ppermute | solution.py:251
  7.5 12.3 %collective-permute-start.2 = (bf16[64,2176]{1,0:T(8,128)(2,1)}, bf16[64,2176]{1,0:T(8,128)(2,1)S(1)}, u32[]{:S(2)}, u32[]{:S(2)}) collective-permute-start(bf16[64,2176]{1,0:T(8,128)(2,1)} %shard_map.82.refs_0_), channel_id=1, source_target_pairs={{0,4},{1,3},{2,6},{3,1},{4,0},{5,7},{6,2},{7,5},{8,12},{9,11},{10,... | collective-permute-start | bytes 835592 | tf_op jit(solution)/shard_map/ppermute | solution.py:251
  19.9 3.7 %collective-permute-start.5 = (bf16[192,2176]{1,0:T(8,128)(2,1)S(1)}, bf16[192,2176]{1,0:T(8,128)(2,1)S(1)}, u32[]{:S(2)}, u32[]{:S(2)}) collective-permute-start(bf16[192,2176]{1,0:T(8,128)(2,1)S(1)} %shard_map.85), channel_id=1, source_target_pairs={{0,1},{1,0},{2,3},{3,2},{4,5},{5,4},{6,7},{7,6},{8,9},{9,8},{10,11... | collective-permute-start | bytes 2506760 | tf_op jit(solution)/shard_map/ppermute | solution.py:255
  19.9 8.9 %collective-permute-start.4 = (bf16[64,2176]{1,0:T(8,128)(2,1)S(1)}, bf16[64,2176]{1,0:T(8,128)(2,1)S(1)}, u32[]{:S(2)}, u32[]{:S(2)}) collective-permute-start(bf16[64,2176]{1,0:T(8,128)(2,1)S(1)} %collective-permute-done.refs_1_.refs_0_), channel_id=1, source_target_pairs={{0,4},{1,3},{2,6},{3,1},{4,0},{5,7},{6,2},{7,5},{8,12},{9,11},{10,... | collective-permute-start | bytes 835592 | tf_op jit(solution)/shard_map/ppermute | solution.py:251
  21.5 10.8 %collective-permute-start.6 = (bf16[64,2176]{1,0:T(8,128)(2,1)S(1)}, bf16[64,2176]{1,0:T(8,128)(2,1)S(1)}, u32[]{:S(2)}, u32[]{:S(2)}) collective-permute-start(bf16[64,2176]{1,0:T(8,128)(2,1)S(1)} %collective-permute-done.refs_1_.refs_0_), channel_id=1, source_target_pairs={{0,2},{1,5},{2,0},{3,7},{4,6},{5,1},{6,4},{7,3},{8,10},{9,13},{10,... | collective-permute-start | bytes 835592 | tf_op jit(solution)/shard_map/ppermute | solution.py:251
  23.0 9.0 %collective-permute-start.7 = (bf16[64,2176]{1,0:T(8,128)(2,1)S(1)}, bf16[64,2176]{1,0:T(8,128)(2,1)S(1)}, u32[]{:S(2)}, u32[]{:S(2)}) collective-permute-start(bf16[64,2176]{1,0:T(8,128)(2,1)S(1)} %collective-permute-done.2.refs_2_.refs_1_), channel_id=1, source_target_pairs={{0,2},{1,5},{2,0},{3,7},{4,6},{5,1},{6,4},{7,3},{8,10},{9,13},{10,... | collective-permute-start | bytes 835592 | tf_op jit(solution)/shard_map/ppermute | solution.py:251
  28.8 6.7 %collective-permute-start.8 = (bf16[64,2176]{1,0:T(8,128)(2,1)S(1)}, bf16[64,2176]{1,0:T(8,128)(2,1)S(1)}, u32[]{:S(2)}, u32[]{:S(2)}) collective-permute-start(bf16[64,2176]{1,0:T(8,128)(2,1)S(1)} %collective-permute-done.4.refs_0_.refs_6_), channel_id=1, source_target_pairs={{0,2},{1,5},{2,0},{3,7},{4,6},{5,1},{6,4},{7,3},{8,10},{9,13},{10,... | collective-permute-start | bytes 835592 | tf_op jit(solution)/shard_map/ppermute | solution.py:251
  32.0 5.4 %collective-permute-start.10 = (bf16[64,2176]{1,0:T(8,128)(2,1)S(1)}, bf16[64,2176]{1,0:T(8,128)(2,1)S(1)}, u32[]{:S(2)}, u32[]{:S(2)}) collective-permute-start(bf16[64,2176]{1,0:T(8,128)(2,1)S(1)} %collective-permute-done.7.refs_2_.refs_7_), channel_id=1, source_target_pairs={{0,1},{1,0},{2,3},{3,2},{4,5},{5,4},{6,7},{7,6},{8,9},{9,8},{10,11... | collective-permute-start | bytes 835592 | tf_op jit(solution)/shard_map/ppermute | solution.py:255
  32.3 5.1 %collective-permute-start.11 = (bf16[64,2176]{1,0:T(8,128)(2,1)S(1)}, bf16[64,2176]{1,0:T(8,128)(2,1)S(1)}, u32[]{:S(2)}, u32[]{:S(2)}) collective-permute-start(bf16[64,2176]{1,0:T(8,128)(2,1)S(1)} %collective-permute-done.6.refs_1_.refs_4_), channel_id=1, source_target_pairs={{0,1},{1,0},{2,3},{3,2},{4,5},{5,4},{6,7},{7,6},{8,9},{9,8},{10,11... | collective-permute-start | bytes 835592 | tf_op jit(solution)/shard_map/ppermute | solution.py:255
  32.5 4.9 %collective-permute-start.9 = (bf16[64,2176]{1,0:T(8,128)(2,1)S(1)}, bf16[64,2176]{1,0:T(8,128)(2,1)S(1)}, u32[]{:S(2)}, u32[]{:S(2)}) collective-permute-start(bf16[64,2176]{1,0:T(8,128)(2,1)S(1)} %collective-permute-done.4.refs_0_.refs_6_), channel_id=1, source_target_pairs={{0,1},{1,0},{2,3},{3,2},{4,5},{5,4},{6,7},{7,6},{8,9},{9,8},{10,11... | collective-permute-start | bytes 835592 | tf_op jit(solution)/shard_map/ppermute | solution.py:255
  35.5 1.9 %collective-permute-start.12 = (bf16[64,2176]{1,0:T(8,128)(2,1)S(1)}, bf16[64,2176]{1,0:T(8,128)(2,1)S(1)}, u32[]{:S(2)}, u32[]{:S(2)}) collective-permute-start(bf16[64,2176]{1,0:T(8,128)(2,1)S(1)} %collective-permute-done.8.refs_0_.refs_5_), channel_id=1, source_target_pairs={{0,1},{1,0},{2,3},{3,2},{4,5},{5,4},{6,7},{7,6},{8,9},{9,8},{10,11... | collective-permute-start | bytes 835592 | tf_op jit(solution)/shard_map/ppermute | solution.py:255
  37.4 2.7 %copy-start.3 = (bf16[64,2176]{1,0:T(8,128)(2,1)S(1)}, bf16[64,2176]{1,0:T(8,128)(2,1)}, u32[]{:S(2)}) copy-start(bf16[64,2176]{1,0:T(8,128)(2,1)} %shard_map.82.refs_0_) | copy-start | bytes 835588
  42.0 12.3 %collective-permute-start.16 = (bf16[256,2048]{1,0:T(8,128)(2,1)S(1)}, bf16[256,2048]{1,0:T(8,128)(2,1)S(1)}, u32[]{:S(2)}, u32[]{:S(2)}) collective-permute-start(bf16[256,2048]{1,0:T(8,128)(2,1)S(1)} %shard_map.86), channel_id=1, source_target_pairs={{0,1},{1,0},{2,3},{3,2},{4,5},{5,4},{6,7},{7,6},{8,9},{9,8},{10,11... | collective-permute-start | bytes 3145736 | tf_op jit(solution)/shard_map/ppermute | solution.py:255
  42.5 3.0 %collective-permute-start.13 = (bf16[128,2048]{1,0:T(8,128)(2,1)S(1)}, bf16[128,2048]{1,0:T(8,128)(2,1)S(1)}, u32[]{:S(2)}, u32[]{:S(2)}) collective-permute-start(bf16[128,2048]{1,0:T(8,128)(2,1)S(1)} %get-tuple-element.63), channel_id=1, source_target_pairs={{0,1},{1,0},{2,3},{3,2},{4,5},{5,4},{6,7},{7,6},{8,9},{9,8},{10,11... | collective-permute-start | bytes 1572872 | tf_op jit(solution)/shard_map/ppermute | solution.py:255
  42.6 9.7 %collective-permute-start.15 = (bf16[128,2048]{1,0:T(8,128)(2,1)S(1)}, bf16[128,2048]{1,0:T(8,128)(2,1)S(1)}, u32[]{:S(2)}, u32[]{:S(2)}) collective-permute-start(bf16[128,2048]{1,0:T(8,128)(2,1)S(1)} %get-tuple-element.72), channel_id=1, source_target_pairs={{0,1},{1,0},{2,3},{3,2},{4,5},{5,4},{6,7},{7,6},{8,9},{9,8},{10,11... | collective-permute-start | bytes 1572872 | tf_op jit(solution)/shard_map/ppermute | solution.py:255
  45.9 6.4 %collective-permute-start.14 = (bf16[64,2048]{1,0:T(8,128)(2,1)S(1)}, bf16[64,2048]{1,0:T(8,128)(2,1)S(1)}, u32[]{:S(2)}, u32[]{:S(2)}) collective-permute-start(bf16[64,2048]{1,0:T(8,128)(2,1)S(1)} %get-tuple-element.70), channel_id=1, source_target_pairs={{0,2},{1,5},{2,0},{3,7},{4,6},{5,1},{6,4},{7,3},{8,10},{9,13},{10,... | collective-permute-start | bytes 786440 | tf_op jit(solution)/shard_map/ppermute | solution.py:251
  50.6 8.3 %collective-permute-start.19 = (bf16[64,2048]{1,0:T(8,128)(2,1)S(1)}, bf16[64,2048]{1,0:T(8,128)(2,1)S(1)}, u32[]{:S(2)}, u32[]{:S(2)}) collective-permute-start(bf16[64,2048]{1,0:T(8,128)(2,1)S(1)} %get-tuple-element.79), channel_id=1, source_target_pairs={{0,2},{1,5},{2,0},{3,7},{4,6},{5,1},{6,4},{7,3},{8,10},{9,13},{10,... | collective-permute-start | bytes 786440 | tf_op jit(solution)/shard_map/ppermute | solution.py:251
  52.7 8.7 %collective-permute-start.18 = (bf16[64,2048]{1,0:T(8,128)(2,1)S(1)}, bf16[64,2048]{1,0:T(8,128)(2,1)S(1)}, u32[]{:S(2)}, u32[]{:S(2)}) collective-permute-start(bf16[64,2048]{1,0:T(8,128)(2,1)S(1)} %get-tuple-element.74), channel_id=1, source_target_pairs={{0,4},{1,3},{2,6},{3,1},{4,0},{5,7},{6,2},{7,5},{8,12},{9,11},{10,... | collective-permute-start | bytes 786440 | tf_op jit(solution)/shard_map/ppermute | solution.py:251
  54.5 11.5 %collective-permute-start.17 = (bf16[64,2048]{1,0:T(8,128)(2,1)S(1)}, bf16[64,2048]{1,0:T(8,128)(2,1)S(1)}, u32[]{:S(2)}, u32[]{:S(2)}) collective-permute-start(bf16[64,2048]{1,0:T(8,128)(2,1)S(1)} %get-tuple-element.78), channel_id=1, source_target_pairs={{0,2},{1,5},{2,0},{3,7},{4,6},{5,1},{6,4},{7,3},{8,10},{9,13},{10,... | collective-permute-start | bytes 786440 | tf_op jit(solution)/shard_map/ppermute | solution.py:251
  61.4 7.6 %collective-permute-start.22 = (bf16[64,2048]{1,0:T(8,128)(2,1)S(1)}, bf16[64,2048]{1,0:T(8,128)(2,1)S(1)}, u32[]{:S(2)}, u32[]{:S(2)}) collective-permute-start(bf16[64,2048]{1,0:T(8,128)(2,1)S(1)} %shard_map.93), channel_id=1, source_target_pairs={{0,2},{1,5},{2,0},{3,7},{4,6},{5,1},{6,4},{7,3},{8,10},{9,13},{10,... | collective-permute-start | bytes 786440 | tf_op jit(solution)/shard_map/ppermute | solution.py:251
  63.5 13.6 %collective-permute-start.21 = (bf16[64,2048]{1,0:T(8,128)(2,1)S(1)}, bf16[64,2048]{1,0:T(8,128)(2,1)S(1)}, u32[]{:S(2)}, u32[]{:S(2)}) collective-permute-start(bf16[64,2048]{1,0:T(8,128)(2,1)S(1)} %shard_map.94), channel_id=1, source_target_pairs={{0,8},{1,9},{2,10},{3,11},{4,12},{5,13},{6,14},{7,15},{8,0},{9,1},... | collective-permute-start | bytes 786440 | tf_op jit(solution)/shard_map/ppermute | solution.py:251
  66.2 11.1 %collective-permute-start.20 = (bf16[64,2048]{1,0:T(8,128)(2,1)S(1)}, bf16[64,2048]{1,0:T(8,128)(2,1)S(1)}, u32[]{:S(2)}, u32[]{:S(2)}) collective-permute-start(bf16[64,2048]{1,0:T(8,128)(2,1)S(1)} %shard_map.95), channel_id=1, source_target_pairs={{0,4},{1,3},{2,6},{3,1},{4,0},{5,7},{6,2},{7,5},{8,12},{9,11},{10,... | collective-permute-start | bytes 786440 | tf_op jit(solution)/shard_map/ppermute | solution.py:251
  (4 other events, 8.4 us)

commit v16 on v11

--- a/solution.py
+++ b/solution.py
@@ -290,7 +290,7 @@
     first_back = cross(first_back)
     near = [held, own1, own2, own4]
     weights = weigh(me, capacity, near + far + [first, crossed, *far_crossed, last_crossed], top, tok_rows)
-    weights, theirs, last_back = lax.optimization_barrier((weights, theirs, last_back))
+    weights, last_back = lax.optimization_barrier((weights, last_back))
     last_back = cross(last_back)
 
     def part(mine, back, block, place):
@@ -306,6 +306,7 @@
         weights,
         [[(0, 0, 6), (1, 0, 14), (2, 0, None)], [(0, 2, 7), (1, 1, 15)]],
     )
+    send3, theirs = lax.optimization_barrier((send3, theirs))
     back3 = send(send3, ep, [-2])
     near_made = expert(near, matrices)
     near_made, send6 = lax.optimization_barrier((near_made, send6))

time: 72 us -> 75.6 us (1.050)
  starting transfers between devices: 23.9 us -> 26.3 us
  waiting for transfers between devices: 23.2 us -> 24.5 us
    ppermute x14, starting transfers between devices: 21.3 us -> 24.1 us  [send(): return lax.ppermute(array, ('ep', 'sub'), pairs)]
    ppermute x14, waiting for transfers between devices: 22.8 us -> 24.5 us  [send(): return lax.ppermute(array, ('ep', 'sub'), pairs)]
  transfers between devices with their start and end apart: 23 -> 23, of which waited for: 10 -> 10; matrix products, arithmetic and copies ran while one was open for 0% -> 0% of each run, Pallas kernels for 19% -> 17%
where the time goes in v16:
time: 75.6 us; the launch traced here: 75.4 us
  starting transfers between devices  26.3 us (35%)
  waiting for transfers between devices  24.5 us (32%)
  Pallas kernels  18.7 us (25%)
  local copies, waits for them, and re-layouts  5.68 us (8%)
    ppermute x14, waiting for transfers between devices, send(): return lax.ppermute(array, ('ep', 'sub'), pairs)  24.5 us
    ppermute x14, starting transfers between devices, send(): return lax.ppermute(array, ('ep', 'sub'), pairs)  24.1 us
    pallas_call x5, Pallas kernels, expert(): pl.pallas_call(functools.partial(expert_kernel, pieces), in_specs=[pl.Blo...  11.8 us
    unnamed x10, local copies, waits for them, and re-layouts  5.68 us
    pallas_call x8, Pallas kernels, combine(): pl.pallas_call(functools.partial(combine_kernel, rows, sums, len(arrays))...  2.37 us
    ppermute x9, starting transfers between devices, cross(): return lax.ppermute(array, 'sub', [(0, 1), (1, 0)])  2.19 us
    pallas_call x1, Pallas kernels, prepare(): pl.pallas_call(prepare_kernel, in_specs=[pl.BlockSpec(memory_space=pltpu....  1.95 us
    pallas_call x1, Pallas kernels, weigh(): pl.pallas_call(functools.partial(weigh_kernel, top, tok_rows), in_specs=[...  1.89 us
  transfers between devices with their start and end apart: 23, of which 10 were waited for; matrix products, arithmetic and copies ran while one was open for 0% of the time, Pallas kernels for 17%

profile of v16, /device:TPU:0, one launch (start us, length us, event | category | flops | bytes accessed | tf_op | source)
XLA Modules:
  0.0 75.4 jit_solution(12363989394296390181)
XLA Ops:
  0.0 1.9 %shard_map.82.refs_0_ = bf16[64,2176]{1,0:T(8,128)(2,1)} custom-call(s32[1]{0:T(128)} %bitcast.me_ref, bf16[64,2048]{1,0:T(8,128)(2,1)} %tokens_ref.1, s32[8,64]{1,0:T(8,128)} %bitcast.4, f32[8,64]{1,0:T(8,128)} %bitcast.5, s32[1,64]{1,0:T(1,128)} %bitcast.6), custom_call_target="tpu_custom_call" | custom-call | tf_op jit(solution)/shard_map/pallas_call | solution.py:48
  2.4 3.6 %collective-permute-start = (bf16[64,2176]{1,0:T(8,128)(2,1)}, bf16[64,2176]{1,0:T(8,128)(2,1)S(1)}, u32[]{:S(2)}, u32[]{:S(2)}) collective-permute-start(bf16[64,2176]{1,0:T(8,128)(2,1)} %shard_map.82.refs_0_), channel_id=1, source_target_pairs={{0,8},{1,9},{2,10},{3,11},{4,12},{5,13},{6,14},{7,15},{8,0},{9,1},... | collective-permute-start | bytes 835592 | tf_op jit(solution)/shard_map/ppermute | solution.py:251
  7.5 1.6 %collective-permute-start.2 = (bf16[64,2176]{1,0:T(8,128)(2,1)}, bf16[64,2176]{1,0:T(8,128)(2,1)S(1)}, u32[]{:S(2)}, u32[]{:S(2)}) collective-permute-start(bf16[64,2176]{1,0:T(8,128)(2,1)} %shard_map.82.refs_0_), channel_id=1, source_target_pairs={{0,4},{1,3},{2,6},{3,1},{4,0},{5,7},{6,2},{7,5},{8,12},{9,11},{10,... | collective-permute-start | bytes 835592 | tf_op jit(solution)/shard_map/ppermute | solution.py:251
  9.1 1.9 %copy-done = bf16[1,2048,768]{2,1,0:T(8,128)(2,1)S(1)} copy-done((bf16[1,2048,768]{2,1,0:T(8,128)(2,1)S(1)}, bf16[1,2048,768]{2,1,0:T(8,128)(2,1)}, u32[]{:S(2)}) %copy-start) | copy-done | bytes 3145752
  11.0 1.9 %copy-done.1 = bf16[1,2048,768]{2,1,0:T(8,128)(2,1)S(1)} copy-done((bf16[1,2048,768]{2,1,0:T(8,128)(2,1)S(1)}, bf16[1,2048,768]{2,1,0:T(8,128)(2,1)}, u32[]{:S(2)}) %copy-start.1) | copy-done | bytes 3145752
  12.9 1.9 %copy-done.2 = bf16[1,768,2048]{2,1,0:T(8,128)(2,1)S(1)} copy-done((bf16[1,768,2048]{2,1,0:T(8,128)(2,1)S(1)}, bf16[1,768,2048]{2,1,0:T(8,128)(2,1)}, u32[]{:S(2)}) %copy-start.2) | copy-done | bytes 3145752
  15.4 4.2 %collective-permute-done.refs_1_.refs_0_ = bf16[64,2176]{1,0:T(8,128)(2,1)S(1)} collective-permute-done((bf16[64,2176]{1,0:T(8,128)(2,1)}, bf16[64,2176]{1,0:T(8,128)(2,1)S(1)}, u32[]{:S(2)}, u32[]{:S(2)}) %collective-permute-start) | collective-permute-done | bytes 278560 | tf_op jit(solution)/shard_map/ppermute | solution.py:251
  19.9 1.6 %collective-permute-start.4 = (bf16[64,2176]{1,0:T(8,128)(2,1)S(1)}, bf16[64,2176]{1,0:T(8,128)(2,1)S(1)}, u32[]{:S(2)}, u32[]{:S(2)}) collective-permute-start(bf16[64,2176]{1,0:T(8,128)(2,1)S(1)} %collective-permute-done.refs_1_.refs_0_), channel_id=1, source_target_pairs={{0,4},{1,3},{2,6},{3,1},{4,0},{5,7},{6,2},{7,5},{8,12},{9,11},{10,... | collective-permute-start | bytes 835592 | tf_op jit(solution)/shard_map/ppermute | solution.py:251
  23.5 2.6 %shard_map.86 = bf16[256,2048]{1,0:T(8,128)(2,1)S(1)} custom-call(bf16[64,2176]{1,0:T(8,128)(2,1)S(1)} %collective-permute-done.1.refs_0_.refs_8_, bf16[192,2176]{1,0:T(8,128)(2,1)S(1)} %collective-permute-done.5.refs_1_.refs_9_, bf16[1,2048,768]{2,1,0:T(8,128)(2,1)S(1)} %get-tuple-element.49.refs_4_.refs_2_.refs_3_.refs_1_, ...), custom_call_target="tpu_custom_call" | custom-call | flops 1 | bytes 1 | tf_op jit(solution)/shard_map/pallas_call | solution.py:226
  26.1 2.7 %collective-permute-done.4.refs_0_.refs_6_ = bf16[64,2176]{1,0:T(8,128)(2,1)S(1)} collective-permute-done((bf16[64,2176]{1,0:T(8,128)(2,1)S(1)}, bf16[64,2176]{1,0:T(8,128)(2,1)S(1)}, u32[]{:S(2)}, u32[]{:S(2)}) %collective-permute-start.4) | collective-permute-done | bytes 278560 | tf_op jit(solution)/shard_map/ppermute | solution.py:251
  28.8 2.2 %collective-permute-start.8 = (bf16[64,2176]{1,0:T(8,128)(2,1)S(1)}, bf16[64,2176]{1,0:T(8,128)(2,1)S(1)}, u32[]{:S(2)}, u32[]{:S(2)}) collective-permute-start(bf16[64,2176]{1,0:T(8,128)(2,1)S(1)} %collective-permute-done.4.refs_0_.refs_6_), channel_id=1, source_target_pairs={{0,2},{1,5},{2,0},{3,7},{4,6},{5,1},{6,4},{7,3},{8,10},{9,13},{10,... | collective-permute-start | bytes 835592 | tf_op jit(solution)/shard_map/ppermute | solution.py:251
  32.8 2.0 %shard_map.87.refs_0_ = bf16[192,2048]{1,0:T(8,128)(2,1)S(1)} custom-call(bf16[64,2176]{1,0:T(8,128)(2,1)S(1)} %collective-permute-done.4.refs_0_.refs_6_, bf16[64,2176]{1,0:T(8,128)(2,1)S(1)} %collective-permute-done.6.refs_1_.refs_4_, bf16[64,2176]{1,0:T(8,128)(2,1)S(1)} %collective-permute-done.7.refs_2_.refs_7_, ...), custom_call_target="tpu_custom_call" | custom-call | flops 1 | bytes 1 | tf_op jit(solution)/shard_map/pallas_call | solution.py:226
  35.6 1.8 %shard_map.88.refs_1_ = bf16[64,2048]{1,0:T(8,128)(2,1)S(1)} custom-call(bf16[64,2176]{1,0:T(8,128)(2,1)S(1)} %collective-permute-done.8.refs_0_.refs_5_, bf16[1,2048,768]{2,1,0:T(8,128)(2,1)S(1)} %get-tuple-element.49.refs_4_.refs_2_.refs_3_.refs_1_, bf16[1,2048,768]{2,1,0:T(8,128)(2,1)S(1)} %get-tuple-element.50.refs_5_.refs_3_.refs_4_.refs_2_, ...), custom_call_target="tpu_custom_call" | custom-call | flops 1 | bytes 1 | tf_op jit(solution)/shard_map/pallas_call | solution.py:226
  37.5 2.7 %shard_map.90 = (bf16[128,2048]{1,0:T(8,128)(2,1)S(1)}, bf16[128,2048]{1,0:T(8,128)(2,1)S(1)}) custom-call(bf16[64,2176]{1,0:T(8,128)(2,1)S(1)} %collective-permute-done.9.refs_10_.refs_0_, bf16[64,2176]{1,0:T(8,128)(2,1)S(1)} %collective-permute-done.10.refs_11_.refs_1_, bf16[64,2176]{1,0:T(8,128)(2,1)S(1)} %collective-permute-done.11.refs_12_.refs_2_, ...), custom_call_target="tpu_custom_call" | custom-call | flops 1 | bytes 1 | tf_op jit(solution)/shard_map/pallas_call | solution.py:226
  40.7 1.9 %shard_map.89.refs_3_.refs_2_.refs_4_ = f32[1024,128]{1,0:T(8,128)S(1)} custom-call(s32[1]{0:T(128)} %bitcast.me_ref, s32[16]{0:T(128)S(1)} %copy-done.4, bf16[64,2176]{1,0:T(8,128)(2,1)S(1)} %copy-done.3, bf16[64,2176]{1,0:T(8,128)(2,1)S(1)} %collective-permute-done.refs_1_.refs_0_, bf16[64,2176]{1,0:T(8,128)(2,1)S(1)} %collective-permute-done.2.refs_2_.refs_1_, ...), custom_call_target="tpu_custom_call" | custom-call | flops 1 | bytes 1 | tf_op jit(solution)/shard_map/pallas_call | solution.py:114
  43.1 2.0 %collective-permute-start.15 = (bf16[64,2048]{1,0:T(8,128)(2,1)S(1)}, bf16[64,2048]{1,0:T(8,128)(2,1)S(1)}, u32[]{:S(2)}, u32[]{:S(2)}) collective-permute-start(bf16[64,2048]{1,0:T(8,128)(2,1)S(1)} %get-tuple-element.69), channel_id=1, source_target_pairs={{0,2},{1,5},{2,0},{3,7},{4,6},{5,1},{6,4},{7,3},{8,10},{9,13},{10,... | collective-permute-start | bytes 786440 | tf_op jit(solution)/shard_map/ppermute | solution.py:251
  45.1 4.4 %collective-permute-done.15.refs_2_ = bf16[64,2048]{1,0:T(8,128)(2,1)S(1)} collective-permute-done((bf16[64,2048]{1,0:T(8,128)(2,1)S(1)}, bf16[64,2048]{1,0:T(8,128)(2,1)S(1)}, u32[]{:S(2)}, u32[]{:S(2)}) %collective-permute-start.15) | collective-permute-done | bytes 262176 | tf_op jit(solution)/shard_map/ppermute | solution.py:251
  49.9 2.0 %collective-permute-start.19 = (bf16[64,2048]{1,0:T(8,128)(2,1)S(1)}, bf16[64,2048]{1,0:T(8,128)(2,1)S(1)}, u32[]{:S(2)}, u32[]{:S(2)}) collective-permute-start(bf16[64,2048]{1,0:T(8,128)(2,1)S(1)} %get-tuple-element.77), channel_id=1, source_target_pairs={{0,2},{1,5},{2,0},{3,7},{4,6},{5,1},{6,4},{7,3},{8,10},{9,13},{10,... | collective-permute-start | bytes 786440 | tf_op jit(solution)/shard_map/ppermute | solution.py:251
  52.0 1.5 %collective-permute-start.18 = (bf16[64,2048]{1,0:T(8,128)(2,1)S(1)}, bf16[64,2048]{1,0:T(8,128)(2,1)S(1)}, u32[]{:S(2)}, u32[]{:S(2)}) collective-permute-start(bf16[64,2048]{1,0:T(8,128)(2,1)S(1)} %get-tuple-element.76), channel_id=1, source_target_pairs={{0,4},{1,3},{2,6},{3,1},{4,0},{5,7},{6,2},{7,5},{8,12},{9,11},{10,... | collective-permute-start | bytes 786440 | tf_op jit(solution)/shard_map/ppermute | solution.py:251
  53.5 2.6 %shard_map.84.refs_0_ = bf16[256,2048]{1,0:T(8,128)(2,1)S(1)} custom-call(bf16[64,2176]{1,0:T(8,128)(2,1)S(1)} %copy-done.3, bf16[64,2176]{1,0:T(8,128)(2,1)S(1)} %collective-permute-done.refs_1_.refs_0_, bf16[64,2176]{1,0:T(8,128)(2,1)S(1)} %collective-permute-done.2.refs_2_.refs_1_, bf16[64,2176]{1,0:T(8,128)(2,1)S(1)} %collective-permute-done.3.refs_3_.refs_2_, ...), custom_call_target="tpu_custom_call" | custom-call | flops 1 | bytes 1 | tf_op jit(solution)/shard_map/pallas_call | solution.py:226
  56.5 2.0 %collective-permute-start.22 = (bf16[64,2048]{1,0:T(8,128)(2,1)S(1)}, bf16[64,2048]{1,0:T(8,128)(2,1)S(1)}, u32[]{:S(2)}, u32[]{:S(2)}) collective-permute-start(bf16[64,2048]{1,0:T(8,128)(2,1)S(1)} %shard_map.93), channel_id=1, source_target_pairs={{0,2},{1,5},{2,0},{3,7},{4,6},{5,1},{6,4},{7,3},{8,10},{9,13},{10,... | collective-permute-start | bytes 786440 | tf_op jit(solution)/shard_map/ppermute | solution.py:251
  58.9 2.5 %collective-permute-start.21 = (bf16[64,2048]{1,0:T(8,128)(2,1)S(1)}, bf16[64,2048]{1,0:T(8,128)(2,1)S(1)}, u32[]{:S(2)}, u32[]{:S(2)}) collective-permute-start(bf16[64,2048]{1,0:T(8,128)(2,1)S(1)} %shard_map.94), channel_id=1, source_target_pairs={{0,8},{1,9},{2,10},{3,11},{4,12},{5,13},{6,14},{7,15},{8,0},{9,1},... | collective-permute-start | bytes 786440 | tf_op jit(solution)/shard_map/ppermute | solution.py:251
  64.2 1.5 %collective-permute-done.22.refs_2_ = bf16[64,2048]{1,0:T(8,128)(2,1)S(1)} collective-permute-done((bf16[64,2048]{1,0:T(8,128)(2,1)S(1)}, bf16[64,2048]{1,0:T(8,128)(2,1)S(1)}, u32[]{:S(2)}, u32[]{:S(2)}) %collective-permute-start.22) | collective-permute-done | bytes 262176 | tf_op jit(solution)/shard_map/ppermute | solution.py:251
  65.9 8.6 %collective-permute-done.21.refs_1_ = bf16[64,2048]{1,0:T(8,128)(2,1)S(1)} collective-permute-done((bf16[64,2048]{1,0:T(8,128)(2,1)S(1)}, bf16[64,2048]{1,0:T(8,128)(2,1)S(1)}, u32[]{:S(2)}, u32[]{:S(2)}) %collective-permute-start.21) | collective-permute-done | bytes 262176 | tf_op jit(solution)/shard_map/ppermute | solution.py:251
  (49 shorter events, 13.4 us)
Async XLA Ops:
  1.9 13.5 %collective-permute-start.1 = (bf16[64,2176]{1,0:T(8,128)(2,1)}, bf16[64,2176]{1,0:T(8,128)(2,1)S(1)}, u32[]{:S(2)}, u32[]{:S(2)}) collective-permute-start(bf16[64,2176]{1,0:T(8,128)(2,1)} %shard_map.82.refs_0_), channel_id=1, source_target_pairs={{0,1},{1,0},{2,3},{3,2},{4,5},{5,4},{6,7},{7,6},{8,9},{9,8},{10,11... | collective-permute-start | bytes 835592 | tf_op jit(solution)/shard_map/ppermute | solution.py:255
  2.4 17.2 %collective-permute-start = (bf16[64,2176]{1,0:T(8,128)(2,1)}, bf16[64,2176]{1,0:T(8,128)(2,1)S(1)}, u32[]{:S(2)}, u32[]{:S(2)}) collective-permute-start(bf16[64,2176]{1,0:T(8,128)(2,1)} %shard_map.82.refs_0_), channel_id=1, source_target_pairs={{0,8},{1,9},{2,10},{3,11},{4,12},{5,13},{6,14},{7,15},{8,0},{9,1},... | collective-permute-start | bytes 835592 | tf_op jit(solution)/shard_map/ppermute | solution.py:251
  6.0 13.6 %collective-permute-start.3 = (bf16[64,2176]{1,0:T(8,128)(2,1)}, bf16[64,2176]{1,0:T(8,128)(2,1)S(1)}, u32[]{:S(2)}, u32[]{:S(2)}) collective-permute-start(bf16[64,2176]{1,0:T(8,128)(2,1)} %shard_map.82.refs_0_), channel_id=1, source_target_pairs={{0,2},{1,5},{2,0},{3,7},{4,6},{5,1},{6,4},{7,3},{8,10},{9,13},{10,... | collective-permute-start | bytes 835592 | tf_op jit(solution)/shard_map/ppermute | solution.py:251
  7.5 12.3 %collective-permute-start.2 = (bf16[64,2176]{1,0:T(8,128)(2,1)}, bf16[64,2176]{1,0:T(8,128)(2,1)S(1)}, u32[]{:S(2)}, u32[]{:S(2)}) collective-permute-start(bf16[64,2176]{1,0:T(8,128)(2,1)} %shard_map.82.refs_0_), channel_id=1, source_target_pairs={{0,4},{1,3},{2,6},{3,1},{4,0},{5,7},{6,2},{7,5},{8,12},{9,11},{10,... | collective-permute-start | bytes 835592 | tf_op jit(solution)/shard_map/ppermute | solution.py:251
  19.9 3.7 %collective-permute-start.5 = (bf16[192,2176]{1,0:T(8,128)(2,1)S(1)}, bf16[192,2176]{1,0:T(8,128)(2,1)S(1)}, u32[]{:S(2)}, u32[]{:S(2)}) collective-permute-start(bf16[192,2176]{1,0:T(8,128)(2,1)S(1)} %shard_map.85), channel_id=1, source_target_pairs={{0,1},{1,0},{2,3},{3,2},{4,5},{5,4},{6,7},{7,6},{8,9},{9,8},{10,11... | collective-permute-start | bytes 2506760 | tf_op jit(solution)/shard_map/ppermute | solution.py:255
  19.9 8.9 %collective-permute-start.4 = (bf16[64,2176]{1,0:T(8,128)(2,1)S(1)}, bf16[64,2176]{1,0:T(8,128)(2,1)S(1)}, u32[]{:S(2)}, u32[]{:S(2)}) collective-permute-start(bf16[64,2176]{1,0:T(8,128)(2,1)S(1)} %collective-permute-done.refs_1_.refs_0_), channel_id=1, source_target_pairs={{0,4},{1,3},{2,6},{3,1},{4,0},{5,7},{6,2},{7,5},{8,12},{9,11},{10,... | collective-permute-start | bytes 835592 | tf_op jit(solution)/shard_map/ppermute | solution.py:251
  21.5 10.8 %collective-permute-start.6 = (bf16[64,2176]{1,0:T(8,128)(2,1)S(1)}, bf16[64,2176]{1,0:T(8,128)(2,1)S(1)}, u32[]{:S(2)}, u32[]{:S(2)}) collective-permute-start(bf16[64,2176]{1,0:T(8,128)(2,1)S(1)} %collective-permute-done.refs_1_.refs_0_), channel_id=1, source_target_pairs={{0,2},{1,5},{2,0},{3,7},{4,6},{5,1},{6,4},{7,3},{8,10},{9,13},{10,... | collective-permute-start | bytes 835592 | tf_op jit(solution)/shard_map/ppermute | solution.py:251
  23.0 9.0 %collective-permute-start.7 = (bf16[64,2176]{1,0:T(8,128)(2,1)S(1)}, bf16[64,2176]{1,0:T(8,128)(2,1)S(1)}, u32[]{:S(2)}, u32[]{:S(2)}) collective-permute-start(bf16[64,2176]{1,0:T(8,128)(2,1)S(1)} %collective-permute-done.2.refs_2_.refs_1_), channel_id=1, source_target_pairs={{0,2},{1,5},{2,0},{3,7},{4,6},{5,1},{6,4},{7,3},{8,10},{9,13},{10,... | collective-permute-start | bytes 835592 | tf_op jit(solution)/shard_map/ppermute | solution.py:251
  28.8 6.7 %collective-permute-start.8 = (bf16[64,2176]{1,0:T(8,128)(2,1)S(1)}, bf16[64,2176]{1,0:T(8,128)(2,1)S(1)}, u32[]{:S(2)}, u32[]{:S(2)}) collective-permute-start(bf16[64,2176]{1,0:T(8,128)(2,1)S(1)} %collective-permute-done.4.refs_0_.refs_6_), channel_id=1, source_target_pairs={{0,2},{1,5},{2,0},{3,7},{4,6},{5,1},{6,4},{7,3},{8,10},{9,13},{10,... | collective-permute-start | bytes 835592 | tf_op jit(solution)/shard_map/ppermute | solution.py:251
  32.0 5.5 %collective-permute-start.10 = (bf16[64,2176]{1,0:T(8,128)(2,1)S(1)}, bf16[64,2176]{1,0:T(8,128)(2,1)S(1)}, u32[]{:S(2)}, u32[]{:S(2)}) collective-permute-start(bf16[64,2176]{1,0:T(8,128)(2,1)S(1)} %collective-permute-done.7.refs_2_.refs_7_), channel_id=1, source_target_pairs={{0,1},{1,0},{2,3},{3,2},{4,5},{5,4},{6,7},{7,6},{8,9},{9,8},{10,11... | collective-permute-start | bytes 835592 | tf_op jit(solution)/shard_map/ppermute | solution.py:255
  32.3 5.1 %collective-permute-start.11 = (bf16[64,2176]{1,0:T(8,128)(2,1)S(1)}, bf16[64,2176]{1,0:T(8,128)(2,1)S(1)}, u32[]{:S(2)}, u32[]{:S(2)}) collective-permute-start(bf16[64,2176]{1,0:T(8,128)(2,1)S(1)} %collective-permute-done.6.refs_1_.refs_4_), channel_id=1, source_target_pairs={{0,1},{1,0},{2,3},{3,2},{4,5},{5,4},{6,7},{7,6},{8,9},{9,8},{10,11... | collective-permute-start | bytes 835592 | tf_op jit(solution)/shard_map/ppermute | solution.py:255
  32.5 5.0 %collective-permute-start.9 = (bf16[64,2176]{1,0:T(8,128)(2,1)S(1)}, bf16[64,2176]{1,0:T(8,128)(2,1)S(1)}, u32[]{:S(2)}, u32[]{:S(2)}) collective-permute-start(bf16[64,2176]{1,0:T(8,128)(2,1)S(1)} %collective-permute-done.4.refs_0_.refs_6_), channel_id=1, source_target_pairs={{0,1},{1,0},{2,3},{3,2},{4,5},{5,4},{6,7},{7,6},{8,9},{9,8},{10,11... | collective-permute-start | bytes 835592 | tf_op jit(solution)/shard_map/ppermute | solution.py:255
  35.5 1.9 %collective-permute-start.12 = (bf16[64,2176]{1,0:T(8,128)(2,1)S(1)}, bf16[64,2176]{1,0:T(8,128)(2,1)S(1)}, u32[]{:S(2)}, u32[]{:S(2)}) collective-permute-start(bf16[64,2176]{1,0:T(8,128)(2,1)S(1)} %collective-permute-done.8.refs_0_.refs_5_), channel_id=1, source_target_pairs={{0,1},{1,0},{2,3},{3,2},{4,5},{5,4},{6,7},{7,6},{8,9},{9,8},{10,11... | collective-permute-start | bytes 835592 | tf_op jit(solution)/shard_map/ppermute | solution.py:255
  37.4 3.2 %copy-start.3 = (bf16[64,2176]{1,0:T(8,128)(2,1)S(1)}, bf16[64,2176]{1,0:T(8,128)(2,1)}, u32[]{:S(2)}) copy-start(bf16[64,2176]{1,0:T(8,128)(2,1)} %shard_map.82.refs_0_) | copy-start | bytes 835588
  40.2 2.5 %collective-permute-start.14 = (bf16[128,2048]{1,0:T(8,128)(2,1)S(1)}, bf16[128,2048]{1,0:T(8,128)(2,1)S(1)}, u32[]{:S(2)}, u32[]{:S(2)}) collective-permute-start(bf16[128,2048]{1,0:T(8,128)(2,1)S(1)} %get-tuple-element.67), channel_id=1, source_target_pairs={{0,1},{1,0},{2,3},{3,2},{4,5},{5,4},{6,7},{7,6},{8,9},{9,8},{10,11... | collective-permute-start | bytes 1572872 | tf_op jit(solution)/shard_map/ppermute | solution.py:255
  42.6 2.5 %collective-permute-start.13 = (bf16[128,2048]{1,0:T(8,128)(2,1)S(1)}, bf16[128,2048]{1,0:T(8,128)(2,1)S(1)}, u32[]{:S(2)}, u32[]{:S(2)}) collective-permute-start(bf16[128,2048]{1,0:T(8,128)(2,1)S(1)} %get-tuple-element.65), channel_id=1, source_target_pairs={{0,1},{1,0},{2,3},{3,2},{4,5},{5,4},{6,7},{7,6},{8,9},{9,8},{10,11... | collective-permute-start | bytes 1572872 | tf_op jit(solution)/shard_map/ppermute | solution.py:255
  43.1 6.4 %collective-permute-start.15 = (bf16[64,2048]{1,0:T(8,128)(2,1)S(1)}, bf16[64,2048]{1,0:T(8,128)(2,1)S(1)}, u32[]{:S(2)}, u32[]{:S(2)}) collective-permute-start(bf16[64,2048]{1,0:T(8,128)(2,1)S(1)} %get-tuple-element.69), channel_id=1, source_target_pairs={{0,2},{1,5},{2,0},{3,7},{4,6},{5,1},{6,4},{7,3},{8,10},{9,13},{10,... | collective-permute-start | bytes 786440 | tf_op jit(solution)/shard_map/ppermute | solution.py:251
  49.9 6.5 %collective-permute-start.16 = (bf16[256,2048]{1,0:T(8,128)(2,1)S(1)}, bf16[256,2048]{1,0:T(8,128)(2,1)S(1)}, u32[]{:S(2)}, u32[]{:S(2)}) collective-permute-start(bf16[256,2048]{1,0:T(8,128)(2,1)S(1)} %shard_map.86), channel_id=1, source_target_pairs={{0,1},{1,0},{2,3},{3,2},{4,5},{5,4},{6,7},{7,6},{8,9},{9,8},{10,11... | collective-permute-start | bytes 3145736 | tf_op jit(solution)/shard_map/ppermute | solution.py:255
  49.9 8.6 %collective-permute-start.19 = (bf16[64,2048]{1,0:T(8,128)(2,1)S(1)}, bf16[64,2048]{1,0:T(8,128)(2,1)S(1)}, u32[]{:S(2)}, u32[]{:S(2)}) collective-permute-start(bf16[64,2048]{1,0:T(8,128)(2,1)S(1)} %get-tuple-element.77), channel_id=1, source_target_pairs={{0,2},{1,5},{2,0},{3,7},{4,6},{5,1},{6,4},{7,3},{8,10},{9,13},{10,... | collective-permute-start | bytes 786440 | tf_op jit(solution)/shard_map/ppermute | solution.py:251
  52.0 6.7 %collective-permute-start.18 = (bf16[64,2048]{1,0:T(8,128)(2,1)S(1)}, bf16[64,2048]{1,0:T(8,128)(2,1)S(1)}, u32[]{:S(2)}, u32[]{:S(2)}) collective-permute-start(bf16[64,2048]{1,0:T(8,128)(2,1)S(1)} %get-tuple-element.76), channel_id=1, source_target_pairs={{0,4},{1,3},{2,6},{3,1},{4,0},{5,7},{6,2},{7,5},{8,12},{9,11},{10,... | collective-permute-start | bytes 786440 | tf_op jit(solution)/shard_map/ppermute | solution.py:251
  56.2 6.4 %collective-permute-start.17 = (bf16[64,2048]{1,0:T(8,128)(2,1)S(1)}, bf16[64,2048]{1,0:T(8,128)(2,1)S(1)}, u32[]{:S(2)}, u32[]{:S(2)}) collective-permute-start(bf16[64,2048]{1,0:T(8,128)(2,1)S(1)} %get-tuple-element.75), channel_id=1, source_target_pairs={{0,2},{1,5},{2,0},{3,7},{4,6},{5,1},{6,4},{7,3},{8,10},{9,13},{10,... | collective-permute-start | bytes 786440 | tf_op jit(solution)/shard_map/ppermute | solution.py:251
  56.5 9.2 %collective-permute-start.22 = (bf16[64,2048]{1,0:T(8,128)(2,1)S(1)}, bf16[64,2048]{1,0:T(8,128)(2,1)S(1)}, u32[]{:S(2)}, u32[]{:S(2)}) collective-permute-start(bf16[64,2048]{1,0:T(8,128)(2,1)S(1)} %shard_map.93), channel_id=1, source_target_pairs={{0,2},{1,5},{2,0},{3,7},{4,6},{5,1},{6,4},{7,3},{8,10},{9,13},{10,... | collective-permute-start | bytes 786440 | tf_op jit(solution)/shard_map/ppermute | solution.py:251
  58.9 15.7 %collective-permute-start.21 = (bf16[64,2048]{1,0:T(8,128)(2,1)S(1)}, bf16[64,2048]{1,0:T(8,128)(2,1)S(1)}, u32[]{:S(2)}, u32[]{:S(2)}) collective-permute-start(bf16[64,2048]{1,0:T(8,128)(2,1)S(1)} %shard_map.94), channel_id=1, source_target_pairs={{0,8},{1,9},{2,10},{3,11},{4,12},{5,13},{6,14},{7,15},{8,0},{9,1},... | collective-permute-start | bytes 786440 | tf_op jit(solution)/shard_map/ppermute | solution.py:251
  62.8 11.8 %collective-permute-start.20 = (bf16[64,2048]{1,0:T(8,128)(2,1)S(1)}, bf16[64,2048]{1,0:T(8,128)(2,1)S(1)}, u32[]{:S(2)}, u32[]{:S(2)}) collective-permute-start(bf16[64,2048]{1,0:T(8,128)(2,1)S(1)} %shard_map.95), channel_id=1, source_target_pairs={{0,4},{1,3},{2,6},{3,1},{4,0},{5,7},{6,2},{7,5},{8,12},{9,11},{10,... | collective-permute-start | bytes 786440 | tf_op jit(solution)/shard_map/ppermute | solution.py:251
  (4 other events, 8.9 us)

commit v17 on v11

--- a/solution.py
+++ b/solution.py
@@ -195,7 +195,7 @@
     )(*arrays)
 
 
-FF_TILE, OUT_TILE = 256, 512
+FF_TILE, OUT_TILE = 768, 1024
 
 
 def expert_kernel(pieces, *refs):

time: 72 us -> 72 us (level)
  no operation moved by 1% of the time
where the time goes in v17:
time: 72 us; the launch traced here: 71.7 us
  starting transfers between devices  23.9 us (33%)
  waiting for transfers between devices  23.2 us (32%)
  Pallas kernels  18.7 us (26%)
  local copies, waits for them, and re-layouts  5.68 us (8%)
    ppermute x14, waiting for transfers between devices, send(): return lax.ppermute(array, ('ep', 'sub'), pairs)  22.8 us
    ppermute x14, starting transfers between devices, send(): return lax.ppermute(array, ('ep', 'sub'), pairs)  21.3 us
    pallas_call x5, Pallas kernels, expert(): pl.pallas_call(functools.partial(expert_kernel, pieces), in_specs=[pl.Blo...  11.8 us
    unnamed x10, local copies, waits for them, and re-layouts  5.68 us
    ppermute x9, starting transfers between devices, cross(): return lax.ppermute(array, 'sub', [(0, 1), (1, 0)])  2.55 us
    pallas_call x8, Pallas kernels, combine(): pl.pallas_call(functools.partial(combine_kernel, rows, sums, len(arrays))...  2.37 us
    pallas_call x1, Pallas kernels, prepare(): pl.pallas_call(prepare_kernel, in_specs=[pl.BlockSpec(memory_space=pltpu....  1.95 us
    pallas_call x1, Pallas kernels, weigh(): pl.pallas_call(functools.partial(weigh_kernel, top, tok_rows), in_specs=[...  1.89 us
  transfers between devices with their start and end apart: 23, of which 10 were waited for; matrix products, arithmetic and copies ran while one was open for 0% of the time, Pallas kernels for 19%

profile of v17, /device:TPU:0, one launch (start us, length us, event | category | flops | bytes accessed | tf_op | source)
XLA Modules:
  0.0 71.7 jit_solution(11429809914151119927)
XLA Ops:
  0.0 1.9 %shard_map.82.refs_0_ = bf16[64,2176]{1,0:T(8,128)(2,1)} custom-call(s32[1]{0:T(128)} %bitcast.me_ref, bf16[64,2048]{1,0:T(8,128)(2,1)} %tokens_ref.1, s32[8,64]{1,0:T(8,128)} %bitcast.4, f32[8,64]{1,0:T(8,128)} %bitcast.5, s32[1,64]{1,0:T(1,128)} %bitcast.6), custom_call_target="tpu_custom_call" | custom-call | tf_op jit(solution)/shard_map/pallas_call | solution.py:48
  2.4 3.6 %collective-permute-start = (bf16[64,2176]{1,0:T(8,128)(2,1)}, bf16[64,2176]{1,0:T(8,128)(2,1)S(1)}, u32[]{:S(2)}, u32[]{:S(2)}) collective-permute-start(bf16[64,2176]{1,0:T(8,128)(2,1)} %shard_map.82.refs_0_), channel_id=1, source_target_pairs={{0,8},{1,9},{2,10},{3,11},{4,12},{5,13},{6,14},{7,15},{8,0},{9,1},... | collective-permute-start | bytes 835592 | tf_op jit(solution)/shard_map/ppermute | solution.py:251
  6.0 1.5 %collective-permute-start.3 = (bf16[64,2176]{1,0:T(8,128)(2,1)}, bf16[64,2176]{1,0:T(8,128)(2,1)S(1)}, u32[]{:S(2)}, u32[]{:S(2)}) collective-permute-start(bf16[64,2176]{1,0:T(8,128)(2,1)} %shard_map.82.refs_0_), channel_id=1, source_target_pairs={{0,2},{1,5},{2,0},{3,7},{4,6},{5,1},{6,4},{7,3},{8,10},{9,13},{10,... | collective-permute-start | bytes 835592 | tf_op jit(solution)/shard_map/ppermute | solution.py:251
  7.5 1.6 %collective-permute-start.2 = (bf16[64,2176]{1,0:T(8,128)(2,1)}, bf16[64,2176]{1,0:T(8,128)(2,1)S(1)}, u32[]{:S(2)}, u32[]{:S(2)}) collective-permute-start(bf16[64,2176]{1,0:T(8,128)(2,1)} %shard_map.82.refs_0_), channel_id=1, source_target_pairs={{0,4},{1,3},{2,6},{3,1},{4,0},{5,7},{6,2},{7,5},{8,12},{9,11},{10,... | collective-permute-start | bytes 835592 | tf_op jit(solution)/shard_map/ppermute | solution.py:251
  9.1 1.9 %copy-done = bf16[1,2048,768]{2,1,0:T(8,128)(2,1)S(1)} copy-done((bf16[1,2048,768]{2,1,0:T(8,128)(2,1)S(1)}, bf16[1,2048,768]{2,1,0:T(8,128)(2,1)}, u32[]{:S(2)}) %copy-start) | copy-done | bytes 3145752
  11.0 1.9 %copy-done.1 = bf16[1,2048,768]{2,1,0:T(8,128)(2,1)S(1)} copy-done((bf16[1,2048,768]{2,1,0:T(8,128)(2,1)S(1)}, bf16[1,2048,768]{2,1,0:T(8,128)(2,1)}, u32[]{:S(2)}) %copy-start.1) | copy-done | bytes 3145752
  12.9 1.9 %copy-done.2 = bf16[1,768,2048]{2,1,0:T(8,128)(2,1)S(1)} copy-done((bf16[1,768,2048]{2,1,0:T(8,128)(2,1)S(1)}, bf16[1,768,2048]{2,1,0:T(8,128)(2,1)}, u32[]{:S(2)}) %copy-start.2) | copy-done | bytes 3145752
  15.4 4.2 %collective-permute-done.refs_1_.refs_0_ = bf16[64,2176]{1,0:T(8,128)(2,1)S(1)} collective-permute-done((bf16[64,2176]{1,0:T(8,128)(2,1)}, bf16[64,2176]{1,0:T(8,128)(2,1)S(1)}, u32[]{:S(2)}, u32[]{:S(2)}) %collective-permute-start) | collective-permute-done | bytes 278560 | tf_op jit(solution)/shard_map/ppermute | solution.py:251
  19.9 1.6 %collective-permute-start.4 = (bf16[64,2176]{1,0:T(8,128)(2,1)S(1)}, bf16[64,2176]{1,0:T(8,128)(2,1)S(1)}, u32[]{:S(2)}, u32[]{:S(2)}) collective-permute-start(bf16[64,2176]{1,0:T(8,128)(2,1)S(1)} %collective-permute-done.refs_1_.refs_0_), channel_id=1, source_target_pairs={{0,4},{1,3},{2,6},{3,1},{4,0},{5,7},{6,2},{7,5},{8,12},{9,11},{10,... | collective-permute-start | bytes 835592 | tf_op jit(solution)/shard_map/ppermute | solution.py:251
  23.5 2.6 %shard_map.86 = bf16[256,2048]{1,0:T(8,128)(2,1)S(1)} custom-call(bf16[64,2176]{1,0:T(8,128)(2,1)S(1)} %collective-permute-done.1.refs_0_.refs_8_, bf16[192,2176]{1,0:T(8,128)(2,1)S(1)} %collective-permute-done.5.refs_1_.refs_9_, bf16[1,2048,768]{2,1,0:T(8,128)(2,1)S(1)} %get-tuple-element.48.refs_4_.refs_2_.refs_3_.refs_1_, ...), custom_call_target="tpu_custom_call" | custom-call | flops 1 | bytes 1 | tf_op jit(solution)/shard_map/pallas_call | solution.py:226
  26.1 2.7 %collective-permute-done.4.refs_0_.refs_6_ = bf16[64,2176]{1,0:T(8,128)(2,1)S(1)} collective-permute-done((bf16[64,2176]{1,0:T(8,128)(2,1)S(1)}, bf16[64,2176]{1,0:T(8,128)(2,1)S(1)}, u32[]{:S(2)}, u32[]{:S(2)}) %collective-permute-start.4) | collective-permute-done | bytes 278560 | tf_op jit(solution)/shard_map/ppermute | solution.py:251
  28.8 2.2 %collective-permute-start.8 = (bf16[64,2176]{1,0:T(8,128)(2,1)S(1)}, bf16[64,2176]{1,0:T(8,128)(2,1)S(1)}, u32[]{:S(2)}, u32[]{:S(2)}) collective-permute-start(bf16[64,2176]{1,0:T(8,128)(2,1)S(1)} %collective-permute-done.4.refs_0_.refs_6_), channel_id=1, source_target_pairs={{0,2},{1,5},{2,0},{3,7},{4,6},{5,1},{6,4},{7,3},{8,10},{9,13},{10,... | collective-permute-start | bytes 835592 | tf_op jit(solution)/shard_map/ppermute | solution.py:251
  32.8 2.1 %shard_map.87.refs_0_ = bf16[192,2048]{1,0:T(8,128)(2,1)S(1)} custom-call(bf16[64,2176]{1,0:T(8,128)(2,1)S(1)} %collective-permute-done.4.refs_0_.refs_6_, bf16[64,2176]{1,0:T(8,128)(2,1)S(1)} %collective-permute-done.6.refs_1_.refs_4_, bf16[64,2176]{1,0:T(8,128)(2,1)S(1)} %collective-permute-done.7.refs_2_.refs_7_, ...), custom_call_target="tpu_custom_call" | custom-call | flops 1 | bytes 1 | tf_op jit(solution)/shard_map/pallas_call | solution.py:226
  35.6 1.8 %shard_map.88.refs_1_ = bf16[64,2048]{1,0:T(8,128)(2,1)S(1)} custom-call(bf16[64,2176]{1,0:T(8,128)(2,1)S(1)} %collective-permute-done.8.refs_0_.refs_5_, bf16[1,2048,768]{2,1,0:T(8,128)(2,1)S(1)} %get-tuple-element.48.refs_4_.refs_2_.refs_3_.refs_1_, bf16[1,2048,768]{2,1,0:T(8,128)(2,1)S(1)} %get-tuple-element.49.refs_5_.refs_3_.refs_4_.refs_2_, ...), custom_call_target="tpu_custom_call" | custom-call | flops 1 | bytes 1 | tf_op jit(solution)/shard_map/pallas_call | solution.py:226
  37.5 2.6 %shard_map.90 = (bf16[128,2048]{1,0:T(8,128)(2,1)S(1)}, bf16[128,2048]{1,0:T(8,128)(2,1)S(1)}) custom-call(bf16[64,2176]{1,0:T(8,128)(2,1)S(1)} %collective-permute-done.9.refs_10_.refs_0_, bf16[64,2176]{1,0:T(8,128)(2,1)S(1)} %collective-permute-done.10.refs_11_.refs_1_, bf16[64,2176]{1,0:T(8,128)(2,1)S(1)} %collective-permute-done.11.refs_12_.refs_2_, ...), custom_call_target="tpu_custom_call" | custom-call | flops 1 | bytes 1 | tf_op jit(solution)/shard_map/pallas_call | solution.py:226
  40.6 1.9 %shard_map.89.refs_3_.refs_2_.refs_4_ = f32[1024,128]{1,0:T(8,128)S(1)} custom-call(s32[1]{0:T(128)} %bitcast.me_ref, s32[16]{0:T(128)S(1)} %copy-done.4, bf16[64,2176]{1,0:T(8,128)(2,1)S(1)} %copy-done.3, bf16[64,2176]{1,0:T(8,128)(2,1)S(1)} %collective-permute-done.refs_1_.refs_0_, bf16[64,2176]{1,0:T(8,128)(2,1)S(1)} %collective-permute-done.2.refs_2_.refs_1_, ...), custom_call_target="tpu_custom_call" | custom-call | flops 1 | bytes 1 | tf_op jit(solution)/shard_map/pallas_call | solution.py:114
  43.5 2.1 %collective-permute-start.15 = (bf16[64,2048]{1,0:T(8,128)(2,1)S(1)}, bf16[64,2048]{1,0:T(8,128)(2,1)S(1)}, u32[]{:S(2)}, u32[]{:S(2)}) collective-permute-start(bf16[64,2048]{1,0:T(8,128)(2,1)S(1)} %get-tuple-element.69), channel_id=1, source_target_pairs={{0,2},{1,5},{2,0},{3,7},{4,6},{5,1},{6,4},{7,3},{8,10},{9,13},{10,... | collective-permute-start | bytes 786440 | tf_op jit(solution)/shard_map/ppermute | solution.py:251
  46.0 3.9 %collective-permute-done.15.refs_2_ = bf16[64,2048]{1,0:T(8,128)(2,1)S(1)} collective-permute-done((bf16[64,2048]{1,0:T(8,128)(2,1)S(1)}, bf16[64,2048]{1,0:T(8,128)(2,1)S(1)}, u32[]{:S(2)}, u32[]{:S(2)}) %collective-permute-start.15) | collective-permute-done | bytes 262176 | tf_op jit(solution)/shard_map/ppermute | solution.py:251
  50.3 1.6 %collective-permute-start.18 = (bf16[64,2048]{1,0:T(8,128)(2,1)S(1)}, bf16[64,2048]{1,0:T(8,128)(2,1)S(1)}, u32[]{:S(2)}, u32[]{:S(2)}) collective-permute-start(bf16[64,2048]{1,0:T(8,128)(2,1)S(1)} %get-tuple-element.74), channel_id=1, source_target_pairs={{0,4},{1,3},{2,6},{3,1},{4,0},{5,7},{6,2},{7,5},{8,12},{9,11},{10,... | collective-permute-start | bytes 786440 | tf_op jit(solution)/shard_map/ppermute | solution.py:251
  51.9 2.6 %shard_map.84.refs_0_ = bf16[256,2048]{1,0:T(8,128)(2,1)S(1)} custom-call(bf16[64,2176]{1,0:T(8,128)(2,1)S(1)} %copy-done.3, bf16[64,2176]{1,0:T(8,128)(2,1)S(1)} %collective-permute-done.refs_1_.refs_0_, bf16[64,2176]{1,0:T(8,128)(2,1)S(1)} %collective-permute-done.2.refs_2_.refs_1_, bf16[64,2176]{1,0:T(8,128)(2,1)S(1)} %collective-permute-done.3.refs_3_.refs_2_, ...), custom_call_target="tpu_custom_call" | custom-call | flops 1 | bytes 1 | tf_op jit(solution)/shard_map/pallas_call | solution.py:226
  54.5 2.1 %collective-permute-start.17 = (bf16[64,2048]{1,0:T(8,128)(2,1)S(1)}, bf16[64,2048]{1,0:T(8,128)(2,1)S(1)}, u32[]{:S(2)}, u32[]{:S(2)}) collective-permute-start(bf16[64,2048]{1,0:T(8,128)(2,1)S(1)} %get-tuple-element.73), channel_id=1, source_target_pairs={{0,2},{1,5},{2,0},{3,7},{4,6},{5,1},{6,4},{7,3},{8,10},{9,13},{10,... | collective-permute-start | bytes 786440 | tf_op jit(solution)/shard_map/ppermute | solution.py:251
  57.2 2.4 %collective-permute-start.21 = (bf16[64,2048]{1,0:T(8,128)(2,1)S(1)}, bf16[64,2048]{1,0:T(8,128)(2,1)S(1)}, u32[]{:S(2)}, u32[]{:S(2)}) collective-permute-start(bf16[64,2048]{1,0:T(8,128)(2,1)S(1)} %shard_map.94), channel_id=1, source_target_pairs={{0,8},{1,9},{2,10},{3,11},{4,12},{5,13},{6,14},{7,15},{8,0},{9,1},... | collective-permute-start | bytes 786440 | tf_op jit(solution)/shard_map/ppermute | solution.py:251
  61.7 2.9 %collective-permute-done.22.refs_2_ = bf16[64,2048]{1,0:T(8,128)(2,1)S(1)} collective-permute-done((bf16[64,2048]{1,0:T(8,128)(2,1)S(1)}, bf16[64,2048]{1,0:T(8,128)(2,1)S(1)}, u32[]{:S(2)}, u32[]{:S(2)}) %collective-permute-start.22) | collective-permute-done | bytes 262176 | tf_op jit(solution)/shard_map/ppermute | solution.py:251
  64.9 6.0 %collective-permute-done.21.refs_1_ = bf16[64,2048]{1,0:T(8,128)(2,1)S(1)} collective-permute-done((bf16[64,2048]{1,0:T(8,128)(2,1)S(1)}, bf16[64,2048]{1,0:T(8,128)(2,1)S(1)}, u32[]{:S(2)}, u32[]{:S(2)}) %collective-permute-start.21) | collective-permute-done | bytes 262176 | tf_op jit(solution)/shard_map/ppermute | solution.py:251
  (49 shorter events, 12.0 us)
Async XLA Ops:
  1.9 13.5 %collective-permute-start.1 = (bf16[64,2176]{1,0:T(8,128)(2,1)}, bf16[64,2176]{1,0:T(8,128)(2,1)S(1)}, u32[]{:S(2)}, u32[]{:S(2)}) collective-permute-start(bf16[64,2176]{1,0:T(8,128)(2,1)} %shard_map.82.refs_0_), channel_id=1, source_target_pairs={{0,1},{1,0},{2,3},{3,2},{4,5},{5,4},{6,7},{7,6},{8,9},{9,8},{10,11... | collective-permute-start | bytes 835592 | tf_op jit(solution)/shard_map/ppermute | solution.py:255
  2.4 17.2 %collective-permute-start = (bf16[64,2176]{1,0:T(8,128)(2,1)}, bf16[64,2176]{1,0:T(8,128)(2,1)S(1)}, u32[]{:S(2)}, u32[]{:S(2)}) collective-permute-start(bf16[64,2176]{1,0:T(8,128)(2,1)} %shard_map.82.refs_0_), channel_id=1, source_target_pairs={{0,8},{1,9},{2,10},{3,11},{4,12},{5,13},{6,14},{7,15},{8,0},{9,1},... | collective-permute-start | bytes 835592 | tf_op jit(solution)/shard_map/ppermute | solution.py:251
  6.0 13.6 %collective-permute-start.3 = (bf16[64,2176]{1,0:T(8,128)(2,1)}, bf16[64,2176]{1,0:T(8,128)(2,1)S(1)}, u32[]{:S(2)}, u32[]{:S(2)}) collective-permute-start(bf16[64,2176]{1,0:T(8,128)(2,1)} %shard_map.82.refs_0_), channel_id=1, source_target_pairs={{0,2},{1,5},{2,0},{3,7},{4,6},{5,1},{6,4},{7,3},{8,10},{9,13},{10,... | collective-permute-start | bytes 835592 | tf_op jit(solution)/shard_map/ppermute | solution.py:251
  7.5 12.3 %collective-permute-start.2 = (bf16[64,2176]{1,0:T(8,128)(2,1)}, bf16[64,2176]{1,0:T(8,128)(2,1)S(1)}, u32[]{:S(2)}, u32[]{:S(2)}) collective-permute-start(bf16[64,2176]{1,0:T(8,128)(2,1)} %shard_map.82.refs_0_), channel_id=1, source_target_pairs={{0,4},{1,3},{2,6},{3,1},{4,0},{5,7},{6,2},{7,5},{8,12},{9,11},{10,... | collective-permute-start | bytes 835592 | tf_op jit(solution)/shard_map/ppermute | solution.py:251
  19.9 3.7 %collective-permute-start.5 = (bf16[192,2176]{1,0:T(8,128)(2,1)S(1)}, bf16[192,2176]{1,0:T(8,128)(2,1)S(1)}, u32[]{:S(2)}, u32[]{:S(2)}) collective-permute-start(bf16[192,2176]{1,0:T(8,128)(2,1)S(1)} %shard_map.85), channel_id=1, source_target_pairs={{0,1},{1,0},{2,3},{3,2},{4,5},{5,4},{6,7},{7,6},{8,9},{9,8},{10,11... | collective-permute-start | bytes 2506760 | tf_op jit(solution)/shard_map/ppermute | solution.py:255
  19.9 8.9 %collective-permute-start.4 = (bf16[64,2176]{1,0:T(8,128)(2,1)S(1)}, bf16[64,2176]{1,0:T(8,128)(2,1)S(1)}, u32[]{:S(2)}, u32[]{:S(2)}) collective-permute-start(bf16[64,2176]{1,0:T(8,128)(2,1)S(1)} %collective-permute-done.refs_1_.refs_0_), channel_id=1, source_target_pairs={{0,4},{1,3},{2,6},{3,1},{4,0},{5,7},{6,2},{7,5},{8,12},{9,11},{10,... | collective-permute-start | bytes 835592 | tf_op jit(solution)/shard_map/ppermute | solution.py:251
  21.5 10.8 %collective-permute-start.6 = (bf16[64,2176]{1,0:T(8,128)(2,1)S(1)}, bf16[64,2176]{1,0:T(8,128)(2,1)S(1)}, u32[]{:S(2)}, u32[]{:S(2)}) collective-permute-start(bf16[64,2176]{1,0:T(8,128)(2,1)S(1)} %collective-permute-done.refs_1_.refs_0_), channel_id=1, source_target_pairs={{0,2},{1,5},{2,0},{3,7},{4,6},{5,1},{6,4},{7,3},{8,10},{9,13},{10,... | collective-permute-start | bytes 835592 | tf_op jit(solution)/shard_map/ppermute | solution.py:251
  23.0 9.0 %collective-permute-start.7 = (bf16[64,2176]{1,0:T(8,128)(2,1)S(1)}, bf16[64,2176]{1,0:T(8,128)(2,1)S(1)}, u32[]{:S(2)}, u32[]{:S(2)}) collective-permute-start(bf16[64,2176]{1,0:T(8,128)(2,1)S(1)} %collective-permute-done.2.refs_2_.refs_1_), channel_id=1, source_target_pairs={{0,2},{1,5},{2,0},{3,7},{4,6},{5,1},{6,4},{7,3},{8,10},{9,13},{10,... | collective-permute-start | bytes 835592 | tf_op jit(solution)/shard_map/ppermute | solution.py:251
  28.8 6.7 %collective-permute-start.8 = (bf16[64,2176]{1,0:T(8,128)(2,1)S(1)}, bf16[64,2176]{1,0:T(8,128)(2,1)S(1)}, u32[]{:S(2)}, u32[]{:S(2)}) collective-permute-start(bf16[64,2176]{1,0:T(8,128)(2,1)S(1)} %collective-permute-done.4.refs_0_.refs_6_), channel_id=1, source_target_pairs={{0,2},{1,5},{2,0},{3,7},{4,6},{5,1},{6,4},{7,3},{8,10},{9,13},{10,... | collective-permute-start | bytes 835592 | tf_op jit(solution)/shard_map/ppermute | solution.py:251
  32.0 5.5 %collective-permute-start.10 = (bf16[64,2176]{1,0:T(8,128)(2,1)S(1)}, bf16[64,2176]{1,0:T(8,128)(2,1)S(1)}, u32[]{:S(2)}, u32[]{:S(2)}) collective-permute-start(bf16[64,2176]{1,0:T(8,128)(2,1)S(1)} %collective-permute-done.7.refs_2_.refs_7_), channel_id=1, source_target_pairs={{0,1},{1,0},{2,3},{3,2},{4,5},{5,4},{6,7},{7,6},{8,9},{9,8},{10,11... | collective-permute-start | bytes 835592 | tf_op jit(solution)/shard_map/ppermute | solution.py:255
  32.3 5.1 %collective-permute-start.11 = (bf16[64,2176]{1,0:T(8,128)(2,1)S(1)}, bf16[64,2176]{1,0:T(8,128)(2,1)S(1)}, u32[]{:S(2)}, u32[]{:S(2)}) collective-permute-start(bf16[64,2176]{1,0:T(8,128)(2,1)S(1)} %collective-permute-done.6.refs_1_.refs_4_), channel_id=1, source_target_pairs={{0,1},{1,0},{2,3},{3,2},{4,5},{5,4},{6,7},{7,6},{8,9},{9,8},{10,11... | collective-permute-start | bytes 835592 | tf_op jit(solution)/shard_map/ppermute | solution.py:255
  32.5 5.0 %collective-permute-start.9 = (bf16[64,2176]{1,0:T(8,128)(2,1)S(1)}, bf16[64,2176]{1,0:T(8,128)(2,1)S(1)}, u32[]{:S(2)}, u32[]{:S(2)}) collective-permute-start(bf16[64,2176]{1,0:T(8,128)(2,1)S(1)} %collective-permute-done.4.refs_0_.refs_6_), channel_id=1, source_target_pairs={{0,1},{1,0},{2,3},{3,2},{4,5},{5,4},{6,7},{7,6},{8,9},{9,8},{10,11... | collective-permute-start | bytes 835592 | tf_op jit(solution)/shard_map/ppermute | solution.py:255
  35.5 1.9 %collective-permute-start.12 = (bf16[64,2176]{1,0:T(8,128)(2,1)S(1)}, bf16[64,2176]{1,0:T(8,128)(2,1)S(1)}, u32[]{:S(2)}, u32[]{:S(2)}) collective-permute-start(bf16[64,2176]{1,0:T(8,128)(2,1)S(1)} %collective-permute-done.8.refs_0_.refs_5_), channel_id=1, source_target_pairs={{0,1},{1,0},{2,3},{3,2},{4,5},{5,4},{6,7},{7,6},{8,9},{9,8},{10,11... | collective-permute-start | bytes 835592 | tf_op jit(solution)/shard_map/ppermute | solution.py:255
  37.4 3.2 %copy-start.3 = (bf16[64,2176]{1,0:T(8,128)(2,1)S(1)}, bf16[64,2176]{1,0:T(8,128)(2,1)}, u32[]{:S(2)}) copy-start(bf16[64,2176]{1,0:T(8,128)(2,1)} %shard_map.82.refs_0_) | copy-start | bytes 835588
  40.1 3.0 %collective-permute-start.14 = (bf16[128,2048]{1,0:T(8,128)(2,1)S(1)}, bf16[128,2048]{1,0:T(8,128)(2,1)S(1)}, u32[]{:S(2)}, u32[]{:S(2)}) collective-permute-start(bf16[128,2048]{1,0:T(8,128)(2,1)S(1)} %get-tuple-element.67), channel_id=1, source_target_pairs={{0,1},{1,0},{2,3},{3,2},{4,5},{5,4},{6,7},{7,6},{8,9},{9,8},{10,11... | collective-permute-start | bytes 1572872 | tf_op jit(solution)/shard_map/ppermute | solution.py:255
  42.5 14.1 %collective-permute-start.16 = (bf16[256,2048]{1,0:T(8,128)(2,1)S(1)}, bf16[256,2048]{1,0:T(8,128)(2,1)S(1)}, u32[]{:S(2)}, u32[]{:S(2)}) collective-permute-start(bf16[256,2048]{1,0:T(8,128)(2,1)S(1)} %shard_map.86), channel_id=1, source_target_pairs={{0,1},{1,0},{2,3},{3,2},{4,5},{5,4},{6,7},{7,6},{8,9},{9,8},{10,11... | collective-permute-start | bytes 3145736 | tf_op jit(solution)/shard_map/ppermute | solution.py:255
  42.7 3.3 %collective-permute-start.13 = (bf16[128,2048]{1,0:T(8,128)(2,1)S(1)}, bf16[128,2048]{1,0:T(8,128)(2,1)S(1)}, u32[]{:S(2)}, u32[]{:S(2)}) collective-permute-start(bf16[128,2048]{1,0:T(8,128)(2,1)S(1)} %get-tuple-element.65), channel_id=1, source_target_pairs={{0,1},{1,0},{2,3},{3,2},{4,5},{5,4},{6,7},{7,6},{8,9},{9,8},{10,11... | collective-permute-start | bytes 1572872 | tf_op jit(solution)/shard_map/ppermute | solution.py:255
  43.5 6.4 %collective-permute-start.15 = (bf16[64,2048]{1,0:T(8,128)(2,1)S(1)}, bf16[64,2048]{1,0:T(8,128)(2,1)S(1)}, u32[]{:S(2)}, u32[]{:S(2)}) collective-permute-start(bf16[64,2048]{1,0:T(8,128)(2,1)S(1)} %get-tuple-element.69), channel_id=1, source_target_pairs={{0,2},{1,5},{2,0},{3,7},{4,6},{5,1},{6,4},{7,3},{8,10},{9,13},{10,... | collective-permute-start | bytes 786440 | tf_op jit(solution)/shard_map/ppermute | solution.py:251
  45.6 11.3 %collective-permute-start.19 = (bf16[64,2048]{1,0:T(8,128)(2,1)S(1)}, bf16[64,2048]{1,0:T(8,128)(2,1)S(1)}, u32[]{:S(2)}, u32[]{:S(2)}) collective-permute-start(bf16[64,2048]{1,0:T(8,128)(2,1)S(1)} %get-tuple-element.75), channel_id=1, source_target_pairs={{0,2},{1,5},{2,0},{3,7},{4,6},{5,1},{6,4},{7,3},{8,10},{9,13},{10,... | collective-permute-start | bytes 786440 | tf_op jit(solution)/shard_map/ppermute | solution.py:251
  50.3 6.6 %collective-permute-start.18 = (bf16[64,2048]{1,0:T(8,128)(2,1)S(1)}, bf16[64,2048]{1,0:T(8,128)(2,1)S(1)}, u32[]{:S(2)}, u32[]{:S(2)}) collective-permute-start(bf16[64,2048]{1,0:T(8,128)(2,1)S(1)} %get-tuple-element.74), channel_id=1, source_target_pairs={{0,4},{1,3},{2,6},{3,1},{4,0},{5,7},{6,2},{7,5},{8,12},{9,11},{10,... | collective-permute-start | bytes 786440 | tf_op jit(solution)/shard_map/ppermute | solution.py:251
  54.5 6.4 %collective-permute-start.17 = (bf16[64,2048]{1,0:T(8,128)(2,1)S(1)}, bf16[64,2048]{1,0:T(8,128)(2,1)S(1)}, u32[]{:S(2)}, u32[]{:S(2)}) collective-permute-start(bf16[64,2048]{1,0:T(8,128)(2,1)S(1)} %get-tuple-element.73), channel_id=1, source_target_pairs={{0,2},{1,5},{2,0},{3,7},{4,6},{5,1},{6,4},{7,3},{8,10},{9,13},{10,... | collective-permute-start | bytes 786440 | tf_op jit(solution)/shard_map/ppermute | solution.py:251
  56.8 7.8 %collective-permute-start.22 = (bf16[64,2048]{1,0:T(8,128)(2,1)S(1)}, bf16[64,2048]{1,0:T(8,128)(2,1)S(1)}, u32[]{:S(2)}, u32[]{:S(2)}) collective-permute-start(bf16[64,2048]{1,0:T(8,128)(2,1)S(1)} %shard_map.93), channel_id=1, source_target_pairs={{0,2},{1,5},{2,0},{3,7},{4,6},{5,1},{6,4},{7,3},{8,10},{9,13},{10,... | collective-permute-start | bytes 786440 | tf_op jit(solution)/shard_map/ppermute | solution.py:251
  57.2 13.7 %collective-permute-start.21 = (bf16[64,2048]{1,0:T(8,128)(2,1)S(1)}, bf16[64,2048]{1,0:T(8,128)(2,1)S(1)}, u32[]{:S(2)}, u32[]{:S(2)}) collective-permute-start(bf16[64,2048]{1,0:T(8,128)(2,1)S(1)} %shard_map.94), channel_id=1, source_target_pairs={{0,8},{1,9},{2,10},{3,11},{4,12},{5,13},{6,14},{7,15},{8,0},{9,1},... | collective-permute-start | bytes 786440 | tf_op jit(solution)/shard_map/ppermute | solution.py:251
  61.2 9.8 %collective-permute-start.20 = (bf16[64,2048]{1,0:T(8,128)(2,1)S(1)}, bf16[64,2048]{1,0:T(8,128)(2,1)S(1)}, u32[]{:S(2)}, u32[]{:S(2)}) collective-permute-start(bf16[64,2048]{1,0:T(8,128)(2,1)S(1)} %shard_map.95), channel_id=1, source_target_pairs={{0,4},{1,3},{2,6},{3,1},{4,0},{5,7},{6,2},{7,5},{8,12},{9,11},{10,... | collective-permute-start | bytes 786440 | tf_op jit(solution)/shard_map/ppermute | solution.py:251
  (4 other events, 8.9 us)
